TPU v7x, 32 devices: a whole 2x2x4 slice. The times are simulated.
32 devices in a mesh: fsdp: 8 (over z, x), tp: 4 (over y, core).
Axes of the slice: x: 2, y: 2, z: 4, core: 2. Of those that a mesh axis runs over, the one named last changes fastest.
Arguments:
- inputs: bfloat16 [256, 16, 768], P('tp', 'fsdp'), may hold values from -6 to 6
- conditioning: bfloat16 [16, 768], P('fsdp'), may hold values from -6 to 6
- ada_weight: bfloat16 [768, 4608], P('fsdp'), may hold values from -0.21875 to 0.21875
- ada_bias: bfloat16 [4608], P('fsdp'), may hold values from -3 to 3
- query_key_value_weight: bfloat16 [768, 3, 768], P('fsdp', None, 'tp'), may hold values from -0.21875 to 0.21875
- qv_bias: bfloat16 [2, 768], P(None, 'fsdp'), may hold values from -3 to 3
- attention_output_weight: bfloat16 [768, 768], P('tp', 'fsdp'), may hold values from -0.875 to 0.875
- attention_output_bias: bfloat16 [768], P('fsdp'), may hold values from -3 to 3
- expand_weight: bfloat16 [768, 3072], P('fsdp', 'tp'), may hold values from -0.21875 to 0.21875
- hidden_layer_bias: bfloat16 [3072], P('fsdp'), may hold values from -3 to 3
- contract_weight: bfloat16 [3072, 768], P('tp', 'fsdp'), may hold values from -0.109375 to 0.109375
- contract_bias: bfloat16 [768], P('fsdp'), may hold values from -3 to 3
- out_cotangent: bfloat16 [256, 16, 768], P('tp', 'fsdp'), may hold values from -6 to 6
Outputs:
- output: bfloat16 [256, 16, 768], P('tp', 'fsdp')
- inputs_grad: float32 [256, 16, 768], P('tp', 'fsdp')
- cond_grad: float32 [16, 768], P('fsdp')
- ada_weight_grad: float32 [768, 4608], P('fsdp')
- ada_bias_grad: float32 [4608], P('fsdp')
- qkv_weight_grad: float32 [768, 3, 768], P('fsdp', None, 'tp')
- qv_bias_grad: float32 [2, 768], P(None, 'fsdp')
- proj_weight_grad: float32 [768, 768], P('tp', 'fsdp')
- proj_bias_grad: float32 [768], P('fsdp')
- fc1_weight_grad: float32 [768, 3072], P('fsdp', 'tp')
- fc1_bias_grad: float32 [3072], P('fsdp')
- fc2_weight_grad: float32 [3072, 768], P('tp', 'fsdp')
- fc2_bias_grad: float32 [768], P('fsdp')
All inputs are finite; a program needn't handle non-finite values.
Results may differ from a plain program's by a relative error of at most 0.019.
The roundings to bfloat16 on the way count: a program that leaves them out, or rounds other values in their place, can miss the bound.
Values may be sent and summed in bfloat16 or wider, within the bound.
No kernel may reach another device: no remote copies, remote signals or barrier semaphores. Data moves between devices by JAX's collectives and lax.ppermute only.
A program may use at most 64 MiB of HBM per device.

v0:
```python
import math

import jax
import jax.numpy as jnp
from jax import lax
from jax.sharding import PartitionSpec as P

HEAD = 64


EPS = 1e-06


def layer_norm(values_in):
    average = jnp.mean(values_in, axis=-1, keepdims=True)
    centered = values_in - average
    variance = jnp.mean(centered * centered, axis=-1, keepdims=True)
    return centered * lax.rsqrt(variance + EPS)


def modulate(values_in, shifts, scales):
    return layer_norm(values_in) * (1.0 + scales) + shifts


def gelu_tanh(values_in):
    return jax.nn.gelu(values_in, approximate=True)


def attention_scores(queries, key_rows):
    scores = jnp.einsum("slhe,tlhe->lhst", queries, key_rows, preferred_element_type=jnp.float32)
    return scores * (1.0 / math.sqrt(queries.shape[3]))


def shards(
    inputs,
    conditioning,
    ada_weight,
    ada_bias,
    query_key_value_weight,
    qv_bias,
    attention_output_weight,
    attention_output_bias,
    expand_weight,
    hidden_layer_bias,
    contract_weight,
    contract_bias,
    out_cotangent,
):
    tp_rank = lax.axis_index("tp")
    tp_count = lax.axis_size("tp")
    fsdp_rank = lax.axis_index("fsdp")
    latents = inputs.shape[1]
    width = inputs.shape[2]
    feat_rows = ada_weight.shape[0]
    head_cols = query_key_value_weight.shape[2]
    head_count = head_cols // HEAD
    hidden_cols = expand_weight.shape[1]
    cond_float = conditioning.astype(jnp.float32)
    cond_low = jax.nn.silu(cond_float).astype(jnp.bfloat16)
    gathered = (
        lax.all_gather(cond_low, "fsdp", axis=0, tiled=True),
        lax.all_gather(ada_bias, "fsdp", axis=0, tiled=True),
        lax.all_gather(query_key_value_weight, "fsdp", axis=0, tiled=True),
        lax.all_gather(qv_bias, "fsdp", axis=1, tiled=True),
        lax.all_gather(attention_output_weight, "fsdp", axis=1, tiled=True),
        lax.all_gather(attention_output_bias, "fsdp", axis=0, tiled=True),
        lax.all_gather(expand_weight, "fsdp", axis=0, tiled=True),
        lax.all_gather(hidden_layer_bias, "fsdp", axis=0, tiled=True),
        lax.all_gather(contract_weight, "fsdp", axis=1, tiled=True),
        lax.all_gather(contract_bias, "fsdp", axis=0, tiled=True),
    )
    (
        cond_all,
        ada_shift,
        query_key_value_full,
        qv_all,
        output_linear_full,
        proj_shift,
        first_linear_full,
        fc1_shift,
        second_linear_full,
        fc2_shift,
    ) = gathered
    cond_cols = lax.dynamic_slice_in_dim(cond_all, fsdp_rank * feat_rows, feat_rows, 1)
    mod_partial = jnp.dot(cond_cols, ada_weight, preferred_element_type=jnp.float32)
    mod_pre = lax.psum_scatter(mod_partial, "fsdp", scatter_dimension=0, tiled=True)
    modulation = (mod_pre + ada_shift.astype(jnp.float32)).reshape(latents, 6, width)
    shift_attn, scale_attn, gate_attn = (modulation[:, 0], modulation[:, 1], modulation[:, 2])
    shift_mlp, scale_mlp, gate_mlp = (modulation[:, 3], modulation[:, 4], modulation[:, 5])
    query_bias = lax.dynamic_slice_in_dim(
        qv_all[0].astype(jnp.float32), tp_rank * head_cols, head_cols, 0
    )
    value_bias = lax.dynamic_slice_in_dim(
        qv_all[1].astype(jnp.float32), tp_rank * head_cols, head_cols, 0
    )
    hidden_bias = lax.dynamic_slice_in_dim(
        fc1_shift.astype(jnp.float32), tp_rank * hidden_cols, hidden_cols, 0
    )
    residual_in = inputs.astype(jnp.float32)
    attention_normed_input = modulate(residual_in, shift_attn, scale_attn).astype(jnp.bfloat16)
    attention_full_rows = lax.all_gather(attention_normed_input, "tp", axis=0, tiled=True)
    positions = attention_full_rows.shape[0]
    attention_projected = jnp.einsum(
        "fqt,tbj->bfqj",
        attention_full_rows,
        query_key_value_full,
        preferred_element_type=jnp.float32,
    )
    queries = (
        (attention_projected[0] + query_bias)
        .astype(jnp.bfloat16)
        .reshape(positions, latents, head_count, HEAD)
    )
    key_rows = (
        attention_projected[1].astype(jnp.bfloat16).reshape(positions, latents, head_count, HEAD)
    )
    value_rows = (
        (attention_projected[2] + value_bias)
        .astype(jnp.bfloat16)
        .reshape(positions, latents, head_count, HEAD)
    )
    scores = attention_scores(queries, key_rows)
    top_score = jnp.max(scores, axis=-1, keepdims=True)
    log_total = top_score + jnp.log(jnp.sum(jnp.exp(scores - top_score), axis=-1, keepdims=True))
    probs_float = jnp.exp(scores - log_total)
    probs_low = probs_float.astype(jnp.bfloat16)
    attention_mixed = jnp.einsum(
        "lhst,tlhe->slhe", probs_low, value_rows, preferred_element_type=jnp.float32
    )
    attention_mixed = attention_mixed.reshape(positions, latents, head_cols).astype(jnp.bfloat16)
    local_row_count = attention_mixed
    attention_residual_path = lax.psum_scatter(
        jnp.einsum(
            "nbv,vr->nbr", local_row_count, output_linear_full, preferred_element_type=jnp.float32
        ).astype(jnp.bfloat16),
        "tp",
        scatter_dimension=0,
        tiled=True,
    ).astype(jnp.float32) + proj_shift.astype(jnp.float32)
    middle = residual_in + gate_attn * attention_residual_path
    perceptron_normed_input = modulate(middle, shift_mlp, scale_mlp).astype(jnp.bfloat16)
    perceptron_full_rows = lax.all_gather(perceptron_normed_input, "tp", axis=0, tiled=True)
    hidden_preactivation = (
        jnp.einsum(
            "wqg,gi->wqi",
            perceptron_full_rows,
            first_linear_full,
            preferred_element_type=jnp.float32,
        )
        + hidden_bias
    )
    hidden_activated = gelu_tanh(hidden_preactivation).astype(jnp.bfloat16)
    local_row_count = hidden_activated
    perceptron_residual_path = lax.psum_scatter(
        jnp.einsum(
            "zra,au->zru", local_row_count, second_linear_full, preferred_element_type=jnp.float32
        ).astype(jnp.bfloat16),
        "tp",
        scatter_dimension=0,
        tiled=True,
    ).astype(jnp.float32) + fc2_shift.astype(jnp.float32)
    output = (middle + gate_mlp * perceptron_residual_path).astype(jnp.bfloat16)
    cotangent = out_cotangent.astype(jnp.float32)
    grad_gate_mlp = jnp.sum(cotangent * perceptron_residual_path, axis=0)
    grad_mlp = (cotangent * gate_mlp).astype(jnp.bfloat16)
    grad_fc2_bias = jnp.sum(grad_mlp, axis=(0, 1), dtype=jnp.float32)
    perceptron_full_gradient = lax.all_gather(grad_mlp, "tp", axis=0, tiled=True)
    grad_fc2 = jnp.einsum(
        "yoz,yow->zw",
        hidden_activated,
        perceptron_full_gradient,
        preferred_element_type=jnp.float32,
    )
    activation_gradient = jnp.einsum(
        "peo,ko->pek",
        perceptron_full_gradient,
        second_linear_full,
        preferred_element_type=jnp.float32,
    )
    preactivation_gradient = jax.vjp(gelu_tanh, hidden_preactivation)[1](activation_gradient)[
        0
    ].astype(jnp.bfloat16)
    grad_fc1_bias = jnp.sum(preactivation_gradient, axis=(0, 1), dtype=jnp.float32)
    expand_gradient = jnp.einsum(
        "yix,yih->xh",
        perceptron_full_rows,
        preactivation_gradient,
        preferred_element_type=jnp.float32,
    )
    local_row_count = preactivation_gradient
    grad_mlp_input = lax.psum_scatter(
        jnp.einsum(
            "eiz,oz->eio", local_row_count, first_linear_full, preferred_element_type=jnp.float32
        ).astype(jnp.bfloat16),
        "tp",
        scatter_dimension=0,
        tiled=True,
    ).astype(jnp.float32)
    grad_middle_norm, grad_shift_mlp, grad_scale_mlp = jax.vjp(
        modulate, middle, shift_mlp, scale_mlp
    )[1](grad_mlp_input)
    grad_middle = cotangent + grad_middle_norm
    grad_gate_attn = jnp.sum(grad_middle * attention_residual_path, axis=0)
    grad_attn = (grad_middle * gate_attn).astype(jnp.bfloat16)
    grad_proj_bias = jnp.sum(grad_attn, axis=(0, 1), dtype=jnp.float32)
    attention_full_gradient = lax.all_gather(grad_attn, "tp", axis=0, tiled=True)
    grad_proj = jnp.einsum(
        "mon,moa->na", attention_mixed, attention_full_gradient, preferred_element_type=jnp.float32
    )
    grad_attended = jnp.einsum(
        "qfh,gh->qfg",
        attention_full_gradient,
        output_linear_full,
        preferred_element_type=jnp.float32,
    )
    grad_attended = grad_attended.astype(jnp.bfloat16).reshape(positions, latents, head_count, HEAD)
    again = jnp.exp(attention_scores(queries, key_rows) - log_total)
    grad_values = jnp.einsum(
        "lhst,slhe->tlhe",
        again.astype(jnp.bfloat16),
        grad_attended,
        preferred_element_type=jnp.float32,
    )
    grad_probs = jnp.einsum(
        "slhe,tlhe->lhst", grad_attended, value_rows, preferred_element_type=jnp.float32
    )
    grad_scores = (
        again * (grad_probs - jnp.sum(again * grad_probs, axis=-1, keepdims=True))
    ).astype(jnp.bfloat16)
    factor = 1.0 / math.sqrt(HEAD)
    grad_queries = (
        jnp.einsum("lhst,tlhe->slhe", grad_scores, key_rows, preferred_element_type=jnp.float32)
        * factor
    )
    grad_keys = (
        jnp.einsum("lhst,slhe->tlhe", grad_scores, queries, preferred_element_type=jnp.float32)
        * factor
    )
    query_key_value_gradient = (
        jnp.stack([grad_queries, grad_keys, grad_values])
        .astype(jnp.bfloat16)
        .reshape(3, positions, latents, head_cols)
    )
    grad_qkv_weight = jnp.einsum(
        "qnm,rqnw->mrw",
        attention_full_rows,
        query_key_value_gradient,
        preferred_element_type=jnp.float32,
    )
    grad_qv_local = jnp.stack(
        [
            jnp.sum(query_key_value_gradient[0], axis=(0, 1), dtype=jnp.float32),
            jnp.sum(query_key_value_gradient[2], axis=(0, 1), dtype=jnp.float32),
        ]
    )
    local_row_count = query_key_value_gradient
    grad_attn_input = lax.psum_scatter(
        jnp.einsum(
            "aoin,xan->oix",
            local_row_count,
            query_key_value_full,
            preferred_element_type=jnp.float32,
        ).astype(jnp.bfloat16),
        "tp",
        scatter_dimension=0,
        tiled=True,
    ).astype(jnp.float32)
    grad_input_norm, grad_shift_attn, grad_scale_attn = jax.vjp(
        modulate, residual_in, shift_attn, scale_attn
    )[1](grad_attn_input)
    inputs_grad = grad_middle + grad_input_norm
    grad_modulation = jnp.stack(
        [
            grad_shift_attn,
            grad_scale_attn,
            grad_gate_attn,
            grad_shift_mlp,
            grad_scale_mlp,
            grad_gate_mlp,
        ],
        axis=1,
    ).reshape(latents, 6 * width)
    grad_qv_full = lax.dynamic_update_slice(
        jnp.zeros((2, width), jnp.float32), grad_qv_local, (0, tp_rank * head_cols)
    )
    grad_fc1_full = lax.dynamic_update_slice(
        jnp.zeros((hidden_cols * tp_count,), jnp.float32), grad_fc1_bias, (tp_rank * hidden_cols,)
    )
    grad_modulation, grad_qv_full, grad_proj_bias, grad_fc1_full, grad_fc2_bias = (
        lax.psum(grad_modulation.astype(jnp.bfloat16), "tp").astype(jnp.float32),
        lax.psum(grad_qv_full.astype(jnp.bfloat16), "tp").astype(jnp.float32),
        lax.psum(grad_proj_bias.astype(jnp.bfloat16), "tp").astype(jnp.float32),
        lax.psum(grad_fc1_full.astype(jnp.bfloat16), "tp").astype(jnp.float32),
        lax.psum(grad_fc2_bias.astype(jnp.bfloat16), "tp").astype(jnp.float32),
    )
    grad_ada_bias = jnp.sum(grad_modulation, axis=0)
    grad_mod_low = grad_modulation.astype(jnp.bfloat16)
    grad_mod_all = lax.all_gather(grad_mod_low, "fsdp", axis=0, tiled=True)
    ada_weight_grad = jnp.einsum(
        "ld,lc->dc", cond_cols, grad_mod_all, preferred_element_type=jnp.float32
    )
    silu_cols = jnp.einsum(
        "lc,dc->ld", grad_mod_all, ada_weight, preferred_element_type=jnp.float32
    )
    grad_first = lax.dynamic_update_slice(
        jnp.zeros((grad_mod_all.shape[0], width), jnp.float32),
        silu_cols,
        (0, fsdp_rank * feat_rows),
    )
    scattered = (
        lax.psum_scatter(grad_first, "fsdp", scatter_dimension=0, tiled=True),
        lax.psum_scatter(grad_ada_bias, "fsdp", scatter_dimension=0, tiled=True),
        lax.psum_scatter(grad_qkv_weight, "fsdp", scatter_dimension=0, tiled=True),
        lax.psum_scatter(grad_qv_full, "fsdp", scatter_dimension=1, tiled=True),
        lax.psum_scatter(grad_proj, "fsdp", scatter_dimension=1, tiled=True),
        lax.psum_scatter(grad_proj_bias, "fsdp", scatter_dimension=0, tiled=True),
        lax.psum_scatter(expand_gradient, "fsdp", scatter_dimension=0, tiled=True),
        lax.psum_scatter(grad_fc1_full, "fsdp", scatter_dimension=0, tiled=True),
        lax.psum_scatter(grad_fc2, "fsdp", scatter_dimension=1, tiled=True),
        lax.psum_scatter(grad_fc2_bias, "fsdp", scatter_dimension=0, tiled=True),
    )
    (
        first_grad,
        ada_bias_grad,
        qkv_weight_grad,
        qv_bias_grad,
        proj_weight_grad,
        proj_bias_grad,
        fc1_weight_grad,
        fc1_bias_grad,
        fc2_weight_grad,
        fc2_bias_grad,
    ) = scattered
    cond_grad = jax.vjp(jax.nn.silu, cond_float)[1](first_grad)[0]
    return (
        output,
        inputs_grad,
        cond_grad,
        ada_weight_grad,
        ada_bias_grad,
        qkv_weight_grad,
        qv_bias_grad,
        proj_weight_grad,
        proj_bias_grad,
        fc1_weight_grad,
        fc1_bias_grad,
        fc2_weight_grad,
        fc2_bias_grad,
    )


def solution(mesh):
    return jax.shard_map(
        shards,
        mesh=mesh,
        in_specs=(
            P("tp", "fsdp", None),
            P("fsdp", None),
            P("fsdp", None),
            P("fsdp"),
            P("fsdp", None, "tp"),
            P(None, "fsdp"),
            P("tp", "fsdp"),
            P("fsdp"),
            P("fsdp", "tp"),
            P("fsdp"),
            P("tp", "fsdp"),
            P("fsdp"),
            P("tp", "fsdp", None),
        ),
        out_specs=(
            P("tp", "fsdp", None),
            P("tp", "fsdp", None),
            P("fsdp", None),
            P("fsdp", None),
            P("fsdp"),
            P("fsdp", None, "tp"),
            P(None, "fsdp"),
            P("tp", "fsdp"),
            P("fsdp"),
            P("fsdp", "tp"),
            P("fsdp"),
            P("tp", "fsdp"),
            P("fsdp"),
        ),
        check_vma=False,
    )
```

profile of v0, /device:TPU:0, one launch (start us, length us, event | category | flops | bytes accessed | tf_op | source)
XLA Modules:
  0.0 728.6 jit_solution(14443567794762782646)
XLA Ops:
  8.1 32.1 %all-gather = bf16[8,2,768]{2,1,0:T(2,128)(2,1)S(1)} all-gather(bf16[1,2,768]{2,1,0:T(2,128)(2,1)S(1)} %fusion.53), channel_id=1, replica_groups=mesh['fsdp'=8,'tp'=4] {'fsdp'}, dimensions={0}, use_global_device_ids=true | all-gather | bytes 27648 | tf_op jit(solution)/shard_map/all_gather | solution.py:61
  40.2 1.0 fusion.51
  44.0 37.7 %all-reduce.10 = (bf16[4608]{0:T(1024)(128)(2,1)S(1)}, bf16[768]{0:T(1024)(128)(2,1)}, bf16[768]{0:T(1024)(128)(2,1)}) all-reduce(bf16[4608]{0:T(1024)(128)(2,1)S(1)} %dynamic-update-slice, bf16[768]{0:T(1024)(128)(2,1)S(1)} %dynamic-update-slice.1, bf16[768]{0:T(1024)(128)(2,1)S(1)} %dynamic-update-slice.2), channel_id=1, replica_groups=mesh['fsdp'=8,'tp'=4] {'fsdp'}, use_global_device_ids=true, to_apply=%add | all-reduce | flops 6144 | bytes 24576
  82.4 35.7 %all_gather.48 = bf16[768,3,192]{2,1,0:T(4,128)(2,1)S(1)} all-gather(bf16[96,3,192]{2,1,0:T(4,128)(2,1)S(1)} %copy.75), channel_id=1, replica_groups=mesh['fsdp'=8,'tp'=4] {'fsdp'}, dimensions={0}, use_global_device_ids=true | all-gather | bytes 995328 | tf_op jit(solution)/shard_map/all_gather | solution.py:63
  120.1 17.6 %all-gather.1 = bf16[8,96,2]{1,2,0:T(2,128)(2,1)S(1)} all-gather(bf16[1,96,2]{1,2,0:T(2,128)(2,1)S(1)} %bitcast.188), channel_id=1, replica_groups=mesh['fsdp'=8,'tp'=4] {'fsdp'}, dimensions={0}, use_global_device_ids=true | all-gather | bytes 3456 | tf_op jit(solution)/shard_map/all_gather | solution.py:64
  139.4 1.5 copy.79
  141.6 33.3 %all_gather.50 = bf16[192,768]{0,1:T(8,128)(2,1)} all-gather(bf16[192,96]{0,1:T(8,128)(2,1)} %copy.79), channel_id=1, replica_groups=mesh['fsdp'=8,'tp'=4] {'fsdp'}, dimensions={1}, use_global_device_ids=true | all-gather | bytes 331776 | tf_op jit(solution)/shard_map/all_gather | solution.py:65
  176.8 8.9 %all_gather.47 = bf16[256,2,768]{2,0,1:T(8,128)(2,1)S(1)} all-gather(bf16[64,2,768]{2,0,1:T(8,128)(2,1)S(1)} %fusion.28), channel_id=1, replica_groups=mesh['fsdp'=8,'tp'=4] {'tp'}, dimensions={0}, use_global_device_ids=true | all-gather | bytes 983040 | tf_op jit(solution)/shard_map/all_gather | solution.py:101
  188.9 1.3 convolution_convert_fusion.2
  191.6 25.9 %all-gather.2 = bf16[8,1,384]{2,1,0:T(2,128)(2,1)S(1)} all-gather(bf16[1,1,384]{2,1,0:T(2,128)(2,1)S(1)} %reshape.186), channel_id=1, replica_groups=mesh['fsdp'=8,'tp'=4] {'fsdp'}, dimensions={0}, use_global_device_ids=true | all-gather | bytes 6912 | tf_op jit(solution)/shard_map/all_gather | solution.py:68
  218.3 7.8 %all_gather.57 = bf16[256,2,768]{2,0,1:T(8,128)(2,1)} all-gather(bf16[64,2,768]{2,0,1:T(8,128)(2,1)S(1)} %get-tuple-element.85), channel_id=1, replica_groups=mesh['fsdp'=8,'tp'=4] {'tp'}, dimensions={0}, use_global_device_ids=true | all-gather | bytes 983040 | tf_op jit(solution)/shard_map/all_gather | solution.py:167
  226.1 1.1 fusion.62
  227.2 1.1 multiply_reduce_fusion.2
  228.3 1.2 add_convert_fusion.1
  229.5 9.3 %all_gather.52 = bf16[256,2,768]{2,0,1:T(8,128)(2,1)} all-gather(bf16[64,2,768]{2,0,1:T(8,128)(2,1)S(1)} %add_convert_fusion.1), channel_id=1, replica_groups=mesh['fsdp'=8,'tp'=4] {'tp'}, dimensions={0}, use_global_device_ids=true | all-gather | bytes 983040 | tf_op jit(solution)/shard_map/all_gather | solution.py:142
  238.8 14.4 %all-gather.7.cloned.1.call-done = bf16[768,768]{1,0:T(8,128)(2,1)} async-done(((bf16[96,768]{1,0:T(8,128)(2,1)}), bf16[768,768]{1,0:T(8,128)(2,1)}) %all-gather.7.cloned.1.call-update) | async-done | bytes 1179664 | tf_op jit(solution)/shard_map/all_gather | solution.py:67
  253.2 3.4 convolution_add_fusion
  256.7 38.5 %all-gather.9.cloned.1.call-done = bf16[768,768]{0,1:T(8,128)(2,1)} async-done(((bf16[768,96]{0,1:T(8,128)(2,1)}), bf16[768,768]{0,1:T(8,128)(2,1)}) %all-gather.9.cloned.1.call-update) | async-done | bytes 1179664 | tf_op jit(solution)/shard_map/all_gather | solution.py:69
  295.1 3.6 convert_reduce_fusion
  299.7 1.7 convolution_convert_fusion
  301.5 3.7 convolution_convert_fusion.1
  305.3 18.3 %reduce-scatter.18.cloned.1.call-done = bf16[64,2,768]{2,0,1:T(8,128)(2,1)} async-done(((bf16[256,2,768]{2,0,1:T(8,128)(2,1)}), bf16[64,2,768]{2,0,1:T(8,128)(2,1)}) %reduce-scatter.18.cloned.1.call-update) | async-done | bytes 196624 | tf_op jit(solution)/shard_map/reduce_scatter | solution.py:191
  323.6 1.2 fusion.29
  324.9 1.2 fusion.41
  326.1 1.9 fusion.65
  328.0 8.4 %all_gather.58 = bf16[256,2,768]{2,0,1:T(8,128)(2,1)S(1)} all-gather(bf16[64,2,768]{2,0,1:T(8,128)(2,1)S(1)} %get-tuple-element.87), channel_id=1, replica_groups=mesh['fsdp'=8,'tp'=4] {'tp'}, dimensions={0}, use_global_device_ids=true | all-gather | bytes 983040 | tf_op jit(solution)/shard_map/all_gather | solution.py:206
  341.0 1.7 bitcast_convert_fusion
  343.5 1.3 convolution_bitcast_fusion.4
  344.9 4.6 reduce-scatter.16.cloned.1.call-done
  349.5 25.8 %reduce-scatter.20.cloned.1.call-done = bf16[64,2,768]{2,0,1:T(8,128)(2,1)} async-done(((bf16[256,2,768]{2,0,1:T(8,128)(2,1)}), bf16[64,2,768]{2,0,1:T(8,128)(2,1)}) %reduce-scatter.20.cloned.1.call-update) | async-done | bytes 196624 | tf_op jit(solution)/shard_map/reduce_scatter | solution.py:257
  375.3 1.7 fusion.30
  377.0 1.0 reduce.4
  379.0 10.9 %all-reduce.11 = (bf16[2,768]{1,0:T(2,128)(2,1)S(1)}, bf16[768]{0:T(1024)(128)(2,1)}, bf16[3072]{0:T(1024)(128)(2,1)S(1)}, bf16[768]{0:T(1024)(128)(2,1)}, bf16[2,4608]{1,0:T(2,128)(2,1)S(1)}) all-reduce(bf16[2,768]{1,0:T(2,128)(2,1)S(1)} %dynamic_update_slice.10, ...), channel_id=1, replica_groups=mesh['fsdp'=8,'tp'=4] {'tp'}, use_global_device_ids=true, to_apply=%region_29.30 | all-reduce | flops 15360 | bytes 61440 | tf_op jit(solution)/shard_map/psum | solution.py:291
  390.9 3.4 convolution_bitcast_fusion.2
  394.3 1.1 copy-done.20
  395.4 3.8 convolution_bitcast_fusion.1
  399.2 1.1 copy-done.14
  400.3 2.3 convolution_bitcast_fusion
  404.6 36.8 %reduce-scatter.30.cloned.1.call-done = f32[96,192]{1,0:T(8,128)} async-done(((f32[768,192]{1,0:T(8,128)}), f32[96,192]{1,0:T(8,128)}) %reduce-scatter.30.cloned.1.call-update) | async-done | bytes 73744
  441.4 1.6 copy.107
  444.3 1.1 copy.92
  445.4 30.7 %all-gather.3 = bf16[8,2,4608]{2,1,0:T(2,128)(2,1)S(1)} all-gather(bf16[1,2,4608]{2,1,0:T(2,128)(2,1)S(1)} %bitcast.179), channel_id=1, replica_groups=mesh['fsdp'=8,'tp'=4] {'fsdp'}, dimensions={0}, use_global_device_ids=true | all-gather | bytes 165888 | tf_op jit(solution)/shard_map/all_gather | solution.py:298
  476.8 36.2 %all-reduce.16 = (f32[16,768]{1,0:T(8,128)S(1)}, f32[4608]{0:T(1024)S(1)}, f32[768]{0:T(1024)S(1)}, f32[3072]{0:T(1024)S(1)}, f32[768]{0:T(1024)S(1)}) all-reduce(f32[16,768]{1,0:T(8,128)S(1)} %dynamic_update_slice.9, f32[4608]{0:T(1024)S(1)} %convert_reduce_fusion.4, ...), channel_id=7, replica_groups=mesh['fsdp'=8,'tp'=4] {'fsdp'}, use_global_device_ids=true, to_apply=%region_23.24.clone | all-reduce | flops 21504 | bytes 162816
  516.2 2.4 fusion.49
  518.5 1.4 copy.105
  520.0 57.7 %reduce-scatter.24.cloned.1.call-done = f32[96,768]{1,0:T(8,128)} async-done(((f32[768,768]{1,0:T(8,128)}), f32[96,768]{1,0:T(8,128)}) %reduce-scatter.24.cloned.1.call-update) | async-done | bytes 294928 | tf_op jit(solution)/shard_map/reduce_scatter | solution.py:317
  577.7 72.1 %reduce-scatter.26.cloned.1.call-done = f32[768,96]{0,1:T(8,128)} async-done(((f32[768,768]{0,1:T(8,128)}), f32[768,96]{0,1:T(8,128)}) %reduce-scatter.26.cloned.1.call-update) | async-done | bytes 294928 | tf_op jit(solution)/shard_map/reduce_scatter | solution.py:319
  649.8 71.9 %reduce-scatter.22.cloned.1.call-done = f32[96,3,192]{2,0,1:T(8,128)} async-done(((f32[768,3,192]{2,0,1:T(8,128)}), f32[96,3,192]{2,0,1:T(8,128)}) %reduce-scatter.22.cloned.1.call-update) | async-done | bytes 221200 | tf_op jit(solution)/shard_map/reduce_scatter | solution.py:313
  (200 shorter events, 27.3 us)
Async XLA Ops:
  7.2 33.0 %copy-start = (bf16[96,4608]{1,0:T(8,128)(2,1)S(1)}, bf16[96,4608]{1,0:T(8,128)(2,1)}, u32[]{:S(2)}) copy-start(bf16[96,4608]{1,0:T(8,128)(2,1)} %param.15) | copy-start | bytes 2654212
  7.2 34.1 %copy-start.37 = (u32[32]{0:T(128)S(1)}, u32[32]{0:T(128)}, u32[]{:S(2)}) copy-start(u32[32]{0:T(128)} %constant.72) | copy-start | bytes 388
  7.2 36.0 %copy-start.42 = (bf16[96]{0:T(256)(128)(2,1)S(1)}, bf16[96]{0:T(256)(128)(2,1)}, u32[]{:S(2)}) copy-start(bf16[96]{0:T(256)(128)(2,1)} %param.20) | copy-start | bytes 580
  7.2 36.3 %copy-start.43 = (bf16[96]{0:T(256)(128)(2,1)S(1)}, bf16[96]{0:T(256)(128)(2,1)}, u32[]{:S(2)}) copy-start(bf16[96]{0:T(256)(128)(2,1)} %param.24) | copy-start | bytes 580
  7.2 36.5 %copy-start.38 = (bf16[576]{0:T(1024)(128)(2,1)S(1)}, bf16[576]{0:T(1024)(128)(2,1)}, u32[]{:S(2)}) copy-start(bf16[576]{0:T(1024)(128)(2,1)} %param.16) | copy-start | bytes 3460
  7.2 75.1 %copy-start.24 = (bf16[96,3,192]{2,0,1:T(8,128)(2,1)S(1)}, bf16[96,3,192]{2,0,1:T(8,128)(2,1)}, u32[]{:S(2)}) copy-start(bf16[96,3,192]{2,0,1:T(8,128)(2,1)} %param.17) | copy-start | bytes 331780
  7.2 168.3 %all-reduce.15.cloned.1.call-start = ((), (), s32[]{:S(2)}) async-start(), calls=%async_computation.20 | async-start | bytes 589824
  40.2 42.2 %copy-start.25 = (bf16[16,768]{1,0:T(8,128)(2,1)}, bf16[16,768]{1,0:T(8,128)(2,1)S(1)}, u32[]{:S(2)}) copy-start(bf16[16,768]{1,0:T(8,128)(2,1)S(1)} %reshape.183) | copy-start | bytes 73732
  41.3 184.8 %reduce-scatter.14.cloned.1.call-start = ((), (), s32[]{:S(2)}) async-start(), calls=%async_computation.9 | async-start | bytes 983040 | tf_op jit(solution)/shard_map/reduce_scatter | solution.py:132
  118.1 56.8 %copy-start.5 = (bf16[768,3,192]{2,1,0:T(4,128)(2,1)}, bf16[768,3,192]{2,1,0:T(4,128)(2,1)S(1)}, u32[]{:S(2)}) copy-start(bf16[768,3,192]{2,1,0:T(4,128)(2,1)S(1)} %all_gather.48) | copy-start | bytes 2654212
  118.1 2.0 copy-start.40
  186.6 1.3 copy-start.18
  188.5 37.6 %copy-start.16 = (bf16[2,3,64,256]{3,2,1,0:T(8,128)(2,1)}, bf16[2,3,64,256]{3,2,1,0:T(8,128)(2,1)S(1)}, u32[]{:S(2)}) copy-start(bf16[2,3,64,256]{3,2,1,0:T(8,128)(2,1)S(1)} %convolution_convert_fusion.5) | copy-start | bytes 589828
  188.5 3.0 copy-start.34
  188.5 3.1 copy-start.39
  188.5 29.1 %copy-start.15 = (bf16[64,2,768]{2,1,0:T(2,128)(2,1)S(1)}, bf16[64,2,768]{2,1,0:T(2,128)(2,1)}, u32[]{:S(2)}) copy-start(bf16[64,2,768]{2,1,0:T(2,128)(2,1)} %param.25) | copy-start | bytes 589828
  190.2 63.1 %all-gather.7.cloned.1.call-start = ((), (), s32[]{:S(2)}) async-start(), calls=%async_computation.10 | async-start | bytes 1327104 | tf_op jit(solution)/shard_map/all_gather | solution.py:67
  190.9 104.2 %all-gather.9.cloned.1.call-start = ((), (), s32[]{:S(2)}) async-start(), calls=%async_computation.11 | async-start | bytes 1327104 | tf_op jit(solution)/shard_map/all_gather | solution.py:69
  191.5 132.1 %reduce-scatter.18.cloned.1.call-start = ((), (), s32[]{:S(2)}) async-start(), calls=%async_computation.13 | async-start | bytes 983040 | tf_op jit(solution)/shard_map/reduce_scatter | solution.py:191
  295.1 4.6 copy-start.41
  301.4 22.2 %copy-start.2 = (bf16[64,2,768]{2,0,1:T(8,128)(2,1)S(1)}, bf16[64,2,768]{2,0,1:T(8,128)(2,1)}, u32[]{:S(2)}) copy-start(bf16[64,2,768]{2,0,1:T(8,128)(2,1)} %reduce-scatter.14.cloned.1.call-done) | copy-start | bytes 589828
  301.4 48.0 %reduce-scatter.16.cloned.1.call-start = ((), (), s32[]{:S(2)}) async-start(), calls=%async_computation.12 | async-start | bytes 983040 | tf_op jit(solution)/shard_map/reduce_scatter | solution.py:154
  305.3 70.0 %reduce-scatter.20.cloned.1.call-start = ((), (), s32[]{:S(2)}) async-start(), calls=%async_computation.14 | async-start | bytes 983040 | tf_op jit(solution)/shard_map/reduce_scatter | solution.py:257
  323.6 13.6 %copy-start.11 = (bf16[192,768]{0,1:T(8,128)(2,1)S(1)}, bf16[192,768]{0,1:T(8,128)(2,1)}, u32[]{:S(2)}) copy-start(bf16[192,768]{0,1:T(8,128)(2,1)} %all_gather.50) | copy-start | bytes 884740
  338.2 1.3 copy-start.9
  339.5 1.5 copy-start.6
  341.0 1.8 copy-start.33
  341.0 2.5 copy-start.4
  341.0 2.5 copy-start.17
  342.7 32.6 %copy-start.7 = (bf16[64,2,768]{2,0,1:T(8,128)(2,1)S(1)}, bf16[64,2,768]{2,0,1:T(8,128)(2,1)}, u32[]{:S(2)}) copy-start(bf16[64,2,768]{2,0,1:T(8,128)(2,1)} %reduce-scatter.18.cloned.1.call-done) | copy-start | bytes 589828
  342.7 98.7 %reduce-scatter.30.cloned.1.call-start = ((), (), s32[]{:S(2)}) async-start(), calls=%async_computation.19 | async-start | bytes 884736
  343.5 33.6 %copy-start.27 = (f32[64,2]{0,1:T(2,128)S(1)}, f32[64,2]{0,1:T(2,128)}, u32[]{:S(2)}) copy-start(f32[64,2]{0,1:T(2,128)} %fusion.32) | copy-start | bytes 1540
  344.8 34.2 %copy-start.30 = (bf16[768]{0:T(1024)(128)(2,1)S(1)}, bf16[768]{0:T(1024)(128)(2,1)}, u32[]{:S(2)}) copy-start(bf16[768]{0:T(1024)(128)(2,1)} %get-tuple-element.84) | copy-start | bytes 4612
  344.8 34.2 %copy-start.31 = (bf16[768]{0:T(1024)(128)(2,1)S(1)}, bf16[768]{0:T(1024)(128)(2,1)}, u32[]{:S(2)}) copy-start(bf16[768]{0:T(1024)(128)(2,1)} %get-tuple-element.86) | copy-start | bytes 4612
  344.8 46.0 %copy-start.21 = (bf16[256,2,768]{2,0,1:T(8,128)(2,1)S(1)}, bf16[256,2,768]{2,0,1:T(8,128)(2,1)}, u32[]{:S(2)}) copy-start(bf16[256,2,768]{2,0,1:T(8,128)(2,1)} %all_gather.52) | copy-start | bytes 2359300
  344.8 173.7 %reduce-scatter.28.cloned.1.call-start = ((), (), s32[]{:S(2)}) async-start(), calls=%async_computation.18 | async-start | bytes 442368
  375.3 2.7 copy-start.12
  377.0 1.9 copy-start.28
  390.8 186.9 %reduce-scatter.24.cloned.1.call-start = ((), (), s32[]{:S(2)}) async-start(), calls=%async_computation.16 | async-start | bytes 2654208 | tf_op jit(solution)/shard_map/reduce_scatter | solution.py:317
  394.2 1.1 copy-start.20
  394.2 255.5 %reduce-scatter.26.cloned.1.call-start = ((), (), s32[]{:S(2)}) async-start(), calls=%async_computation.17 | async-start | bytes 2654208 | tf_op jit(solution)/shard_map/reduce_scatter | solution.py:319
  399.2 1.2 copy-start.23
  399.2 322.5 %reduce-scatter.22.cloned.1.call-start = ((), (), s32[]{:S(2)}) async-start(), calls=%async_computation.15 | async-start | bytes 2654208 | tf_op jit(solution)/shard_map/reduce_scatter | solution.py:313
  402.6 41.3 %copy-start.32 = (f32[64,2]{0,1:T(2,128)S(1)}, f32[64,2]{0,1:T(2,128)}, u32[]{:S(2)}) copy-start(f32[64,2]{0,1:T(2,128)} %get-tuple-element.68) | copy-start | bytes 1540
  402.6 41.3 %copy-start.29 = (f32[64,2]{0,1:T(2,128)S(1)}, f32[64,2]{0,1:T(2,128)}, u32[]{:S(2)}) copy-start(f32[64,2]{0,1:T(2,128)} %copy-done.28) | copy-start | bytes 1540
  443.9 32.9 %copy-start.35 = (bf16[768]{0:T(1024)(128)(2,1)S(1)}, bf16[768]{0:T(1024)(128)(2,1)}, u32[]{:S(2)}) copy-start(bf16[768]{0:T(1024)(128)(2,1)} %get-tuple-element.80) | copy-start | bytes 4612
  443.9 32.9 %copy-start.36 = (bf16[768]{0:T(1024)(128)(2,1)S(1)}, bf16[768]{0:T(1024)(128)(2,1)}, u32[]{:S(2)}) copy-start(bf16[768]{0:T(1024)(128)(2,1)} %get-tuple-element.82) | copy-start | bytes 4612
  444.3 71.2 %copy-start.26 = (bf16[2,768]{1,0:T(2,128)(2,1)S(1)}, bf16[2,768]{1,0:T(2,128)(2,1)}, u32[]{:S(2)}) copy-start(bf16[2,768]{1,0:T(2,128)(2,1)} %param.14) | copy-start | bytes 9220
  (9 other events, 8.3 us)
Sparse Core Ops, SparseCore 0:
  41.4 73.2 all-reduce.14
  190.3 19.6 reduce-scatter.13
  212.1 41.0 all-gather.6
  255.3 39.8 all-gather.8
  301.6 22.0 reduce-scatter.17
  326.2 23.2 reduce-scatter.15
  352.0 23.2 reduce-scatter.19
  379.0 62.4 reduce-scatter.29
  444.7 60.4 reduce-scatter.27
  509.1 68.5 reduce-scatter.23
  581.8 67.9 reduce-scatter.25
  653.7 67.9 reduce-scatter.21
where the time goes:
time: 730 us; the launch traced here: 729 us
  waiting for transfers between devices  342 us (47%)
  blocking collectives  294 us (40%)
  matrix products  33.6 us (5%)
  local copies, waits for them, and re-layouts  21.1 us (3%)
  between operations  18.8 us (3%)
  other arithmetic  18.5 us (3%)
    unnamed x2, blocking collectives  74 us
    reduce_scatter x1, waiting for transfers between devices, shards(): lax.psum_scatter(grad_fc2, 'fsdp', scatter_dimension=1, tiled=True)  72.1 us
    reduce_scatter x1, waiting for transfers between devices, shards(): lax.psum_scatter(grad_qkv_weight, 'fsdp', scatter_dimension=0, tiled=True)  71.9 us
    reduce_scatter x1, waiting for transfers between devices, shards(): lax.psum_scatter(expand_gradient, 'fsdp', scatter_dimension=0, tiled=True)  57.7 us
    all_gather x1, waiting for transfers between devices, shards(): lax.all_gather(contract_weight, 'fsdp', axis=1, tiled=True)  38.5 us
    unnamed x15, waiting for transfers between devices  38.2 us
    all_gather x1, blocking collectives, shards(): lax.all_gather(query_key_value_weight, 'fsdp', axis=0, tiled=True)  35.7 us
    all_gather x1, blocking collectives, shards(): lax.all_gather(attention_output_weight, 'fsdp', axis=1, tiled=True)  33.3 us
  transfers between devices with their start and end apart: 12, of which 9 were waited for; matrix products, arithmetic and copies ran while one was open for 8% of the time, Pallas kernels for 0%

commit v1 on v0

v1 whole, which is shorter than its diff:
```python
import functools
import math

import jax
import jax.numpy as jnp
from jax import lax
from jax.experimental import pallas as pl
from jax.experimental.pallas import tpu as pltpu
from jax.sharding import PartitionSpec as P

HEAD = 64
EPS = 1e-06
BF = jnp.bfloat16
F32 = jnp.float32
VMEM_LIMIT = 48 * 1024 * 1024


def layer_norm(values_in):
    average = jnp.mean(values_in, axis=-1, keepdims=True)
    centered = values_in - average
    variance = jnp.mean(centered * centered, axis=-1, keepdims=True)
    return centered * lax.rsqrt(variance + EPS)


def modulate(values_in, shifts, scales):
    return layer_norm(values_in) * (1.0 + scales) + shifts


def gelu_tanh(values_in):
    return jax.nn.gelu(values_in, approximate=True)


def swap(block, axis, offset):
    count = lax.axis_size(axis)
    return lax.ppermute(block, axis, [(i, i ^ offset) for i in range(count)])


def digits(count):
    bits = count.bit_length() - 1
    found, stride = [], 1
    if bits % 2:
        found.append((1, 2))
        stride = 2
    while stride < count:
        found.append((stride, 4))
        stride *= 4
    return found


def gather_blocks(own):
    count = lax.axis_size("fsdp")
    blocks = {0: own}
    for stride, radix in reversed(digits(count)):
        known = sorted(blocks)
        if len(known) > 4:
            stacked = jnp.stack([blocks[k] for k in known])
            for d in range(1, radix):
                moved = swap(stacked, "fsdp", d * stride)
                for place, k in enumerate(known):
                    blocks[k ^ (d * stride)] = moved[place]
        else:
            for d in range(1, radix):
                for k in known:
                    blocks[k ^ (d * stride)] = swap(blocks[k], "fsdp", d * stride)
    return [blocks[k] for k in range(count)]


def assemble_kernel(rank_ref, *refs):
    out_ref = refs[-1]
    rank = rank_ref[0]
    for k, block in enumerate(refs[:-1]):
        rows = block.shape[0]
        place = jnp.bitwise_xor(rank, k) * rows
        out_ref[pl.ds(pl.multiple_of(place, rows), rows), :] = block[...]


def assemble(blocks, rank):
    rows, cols = blocks[0].shape
    count = len(blocks)
    if rows % 16:
        order = jnp.bitwise_xor(jnp.arange(count), rank)
        return jnp.take(jnp.stack(blocks), order, axis=0).reshape(count * rows, cols)
    return pl.pallas_call(
        assemble_kernel,
        out_shape=jax.ShapeDtypeStruct((count * rows, cols), blocks[0].dtype),
        in_specs=[pl.BlockSpec(memory_space=pltpu.SMEM)]
        + [pl.BlockSpec(memory_space=pltpu.VMEM)] * count,
        out_specs=pl.BlockSpec(memory_space=pltpu.VMEM),
        compiler_params=pltpu.CompilerParams(vmem_limit_bytes=VMEM_LIMIT),
        name="assemble",
    )(rank.reshape(1).astype(jnp.int32), *blocks)


def weight_grad_kernel(rank_ref, left_ref, right_ref, out_ref):
    rank = rank_ref[0]
    count, rows, cols = out_ref.shape
    for at in range(0, cols, 256):
        product = lax.dot_general(
            left_ref[...],
            right_ref[:, at : at + 256],
            (((0,), (0,)), ((), ())),
            preferred_element_type=F32,
        ).astype(BF)
        for k in range(count):
            out_ref[jnp.bitwise_xor(rank, k), :, at : at + 256] = product[
                k * rows : (k + 1) * rows
            ]


def weight_grad(left, right, rank, count):
    rows = left.shape[1] // count
    cols = right.shape[1]
    if rows % 16:
        whole = jnp.dot(left.T, right, preferred_element_type=F32).astype(BF)
        order = jnp.bitwise_xor(jnp.arange(count), rank)
        return jnp.take(whole.reshape(count, rows, cols), order, axis=0)
    return pl.pallas_call(
        weight_grad_kernel,
        out_shape=jax.ShapeDtypeStruct((count, rows, cols), BF),
        in_specs=[
            pl.BlockSpec(memory_space=pltpu.SMEM),
            pl.BlockSpec(memory_space=pltpu.VMEM),
            pl.BlockSpec(memory_space=pltpu.VMEM),
        ],
        out_specs=pl.BlockSpec(memory_space=pltpu.VMEM),
        compiler_params=pltpu.CompilerParams(vmem_limit_bytes=VMEM_LIMIT),
        name="weight_grad",
    )(rank.reshape(1).astype(jnp.int32), left, right)


def scatter_blocks(parts):
    count = lax.axis_size("fsdp")
    blocks = {k: parts[k] for k in range(count)}
    stages = digits(count)
    for at, (stride, radix) in enumerate(stages):
        kept = [k for k in sorted(blocks) if (k // stride) % radix == 0]
        arrived = {k: [] for k in kept}
        if len(kept) > 4:
            for d in range(1, radix):
                sent = jnp.stack([blocks[k ^ (d * stride)] for k in kept])
                got = swap(sent, "fsdp", d * stride)
                for place, k in enumerate(kept):
                    arrived[k].append(got[place])
        else:
            for k in reversed(kept):
                for d in range(1, radix):
                    arrived[k].append(swap(blocks[k ^ (d * stride)], "fsdp", d * stride))
        last = at == len(stages) - 1
        summed = {}
        for k in kept:
            total = blocks[k].astype(F32)
            for part in arrived[k]:
                total = total + part.astype(F32)
            summed[k] = total if last else total.astype(BF)
        blocks = summed
    return blocks[0]


def tp_gather(rows):
    count = lax.axis_size("tp")
    return jnp.concatenate([rows] + [swap(rows, "tp", d) for d in range(1, count)], axis=1)


def tp_scatter(partial, positions):
    count = lax.axis_size("tp")
    total = partial[:, :positions].astype(F32)
    for d in range(1, count):
        total = total + swap(
            partial[:, d * positions : (d + 1) * positions], "tp", d
        ).astype(F32)
    return total


def shards(
    inputs,
    conditioning,
    ada_weight,
    ada_bias,
    query_key_value_weight,
    qv_bias,
    attention_output_weight,
    attention_output_bias,
    expand_weight,
    hidden_layer_bias,
    contract_weight,
    contract_bias,
    out_cotangent,
):
    tp_rank = lax.axis_index("tp")
    tp_count = lax.axis_size("tp")
    rank = lax.axis_index("fsdp")
    count = lax.axis_size("fsdp")
    positions, latents, width = inputs.shape
    feat = ada_weight.shape[0]
    head_cols = query_key_value_weight.shape[2]
    heads = head_cols // HEAD
    hidden_cols = expand_weight.shape[1]
    hidden_part = hidden_layer_bias.shape[0]
    mod_part = ada_bias.shape[0]

    attn_own = jnp.concatenate(
        [query_key_value_weight.reshape(feat, 3 * head_cols), attention_output_weight.T], axis=1
    )
    contract_own = contract_weight.T

    cond_float = conditioning.astype(F32)
    cond_low = jax.nn.silu(cond_float).astype(BF)
    bias_own = jnp.concatenate(
        [qv_bias.reshape(-1), attention_output_bias, hidden_layer_bias, contract_bias]
    )
    cond_sent = cond_low.reshape(latents, count, feat).transpose(1, 0, 2)
    sent = jnp.concatenate(
        [
            cond_sent.reshape(count, latents * feat),
            jnp.broadcast_to(bias_own[None], (count, bias_own.shape[0])),
        ],
        axis=1,
    )
    got = lax.all_to_all(sent, "fsdp", split_axis=0, concat_axis=0, tiled=True)
    cond_cols = got[:, : latents * feat].reshape(count * latents, feat)
    bias_all = got[:, latents * feat :].astype(F32)
    at = 2 * feat
    qv_all = bias_all[:, :at].reshape(count, 2, feat).transpose(1, 0, 2).reshape(2, width)
    proj_shift = bias_all[:, at : at + feat].reshape(width)
    fc1_shift = bias_all[:, at + feat : at + feat + hidden_part].reshape(-1)
    fc2_shift = bias_all[:, at + feat + hidden_part :].reshape(width)
    query_bias = lax.dynamic_slice_in_dim(qv_all[0], tp_rank * head_cols, head_cols, 0)
    value_bias = lax.dynamic_slice_in_dim(qv_all[1], tp_rank * head_cols, head_cols, 0)
    hidden_bias = lax.dynamic_slice_in_dim(fc1_shift, tp_rank * hidden_cols, hidden_cols, 0)

    mod_partial = jnp.dot(cond_cols, ada_weight, preferred_element_type=F32)
    bias_row = lax.dynamic_update_slice(
        jnp.zeros((mod_part * count,), F32), ada_bias.astype(F32), (rank * mod_part,)
    )
    mod_partial = mod_partial + bias_row
    mod_got = lax.all_to_all(mod_partial, "fsdp", split_axis=0, concat_axis=0, tiled=True)
    modulation = jnp.sum(mod_got.reshape(count, latents, 6, 1, width), axis=0)
    shift_attn, scale_attn, gate_attn = (modulation[:, 0], modulation[:, 1], modulation[:, 2])
    shift_mlp, scale_mlp, gate_mlp = (modulation[:, 3], modulation[:, 4], modulation[:, 5])

    attn_blocks = gather_blocks(attn_own)
    first_blocks = gather_blocks(expand_weight)
    second_blocks = gather_blocks(contract_own)

    residual_in = inputs.transpose(1, 0, 2).astype(F32)
    cotangent = out_cotangent.transpose(1, 0, 2).astype(F32)
    tokens = latents * positions * tp_count

    attn_in = modulate(residual_in, shift_attn, scale_attn).astype(BF)
    grad_mlp = (cotangent * gate_mlp).astype(BF)
    attn_rows = tp_gather(attn_in)
    grad_mlp_rows = tp_gather(grad_mlp)
    attn_full = assemble(attn_blocks, rank)
    qkv_full = attn_full[:, : 3 * head_cols]
    proj_full = attn_full[:, 3 * head_cols :]
    projected = jnp.dot(
        attn_rows.reshape(tokens, width), qkv_full, preferred_element_type=F32
    )
    split = (latents, positions * tp_count, heads, HEAD)
    queries = (projected[:, :head_cols] + query_bias).astype(BF).reshape(split)
    keys = projected[:, head_cols : 2 * head_cols].astype(BF).reshape(split)
    values = (projected[:, 2 * head_cols :] + value_bias).astype(BF).reshape(split)
    factor = 1.0 / math.sqrt(HEAD)
    scores = jnp.einsum("lshe,lthe->lhst", queries, keys, preferred_element_type=F32) * factor
    top = jnp.max(scores, axis=-1, keepdims=True)
    weights = jnp.exp(scores - top)
    probs = weights / jnp.sum(weights, axis=-1, keepdims=True)
    probs_low = probs.astype(BF)
    attended = (
        jnp.einsum("lhst,lthe->lshe", probs_low, values, preferred_element_type=F32)
        .astype(BF)
        .reshape(tokens, head_cols)
    )
    attn_partial = lax.dot_general(
        attended, proj_full, (((1,), (1,)), ((), ())), preferred_element_type=F32
    ).astype(BF)
    attn_branch = (
        tp_scatter(attn_partial.reshape(latents, -1, width), positions) + proj_shift
    )
    middle = residual_in + gate_attn * attn_branch
    mlp_in = modulate(middle, shift_mlp, scale_mlp).astype(BF)
    mlp_rows = tp_gather(mlp_in).reshape(tokens, width)
    grad_rows = grad_mlp_rows.reshape(tokens, width)
    first_full = assemble(first_blocks, rank)
    second_full = assemble(second_blocks, rank)
    hidden_pre = jnp.dot(mlp_rows, first_full, preferred_element_type=F32) + hidden_bias
    hidden_act = gelu_tanh(hidden_pre).astype(BF)
    act_grad = jnp.dot(grad_rows, second_full, preferred_element_type=F32)
    grad_pre = jax.vjp(gelu_tanh, hidden_pre)[1](act_grad)[0].astype(BF)
    grad_in_partial = lax.dot_general(
        grad_pre, first_full, (((1,), (1,)), ((), ())), preferred_element_type=F32
    ).astype(BF)
    grad_mlp_input = tp_scatter(grad_in_partial.reshape(latents, -1, width), positions)
    mlp_partial = lax.dot_general(
        hidden_act, second_full, (((1,), (1,)), ((), ())), preferred_element_type=F32
    ).astype(BF)
    mlp_branch = tp_scatter(mlp_partial.reshape(latents, -1, width), positions) + fc2_shift
    output = (middle + gate_mlp * mlp_branch).astype(BF)

    second_grad = weight_grad(grad_rows, hidden_act, rank, count)
    first_grad = weight_grad(mlp_rows, grad_pre, rank, count)

    grad_gate_mlp = jnp.sum(cotangent * mlp_branch, axis=1)
    grad_fc2_bias = jnp.sum(grad_mlp.astype(F32), axis=(0, 1))
    grad_fc1_bias = jnp.sum(grad_pre.astype(F32), axis=0)

    grad_middle_norm, grad_shift_mlp, grad_scale_mlp = jax.vjp(
        modulate, middle, shift_mlp, scale_mlp
    )[1](grad_mlp_input)
    grad_middle = cotangent + grad_middle_norm
    grad_gate_attn = jnp.sum(grad_middle * attn_branch, axis=1)
    grad_attn = (grad_middle * gate_attn).astype(BF)
    grad_proj_bias = jnp.sum(grad_attn.astype(F32), axis=(0, 1))
    grad_attn_rows = tp_gather(grad_attn).reshape(tokens, width)
    grad_attended = (
        jnp.dot(grad_attn_rows, proj_full, preferred_element_type=F32).astype(BF).reshape(split)
    )
    grad_values = jnp.einsum(
        "lhst,lshe->lthe", probs_low, grad_attended, preferred_element_type=F32
    )
    grad_probs = jnp.einsum("lshe,lthe->lhst", grad_attended, values, preferred_element_type=F32)
    grad_scores = (
        probs * (grad_probs - jnp.sum(probs * grad_probs, axis=-1, keepdims=True))
    ).astype(BF)
    grad_queries = (
        jnp.einsum("lhst,lthe->lshe", grad_scores, keys, preferred_element_type=F32) * factor
    )
    grad_keys = (
        jnp.einsum("lhst,lshe->lthe", grad_scores, queries, preferred_element_type=F32) * factor
    )
    grad_qkv = jnp.concatenate(
        [
            part.astype(BF).reshape(tokens, head_cols)
            for part in (grad_queries, grad_keys, grad_values)
        ],
        axis=1,
    )
    grad_in_partial = lax.dot_general(
        grad_qkv, qkv_full, (((1,), (1,)), ((), ())), preferred_element_type=F32
    ).astype(BF)
    grad_attn_input = tp_scatter(grad_in_partial.reshape(latents, -1, width), positions)
    qkv_grad = weight_grad(attn_rows.reshape(tokens, width), grad_qkv, rank, count)
    proj_grad = weight_grad(grad_attn_rows, attended, rank, count)
    grad_qv = jnp.sum(grad_qkv.astype(F32), axis=0)

    grad_input_norm, grad_shift_attn, grad_scale_attn = jax.vjp(
        modulate, residual_in, shift_attn, scale_attn
    )[1](grad_attn_input)
    inputs_grad = grad_middle + grad_input_norm

    grad_mod_own = jnp.stack(
        [
            grad_shift_attn.reshape(latents, width),
            grad_scale_attn.reshape(latents, width),
            grad_gate_attn,
            grad_shift_mlp.reshape(latents, width),
            grad_scale_mlp.reshape(latents, width),
            grad_gate_mlp,
        ],
        axis=1,
    ).reshape(latents, 6 * width)
    zero = jnp.zeros((), jnp.int32)
    grad_qv_own = lax.dynamic_update_slice(
        jnp.zeros((2, width), F32),
        jnp.stack([grad_qv[:head_cols], grad_qv[2 * head_cols :]]),
        (zero, tp_rank * head_cols),
    )
    grad_fc1_own = lax.dynamic_update_slice(
        jnp.zeros((hidden_cols * tp_count,), F32), grad_fc1_bias, (tp_rank * hidden_cols,)
    )
    packed = jnp.concatenate(
        [
            grad_mod_own.reshape(-1),
            grad_qv_own.reshape(-1),
            grad_proj_bias,
            grad_fc1_own,
            grad_fc2_bias,
        ]
    ).astype(BF)
    packed_total = packed.astype(F32)
    for d in range(1, tp_count):
        packed_total = packed_total + swap(packed, "tp", d).astype(F32)
    mods = latents * 6 * width
    grad_mod_low = packed_total[:mods].astype(BF)
    rest = packed_total[mods:]
    qv_sum = rest[: 2 * width].reshape(2, count, feat).transpose(1, 0, 2).reshape(count, -1)
    proj_sum = rest[2 * width : 3 * width].reshape(count, feat)
    fc1_sum = rest[3 * width : 3 * width + hidden_cols * tp_count].reshape(count, hidden_part)
    fc2_sum = rest[3 * width + hidden_cols * tp_count :].reshape(count, feat)
    sent = jnp.concatenate(
        [
            jnp.broadcast_to(grad_mod_low[None], (count, mods)),
            jnp.concatenate([qv_sum, proj_sum, fc1_sum, fc2_sum], axis=1).astype(BF),
        ],
        axis=1,
    )
    got = lax.all_to_all(sent, "fsdp", split_axis=0, concat_axis=0, tiled=True)
    grad_mod_all = got[:, :mods].reshape(count * latents, 6 * width)
    bias_grads = jnp.sum(got[:, mods:].astype(F32), axis=0)
    qv_bias_grad = bias_grads[: 2 * feat].reshape(2, feat)
    proj_bias_grad = bias_grads[2 * feat : 3 * feat]
    fc1_bias_grad = bias_grads[3 * feat : 3 * feat + hidden_part]
    fc2_bias_grad = bias_grads[3 * feat + hidden_part :]
    ada_bias_grad = jnp.sum(
        lax.dynamic_slice_in_dim(grad_mod_all, rank * mod_part, mod_part, 1).astype(F32), axis=0
    )
    ada_weight_grad = lax.dot_general(
        cond_cols, grad_mod_all, (((0,), (0,)), ((), ())), preferred_element_type=F32
    )
    silu_cols = lax.dot_general(
        grad_mod_all, ada_weight, (((1,), (1,)), ((), ())), preferred_element_type=F32
    )
    silu_got = lax.all_to_all(
        silu_cols.reshape(count, latents, feat), "fsdp", split_axis=0, concat_axis=0, tiled=True
    )
    silu_grad = silu_got.transpose(1, 0, 2).reshape(latents, width)
    cond_grad = jax.vjp(jax.nn.silu, cond_float)[1](silu_grad)[0]

    second_sum = scatter_blocks(second_grad)
    first_sum = scatter_blocks(first_grad)
    attn_sum = scatter_blocks(jnp.concatenate([qkv_grad, proj_grad], axis=2))
    return (
        output.transpose(1, 0, 2),
        inputs_grad.transpose(1, 0, 2),
        cond_grad,
        ada_weight_grad,
        ada_bias_grad,
        attn_sum[:, : 3 * head_cols].reshape(feat, 3, head_cols),
        qv_bias_grad,
        attn_sum[:, 3 * head_cols :].T,
        proj_bias_grad,
        first_sum,
        fc1_bias_grad,
        second_sum.T,
        fc2_bias_grad,
    )


def solution(mesh):
    return jax.shard_map(
        shards,
        mesh=mesh,
        in_specs=(
            P("tp", "fsdp", None),
            P("fsdp", None),
            P("fsdp", None),
            P("fsdp"),
            P("fsdp", None, "tp"),
            P(None, "fsdp"),
            P("tp", "fsdp"),
            P("fsdp"),
            P("fsdp", "tp"),
            P("fsdp"),
            P("tp", "fsdp"),
            P("fsdp"),
            P("tp", "fsdp", None),
        ),
        out_specs=(
            P("tp", "fsdp", None),
            P("tp", "fsdp", None),
            P("fsdp", None),
            P("fsdp", None),
            P("fsdp"),
            P("fsdp", None, "tp"),
            P(None, "fsdp"),
            P("tp", "fsdp"),
            P("fsdp"),
            P("fsdp", "tp"),
            P("fsdp"),
            P("tp", "fsdp"),
            P("fsdp"),
        ),
        check_vma=False,
    )
```

time: 730 us -> 298 us (0.41)
  blocking collectives: 294 us -> 0 us
  waiting for transfers between devices: 342 us -> 76.2 us
  starting transfers between devices: 0.49 us -> 96 us
  local copies, waits for them, and re-layouts: 21.1 us -> 55.4 us
  other arithmetic: 18.5 us -> 40.1 us
  between operations: 18.8 us -> 2.79 us
  matrix products: 33.6 us -> 17.9 us
    reduce_scatter x7 -> x0, waiting for transfers between devices: 250 us -> none  [the longest x1 72.1 us: shards(): lax.psum_scatter(grad_fc2, 'fsdp', scatter_dimension=1, tiled=True)]
    all_gather x10 -> x0, blocking collectives: 210 us -> none  [the longest x1 35.7 us: shards(): lax.all_gather(query_key_value_weight, 'fsdp', axis=0, tiled=True)]
    ppermute x0 -> x69, starting transfers between devices: none -> 79.4 us  [swap(): return lax.ppermute(block, axis, [(i, i ^ offset) for i in range(count)])]
    unnamed x2 -> x0, blocking collectives: 74 us -> none
    ppermute x0 -> x69, waiting for transfers between devices: none -> 70.9 us  [swap(): return lax.ppermute(block, axis, [(i, i ^ offset) for i in range(count)])]
    all_gather x2 -> x0, waiting for transfers between devices: 52.9 us -> none  [the longest x1 38.5 us: shards(): lax.all_gather(contract_weight, 'fsdp', axis=1, tiled=True)]
    unnamed x15 -> x0, waiting for transfers between devices: 38.2 us -> none
    dot_general x21 -> x16, matrix products: 33.6 us -> 15.2 us  [the longest x1 2.3 us: shards(): jnp.dot(mlp_rows, first_full, preferred_element_type=F32) + hidden_bias]
  transfers between devices with their start and end apart: 12 -> 73, of which waited for: 9 -> 26; matrix products, arithmetic and copies ran while one was open for 8% -> 27% of each run, Pallas kernels for 0% -> 1%
where the time goes in v1:
time: 298 us; the launch traced here: 294 us
  starting transfers between devices  96 us (32%)
  waiting for transfers between devices  76.2 us (26%)
  local copies, waits for them, and re-layouts  55.4 us (19%)
  other arithmetic  40.1 us (13%)
  matrix products  17.9 us (6%)
  Pallas kernels  5.71 us (2%)
    ppermute x69, starting transfers between devices, swap(): return lax.ppermute(block, axis, [(i, i ^ offset) for i in range(count)])  79.4 us
    ppermute x69, waiting for transfers between devices, swap(): return lax.ppermute(block, axis, [(i, i ^ offset) for i in range(count)])  70.9 us
    unnamed x215, local copies, waits for them, and re-layouts  30.1 us
    all_to_all x2, starting transfers between devices, shards(): got = lax.all_to_all(sent, 'fsdp', split_axis=0, concat_axis=0, tiled=True)  8.26 us
    concatenate x4, other arithmetic, tp_gather(): jnp.concatenate([rows] + [swap(rows, 'tp', d) for d in range(1, count)],...  6.21 us
  transfers between devices with their start and end apart: 73, of which 26 were waited for; matrix products, arithmetic and copies ran while one was open for 27% of the time, Pallas kernels for 1%

profile of v1, /device:TPU:0, one launch (start us, length us, event | category | flops | bytes accessed | tf_op | source)
XLA Modules:
  0.0 294.0 jit_solution(7234010971669957152)
XLA Ops:
  3.1 3.1 %collective-permute-start.4 = (bf16[96,768]{1,0:T(8,128)(2,1)S(1)}, bf16[96,768]{1,0:T(8,128)(2,1)S(1)}, u32[]{:S(2)}, u32[]{:S(2)}) collective-permute-start(bf16[96,768]{1,0:T(8,128)(2,1)S(1)} %pad_maximum_fusion.6.refs_0_), channel_id=1, source_target_pairs={{0,8},{4,12},{8,0},{12,4},{16,24},{20,28},{24,16},{28,20},{1,9},{5... | collective-permute-start | bytes 442376 | tf_op jit(solution)/shard_map/ppermute | solution.py:35
  6.2 2.6 collective-permute-start.6
  8.7 1.7 collective-permute-start.3
  14.7 4.9 %all-to-all-start = ((bf16[8,2,480]{2,1,0:T(2,128)(2,1)}), bf16[8,2,480]{2,1,0:T(2,128)(2,1)S(1)}, u32[]{:S(2)}, u32[]{:S(2)}) async-start(bf16[8,2,480]{2,1,0:T(2,128)(2,1)} %reshape.377), calls=%async_computation | async-start | bytes 32768 | tf_op jit(solution)/shard_map/all_to_all | solution.py:219
  19.6 2.0 collective-permute-start.24
  23.9 2.4 collective-permute-start.26
  29.2 3.3 %collective-permute-start.19 = (bf16[96,768]{1,0:T(8,128)(2,1)S(1)}, bf16[96,768]{1,0:T(8,128)(2,1)}, u32[]{:S(2)}, u32[]{:S(2)}) collective-permute-start(bf16[96,768]{1,0:T(8,128)(2,1)S(1)} %copy-done.11), channel_id=1, source_target_pairs={{0,16},{4,20},{8,24},{12,28},{16,0},{20,4},{24,8},{28,12},{1,17},{... | collective-permute-start | bytes 442376 | tf_op jit(solution)/shard_map/ppermute | solution.py:35
  32.5 8.5 %collective-permute-done.26.refs_4_ = bf16[96,768]{1,0:T(8,128)(2,1)S(1)} collective-permute-done((bf16[96,768]{1,0:T(8,128)(2,1)S(1)}, bf16[96,768]{1,0:T(8,128)(2,1)S(1)}, u32[]{:S(2)}, u32[]{:S(2)}) %collective-permute-start.26) | collective-permute-done | bytes 147488 | tf_op jit(solution)/shard_map/ppermute | solution.py:35
  41.0 2.0 collective-permute-start.21
  44.2 4.3 %all-to-all-start.1 = ((f32[8,2,4608]{2,1,0:T(2,128)}), f32[8,2,4608]{2,1,0:T(2,128)}, u32[]{:S(2)}, u32[]{:S(2)}) async-start(f32[8,2,4608]{2,1,0:T(2,128)} %all_to_all.28), calls=%async_computation.1 | async-start | bytes 589824 | tf_op jit(solution)/shard_map/all_to_all | solution.py:236
  48.5 2.0 collective-permute-start.5
  51.2 2.0 collective-permute-start.9
  53.3 2.0 collective-permute-start.27
  81.2 1.8 assemble.4
  88.9 2.4 fusion.88
  94.8 3.3 %collective-permute-done.2 = bf16[2,64,768]{2,0,1:T(2,128)(2,1)S(1)} collective-permute-done((bf16[2,64,768]{2,0,1:T(2,128)(2,1)S(1)}, bf16[2,64,768]{2,0,1:T(2,128)(2,1)S(1)}, u32[]{:S(2)}, u32[]{:S(2)}) %collective-permute-start.2) | collective-permute-done | bytes 196640 | tf_op jit(solution)/shard_map/ppermute | solution.py:35
  102.7 1.7 reshape.327
  104.4 1.7 reshape.325
  106.0 2.7 fusion.103
  108.8 1.8 fusion.12
  118.4 2.2 pad_maximum_fusion.2
  120.8 3.5 %collective-permute-done.11 = bf16[2,64,768]{2,0,1:T(2,128)(2,1)S(1)} collective-permute-done((bf16[2,64,768]{2,0,1:T(2,128)(2,1)S(1)}, bf16[2,64,768]{2,0,1:T(2,128)(2,1)S(1)}, u32[]{:S(2)}, u32[]{:S(2)}) %collective-permute-start.11) | collective-permute-done | bytes 196640 | tf_op jit(solution)/shard_map/ppermute | solution.py:35
  124.3 2.3 collective-permute-done.12
  131.4 5.4 %collective-permute-done.14 = bf16[2,64,768]{2,0,1:T(2,128)(2,1)S(1)} collective-permute-done((bf16[2,64,768]{2,0,1:T(2,128)(2,1)S(1)}, bf16[2,64,768]{2,0,1:T(2,128)(2,1)S(1)}, u32[]{:S(2)}, u32[]{:S(2)}) %collective-permute-start.14) | collective-permute-done | bytes 196640 | tf_op jit(solution)/shard_map/ppermute | solution.py:35
  136.8 2.5 collective-permute-done.15
  140.7 2.3 convert_reduce_fusion
  167.5 3.1 %collective-permute-done.58 = bf16[96,768]{1,0:T(8,128)(2,1)S(1)} collective-permute-done((bf16[96,768]{1,0:T(8,128)(2,1)}, bf16[96,768]{1,0:T(8,128)(2,1)S(1)}, u32[]{:S(2)}, u32[]{:S(2)}) %collective-permute-start.58) | collective-permute-done | bytes 147488 | tf_op jit(solution)/shard_map/ppermute | solution.py:35
  172.1 1.6 collective-permute-done.60
  177.4 1.9 collective-permute-start.66
  179.3 1.9 collective-permute-done.38
  181.2 2.7 collective-permute-start.68
  184.0 1.6 multiply_reduce_fusion.1
  187.5 3.2 %collective-permute-done.66 = bf16[96,768]{1,0:T(8,128)(2,1)S(1)} collective-permute-done((bf16[96,768]{1,0:T(8,128)(2,1)S(1)}, bf16[96,768]{1,0:T(8,128)(2,1)S(1)}, u32[]{:S(2)}, u32[]{:S(2)}) %collective-permute-start.66) | collective-permute-done | bytes 147488 | tf_op jit(solution)/shard_map/ppermute | solution.py:35
  190.7 2.9 collective-permute-start.61
  193.6 1.8 add_bitcast_fusion.1
  196.9 6.4 %collective-permute-done.59 = bf16[96,768]{1,0:T(8,128)(2,1)S(1)} collective-permute-done((bf16[96,768]{1,0:T(8,128)(2,1)S(1)}, bf16[96,768]{1,0:T(8,128)(2,1)S(1)}, u32[]{:S(2)}, u32[]{:S(2)}) %collective-permute-start.59) | collective-permute-done | bytes 147488 | tf_op jit(solution)/shard_map/ppermute | solution.py:35
  205.2 5.9 %collective-permute-done.40 = bf16[2,64,768]{2,0,1:T(2,128)(2,1)S(1)} collective-permute-done((bf16[2,64,768]{2,0,1:T(2,128)(2,1)S(1)}, bf16[2,64,768]{2,0,1:T(2,128)(2,1)S(1)}, u32[]{:S(2)}, u32[]{:S(2)}) %collective-permute-start.40) | collective-permute-done | bytes 196640 | tf_op jit(solution)/shard_map/ppermute | solution.py:35
  215.2 2.1 multiply_reduce_fusion
  232.2 3.6 %collective-permute-done.43 = bf16[2,64,768]{2,0,1:T(2,128)(2,1)} collective-permute-done((bf16[2,64,768]{2,0,1:T(2,128)(2,1)}, bf16[2,64,768]{2,0,1:T(2,128)(2,1)}, u32[]{:S(2)}, u32[]{:S(2)}) %collective-permute-start.43) | collective-permute-done | bytes 196640 | tf_op jit(solution)/shard_map/ppermute | solution.py:35
  239.6 2.3 multiply_reduce_fusion.3
  244.9 3.8 %fusion.24 = (bf16[2,768]{1,0:T(2,128)(2,1)S(1)}, bf16[2,768]{1,0:T(2,128)(2,1)S(1)}, bf16[64,2,768]{2,1,0:T(2,128)(2,1)}, f32[64,2,768]{2,1,0:T(2,128)}) fusion(bf16[64,2,768]{2,1,0:T(2,128)(2,1)S(1)} %copy-done.39, f32[768]{0:T(1024)S(1)} %copy-done.78, bf16[2,64,768]{2,0,1:T(2,128)(2,1)S(1)} %collective-permute-done.32, ...), kind=kLoop, calls=%fused_computation.71 | loop fusion | flops 2749440 | bytes 3558400 | tf_op jit(solution)/shard_map/reduce_sum | solution.py:303
  252.9 1.8 fusion.45
  254.7 4.6 %collective-permute-start.50 = (bf16[96,768]{1,0:T(8,128)(2,1)}, bf16[96,768]{1,0:T(8,128)(2,1)S(1)}, u32[]{:S(2)}, u32[]{:S(2)}) collective-permute-start(bf16[96,768]{1,0:T(8,128)(2,1)} %get-tuple-element.109), channel_id=1, source_target_pairs={{0,8},{4,12},{8,0},{12,4},{16,24},{20,28},{24,16},{28,20},{1,9},{5... | collective-permute-start | bytes 442376 | tf_op jit(solution)/shard_map/ppermute | solution.py:35
  259.5 2.2 collective-permute-start.54
  263.7 3.4 %all-to-all-start.2 = ((bf16[8,2,4992]{2,1,0:T(2,128)(2,1)}), bf16[8,2,4992]{2,1,0:T(2,128)(2,1)S(1)}, u32[]{:S(2)}, u32[]{:S(2)}) async-start(bf16[8,2,4992]{2,1,0:T(2,128)(2,1)} %reshape.379), calls=%async_computation.2 | async-start | bytes 319488 | tf_op jit(solution)/shard_map/all_to_all | solution.py:397
  267.1 8.0 %collective-permute-done.52 = bf16[96,768]{1,0:T(8,128)(2,1)} collective-permute-done((bf16[96,768]{1,0:T(8,128)(2,1)S(1)}, bf16[96,768]{1,0:T(8,128)(2,1)}, u32[]{:S(2)}, u32[]{:S(2)}) %collective-permute-start.52) | collective-permute-done | bytes 147488 | tf_op jit(solution)/shard_map/ppermute | solution.py:35
  282.2 4.0 %all-to-all-start.3 = ((f32[8,2,96]{2,1,0:T(2,128)}), f32[8,2,96]{2,1,0:T(2,128)S(1)}, u32[]{:S(2)}, u32[]{:S(2)}) async-start(f32[8,2,96]{2,1,0:T(2,128)} %copy.259), calls=%async_computation.3 | async-start | bytes 16384 | tf_op jit(solution)/shard_map/all_to_all | solution.py:413
  288.9 4.0 %all-to-all-done.3 = f32[8,2,96]{2,1,0:T(2,128)S(1)} async-done(((f32[8,2,96]{2,1,0:T(2,128)}), f32[8,2,96]{2,1,0:T(2,128)S(1)}, u32[]{:S(2)}, u32[]{:S(2)}) %all-to-all-start.3) | async-done | bytes 6176 | tf_op jit(solution)/shard_map/all_to_all | solution.py:413
  (467 shorter events, 144.1 us)
Async XLA Ops:
  3.1 20.8 %collective-permute-start.4 = (bf16[96,768]{1,0:T(8,128)(2,1)S(1)}, bf16[96,768]{1,0:T(8,128)(2,1)S(1)}, u32[]{:S(2)}, u32[]{:S(2)}) collective-permute-start(bf16[96,768]{1,0:T(8,128)(2,1)S(1)} %pad_maximum_fusion.6.refs_0_), channel_id=1, source_target_pairs={{0,8},{4,12},{8,0},{12,4},{16,24},{20,28},{24,16},{28,20},{1,9},{5... | collective-permute-start | bytes 442376 | tf_op jit(solution)/shard_map/ppermute | solution.py:35
  6.2 20.4 %collective-permute-start.6 = (bf16[96,768]{1,0:T(8,128)(2,1)S(1)}, bf16[96,768]{1,0:T(8,128)(2,1)S(1)}, u32[]{:S(2)}, u32[]{:S(2)}) collective-permute-start(bf16[96,768]{1,0:T(8,128)(2,1)S(1)} %pad_maximum_fusion.6.refs_0_), channel_id=1, source_target_pairs={{0,16},{4,20},{8,24},{12,28},{16,0},{20,4},{24,8},{28,12},{1,17},{... | collective-permute-start | bytes 442376 | tf_op jit(solution)/shard_map/ppermute | solution.py:35
  8.7 18.4 %collective-permute-start.8 = (bf16[96,768]{1,0:T(8,128)(2,1)S(1)}, bf16[96,768]{1,0:T(8,128)(2,1)S(1)}, u32[]{:S(2)}, u32[]{:S(2)}) collective-permute-start(bf16[96,768]{1,0:T(8,128)(2,1)S(1)} %pad_maximum_fusion.6.refs_0_), channel_id=1, source_target_pairs={{0,24},{4,28},{8,16},{12,20},{16,8},{20,12},{24,0},{28,4},{1,25},{... | collective-permute-start | bytes 442376 | tf_op jit(solution)/shard_map/ppermute | solution.py:35
  8.7 19.9 %collective-permute-start.3 = (bf16[96,768]{1,0:T(8,128)(2,1)S(1)}, bf16[96,768]{1,0:T(8,128)(2,1)S(1)}, u32[]{:S(2)}, u32[]{:S(2)}) collective-permute-start(bf16[96,768]{1,0:T(8,128)(2,1)S(1)} %pad_maximum_fusion.6.refs_0_), channel_id=1, source_target_pairs={{0,4},{4,0},{8,12},{12,8},{16,20},{20,16},{24,28},{28,24},{1,5},{5... | collective-permute-start | bytes 442376 | tf_op jit(solution)/shard_map/ppermute | solution.py:35
  14.7 11.6 %all-to-all-start = ((bf16[8,2,480]{2,1,0:T(2,128)(2,1)}), bf16[8,2,480]{2,1,0:T(2,128)(2,1)S(1)}, u32[]{:S(2)}, u32[]{:S(2)}) async-start(bf16[8,2,480]{2,1,0:T(2,128)(2,1)} %reshape.377), calls=%async_computation | async-start | bytes 32768 | tf_op jit(solution)/shard_map/all_to_all | solution.py:219
  19.6 9.6 %collective-permute-start.24 = (bf16[96,768]{1,0:T(8,128)(2,1)}, bf16[96,768]{1,0:T(8,128)(2,1)S(1)}, u32[]{:S(2)}, u32[]{:S(2)}) collective-permute-start(bf16[96,768]{1,0:T(8,128)(2,1)} %bitcast.246), channel_id=1, source_target_pairs={{0,8},{4,12},{8,0},{12,4},{16,24},{20,28},{24,16},{28,20},{1,9},{5... | collective-permute-start | bytes 442376 | tf_op jit(solution)/shard_map/ppermute | solution.py:35
  23.9 17.2 %collective-permute-start.26 = (bf16[96,768]{1,0:T(8,128)(2,1)S(1)}, bf16[96,768]{1,0:T(8,128)(2,1)S(1)}, u32[]{:S(2)}, u32[]{:S(2)}) collective-permute-start(bf16[96,768]{1,0:T(8,128)(2,1)S(1)} %bitcast.247), channel_id=1, source_target_pairs={{0,16},{4,20},{8,24},{12,28},{16,0},{20,4},{24,8},{28,12},{1,17},{... | collective-permute-start | bytes 442376 | tf_op jit(solution)/shard_map/ppermute | solution.py:35
  26.5 21.9 %collective-permute-start.28 = (bf16[96,768]{1,0:T(8,128)(2,1)S(1)}, bf16[96,768]{1,0:T(8,128)(2,1)S(1)}, u32[]{:S(2)}, u32[]{:S(2)}) collective-permute-start(bf16[96,768]{1,0:T(8,128)(2,1)S(1)} %bitcast.248), channel_id=1, source_target_pairs={{0,24},{4,28},{8,16},{12,20},{16,8},{20,12},{24,0},{28,4},{1,25},{... | collective-permute-start | bytes 442376 | tf_op jit(solution)/shard_map/ppermute | solution.py:35
  27.1 23.4 %collective-permute-start.23 = (bf16[96,768]{1,0:T(8,128)(2,1)S(1)}, bf16[96,768]{1,0:T(8,128)(2,1)S(1)}, u32[]{:S(2)}, u32[]{:S(2)}) collective-permute-start(bf16[96,768]{1,0:T(8,128)(2,1)S(1)} %bitcast.249), channel_id=1, source_target_pairs={{0,4},{4,0},{8,12},{12,8},{16,20},{20,16},{24,28},{28,24},{1,5},{5... | collective-permute-start | bytes 442376 | tf_op jit(solution)/shard_map/ppermute | solution.py:35
  28.7 22.6 %collective-permute-start.17 = (bf16[96,768]{1,0:T(8,128)(2,1)S(1)}, bf16[96,768]{1,0:T(8,128)(2,1)}, u32[]{:S(2)}, u32[]{:S(2)}) collective-permute-start(bf16[96,768]{1,0:T(8,128)(2,1)S(1)} %copy-done.11), channel_id=1, source_target_pairs={{0,8},{4,12},{8,0},{12,4},{16,24},{20,28},{24,16},{28,20},{1,9},{5... | collective-permute-start | bytes 442376 | tf_op jit(solution)/shard_map/ppermute | solution.py:35
  29.2 24.0 %collective-permute-start.19 = (bf16[96,768]{1,0:T(8,128)(2,1)S(1)}, bf16[96,768]{1,0:T(8,128)(2,1)}, u32[]{:S(2)}, u32[]{:S(2)}) collective-permute-start(bf16[96,768]{1,0:T(8,128)(2,1)S(1)} %copy-done.11), channel_id=1, source_target_pairs={{0,16},{4,20},{8,24},{12,28},{16,0},{20,4},{24,8},{28,12},{1,17},{... | collective-permute-start | bytes 442376 | tf_op jit(solution)/shard_map/ppermute | solution.py:35
  41.0 12.3 %collective-permute-start.21 = (bf16[96,768]{1,0:T(8,128)(2,1)S(1)}, bf16[96,768]{1,0:T(8,128)(2,1)}, u32[]{:S(2)}, u32[]{:S(2)}) collective-permute-start(bf16[96,768]{1,0:T(8,128)(2,1)S(1)} %copy-done.11), channel_id=1, source_target_pairs={{0,24},{4,28},{8,16},{12,20},{16,8},{20,12},{24,0},{28,4},{1,25},{... | collective-permute-start | bytes 442376 | tf_op jit(solution)/shard_map/ppermute | solution.py:35
  44.2 39.8 %all-to-all-start.1 = ((f32[8,2,4608]{2,1,0:T(2,128)}), f32[8,2,4608]{2,1,0:T(2,128)}, u32[]{:S(2)}, u32[]{:S(2)}) async-start(f32[8,2,4608]{2,1,0:T(2,128)} %all_to_all.28), calls=%async_computation.1 | async-start | bytes 589824 | tf_op jit(solution)/shard_map/all_to_all | solution.py:236
  51.2 12.5 %collective-permute-start.9 = (bf16[96,768]{1,0:T(8,128)(2,1)S(1)}, bf16[96,768]{1,0:T(8,128)(2,1)S(1)}, u32[]{:S(2)}, u32[]{:S(2)}) collective-permute-start(bf16[96,768]{1,0:T(8,128)(2,1)S(1)} %collective-permute-done.8.refs_6_), channel_id=1, source_target_pairs={{0,4},{4,0},{8,12},{12,8},{16,20},{20,16},{24,28},{28,24},{1,5},{5... | collective-permute-start | bytes 442376 | tf_op jit(solution)/shard_map/ppermute | solution.py:35
  53.2 13.7 %collective-permute-start.25 = (bf16[96,768]{1,0:T(8,128)(2,1)S(1)}, bf16[96,768]{1,0:T(8,128)(2,1)S(1)}, u32[]{:S(2)}, u32[]{:S(2)}) collective-permute-start(bf16[96,768]{1,0:T(8,128)(2,1)S(1)} %collective-permute-done.24.refs_2_), channel_id=1, source_target_pairs={{0,4},{4,0},{8,12},{12,8},{16,20},{20,16},{24,28},{28,24},{1,5},{5... | collective-permute-start | bytes 442376 | tf_op jit(solution)/shard_map/ppermute | solution.py:35
  53.3 16.8 %collective-permute-start.27 = (bf16[96,768]{1,0:T(8,128)(2,1)S(1)}, bf16[96,768]{1,0:T(8,128)(2,1)S(1)}, u32[]{:S(2)}, u32[]{:S(2)}) collective-permute-start(bf16[96,768]{1,0:T(8,128)(2,1)S(1)} %collective-permute-done.26.refs_4_), channel_id=1, source_target_pairs={{0,4},{4,0},{8,12},{12,8},{16,20},{20,16},{24,28},{28,24},{1,5},{5... | collective-permute-start | bytes 442376 | tf_op jit(solution)/shard_map/ppermute | solution.py:35
  58.0 23.1 %collective-permute-start.16 = (bf16[96,768]{1,0:T(8,128)(2,1)S(1)}, bf16[96,768]{1,0:T(8,128)(2,1)}, u32[]{:S(2)}, u32[]{:S(2)}) collective-permute-start(bf16[96,768]{1,0:T(8,128)(2,1)S(1)} %copy-done.11), channel_id=1, source_target_pairs={{0,4},{4,0},{8,12},{12,8},{16,20},{20,16},{24,28},{28,24},{1,5},{5... | collective-permute-start | bytes 442376 | tf_op jit(solution)/shard_map/ppermute | solution.py:35
  61.2 15.3 %collective-permute-start.29 = (bf16[96,768]{1,0:T(8,128)(2,1)S(1)}, bf16[96,768]{1,0:T(8,128)(2,1)}, u32[]{:S(2)}, u32[]{:S(2)}) collective-permute-start(bf16[96,768]{1,0:T(8,128)(2,1)S(1)} %collective-permute-done.28.refs_6_), channel_id=1, source_target_pairs={{0,4},{4,0},{8,12},{12,8},{16,20},{20,16},{24,28},{28,24},{1,5},{5... | collective-permute-start | bytes 442376 | tf_op jit(solution)/shard_map/ppermute | solution.py:35
  64.4 16.8 %collective-permute-start.18 = (bf16[96,768]{1,0:T(8,128)(2,1)}, bf16[96,768]{1,0:T(8,128)(2,1)}, u32[]{:S(2)}, u32[]{:S(2)}) collective-permute-start(bf16[96,768]{1,0:T(8,128)(2,1)} %collective-permute-done.17.refs_2_), channel_id=1, source_target_pairs={{0,4},{4,0},{8,12},{12,8},{16,20},{20,16},{24,28},{28,24},{1,5},{5... | collective-permute-start | bytes 442376 | tf_op jit(solution)/shard_map/ppermute | solution.py:35
  67.5 13.6 %collective-permute-start.20 = (bf16[96,768]{1,0:T(8,128)(2,1)}, bf16[96,768]{1,0:T(8,128)(2,1)}, u32[]{:S(2)}, u32[]{:S(2)}) collective-permute-start(bf16[96,768]{1,0:T(8,128)(2,1)} %collective-permute-done.19.refs_4_), channel_id=1, source_target_pairs={{0,4},{4,0},{8,12},{12,8},{16,20},{20,16},{24,28},{28,24},{1,5},{5... | collective-permute-start | bytes 442376 | tf_op jit(solution)/shard_map/ppermute | solution.py:35
  70.7 10.5 %collective-permute-start.22 = (bf16[96,768]{1,0:T(8,128)(2,1)}, bf16[96,768]{1,0:T(8,128)(2,1)}, u32[]{:S(2)}, u32[]{:S(2)}) collective-permute-start(bf16[96,768]{1,0:T(8,128)(2,1)} %collective-permute-done.21.refs_6_), channel_id=1, source_target_pairs={{0,4},{4,0},{8,12},{12,8},{16,20},{20,16},{24,28},{28,24},{1,5},{5... | collective-permute-start | bytes 442376 | tf_op jit(solution)/shard_map/ppermute | solution.py:35
  91.3 27.0 %collective-permute-start.33 = (bf16[2,64,768]{2,0,1:T(2,128)(2,1)}, bf16[2,64,768]{2,0,1:T(2,128)(2,1)}, u32[]{:S(2)}, u32[]{:S(2)}) collective-permute-start(bf16[2,64,768]{2,0,1:T(2,128)(2,1)} %get-tuple-element.89), channel_id=1, source_target_pairs={{0,1},{1,0},{2,3},{3,2},{4,5},{5,4},{6,7},{7,6},{8,9},{9,8},{10,11... | collective-permute-start | bytes 589832 | tf_op jit(solution)/shard_map/ppermute | solution.py:35
  91.7 26.7 %collective-permute-start.34 = (bf16[2,64,768]{2,0,1:T(2,128)(2,1)}, bf16[2,64,768]{2,0,1:T(2,128)(2,1)}, u32[]{:S(2)}, u32[]{:S(2)}) collective-permute-start(bf16[2,64,768]{2,0,1:T(2,128)(2,1)} %get-tuple-element.89), channel_id=1, source_target_pairs={{0,2},{1,3},{2,0},{3,1},{4,6},{5,7},{6,4},{7,5},{8,10},{9,11},{10,... | collective-permute-start | bytes 589832 | tf_op jit(solution)/shard_map/ppermute | solution.py:35
  93.2 25.2 %collective-permute-start.35 = (bf16[2,64,768]{2,0,1:T(2,128)(2,1)}, bf16[2,64,768]{2,0,1:T(2,128)(2,1)}, u32[]{:S(2)}, u32[]{:S(2)}) collective-permute-start(bf16[2,64,768]{2,0,1:T(2,128)(2,1)} %get-tuple-element.89), channel_id=1, source_target_pairs={{0,3},{1,2},{2,1},{3,0},{4,7},{5,6},{6,5},{7,4},{8,11},{9,10},{10,... | collective-permute-start | bytes 589832 | tf_op jit(solution)/shard_map/ppermute | solution.py:35
  147.9 14.8 %collective-permute-start.63 = (bf16[96,768]{1,0:T(8,128)(2,1)}, bf16[96,768]{1,0:T(8,128)(2,1)}, u32[]{:S(2)}, u32[]{:S(2)}) collective-permute-start(bf16[96,768]{1,0:T(8,128)(2,1)} %get-tuple-element.115), channel_id=1, source_target_pairs={{0,4},{4,0},{8,12},{12,8},{16,20},{20,16},{24,28},{28,24},{1,5},{5... | collective-permute-start | bytes 442376 | tf_op jit(solution)/shard_map/ppermute | solution.py:35
  149.0 14.7 %collective-permute-start.65 = (bf16[96,768]{1,0:T(8,128)(2,1)}, bf16[96,768]{1,0:T(8,128)(2,1)}, u32[]{:S(2)}, u32[]{:S(2)}) collective-permute-start(bf16[96,768]{1,0:T(8,128)(2,1)} %get-tuple-element.114), channel_id=1, source_target_pairs={{0,4},{4,0},{8,12},{12,8},{16,20},{20,16},{24,28},{28,24},{1,5},{5... | collective-permute-start | bytes 442376 | tf_op jit(solution)/shard_map/ppermute | solution.py:35
  149.9 14.9 %collective-permute-start.67 = (bf16[96,768]{1,0:T(8,128)(2,1)}, bf16[96,768]{1,0:T(8,128)(2,1)}, u32[]{:S(2)}, u32[]{:S(2)}) collective-permute-start(bf16[96,768]{1,0:T(8,128)(2,1)} %get-tuple-element.113), channel_id=1, source_target_pairs={{0,4},{4,0},{8,12},{12,8},{16,20},{20,16},{24,28},{28,24},{1,5},{5... | collective-permute-start | bytes 442376 | tf_op jit(solution)/shard_map/ppermute | solution.py:35
  151.0 36.4 %collective-permute-start.62 = (bf16[96,768]{1,0:T(8,128)(2,1)}, bf16[96,768]{1,0:T(8,128)(2,1)}, u32[]{:S(2)}, u32[]{:S(2)}) collective-permute-start(bf16[96,768]{1,0:T(8,128)(2,1)} %get-tuple-element.112), channel_id=1, source_target_pairs={{0,4},{4,0},{8,12},{12,8},{16,20},{20,16},{24,28},{28,24},{1,5},{5... | collective-permute-start | bytes 442376 | tf_op jit(solution)/shard_map/ppermute | solution.py:35
  152.7 14.8 %collective-permute-start.56 = (bf16[96,768]{1,0:T(8,128)(2,1)}, bf16[96,768]{1,0:T(8,128)(2,1)}, u32[]{:S(2)}, u32[]{:S(2)}) collective-permute-start(bf16[96,768]{1,0:T(8,128)(2,1)} %get-tuple-element.122), channel_id=1, source_target_pairs={{0,4},{4,0},{8,12},{12,8},{16,20},{20,16},{24,28},{28,24},{1,5},{5... | collective-permute-start | bytes 442376 | tf_op jit(solution)/shard_map/ppermute | solution.py:35
  163.6 10.1 %collective-permute-start.60 = (bf16[96,768]{1,0:T(8,128)(2,1)}, bf16[96,768]{1,0:T(8,128)(2,1)S(1)}, u32[]{:S(2)}, u32[]{:S(2)}) collective-permute-start(bf16[96,768]{1,0:T(8,128)(2,1)} %get-tuple-element.120), channel_id=1, source_target_pairs={{0,4},{4,0},{8,12},{12,8},{16,20},{20,16},{24,28},{28,24},{1,5},{5... | collective-permute-start | bytes 442376 | tf_op jit(solution)/shard_map/ppermute | solution.py:35
  164.7 30.6 %collective-permute-start.55 = (bf16[96,768]{1,0:T(8,128)(2,1)}, bf16[96,768]{1,0:T(8,128)(2,1)S(1)}, u32[]{:S(2)}, u32[]{:S(2)}) collective-permute-start(bf16[96,768]{1,0:T(8,128)(2,1)} %get-tuple-element.119), channel_id=1, source_target_pairs={{0,4},{4,0},{8,12},{12,8},{16,20},{20,16},{24,28},{28,24},{1,5},{5... | collective-permute-start | bytes 442376 | tf_op jit(solution)/shard_map/ppermute | solution.py:35
  175.5 11.9 %collective-permute-start.64 = (bf16[96,768]{1,0:T(8,128)(2,1)S(1)}, bf16[96,768]{1,0:T(8,128)(2,1)S(1)}, u32[]{:S(2)}, u32[]{:S(2)}) collective-permute-start(bf16[96,768]{1,0:T(8,128)(2,1)S(1)} %get-tuple-element.116), channel_id=1, source_target_pairs={{0,8},{4,12},{8,0},{12,4},{16,24},{20,28},{24,16},{28,20},{1,9},{5... | collective-permute-start | bytes 442376 | tf_op jit(solution)/shard_map/ppermute | solution.py:35
  177.4 13.3 %collective-permute-start.66 = (bf16[96,768]{1,0:T(8,128)(2,1)S(1)}, bf16[96,768]{1,0:T(8,128)(2,1)S(1)}, u32[]{:S(2)}, u32[]{:S(2)}) collective-permute-start(bf16[96,768]{1,0:T(8,128)(2,1)S(1)} %get-tuple-element.118), channel_id=1, source_target_pairs={{0,16},{4,20},{8,24},{12,28},{16,0},{20,4},{24,8},{28,12},{1,17},{... | collective-permute-start | bytes 442376 | tf_op jit(solution)/shard_map/ppermute | solution.py:35
  187.4 55.2 %collective-permute-start.30 = (bf16[2,64,768]{2,0,1:T(2,128)(2,1)}, bf16[2,64,768]{2,0,1:T(2,128)(2,1)}, u32[]{:S(2)}, u32[]{:S(2)}) collective-permute-start(bf16[2,64,768]{2,0,1:T(2,128)(2,1)} %copy.284), channel_id=1, source_target_pairs={{0,1},{1,0},{2,3},{3,2},{4,5},{5,4},{6,7},{7,6},{8,9},{9,8},{10,11... | collective-permute-start | bytes 589832 | tf_op jit(solution)/shard_map/ppermute | solution.py:35
  190.7 12.6 %collective-permute-start.59 = (bf16[96,768]{1,0:T(8,128)(2,1)S(1)}, bf16[96,768]{1,0:T(8,128)(2,1)S(1)}, u32[]{:S(2)}, u32[]{:S(2)}) collective-permute-start(bf16[96,768]{1,0:T(8,128)(2,1)S(1)} %get-tuple-element.125), channel_id=1, source_target_pairs={{0,16},{4,20},{8,24},{12,28},{16,0},{20,4},{24,8},{28,12},{1,17},{... | collective-permute-start | bytes 442376 | tf_op jit(solution)/shard_map/ppermute | solution.py:35
  190.7 13.7 %collective-permute-start.61 = (bf16[96,768]{1,0:T(8,128)(2,1)S(1)}, bf16[96,768]{1,0:T(8,128)(2,1)S(1)}, u32[]{:S(2)}, u32[]{:S(2)}) collective-permute-start(bf16[96,768]{1,0:T(8,128)(2,1)S(1)} %get-tuple-element.124), channel_id=1, source_target_pairs={{0,24},{4,28},{8,16},{12,20},{16,8},{20,12},{24,0},{28,4},{1,25},{... | collective-permute-start | bytes 442376 | tf_op jit(solution)/shard_map/ppermute | solution.py:35
  195.4 47.9 %collective-permute-start.31 = (bf16[2,64,768]{2,0,1:T(2,128)(2,1)}, bf16[2,64,768]{2,0,1:T(2,128)(2,1)}, u32[]{:S(2)}, u32[]{:S(2)}) collective-permute-start(bf16[2,64,768]{2,0,1:T(2,128)(2,1)} %copy.285), channel_id=1, source_target_pairs={{0,2},{1,3},{2,0},{3,1},{4,6},{5,7},{6,4},{7,5},{8,10},{9,11},{10,... | collective-permute-start | bytes 589832 | tf_op jit(solution)/shard_map/ppermute | solution.py:35
  231.2 13.5 %collective-permute-start.32 = (bf16[2,64,768]{2,0,1:T(2,128)(2,1)}, bf16[2,64,768]{2,0,1:T(2,128)(2,1)S(1)}, u32[]{:S(2)}, u32[]{:S(2)}) collective-permute-start(bf16[2,64,768]{2,0,1:T(2,128)(2,1)} %copy.286), channel_id=1, source_target_pairs={{0,3},{1,2},{2,1},{3,0},{4,7},{5,6},{6,5},{7,4},{8,11},{9,10},{10,... | collective-permute-start | bytes 589832 | tf_op jit(solution)/shard_map/ppermute | solution.py:35
  235.8 15.6 %collective-permute-start.49 = (bf16[96,768]{1,0:T(8,128)(2,1)}, bf16[96,768]{1,0:T(8,128)(2,1)}, u32[]{:S(2)}, u32[]{:S(2)}) collective-permute-start(bf16[96,768]{1,0:T(8,128)(2,1)} %get-tuple-element.106), channel_id=1, source_target_pairs={{0,4},{4,0},{8,12},{12,8},{16,20},{20,16},{24,28},{28,24},{1,5},{5... | collective-permute-start | bytes 442376 | tf_op jit(solution)/shard_map/ppermute | solution.py:35
  238.1 13.7 %collective-permute-start.51 = (bf16[96,768]{1,0:T(8,128)(2,1)}, bf16[96,768]{1,0:T(8,128)(2,1)}, u32[]{:S(2)}, u32[]{:S(2)}) collective-permute-start(bf16[96,768]{1,0:T(8,128)(2,1)} %get-tuple-element.107), channel_id=1, source_target_pairs={{0,4},{4,0},{8,12},{12,8},{16,20},{20,16},{24,28},{28,24},{1,5},{5... | collective-permute-start | bytes 442376 | tf_op jit(solution)/shard_map/ppermute | solution.py:35
  242.6 10.2 %collective-permute-start.53 = (bf16[96,768]{1,0:T(8,128)(2,1)}, bf16[96,768]{1,0:T(8,128)(2,1)S(1)}, u32[]{:S(2)}, u32[]{:S(2)}) collective-permute-start(bf16[96,768]{1,0:T(8,128)(2,1)} %get-tuple-element.108), channel_id=1, source_target_pairs={{0,4},{4,0},{8,12},{12,8},{16,20},{20,16},{24,28},{28,24},{1,5},{5... | collective-permute-start | bytes 442376 | tf_op jit(solution)/shard_map/ppermute | solution.py:35
  243.3 23.8 %collective-permute-start.48 = (bf16[96,768]{1,0:T(8,128)(2,1)}, bf16[96,768]{1,0:T(8,128)(2,1)S(1)}, u32[]{:S(2)}, u32[]{:S(2)}) collective-permute-start(bf16[96,768]{1,0:T(8,128)(2,1)} %get-tuple-element.105), channel_id=1, source_target_pairs={{0,4},{4,0},{8,12},{12,8},{16,20},{20,16},{24,28},{28,24},{1,5},{5... | collective-permute-start | bytes 442376 | tf_op jit(solution)/shard_map/ppermute | solution.py:35
  251.8 9.9 %collective-permute-start.47 = (bf16[15360]{0:T(1024)(128)(2,1)S(1)}, bf16[15360]{0:T(1024)(128)(2,1)S(1)}, u32[]{:S(2)}, u32[]{:S(2)}) collective-permute-start(bf16[15360]{0:T(1024)(128)(2,1)S(1)} %dynamic-update-slice.4), channel_id=1, source_target_pairs={{0,3},{1,2},{2,1},{3,0},{4,7},{5,6},{6,5},{7,4},{8,11},{9,10},{10,... | collective-permute-start | bytes 92168 | tf_op jit(solution)/shard_map/ppermute | solution.py:35
  254.7 12.4 %collective-permute-start.50 = (bf16[96,768]{1,0:T(8,128)(2,1)}, bf16[96,768]{1,0:T(8,128)(2,1)S(1)}, u32[]{:S(2)}, u32[]{:S(2)}) collective-permute-start(bf16[96,768]{1,0:T(8,128)(2,1)} %get-tuple-element.109), channel_id=1, source_target_pairs={{0,8},{4,12},{8,0},{12,4},{16,24},{20,28},{24,16},{28,20},{1,9},{5... | collective-permute-start | bytes 442376 | tf_op jit(solution)/shard_map/ppermute | solution.py:35
  259.3 15.8 %collective-permute-start.52 = (bf16[96,768]{1,0:T(8,128)(2,1)S(1)}, bf16[96,768]{1,0:T(8,128)(2,1)}, u32[]{:S(2)}, u32[]{:S(2)}) collective-permute-start(bf16[96,768]{1,0:T(8,128)(2,1)S(1)} %get-tuple-element.110), channel_id=1, source_target_pairs={{0,16},{4,20},{8,24},{12,28},{16,0},{20,4},{24,8},{28,12},{1,17},{... | collective-permute-start | bytes 442376 | tf_op jit(solution)/shard_map/ppermute | solution.py:35
  259.5 15.6 %collective-permute-start.54 = (bf16[96,768]{1,0:T(8,128)(2,1)S(1)}, bf16[96,768]{1,0:T(8,128)(2,1)}, u32[]{:S(2)}, u32[]{:S(2)}) collective-permute-start(bf16[96,768]{1,0:T(8,128)(2,1)S(1)} %get-tuple-element.111), channel_id=1, source_target_pairs={{0,24},{4,28},{8,16},{12,20},{16,8},{20,12},{24,0},{28,4},{1,25},{... | collective-permute-start | bytes 442376 | tf_op jit(solution)/shard_map/ppermute | solution.py:35
  263.7 15.7 %all-to-all-start.2 = ((bf16[8,2,4992]{2,1,0:T(2,128)(2,1)}), bf16[8,2,4992]{2,1,0:T(2,128)(2,1)S(1)}, u32[]{:S(2)}, u32[]{:S(2)}) async-start(bf16[8,2,4992]{2,1,0:T(2,128)(2,1)} %reshape.379), calls=%async_computation.2 | async-start | bytes 319488 | tf_op jit(solution)/shard_map/all_to_all | solution.py:397
  282.2 10.6 %all-to-all-start.3 = ((f32[8,2,96]{2,1,0:T(2,128)}), f32[8,2,96]{2,1,0:T(2,128)S(1)}, u32[]{:S(2)}, u32[]{:S(2)}) async-start(f32[8,2,96]{2,1,0:T(2,128)} %copy.259), calls=%async_computation.3 | async-start | bytes 16384 | tf_op jit(solution)/shard_map/all_to_all | solution.py:413
  (115 other events, 1099.9 us)

commit v2 on v0

v2 whole, which is shorter than its diff:
```python
import functools
import math

import jax
import jax.numpy as jnp
from jax import lax
from jax.experimental import pallas as pl
from jax.experimental.pallas import tpu as pltpu
from jax.sharding import PartitionSpec as P

HEAD = 64
EPS = 1e-06
BF = jnp.bfloat16
F32 = jnp.float32
FACTOR = 1.0 / math.sqrt(HEAD)
CURVE = math.sqrt(2.0 / math.pi)
CUBIC = 0.044715


def call(kernel, name, outs, args, scalars=(), scratch=(), flops=0, ordered=()):
    in_specs = (
        [pl.BlockSpec(memory_space=pltpu.SMEM)] * len(scalars)
        + [pl.BlockSpec(memory_space=pl.ANY)] * len(ordered)
        + [pl.BlockSpec(memory_space=pltpu.VMEM)] * len(args)
    )
    skip = len(scalars)

    def body(*refs):
        kernel(*refs[:skip], *refs[skip + len(ordered) :])

    shapes = [jax.ShapeDtypeStruct(shape, dtype) for shape, dtype in outs]
    moved = sum(math.prod(a.shape) * a.dtype.itemsize for a in args)
    moved += sum(math.prod(s.shape) * s.dtype.itemsize for s in shapes)
    return pl.pallas_call(
        body,
        out_shape=shapes,
        in_specs=in_specs,
        out_specs=[pl.BlockSpec(memory_space=pltpu.VMEM)] * len(outs),
        scratch_shapes=list(scratch),
        compiler_params=pltpu.CompilerParams(vmem_limit_bytes=24 * 1024 * 1024),
        cost_estimate=pl.CostEstimate(
            flops=int(flops), bytes_accessed=int(moved), transcendentals=0
        ),
        name=name,
    )(*[s.reshape(1).astype(jnp.int32) for s in scalars], *ordered, *args)


def dot(a, b, over=(1, 0)):
    return lax.dot_general(
        a, b, (((over[0],), (over[1],)), ((), ())), preferred_element_type=F32
    )


def normed(v):
    centered = v - jnp.mean(v, axis=-1, keepdims=True)
    scale = lax.rsqrt(jnp.mean(centered * centered, axis=-1, keepdims=True) + EPS)
    return centered * scale, scale


def norm_back(n, scale, grad):
    mean = jnp.mean(grad, axis=-1, keepdims=True)
    along = jnp.mean(grad * n, axis=-1, keepdims=True)
    return (grad - mean - n * along) * scale


def swap(block, axis, offset):
    count = lax.axis_size(axis)
    return lax.ppermute(block, axis, [(i, i ^ offset) for i in range(count)])


def tp_gather(rows):
    far = swap(rows, "tp", 2)
    near = swap(rows, "tp", 1)
    return [rows, near, far, swap(far, "tp", 1)]


def tp_scatter(parts):
    return [parts[0], swap(parts[2], "tp", 2), swap(parts[3], "tp", 3), swap(parts[1], "tp", 1)]


def pack_kernel(cond, qv, proj, second, hidden, out):
    count = out.shape[0]
    feat = qv.shape[1]
    latents = cond.shape[0]
    out[...] = jnp.zeros_like(out)
    value = cond[...].astype(F32)
    act = (value / (1.0 + jnp.exp(-value))).astype(BF).astype(F32)
    rows = [qv[...], proj[...], second[...], hidden[...]]
    for k in range(count):
        out[k, 0:latents, 0:feat] = act[:, k * feat : (k + 1) * feat]
        at = latents
        for row in rows:
            out[k, at : at + row.shape[0], 0:feat] = row.astype(F32)
            at += row.shape[0]


def mod_kernel(got, ada, bias, out, cols_out, scr):
    count, latents, _ = out.shape
    feat = ada.shape[0]
    for f in range(count):
        scr[f * latents : (f + 1) * latents, :] = got[f, 0:latents, :]
    cols = scr[:, 0:feat].astype(BF)
    cols_out[...] = cols
    width = ada.shape[1] // 6
    for j in range(6):
        at = slice(j * width, (j + 1) * width)
        part = dot(cols, ada[:, at]) + bias[:, at]
        for f in range(count):
            out[f, :, at] = part[f * latents : (f + 1) * latents]


def bias_kernel(tp_rank, got, qkv_out, proj_out, second_out, hidden_out, *, latents, feat, tp):
    count = got.shape[0]
    per = count // tp
    first = tp_rank[0] * per
    cols = per * feat
    qkv_out[...] = jnp.zeros_like(qkv_out)
    at = latents
    for i in range(per):
        f = first + i
        here = slice(i * feat, (i + 1) * feat)
        qkv_out[0:1, here] = got[f, at : at + 1, 0:feat]
        qkv_out[0:1, 2 * cols + i * feat : 2 * cols + (i + 1) * feat] = got[
            f, at + 1 : at + 2, 0:feat
        ]
        for r in range(tp):
            lane = (i * tp + r) * feat
            hidden_out[0:1, lane : lane + feat] = got[f, at + 4 + r : at + 5 + r, 0:feat]
    for f in range(count):
        here = slice(f * feat, (f + 1) * feat)
        proj_out[0:1, here] = got[f, at + 2 : at + 3, 0:feat]
        second_out[0:1, here] = got[f, at + 3 : at + 4, 0:feat]


def assemble_kernel(rank, *refs):
    *blocks, qkv_out, proj_out = refs
    cut = qkv_out.shape[1]
    for k, block in enumerate(blocks):
        rows = block.shape[0]
        at = pl.ds(pl.multiple_of(jnp.bitwise_xor(rank[0], k) * rows, rows), rows)
        qkv_out[at, :] = block[:, :cut]
        proj_out[at, :] = block[:, cut:]


def first_norm_kernel(got, x, mod_out, out):
    mod = got[0]
    for f in range(1, got.shape[0]):
        mod = mod + got[f]
    mod_out[...] = mod
    latents = mod.shape[0]
    width = x.shape[1]
    rows = x.shape[0] // latents
    for l in range(latents):
        here = slice(l * rows, (l + 1) * rows)
        n, _ = normed(x[here, :].astype(F32))
        shift, scale = mod[l : l + 1, :width], mod[l : l + 1, width : 2 * width]
        out[here, :] = (n * (1.0 + scale) + shift).astype(BF)


def gate_grad_kernel(cot, mod, out, bias_out):
    latents = mod.shape[0]
    width = cot.shape[1]
    rows = cot.shape[0] // latents
    total = jnp.zeros((1, width), F32)
    for l in range(latents):
        here = slice(l * rows, (l + 1) * rows)
        value = (cot[here, :].astype(F32) * mod[l : l + 1, 5 * width :]).astype(BF)
        out[here, :] = value
        total = total + jnp.sum(value.astype(F32), axis=0, keepdims=True)
    bias_out[...] = total


def unpack_rows(blocks, rows, latents):
    part = blocks[0].shape[0] // latents
    whole = part * len(blocks)
    for b, block in enumerate(blocks):
        for l in range(latents):
            rows[l * whole + b * part : l * whole + (b + 1) * part, :] = block[
                l * part : (l + 1) * part, :
            ]


def put_parts(value, parts, latent):
    part = value.shape[0] // len(parts)
    for b, out in enumerate(parts):
        out[latent * part : (latent + 1) * part, :] = value[b * part : (b + 1) * part]


def softmax(q, k):
    scores = dot(q, k, (1, 1)) * FACTOR
    weights = jnp.exp(scores - jnp.max(scores, axis=-1, keepdims=True))
    return weights * (1.0 / jnp.sum(weights, axis=-1, keepdims=True))


def attn_kernel(x0, x1, x2, x3, qkv_w, proj_w, bias, rows, qkv, att, p0, p1, p2, p3, *, latents):
    unpack_rows([x0, x1, x2, x3], rows, latents)
    cols = proj_w.shape[1]
    size = rows.shape[0] // latents
    for l in range(latents):
        here = slice(l * size, (l + 1) * size)
        projected = (dot(rows[here, :], qkv_w[...]) + bias[...]).astype(BF)
        qkv[here, :] = projected
        mixed = []
        for h in range(cols // HEAD):
            q, k, v = [
                projected[:, j * cols + h * HEAD : j * cols + (h + 1) * HEAD] for j in range(3)
            ]
            mixed.append(dot(softmax(q, k).astype(BF), v))
        attended = jnp.concatenate(mixed, axis=1).astype(BF)
        att[here, :] = attended
        put_parts(dot(attended, proj_w[...], (1, 1)).astype(BF), [p0, p1, p2, p3], l)


def middle_kernel(x, p0, p1, p2, p3, bias, mod, branch_out, middle_out, out):
    latents = mod.shape[0]
    width = x.shape[1]
    rows = x.shape[0] // latents
    for l in range(latents):
        here = slice(l * rows, (l + 1) * rows)
        branch = bias[...]
        for part in (p0, p1, p2, p3):
            branch = branch + part[here, :].astype(F32)
        branch_out[here, :] = branch
        gate = mod[l : l + 1, 2 * width : 3 * width]
        middle = x[here, :].astype(F32) + gate * branch
        middle_out[here, :] = middle
        n, _ = normed(middle)
        shift = mod[l : l + 1, 3 * width : 4 * width]
        scale = mod[l : l + 1, 4 * width : 5 * width]
        out[here, :] = (n * (1.0 + scale) + shift).astype(BF)


def mlp_kernel(
    x0, x1, x2, x3, g0, g1, g2, g3, both, bias, act_out, pre_out, p0, p1, p2, p3, *, hidden
):
    rows = x0.shape[0]
    for b, (x, g, part) in enumerate(zip((x0, x1, x2, x3), (g0, g1, g2, g3), (p0, p1, p2, p3))):
        here = slice(b * rows, (b + 1) * rows)
        v = dot(x[...], both[:, :hidden]) + bias[...]
        square = v * v
        t = jnp.tanh(CURVE * v * (1.0 + CUBIC * square))
        act_out[here, :] = (0.5 * v * (1.0 + t)).astype(BF)
        slope = 0.5 * (1.0 + t) + 0.5 * v * (1.0 - t * t) * CURVE * (1.0 + 3.0 * CUBIC * square)
        pre = (dot(g[...], both[:, hidden:]) * slope).astype(BF)
        pre_out[here, :] = pre
        part[...] = dot(pre, both[:, :hidden], (1, 1)).astype(BF)


def store_grad(rank, product, keep, send, cols):
    rows = keep.shape[1]
    place = rank[0] // 2
    for mine in range(2):

        @pl.when(rank[0] % 2 == mine)
        def _():
            for z in range(keep.shape[0]):
                to = jnp.bitwise_xor(place, z)
                keep[to, :, cols] = product[(2 * z + mine) * rows : (2 * z + mine + 1) * rows]
                send[to, :, cols] = product[
                    (2 * z + 1 - mine) * rows : (2 * z + 2 - mine) * rows
                ]


def mlp_grad_kernel(
    rank, x0, x1, x2, x3, g0, g1, g2, g3, act, pre, keep, send, bias_out, rows
):
    size = x0.shape[0]
    hidden = act.shape[1]
    for which, blocks in enumerate(((x0, x1, x2, x3), (g0, g1, g2, g3))):
        for b, block in enumerate(blocks):
            rows[b * size : (b + 1) * size, :] = block[...]
        for at in range(0, hidden, 256):
            right = (pre if which == 0 else act)[:, at : at + 256]
            product = dot(rows[...], right, (0, 0)).astype(BF)
            lane = which * hidden + at
            store_grad(rank, product, keep, send, slice(lane, lane + 256))
    bias_out[...] = jnp.sum(pre[...].astype(F32), axis=0, keepdims=True)


def mlp_out_kernel(act, both, p0, p1, p2, p3, *, hidden):
    rows = p0.shape[0]
    for b, part in enumerate((p0, p1, p2, p3)):
        part[...] = dot(act[b * rows : (b + 1) * rows, :], both[:, hidden:], (1, 1)).astype(BF)


def output_kernel(middle, cot, p0, p1, p2, p3, bias, mod, out, sums):
    latents = mod.shape[0]
    width = middle.shape[1]
    rows = middle.shape[0] // latents
    for l in range(latents):
        here = slice(l * rows, (l + 1) * rows)
        branch = bias[...]
        for part in (p0, p1, p2, p3):
            branch = branch + part[here, :].astype(F32)
        out[here, :] = (middle[here, :] + mod[l : l + 1, 5 * width :] * branch).astype(BF)
        sums[l : l + 1, :] = jnp.sum(cot[here, :].astype(F32) * branch, axis=0, keepdims=True)


def middle_back_kernel(cot, middle, branch, p0, p1, p2, p3, mod, grad_out, out, sums):
    latents = mod.shape[0]
    width = middle.shape[1]
    rows = middle.shape[0] // latents
    total = jnp.zeros((1, width), F32)
    for l in range(latents):
        here = slice(l * rows, (l + 1) * rows)
        grad = p0[here, :].astype(F32)
        for part in (p1, p2, p3):
            grad = grad + part[here, :].astype(F32)
        n, scale = normed(middle[here, :])
        sums[3 * l + 1 : 3 * l + 2, :] = jnp.sum(grad, axis=0, keepdims=True)
        sums[3 * l + 2 : 3 * l + 3, :] = jnp.sum(grad * n, axis=0, keepdims=True)
        factor = 1.0 + mod[l : l + 1, 4 * width : 5 * width]
        whole = cot[here, :].astype(F32) + norm_back(n, scale, grad * factor)
        grad_out[here, :] = whole
        sums[3 * l : 3 * l + 1, :] = jnp.sum(whole * branch[here, :], axis=0, keepdims=True)
        low = (whole * mod[l : l + 1, 2 * width : 3 * width]).astype(BF)
        out[here, :] = low
        total = total + jnp.sum(low.astype(F32), axis=0, keepdims=True)
    sums[3 * latents : 3 * latents + 1, :] = total


def attn_back_kernel(
    g0, g1, g2, g3, qkv_w, proj_w, qkv, rows, grads, p0, p1, p2, p3, *, latents
):
    unpack_rows([g0, g1, g2, g3], rows, latents)
    cols = proj_w.shape[1]
    size = rows.shape[0] // latents
    for l in range(latents):
        here = slice(l * size, (l + 1) * size)
        back = dot(rows[here, :], proj_w[...]).astype(BF)
        projected = qkv[here, :]
        found = [[], [], []]
        for h in range(cols // HEAD):
            q, k, v = [
                projected[:, j * cols + h * HEAD : j * cols + (h + 1) * HEAD] for j in range(3)
            ]
            up = back[:, h * HEAD : (h + 1) * HEAD]
            probs = softmax(q, k)
            grad_probs = dot(up, v, (1, 1))
            inner = jnp.sum(probs * grad_probs, axis=-1, keepdims=True)
            scores = (probs * (grad_probs - inner)).astype(BF)
            found[0].append(dot(scores, k) * FACTOR)
            found[1].append(dot(scores, q, (0, 0)) * FACTOR)
            found[2].append(dot(probs.astype(BF), up, (0, 0)))
        grad = jnp.concatenate(found[0] + found[1] + found[2], axis=1).astype(BF)
        grads[here, :] = grad
        put_parts(dot(grad, qkv_w[...], (1, 1)).astype(BF), [p0, p1, p2, p3], l)


def attn_grad_kernel(rank, rows, grads, back, att, keep, send, bias_out):
    cols = att.shape[1]
    for at in range(0, 3 * cols, cols):
        product = dot(rows[...], grads[:, at : at + cols], (0, 0)).astype(BF)
        store_grad(rank, product, keep, send, slice(at, at + cols))
    product = dot(back[...], att[...], (0, 0)).astype(BF)
    store_grad(rank, product, keep, send, slice(3 * cols, 4 * cols))
    bias_out[...] = jnp.sum(grads[...].astype(F32), axis=0, keepdims=True)


def input_back_kernel(
    x, grad_middle, p0, p1, p2, p3, mod, sums, gates, fc2, fc1, qkv, out, pack, scr
):
    latents = mod.shape[0]
    width = x.shape[1]
    rows = x.shape[0] // latents
    cols = qkv.shape[1] // 3
    scr[...] = jnp.zeros_like(scr)
    for l in range(latents):
        here = slice(l * rows, (l + 1) * rows)
        grad = p0[here, :].astype(F32)
        for part in (p1, p2, p3):
            grad = grad + part[here, :].astype(F32)
        n, scale = normed(x[here, :].astype(F32))
        scr[6 * l : 6 * l + 1, :] = jnp.sum(grad, axis=0, keepdims=True)
        scr[6 * l + 1 : 6 * l + 2, :] = jnp.sum(grad * n, axis=0, keepdims=True)
        scr[6 * l + 2 : 6 * l + 5, :] = sums[3 * l : 3 * l + 3, :]
        scr[6 * l + 5 : 6 * l + 6, :] = gates[l : l + 1, :]
        factor = 1.0 + mod[l : l + 1, width : 2 * width]
        out[here, :] = grad_middle[here, :] + norm_back(n, scale, grad * factor)
    at = 6 * latents
    scr[at : at + 1, :] = sums[3 * latents : 3 * latents + 1, :]
    scr[at + 1 : at + 2, :] = fc2[...]
    scr[at + 2 : at + 3, :] = fc1[...]
    scr[at + 3 : at + 4, 0:cols] = qkv[:, 0:cols]
    scr[at + 3 : at + 4, cols : 2 * cols] = qkv[:, 2 * cols :]
    pack[...] = scr[...].astype(BF)


def spread_kernel(tp_rank, k0, k1, k2, k3, out, parts, total, *, latents, feat):
    count = out.shape[0]
    packs = (k0, k1, k2, k3)
    per = count // len(packs)
    cols = per * feat
    mods = 6 * latents
    summed = jnp.zeros(k0.shape, F32)
    for d, pack in enumerate(packs):
        value = pack[...].astype(F32)
        parts[jnp.bitwise_xor(tp_rank[0], d)] = value
        summed = summed + value
    total[...] = summed
    for k in range(count):
        t, i = k // per, k % per
        here = slice(k * feat, (k + 1) * feat)
        row = slice(mods, mods + 1)
        total[row, :] = jnp.zeros((1, k0.shape[1]), F32)
        total[row, 0:feat] = parts[t, mods + 3 : mods + 4, i * feat : (i + 1) * feat]
        total[row, feat : 2 * feat] = parts[
            t, mods + 3 : mods + 4, cols + i * feat : cols + (i + 1) * feat
        ]
        total[row, 2 * feat : 3 * feat] = summed[mods : mods + 1, here]
        total[row, 3 * feat : 4 * feat] = summed[mods + 1 : mods + 2, here]
        total[row, 4 * feat : 8 * feat] = parts[
            t, mods + 2 : mods + 3, 4 * i * feat : 4 * (i + 1) * feat
        ]
        out[k] = total[...].astype(BF)


def scatter_two(keep, send):
    got = swap(send, "fsdp", 1)
    moved = [swap((keep[d].astype(F32) + got[d].astype(F32)).astype(BF), "fsdp", 2 * d) for d in range(1, keep.shape[0])]
    total = keep[0].astype(F32) + got[0].astype(F32)
    for part in moved:
        total = total + part.astype(F32)
    return total


def shards(
    inputs,
    conditioning,
    ada_weight,
    ada_bias,
    query_key_value_weight,
    qv_bias,
    attention_output_weight,
    attention_output_bias,
    expand_weight,
    hidden_layer_bias,
    contract_weight,
    contract_bias,
    out_cotangent,
):
    tp_rank = lax.axis_index("tp")
    tp_count = lax.axis_size("tp")
    rank = lax.axis_index("fsdp")
    count = lax.axis_size("fsdp")
    positions, latents, width = inputs.shape
    feat = ada_weight.shape[0]
    cols = query_key_value_weight.shape[2]
    hidden = expand_weight.shape[1]
    hidden_part = hidden_layer_bias.shape[0]
    mod_part = ada_bias.shape[0]
    rows = positions * latents
    tokens = rows * tp_count
    mods = 6 * latents
    direct = count == 8
    block = ((rows, width), BF)
    block_f32 = ((rows, width), F32)

    mlp_own = jnp.concatenate([expand_weight, contract_weight.T], axis=1)
    mlp_full = lax.all_gather(mlp_own, "fsdp", axis=0, tiled=True)
    attn_own = jnp.concatenate(
        [query_key_value_weight.reshape(feat, 3 * cols), attention_output_weight.T], axis=1
    )
    if direct:
        blocks = {0: attn_own}
        for d in (2, 4, 6):
            blocks[d] = swap(attn_own, "fsdp", d)
        for d in (0, 2, 4, 6):
            blocks[d + 1] = swap(blocks[d], "fsdp", 1)
        qkv_full, proj_full = call(
            assemble_kernel,
            "attn_weights",
            [((width, 3 * cols), BF), ((width, cols), BF)],
            [blocks[k] for k in range(count)],
            [rank],
        )
    else:
        attn_full = lax.all_gather(attn_own, "fsdp", axis=0, tiled=True)
        qkv_full, proj_full = attn_full[:, : 3 * cols], attn_full[:, 3 * cols :]

    sent = call(
        pack_kernel,
        "pack_conditioning",
        [((count, 16, 128), F32)],
        [
            conditioning,
            qv_bias,
            attention_output_bias.reshape(1, feat),
            contract_bias.reshape(1, feat),
            hidden_layer_bias.reshape(tp_count, feat),
        ],
    )[0]
    got = lax.all_to_all(sent, "fsdp", split_axis=0, concat_axis=0, tiled=True)
    bias_row = lax.dynamic_update_slice(
        jnp.zeros((1, mod_part * count), F32),
        ada_bias.astype(F32).reshape(1, mod_part),
        (0, rank * mod_part),
    )
    mod_partial, cond_cols = call(
        mod_kernel,
        "modulation",
        [((count, latents, 6 * width), F32), ((count * latents, feat), BF)],
        [got, ada_weight, bias_row],
        scratch=[pltpu.VMEM((count * latents, 128), F32)],
    )
    qkv_bias, proj_bias, second_bias, hidden_bias = call(
        functools.partial(bias_kernel, latents=latents, feat=feat, tp=tp_count),
        "biases",
        [((1, 3 * cols), F32), ((1, width), F32), ((1, width), F32), ((1, hidden), F32)],
        [got],
        [tp_rank],
    )
    mod_got = lax.all_to_all(mod_partial, "fsdp", split_axis=0, concat_axis=0, tiled=True)

    x = inputs.transpose(1, 0, 2).reshape(rows, width)
    cot = out_cotangent.transpose(1, 0, 2).reshape(rows, width)
    mod, attn_in = call(
        first_norm_kernel, "first_norm", [((latents, 6 * width), F32), block], [mod_got, x]
    )
    x_blocks = tp_gather(attn_in)
    grad_mlp, fc2_part = call(
        gate_grad_kernel,
        "gate_grad",
        [block, ((1, width), F32)],
        [cot, mod],
        ordered=[x_blocks[2]],
    )
    attn_rows, qkv, att, *parts = call(
        functools.partial(attn_kernel, latents=latents),
        "attention",
        [((tokens, width), BF), ((tokens, 3 * cols), BF), ((tokens, cols), BF)] + [block] * 4,
        [*x_blocks, qkv_full, proj_full, qkv_bias],
        flops=4.6e9,
    )
    g_blocks = tp_gather(grad_mlp)
    branch, middle, mlp_in = call(
        middle_kernel,
        "middle",
        [block_f32, block_f32, block],
        [x, *tp_scatter(parts), proj_bias, mod],
    )
    m_blocks = tp_gather(mlp_in)
    act, pre, *parts = call(
        functools.partial(mlp_kernel, hidden=hidden),
        "mlp",
        [((tokens, hidden), BF)] * 2 + [block] * 4,
        [*m_blocks, *g_blocks, mlp_full, hidden_bias],
        flops=4.0e9,
    )
    grad_in = tp_scatter(parts)
    if direct:
        mlp_keep, mlp_send, fc1_part = call(
            mlp_grad_kernel,
            "mlp_weight_grad",
            [((count // 2, feat, 2 * hidden), BF)] * 2 + [((1, hidden), F32)],
            [*m_blocks, *g_blocks, act, pre],
            [rank],
            scratch=[pltpu.VMEM((tokens, width), BF)],
            flops=2.4e9,
            ordered=[parts[3]],
        )
        mlp_sum = scatter_two(mlp_keep, mlp_send)
    else:
        mlp_grad = jnp.concatenate(
            [
                dot(jnp.concatenate(m_blocks), pre, (0, 0)),
                dot(jnp.concatenate(g_blocks), act, (0, 0)),
            ],
            axis=1,
        )
        mlp_sum = lax.psum_scatter(mlp_grad, "fsdp", scatter_dimension=0, tiled=True)
        fc1_part = jnp.sum(pre.astype(F32), axis=0, keepdims=True)

    grad_middle, grad_attn, sums = call(
        middle_back_kernel,
        "middle_back",
        [block_f32, block, ((8, width), F32)],
        [cot, middle, branch, *grad_in, mod],
    )
    a_blocks = tp_gather(grad_attn)
    parts = call(
        functools.partial(mlp_out_kernel, hidden=hidden),
        "mlp_out",
        [block] * 4,
        [act, mlp_full],
        flops=1.2e9,
        ordered=[a_blocks[2]],
    )
    mlp_parts = tp_scatter(parts)
    back_rows, grads, *parts = call(
        functools.partial(attn_back_kernel, latents=latents),
        "attention_back",
        [((tokens, width), BF), ((tokens, 3 * cols), BF)] + [block] * 4,
        [*a_blocks, qkv_full, proj_full, qkv],
        flops=6.0e9,
    )
    grad_in = tp_scatter(parts)
    output, gates = call(
        output_kernel,
        "output",
        [block, ((8, width), F32)],
        [middle, cot, *mlp_parts, second_bias, mod],
    )
    if direct:
        attn_keep, attn_send, qkv_part = call(
            attn_grad_kernel,
            "attn_weight_grad",
            [((count // 2, feat, 4 * cols), BF)] * 2 + [((1, 3 * cols), F32)],
            [attn_rows, grads, back_rows, att],
            [rank],
            flops=1.2e9,
            ordered=[parts[3]],
        )
        attn_sum = scatter_two(attn_keep, attn_send)
    else:
        attn_grad = jnp.concatenate(
            [dot(attn_rows, grads, (0, 0)), dot(back_rows, att, (0, 0))], axis=1
        )
        attn_sum = lax.psum_scatter(attn_grad, "fsdp", scatter_dimension=0, tiled=True)
        qkv_part = jnp.sum(grads.astype(F32), axis=0, keepdims=True)

    inputs_grad, pack = call(
        input_back_kernel,
        "input_back",
        [block_f32, ((16, width), BF)],
        [x, grad_middle, *grad_in, mod, sums, gates, fc2_part, fc1_part, qkv_part],
        scratch=[pltpu.VMEM((16, width), F32)],
    )
    packs = [pack] + [swap(pack, "tp", d) for d in range(1, tp_count)]
    sent = call(
        functools.partial(spread_kernel, latents=latents, feat=feat),
        "spread",
        [((count, 16, width), BF)],
        packs,
        [tp_rank],
        scratch=[pltpu.VMEM((tp_count, 16, width), F32), pltpu.VMEM((16, width), F32)],
    )[0]
    got = lax.all_to_all(sent, "fsdp", split_axis=0, concat_axis=0, tiled=True)
    grad_mod_all = got[:, :mods].reshape(count * latents, 6 * width)
    silu_cols = dot(grad_mod_all, ada_weight, (1, 1))
    silu_got = lax.all_to_all(
        silu_cols.reshape(count, latents, feat), "fsdp", split_axis=0, concat_axis=0, tiled=True
    )
    ada_weight_grad = dot(cond_cols, grad_mod_all, (0, 0))
    bias_grads = jnp.sum(got[:, mods].astype(F32), axis=0)
    ada_bias_grad = jnp.sum(
        lax.dynamic_slice_in_dim(grad_mod_all, rank * mod_part, mod_part, 1).astype(F32), axis=0
    )
    silu_grad = silu_got.transpose(1, 0, 2).reshape(latents, width)
    cond_grad = jax.vjp(jax.nn.silu, conditioning.astype(F32))[1](silu_grad)[0]

    return (
        output.reshape(latents, positions, width).transpose(1, 0, 2),
        inputs_grad.reshape(latents, positions, width).transpose(1, 0, 2),
        cond_grad,
        ada_weight_grad,
        ada_bias_grad,
        attn_sum[:, : 3 * cols].reshape(feat, 3, cols),
        bias_grads[: 2 * feat].reshape(2, feat),
        attn_sum[:, 3 * cols :].T,
        bias_grads[2 * feat : 3 * feat],
        mlp_sum[:, :hidden],
        bias_grads[4 * feat : 4 * feat + hidden_part],
        mlp_sum[:, hidden:].T,
        bias_grads[3 * feat : 4 * feat],
    )


def solution(mesh):
    return jax.shard_map(
        shards,
        mesh=mesh,
        in_specs=(
            P("tp", "fsdp", None),
            P("fsdp", None),
            P("fsdp", None),
            P("fsdp"),
            P("fsdp", None, "tp"),
            P(None, "fsdp"),
            P("tp", "fsdp"),
            P("fsdp"),
            P("fsdp", "tp"),
            P("fsdp"),
            P("tp", "fsdp"),
            P("fsdp"),
            P("tp", "fsdp", None),
        ),
        out_specs=(
            P("tp", "fsdp", None),
            P("tp", "fsdp", None),
            P("fsdp", None),
            P("fsdp", None),
            P("fsdp"),
            P("fsdp", None, "tp"),
            P(None, "fsdp"),
            P("tp", "fsdp"),
            P("fsdp"),
            P("fsdp", "tp"),
            P("fsdp"),
            P("tp", "fsdp"),
            P("fsdp"),
        ),
        check_vma=False,
    )
```

time: 730 us -> 262 us (0.36)
  blocking collectives: 294 us -> 0 us
  waiting for transfers between devices: 342 us -> 108 us
  starting transfers between devices: 0.49 us -> 76.6 us
  matrix products: 33.6 us -> 1.93 us
  Pallas kernels: 0 us -> 24.9 us
  other arithmetic: 18.5 us -> 8.86 us
    reduce_scatter x7 -> x0, waiting for transfers between devices: 250 us -> none  [the longest x1 72.1 us: shards(): lax.psum_scatter(grad_fc2, 'fsdp', scatter_dimension=1, tiled=True)]
    all_gather x10 -> x0, blocking collectives: 210 us -> none  [the longest x1 35.7 us: shards(): lax.all_gather(query_key_value_weight, 'fsdp', axis=0, tiled=True)]
    unnamed x2 -> x0, blocking collectives: 74 us -> none
    ppermute x0 -> x42, waiting for transfers between devices: none -> 61.5 us  [swap(): return lax.ppermute(block, axis, [(i, i ^ offset) for i in range(count)])]
    all_gather x2 -> x1, waiting for transfers between devices: 52.9 us -> 0.01 us  [shards(): mlp_full = lax.all_gather(mlp_own, 'fsdp', axis=0, tiled=True)]
    ppermute x0 -> x42, starting transfers between devices: none -> 52.3 us  [swap(): return lax.ppermute(block, axis, [(i, i ^ offset) for i in range(count)])]
    all_to_all x0 -> x4, waiting for transfers between devices: none -> 46.4 us  [the longest x1 25.8 us: shards(): lax.all_to_all(silu_cols.reshape(count, latents, feat), 'fsdp', split_axi...]
    unnamed x15 -> x1, waiting for transfers between devices: 38.2 us -> 0.02 us
  transfers between devices with their start and end apart: 12 -> 47, of which waited for: 9 -> 21; matrix products, arithmetic and copies ran while one was open for 8% -> 6% of each run, Pallas kernels for 0% -> 8%
where the time goes in v2:
time: 262 us; the launch traced here: 261 us
  waiting for transfers between devices  108 us (41%)
  starting transfers between devices  76.6 us (29%)
  local copies, waits for them, and re-layouts  26.3 us (10%)
  Pallas kernels  24.9 us (10%)
  between operations  14.5 us (6%)
  other arithmetic  8.86 us (3%)
    ppermute x42, waiting for transfers between devices, swap(): return lax.ppermute(block, axis, [(i, i ^ offset) for i in range(count)])  61.5 us
    ppermute x42, starting transfers between devices, swap(): return lax.ppermute(block, axis, [(i, i ^ offset) for i in range(count)])  52.3 us
    all_to_all x1, waiting for transfers between devices, shards(): lax.all_to_all(silu_cols.reshape(count, latents, feat), 'fsdp', split_axi...  25.8 us
    pallas_call x17, Pallas kernels, call(): pl.pallas_call(body, out_shape=shapes, in_specs=in_specs, out_specs=[pl.B...  24.9 us
    unnamed x86, local copies, waits for them, and re-layouts  18.6 us
    all_to_all x2, starting transfers between devices, shards(): got = lax.all_to_all(sent, 'fsdp', split_axis=0, concat_axis=0, tiled=True)  17.5 us
    all_to_all x2, waiting for transfers between devices, shards(): got = lax.all_to_all(sent, 'fsdp', split_axis=0, concat_axis=0, tiled=True)  10.8 us
    all_to_all x1, waiting for transfers between devices, shards(): lax.all_to_all(mod_partial, 'fsdp', split_axis=0, concat_axis=0, tiled=True)  9.73 us
  transfers between devices with their start and end apart: 47, of which 21 were waited for; matrix products, arithmetic and copies ran while one was open for 6% of the time, Pallas kernels for 8%

profile of v2, /device:TPU:0, one launch (start us, length us, event | category | flops | bytes accessed | tf_op | source)
XLA Modules:
  0.0 260.9 jit_solution(11290518546014833608)
XLA Ops:
  7.2 1.8 pad_maximum_fusion
  13.2 7.3 %all-to-all-start = ((f32[8,16,128]{2,1,0:T(8,128)}), f32[8,16,128]{2,1,0:T(8,128)S(1)}, u32[]{:S(2)}, u32[]{:S(2)}) async-start(f32[8,16,128]{2,1,0:T(8,128)} %pack_conditioning.1), calls=%async_computation | async-start | bytes 131072 | tf_op jit(solution)/shard_map/all_to_all | solution.py:493
  21.3 6.5 %all-to-all-done.refs_0_.refs_1_ = f32[8,16,128]{2,1,0:T(8,128)S(1)} async-done(((f32[8,16,128]{2,1,0:T(8,128)}), f32[8,16,128]{2,1,0:T(8,128)S(1)}, u32[]{:S(2)}, u32[]{:S(2)}) %all-to-all-start) | async-done | bytes 65568 | tf_op jit(solution)/shard_map/all_to_all | solution.py:493
  28.8 3.5 %all-to-all-start.1 = ((f32[8,2,4608]{2,1,0:T(2,128)}), f32[8,2,4608]{2,1,0:T(2,128)S(1)}, u32[]{:S(2)}, u32[]{:S(2)}) async-start(f32[8,2,4608]{2,1,0:T(2,128)} %get-tuple-element.64), calls=%async_computation.1 | async-start | bytes 589824 | tf_op jit(solution)/shard_map/all_to_all | solution.py:513
  32.7 9.7 %all-to-all-done.1.refs_0_ = f32[8,2,4608]{2,1,0:T(2,128)S(1)} async-done(((f32[8,2,4608]{2,1,0:T(2,128)}), f32[8,2,4608]{2,1,0:T(2,128)S(1)}, u32[]{:S(2)}, u32[]{:S(2)}) %all-to-all-start.1) | async-done | bytes 294944 | tf_op jit(solution)/shard_map/all_to_all | solution.py:513
  42.7 1.6 collective-permute-start.1
  44.4 1.2 collective-permute-start.3
  45.6 2.4 collective-permute-start.6
  48.0 2.0 collective-permute-start.8
  50.0 3.1 %collective-permute-done.3.refs_2_ = bf16[96,768]{1,0:T(8,128)(2,1)S(1)} collective-permute-done((bf16[96,768]{1,0:T(8,128)(2,1)S(1)}, bf16[96,768]{1,0:T(8,128)(2,1)S(1)}, u32[]{:S(2)}, u32[]{:S(2)}) %collective-permute-start.3) | collective-permute-done | bytes 147488 | tf_op jit(solution)/shard_map/ppermute | solution.py:68
  53.6 6.9 %collective-permute-done.4.refs_3_ = bf16[96,768]{1,0:T(8,128)(2,1)S(1)} collective-permute-done((bf16[96,768]{1,0:T(8,128)(2,1)S(1)}, bf16[96,768]{1,0:T(8,128)(2,1)S(1)}, u32[]{:S(2)}, u32[]{:S(2)}) %collective-permute-start.4) | collective-permute-done | bytes 147488 | tf_op jit(solution)/shard_map/ppermute | solution.py:68
  60.8 6.6 %collective-permute-done.6.refs_5_ = bf16[96,768]{1,0:T(8,128)(2,1)S(1)} collective-permute-done((bf16[96,768]{1,0:T(8,128)(2,1)S(1)}, bf16[96,768]{1,0:T(8,128)(2,1)S(1)}, u32[]{:S(2)}, u32[]{:S(2)}) %collective-permute-start.6) | collective-permute-done | bytes 147488 | tf_op jit(solution)/shard_map/ppermute | solution.py:68
  69.6 3.0 %collective-permute-done.7.refs_6_ = bf16[96,768]{1,0:T(8,128)(2,1)S(1)} collective-permute-done((bf16[96,768]{1,0:T(8,128)(2,1)S(1)}, bf16[96,768]{1,0:T(8,128)(2,1)S(1)}, u32[]{:S(2)}, u32[]{:S(2)}) %collective-permute-start.7) | collective-permute-done | bytes 147488 | tf_op jit(solution)/shard_map/ppermute | solution.py:68
  72.6 1.6 collective-permute-done.9.refs_8_
  74.4 3.8 %attention.1 = (bf16[512,768]{1,0:T(8,128)(2,1)S(1)}, bf16[512,576]{1,0:T(8,128)(2,1)S(1)}, bf16[512,192]{1,0:T(8,128)(2,1)S(1)}, bf16[128,768]{1,0:T(8,128)(2,1...) custom-call(bf16[128,768]{1,0:T(8,128)(2,1)S(1)} %get-tuple-element.65.refs_0_, ...), custom_call_target="tpu_custom_call" | custom-call | flops 4600000000 | bytes 4327680 | tf_op jit(solution)/shard_map/attention/pallas_call | solution.py:34
  79.3 1.9 collective-permute-start.12
  81.6 5.2 %collective-permute-done.10.refs_2_ = bf16[128,768]{1,0:T(8,128)(2,1)S(1)} collective-permute-done((bf16[128,768]{1,0:T(8,128)(2,1)S(1)}, bf16[128,768]{1,0:T(8,128)(2,1)S(1)}, u32[]{:S(2)}, u32[]{:S(2)}) %collective-permute-start.10) | collective-permute-done | bytes 196640 | tf_op jit(solution)/shard_map/ppermute | solution.py:68
  87.9 2.7 %collective-permute-start.14 = (bf16[128,768]{1,0:T(8,128)(2,1)S(1)}, bf16[128,768]{1,0:T(8,128)(2,1)S(1)}, u32[]{:S(2)}, u32[]{:S(2)}) collective-permute-start(bf16[128,768]{1,0:T(8,128)(2,1)S(1)} %get-tuple-element.77.refs_0_.refs_2_), channel_id=1, source_target_pairs={{0,2},{1,3},{2,0},{3,1},{4,6},{5,7},{6,4},{7,5},{8,10},{9,11},{10,... | collective-permute-start | bytes 589832 | tf_op jit(solution)/shard_map/ppermute | solution.py:68
  91.0 1.8 collective-permute-done.17.refs_6_.refs_8_
  94.7 1.6 collective-permute-done.14.refs_2_.refs_4_
  99.6 1.7 copy-done.8
  106.8 3.1 %mlp.1 = (bf16[512,768]{1,0:T(8,128)(2,1)S(1)}, bf16[512,768]{1,0:T(8,128)(2,1)S(1)}, bf16[128,768]{1,0:T(8,128)(2,1)S(1)}, bf16[128,768]{1,0:T(8,128)(2,1)S(1)}...) custom-call(bf16[128,768]{1,0:T(8,128)(2,1)S(1)} %copy-done.18, bf16[128,768]{1,0:T(8,128)(2,1)S(1)} %copy-done.27, ...), custom_call_target="tpu_custom_call" | custom-call | flops 4000000000 | bytes 6294528 | tf_op jit(solution)/shard_map/mlp/pallas_call | solution.py:34
  109.9 1.2 collective-permute-start.19
  112.1 5.6 %collective-permute-done.19.refs_4_ = bf16[128,768]{1,0:T(8,128)(2,1)S(1)} collective-permute-done((bf16[128,768]{1,0:T(8,128)(2,1)S(1)}, bf16[128,768]{1,0:T(8,128)(2,1)S(1)}, u32[]{:S(2)}, u32[]{:S(2)}) %collective-permute-start.19) | collective-permute-done | bytes 196640 | tf_op jit(solution)/shard_map/ppermute | solution.py:68
  117.8 2.5 collective-permute-done.20.refs_5_
  120.8 2.2 collective-permute-start.22
  122.9 5.3 %collective-permute-done.22.refs_0_.refs_2_ = bf16[128,768]{1,0:T(8,128)(2,1)S(1)} collective-permute-done((bf16[128,768]{1,0:T(8,128)(2,1)S(1)}, bf16[128,768]{1,0:T(8,128)(2,1)S(1)}, u32[]{:S(2)}, u32[]{:S(2)}) %collective-permute-start.22) | collective-permute-done | bytes 196640 | tf_op jit(solution)/shard_map/ppermute | solution.py:68
  128.3 1.6 mlp_out.1
  129.9 1.7 collective-permute-start.23
  132.2 4.9 %attention_back.1 = (bf16[512,768]{1,0:T(8,128)(2,1)S(1)}, bf16[512,576]{1,0:T(8,128)(2,1)S(1)}, bf16[128,768]{1,0:T(8,128)(2,1)S(1)}, bf16[128,768]{1,0:T(8,128...) custom-call(bf16[128,768]{1,0:T(8,128)(2,1)S(1)} %get-tuple-element.84.refs_0_, ...), custom_call_target="tpu_custom_call" | custom-call | flops 6000000000 | bytes 4718592 | tf_op jit(solution)/shard_map/attention_back/pallas_call | solution.py:34
  137.1 1.7 collective-permute-start.28
  139.3 3.9 %mlp_weight_grad.1 = (bf16[4,96,1536]{2,1,0:T(8,128)(2,1)S(1)}, bf16[4,96,1536]{2,1,0:T(8,128)(2,1)S(1)}, f32[1,768]{1,0:T(1,128)S(1)}) custom-call(s32[1]{0:T(128)} %bitcast.4.refs_0_, bf16[128,768]{1,0:T(8,128)(2,1)S(1)} %get-tuple-element.82.refs_1_, bf16[128,768]{1,0:T(8,128)(2,1)S(1)} %copy-done.19, bf16[128,768]{1,0:T(8,128)(2,1)S(1)} %copy-done.27, ...), custom_call_target="tpu_custom_call" | custom-call | flops 2400000000 | bytes 5508096 | tf_op jit(solution)/shard_map/mlp_weight_grad/pallas_call | solution.py:34
  145.5 2.9 %attn_weight_grad.1 = (bf16[4,96,768]{2,1,0:T(8,128)(2,1)S(1)}, bf16[4,96,768]{2,1,0:T(8,128)(2,1)S(1)}, f32[1,576]{1,0:T(1,128)S(1)}) custom-call(s32[1]{0:T(128)} %bitcast.4.refs_0_, bf16[128,768]{1,0:T(8,128)(2,1)S(1)} %get-tuple-element.96.refs_1_, bf16[512,768]{1,0:T(8,128)(2,1)S(1)} %copy-done.32, bf16[512,576]{1,0:T(8,128)(2,1)S(1)} %get-tuple-element.104.refs_3_, ...), custom_call_target="tpu_custom_call" | custom-call | flops 1200000000 | bytes 3541248 | tf_op jit(solution)/shard_map/attn_weight_grad/pallas_call | solution.py:34
  150.3 1.7 collective-permute-start.32
  152.0 2.1 collective-permute-done.32.refs_3_
  156.2 10.2 %all-to-all-start.2 = ((bf16[8,16,768]{2,1,0:T(8,128)(2,1)}), bf16[8,16,768]{2,1,0:T(8,128)(2,1)S(1)}, u32[]{:S(2)}, u32[]{:S(2)}) async-start(bf16[8,16,768]{2,1,0:T(8,128)(2,1)} %spread.1), calls=%async_computation.2 | async-start | bytes 393216 | tf_op jit(solution)/shard_map/all_to_all | solution.py:638
  166.4 2.0 collective-permute-start.38
  170.4 4.4 %all-to-all-done.2 = bf16[8,16,768]{2,1,0:T(8,128)(2,1)S(1)} async-done(((bf16[8,16,768]{2,1,0:T(8,128)(2,1)}), bf16[8,16,768]{2,1,0:T(8,128)(2,1)S(1)}, u32[]{:S(2)}, u32[]{:S(2)}) %all-to-all-start.2) | async-done | bytes 196640 | tf_op jit(solution)/shard_map/all_to_all | solution.py:638
  175.9 3.3 %all-to-all-start.3 = ((f32[8,2,96]{2,1,0:T(2,128)}), f32[8,2,96]{2,1,0:T(2,128)S(1)}, u32[]{:S(2)}, u32[]{:S(2)}) async-start(f32[8,2,96]{2,1,0:T(2,128)} %copy.66), calls=%async_computation.3 | async-start | bytes 16384 | tf_op jit(solution)/shard_map/all_to_all | solution.py:641
  179.3 1.6 fusion.20
  183.4 25.8 %all-to-all-done.3 = f32[8,2,96]{2,1,0:T(2,128)S(1)} async-done(((f32[8,2,96]{2,1,0:T(2,128)}), f32[8,2,96]{2,1,0:T(2,128)S(1)}, u32[]{:S(2)}, u32[]{:S(2)}) %all-to-all-start.3) | async-done | bytes 6176 | tf_op jit(solution)/shard_map/all_to_all | solution.py:641
  211.1 3.3 %collective-permute-start.37 = (bf16[96,768]{1,0:T(8,128)(2,1)S(1)}, bf16[96,768]{1,0:T(8,128)(2,1)S(1)}, u32[]{:S(2)}, u32[]{:S(2)}) collective-permute-start(bf16[96,768]{1,0:T(8,128)(2,1)S(1)} %get-tuple-element.171), channel_id=1, source_target_pairs={{0,24},{4,28},{8,16},{12,20},{16,8},{20,12},{24,0},{28,4},{1,25},{... | collective-permute-start | bytes 442376 | tf_op jit(solution)/shard_map/ppermute | solution.py:68
  215.5 2.2 fusion.4
  217.7 3.3 %collective-permute-start.41 = (bf16[96,1536]{1,0:T(8,128)(2,1)}, bf16[96,1536]{1,0:T(8,128)(2,1)S(1)}, u32[]{:S(2)}, u32[]{:S(2)}) collective-permute-start(bf16[96,1536]{1,0:T(8,128)(2,1)} %get-tuple-element.168), channel_id=1, source_target_pairs={{0,24},{4,28},{8,16},{12,20},{16,8},{20,12},{24,0},{28,4},{1,25},{... | collective-permute-start | bytes 884744 | tf_op jit(solution)/shard_map/ppermute | solution.py:68
  221.0 15.1 %collective-permute-start.39 = (bf16[96,1536]{1,0:T(8,128)(2,1)S(1)}, bf16[96,1536]{1,0:T(8,128)(2,1)}, u32[]{:S(2)}, u32[]{:S(2)}) collective-permute-start(bf16[96,1536]{1,0:T(8,128)(2,1)S(1)} %get-tuple-element.167), channel_id=1, source_target_pairs={{0,8},{4,12},{8,0},{12,4},{16,24},{20,28},{24,16},{28,20},{1,9},{5... | collective-permute-start | bytes 884744 | tf_op jit(solution)/shard_map/ppermute | solution.py:68
  236.0 4.2 %collective-permute-done.36 = bf16[96,768]{1,0:T(8,128)(2,1)S(1)} collective-permute-done((bf16[96,768]{1,0:T(8,128)(2,1)S(1)}, bf16[96,768]{1,0:T(8,128)(2,1)S(1)}, u32[]{:S(2)}, u32[]{:S(2)}) %collective-permute-start.36) | collective-permute-done | bytes 147488 | tf_op jit(solution)/shard_map/ppermute | solution.py:68
  243.2 8.7 %collective-permute-done.40 = bf16[96,1536]{1,0:T(8,128)(2,1)} collective-permute-done((bf16[96,1536]{1,0:T(8,128)(2,1)}, bf16[96,1536]{1,0:T(8,128)(2,1)}, u32[]{:S(2)}, u32[]{:S(2)}) %collective-permute-start.40) | collective-permute-done | bytes 294944 | tf_op jit(solution)/shard_map/ppermute | solution.py:68
  251.9 1.3 fusion.3
  (183 shorter events, 44.8 us)
Async XLA Ops:
  7.2 92.4 %all-gather.2.cloned.1.call-start = ((), (), s32[]{:S(2)}) async-start(), calls=%async_computation.4 | async-start | bytes 2654208 | tf_op jit(solution)/shard_map/all_gather | solution.py:460
  13.2 14.6 %all-to-all-start = ((f32[8,16,128]{2,1,0:T(8,128)}), f32[8,16,128]{2,1,0:T(8,128)S(1)}, u32[]{:S(2)}, u32[]{:S(2)}) async-start(f32[8,16,128]{2,1,0:T(8,128)} %pack_conditioning.1), calls=%async_computation | async-start | bytes 131072 | tf_op jit(solution)/shard_map/all_to_all | solution.py:493
  28.8 13.7 %all-to-all-start.1 = ((f32[8,2,4608]{2,1,0:T(2,128)}), f32[8,2,4608]{2,1,0:T(2,128)S(1)}, u32[]{:S(2)}, u32[]{:S(2)}) async-start(f32[8,2,4608]{2,1,0:T(2,128)} %get-tuple-element.64), calls=%async_computation.1 | async-start | bytes 589824 | tf_op jit(solution)/shard_map/all_to_all | solution.py:513
  42.7 10.3 %collective-permute-start.1 = (bf16[128,768]{1,0:T(8,128)(2,1)S(1)}, bf16[128,768]{1,0:T(8,128)(2,1)S(1)}, u32[]{:S(2)}, u32[]{:S(2)}) collective-permute-start(bf16[128,768]{1,0:T(8,128)(2,1)S(1)} %get-tuple-element.65.refs_0_), channel_id=1, source_target_pairs={{0,2},{1,3},{2,0},{3,1},{4,6},{5,7},{6,4},{7,5},{8,10},{9,11},{10,... | collective-permute-start | bytes 589832 | tf_op jit(solution)/shard_map/ppermute | solution.py:68
  44.4 8.7 %collective-permute-start.3 = (bf16[96,768]{1,0:T(8,128)(2,1)S(1)}, bf16[96,768]{1,0:T(8,128)(2,1)S(1)}, u32[]{:S(2)}, u32[]{:S(2)}) collective-permute-start(bf16[96,768]{1,0:T(8,128)(2,1)S(1)} %pad_maximum_fusion.1.refs_1_), channel_id=1, source_target_pairs={{0,4},{4,0},{8,12},{12,8},{16,20},{20,16},{24,28},{28,24},{1,5},{5... | collective-permute-start | bytes 442376 | tf_op jit(solution)/shard_map/ppermute | solution.py:68
  45.6 14.9 %collective-permute-start.4 = (bf16[96,768]{1,0:T(8,128)(2,1)S(1)}, bf16[96,768]{1,0:T(8,128)(2,1)S(1)}, u32[]{:S(2)}, u32[]{:S(2)}) collective-permute-start(bf16[96,768]{1,0:T(8,128)(2,1)S(1)} %pad_maximum_fusion.1.refs_1_), channel_id=1, source_target_pairs={{0,8},{4,12},{8,0},{12,4},{16,24},{20,28},{24,16},{28,20},{1,9},{5... | collective-permute-start | bytes 442376 | tf_op jit(solution)/shard_map/ppermute | solution.py:68
  45.6 21.8 %collective-permute-start.6 = (bf16[96,768]{1,0:T(8,128)(2,1)S(1)}, bf16[96,768]{1,0:T(8,128)(2,1)S(1)}, u32[]{:S(2)}, u32[]{:S(2)}) collective-permute-start(bf16[96,768]{1,0:T(8,128)(2,1)S(1)} %pad_maximum_fusion.1.refs_1_), channel_id=1, source_target_pairs={{0,16},{4,20},{8,24},{12,28},{16,0},{20,4},{24,8},{28,12},{1,17},{... | collective-permute-start | bytes 442376 | tf_op jit(solution)/shard_map/ppermute | solution.py:68
  48.0 20.4 %collective-permute-start.8 = (bf16[96,768]{1,0:T(8,128)(2,1)S(1)}, bf16[96,768]{1,0:T(8,128)(2,1)S(1)}, u32[]{:S(2)}, u32[]{:S(2)}) collective-permute-start(bf16[96,768]{1,0:T(8,128)(2,1)S(1)} %pad_maximum_fusion.1.refs_1_), channel_id=1, source_target_pairs={{0,24},{4,28},{8,16},{12,20},{16,8},{20,12},{24,0},{28,4},{1,25},{... | collective-permute-start | bytes 442376 | tf_op jit(solution)/shard_map/ppermute | solution.py:68
  53.0 21.4 %collective-permute-start = (bf16[128,768]{1,0:T(8,128)(2,1)S(1)}, bf16[128,768]{1,0:T(8,128)(2,1)S(1)}, u32[]{:S(2)}, u32[]{:S(2)}) collective-permute-start(bf16[128,768]{1,0:T(8,128)(2,1)S(1)} %get-tuple-element.65.refs_0_), channel_id=1, source_target_pairs={{0,1},{1,0},{2,3},{3,2},{4,5},{5,4},{6,7},{7,6},{8,9},{9,8},{10,11... | collective-permute-start | bytes 589832 | tf_op jit(solution)/shard_map/ppermute | solution.py:68
  53.0 21.4 %collective-permute-start.2 = (bf16[128,768]{1,0:T(8,128)(2,1)S(1)}, bf16[128,768]{1,0:T(8,128)(2,1)}, u32[]{:S(2)}, u32[]{:S(2)}) collective-permute-start(bf16[128,768]{1,0:T(8,128)(2,1)S(1)} %collective-permute-done.1.refs_2_.refs_0_), channel_id=1, source_target_pairs={{0,1},{1,0},{2,3},{3,2},{4,5},{5,4},{6,7},{7,6},{8,9},{9,8},{10,11... | collective-permute-start | bytes 589832 | tf_op jit(solution)/shard_map/ppermute | solution.py:68
  60.5 9.1 %collective-permute-start.5 = (bf16[96,768]{1,0:T(8,128)(2,1)S(1)}, bf16[96,768]{1,0:T(8,128)(2,1)S(1)}, u32[]{:S(2)}, u32[]{:S(2)}) collective-permute-start(bf16[96,768]{1,0:T(8,128)(2,1)S(1)} %collective-permute-done.4.refs_3_), channel_id=1, source_target_pairs={{0,4},{4,0},{8,12},{12,8},{16,20},{20,16},{24,28},{28,24},{1,5},{5... | collective-permute-start | bytes 442376 | tf_op jit(solution)/shard_map/ppermute | solution.py:68
  67.4 5.1 %collective-permute-start.7 = (bf16[96,768]{1,0:T(8,128)(2,1)S(1)}, bf16[96,768]{1,0:T(8,128)(2,1)S(1)}, u32[]{:S(2)}, u32[]{:S(2)}) collective-permute-start(bf16[96,768]{1,0:T(8,128)(2,1)S(1)} %collective-permute-done.6.refs_5_), channel_id=1, source_target_pairs={{0,4},{4,0},{8,12},{12,8},{16,20},{20,16},{24,28},{28,24},{1,5},{5... | collective-permute-start | bytes 442376 | tf_op jit(solution)/shard_map/ppermute | solution.py:68
  68.4 5.7 %collective-permute-start.9 = (bf16[96,768]{1,0:T(8,128)(2,1)S(1)}, bf16[96,768]{1,0:T(8,128)(2,1)S(1)}, u32[]{:S(2)}, u32[]{:S(2)}) collective-permute-start(bf16[96,768]{1,0:T(8,128)(2,1)S(1)} %collective-permute-done.8.refs_7_), channel_id=1, source_target_pairs={{0,4},{4,0},{8,12},{12,8},{16,20},{20,16},{24,28},{28,24},{1,5},{5... | collective-permute-start | bytes 442376 | tf_op jit(solution)/shard_map/ppermute | solution.py:68
  79.0 7.8 %collective-permute-start.10 = (bf16[128,768]{1,0:T(8,128)(2,1)S(1)}, bf16[128,768]{1,0:T(8,128)(2,1)S(1)}, u32[]{:S(2)}, u32[]{:S(2)}) collective-permute-start(bf16[128,768]{1,0:T(8,128)(2,1)S(1)} %get-tuple-element.70), channel_id=1, source_target_pairs={{0,2},{1,3},{2,0},{3,1},{4,6},{5,7},{6,4},{7,5},{8,10},{9,11},{10,... | collective-permute-start | bytes 589832 | tf_op jit(solution)/shard_map/ppermute | solution.py:68
  79.3 8.3 %collective-permute-start.11 = (bf16[128,768]{1,0:T(8,128)(2,1)S(1)}, bf16[128,768]{1,0:T(8,128)(2,1)S(1)}, u32[]{:S(2)}, u32[]{:S(2)}) collective-permute-start(bf16[128,768]{1,0:T(8,128)(2,1)S(1)} %get-tuple-element.71), channel_id=1, source_target_pairs={{0,3},{1,2},{2,1},{3,0},{4,7},{5,6},{6,5},{7,4},{8,11},{9,10},{10,... | collective-permute-start | bytes 589832 | tf_op jit(solution)/shard_map/ppermute | solution.py:68
  79.3 8.3 %collective-permute-start.12 = (bf16[128,768]{1,0:T(8,128)(2,1)S(1)}, bf16[128,768]{1,0:T(8,128)(2,1)S(1)}, u32[]{:S(2)}, u32[]{:S(2)}) collective-permute-start(bf16[128,768]{1,0:T(8,128)(2,1)S(1)} %get-tuple-element.72), channel_id=1, source_target_pairs={{0,1},{1,0},{2,3},{3,2},{4,5},{5,4},{6,7},{7,6},{8,9},{9,8},{10,11... | collective-permute-start | bytes 589832 | tf_op jit(solution)/shard_map/ppermute | solution.py:68
  81.3 11.5 %collective-permute-start.17 = (bf16[128,768]{1,0:T(8,128)(2,1)S(1)}, bf16[128,768]{1,0:T(8,128)(2,1)S(1)}, u32[]{:S(2)}, u32[]{:S(2)}) collective-permute-start(bf16[128,768]{1,0:T(8,128)(2,1)S(1)} %get-tuple-element.78.refs_4_.refs_6_), channel_id=1, source_target_pairs={{0,2},{1,3},{2,0},{3,1},{4,6},{5,7},{6,4},{7,5},{8,10},{9,11},{10,... | collective-permute-start | bytes 589832 | tf_op jit(solution)/shard_map/ppermute | solution.py:68
  87.9 8.3 %collective-permute-start.14 = (bf16[128,768]{1,0:T(8,128)(2,1)S(1)}, bf16[128,768]{1,0:T(8,128)(2,1)S(1)}, u32[]{:S(2)}, u32[]{:S(2)}) collective-permute-start(bf16[128,768]{1,0:T(8,128)(2,1)S(1)} %get-tuple-element.77.refs_0_.refs_2_), channel_id=1, source_target_pairs={{0,2},{1,3},{2,0},{3,1},{4,6},{5,7},{6,4},{7,5},{8,10},{9,11},{10,... | collective-permute-start | bytes 589832 | tf_op jit(solution)/shard_map/ppermute | solution.py:68
  90.6 6.9 %collective-permute-start.16 = (bf16[128,768]{1,0:T(8,128)(2,1)S(1)}, bf16[128,768]{1,0:T(8,128)(2,1)S(1)}, u32[]{:S(2)}, u32[]{:S(2)}) collective-permute-start(bf16[128,768]{1,0:T(8,128)(2,1)S(1)} %get-tuple-element.78.refs_4_.refs_6_), channel_id=1, source_target_pairs={{0,1},{1,0},{2,3},{3,2},{4,5},{5,4},{6,7},{7,6},{8,9},{9,8},{10,11... | collective-permute-start | bytes 589832 | tf_op jit(solution)/shard_map/ppermute | solution.py:68
  92.8 4.7 %collective-permute-start.18 = (bf16[128,768]{1,0:T(8,128)(2,1)S(1)}, bf16[128,768]{1,0:T(8,128)(2,1)S(1)}, u32[]{:S(2)}, u32[]{:S(2)}) collective-permute-start(bf16[128,768]{1,0:T(8,128)(2,1)S(1)} %collective-permute-done.17.refs_6_.refs_8_), channel_id=1, source_target_pairs={{0,1},{1,0},{2,3},{3,2},{4,5},{5,4},{6,7},{7,6},{8,9},{9,8},{10,11... | collective-permute-start | bytes 589832 | tf_op jit(solution)/shard_map/ppermute | solution.py:68
  93.5 4.7 %collective-permute-start.13 = (bf16[128,768]{1,0:T(8,128)(2,1)S(1)}, bf16[128,768]{1,0:T(8,128)(2,1)S(1)}, u32[]{:S(2)}, u32[]{:S(2)}) collective-permute-start(bf16[128,768]{1,0:T(8,128)(2,1)S(1)} %get-tuple-element.77.refs_0_.refs_2_), channel_id=1, source_target_pairs={{0,1},{1,0},{2,3},{3,2},{4,5},{5,4},{6,7},{7,6},{8,9},{9,8},{10,11... | collective-permute-start | bytes 589832 | tf_op jit(solution)/shard_map/ppermute | solution.py:68
  96.2 2.7 %collective-permute-start.15 = (bf16[128,768]{1,0:T(8,128)(2,1)S(1)}, bf16[128,768]{1,0:T(8,128)(2,1)S(1)}, u32[]{:S(2)}, u32[]{:S(2)}) collective-permute-start(bf16[128,768]{1,0:T(8,128)(2,1)S(1)} %collective-permute-done.14.refs_2_.refs_4_), channel_id=1, source_target_pairs={{0,1},{1,0},{2,3},{3,2},{4,5},{5,4},{6,7},{7,6},{8,9},{9,8},{10,11... | collective-permute-start | bytes 589832 | tf_op jit(solution)/shard_map/ppermute | solution.py:68
  109.9 7.8 %collective-permute-start.19 = (bf16[128,768]{1,0:T(8,128)(2,1)S(1)}, bf16[128,768]{1,0:T(8,128)(2,1)S(1)}, u32[]{:S(2)}, u32[]{:S(2)}) collective-permute-start(bf16[128,768]{1,0:T(8,128)(2,1)S(1)} %get-tuple-element.81), channel_id=1, source_target_pairs={{0,2},{1,3},{2,0},{3,1},{4,6},{5,7},{6,4},{7,5},{8,10},{9,11},{10,... | collective-permute-start | bytes 589832 | tf_op jit(solution)/shard_map/ppermute | solution.py:68
  111.2 9.0 %collective-permute-start.20 = (bf16[128,768]{1,0:T(8,128)(2,1)S(1)}, bf16[128,768]{1,0:T(8,128)(2,1)S(1)}, u32[]{:S(2)}, u32[]{:S(2)}) collective-permute-start(bf16[128,768]{1,0:T(8,128)(2,1)S(1)} %get-tuple-element.82.refs_1_), channel_id=1, source_target_pairs={{0,3},{1,2},{2,1},{3,0},{4,7},{5,6},{6,5},{7,4},{8,11},{9,10},{10,... | collective-permute-start | bytes 589832 | tf_op jit(solution)/shard_map/ppermute | solution.py:68
  111.4 8.9 %collective-permute-start.21 = (bf16[128,768]{1,0:T(8,128)(2,1)S(1)}, bf16[128,768]{1,0:T(8,128)(2,1)S(1)}, u32[]{:S(2)}, u32[]{:S(2)}) collective-permute-start(bf16[128,768]{1,0:T(8,128)(2,1)S(1)} %get-tuple-element.83), channel_id=1, source_target_pairs={{0,1},{1,0},{2,3},{3,2},{4,5},{5,4},{6,7},{7,6},{8,9},{9,8},{10,11... | collective-permute-start | bytes 589832 | tf_op jit(solution)/shard_map/ppermute | solution.py:68
  120.8 7.5 %collective-permute-start.22 = (bf16[128,768]{1,0:T(8,128)(2,1)S(1)}, bf16[128,768]{1,0:T(8,128)(2,1)S(1)}, u32[]{:S(2)}, u32[]{:S(2)}) collective-permute-start(bf16[128,768]{1,0:T(8,128)(2,1)S(1)} %get-tuple-element.84.refs_0_), channel_id=1, source_target_pairs={{0,2},{1,3},{2,0},{3,1},{4,6},{5,7},{6,4},{7,5},{8,10},{9,11},{10,... | collective-permute-start | bytes 589832 | tf_op jit(solution)/shard_map/ppermute | solution.py:68
  122.9 9.2 %collective-permute-start.26 = (bf16[128,768]{1,0:T(8,128)(2,1)S(1)}, bf16[128,768]{1,0:T(8,128)(2,1)S(1)}, u32[]{:S(2)}, u32[]{:S(2)}) collective-permute-start(bf16[128,768]{1,0:T(8,128)(2,1)S(1)} %get-tuple-element.84.refs_0_), channel_id=1, source_target_pairs={{0,1},{1,0},{2,3},{3,2},{4,5},{5,4},{6,7},{7,6},{8,9},{9,8},{10,11... | collective-permute-start | bytes 589832 | tf_op jit(solution)/shard_map/ppermute | solution.py:68
  128.3 3.9 %collective-permute-start.27 = (bf16[128,768]{1,0:T(8,128)(2,1)S(1)}, bf16[128,768]{1,0:T(8,128)(2,1)S(1)}, u32[]{:S(2)}, u32[]{:S(2)}) collective-permute-start(bf16[128,768]{1,0:T(8,128)(2,1)S(1)} %collective-permute-done.22.refs_0_.refs_2_), channel_id=1, source_target_pairs={{0,1},{1,0},{2,3},{3,2},{4,5},{5,4},{6,7},{7,6},{8,9},{9,8},{10,11... | collective-permute-start | bytes 589832 | tf_op jit(solution)/shard_map/ppermute | solution.py:68
  129.9 8.9 %collective-permute-start.23 = (bf16[128,768]{1,0:T(8,128)(2,1)S(1)}, bf16[128,768]{1,0:T(8,128)(2,1)S(1)}, u32[]{:S(2)}, u32[]{:S(2)}) collective-permute-start(bf16[128,768]{1,0:T(8,128)(2,1)S(1)} %get-tuple-element.87), channel_id=1, source_target_pairs={{0,2},{1,3},{2,0},{3,1},{4,6},{5,7},{6,4},{7,5},{8,10},{9,11},{10,... | collective-permute-start | bytes 589832 | tf_op jit(solution)/shard_map/ppermute | solution.py:68
  131.7 12.5 %collective-permute-start.24 = (bf16[128,768]{1,0:T(8,128)(2,1)S(1)}, bf16[128,768]{1,0:T(8,128)(2,1)S(1)}, u32[]{:S(2)}, u32[]{:S(2)}) collective-permute-start(bf16[128,768]{1,0:T(8,128)(2,1)S(1)} %get-tuple-element.88), channel_id=1, source_target_pairs={{0,3},{1,2},{2,1},{3,0},{4,7},{5,6},{6,5},{7,4},{8,11},{9,10},{10,... | collective-permute-start | bytes 589832 | tf_op jit(solution)/shard_map/ppermute | solution.py:68
  131.9 12.3 %collective-permute-start.25 = (bf16[128,768]{1,0:T(8,128)(2,1)S(1)}, bf16[128,768]{1,0:T(8,128)(2,1)S(1)}, u32[]{:S(2)}, u32[]{:S(2)}) collective-permute-start(bf16[128,768]{1,0:T(8,128)(2,1)S(1)} %get-tuple-element.89), channel_id=1, source_target_pairs={{0,1},{1,0},{2,3},{3,2},{4,5},{5,4},{6,7},{7,6},{8,9},{9,8},{10,11... | collective-permute-start | bytes 589832 | tf_op jit(solution)/shard_map/ppermute | solution.py:68
  137.1 11.3 %collective-permute-start.28 = (bf16[128,768]{1,0:T(8,128)(2,1)S(1)}, bf16[128,768]{1,0:T(8,128)(2,1)S(1)}, u32[]{:S(2)}, u32[]{:S(2)}) collective-permute-start(bf16[128,768]{1,0:T(8,128)(2,1)S(1)} %get-tuple-element.95), channel_id=1, source_target_pairs={{0,2},{1,3},{2,0},{3,1},{4,6},{5,7},{6,4},{7,5},{8,10},{9,11},{10,... | collective-permute-start | bytes 589832 | tf_op jit(solution)/shard_map/ppermute | solution.py:68
  138.8 10.7 %collective-permute-start.29 = (bf16[128,768]{1,0:T(8,128)(2,1)S(1)}, bf16[128,768]{1,0:T(8,128)(2,1)S(1)}, u32[]{:S(2)}, u32[]{:S(2)}) collective-permute-start(bf16[128,768]{1,0:T(8,128)(2,1)S(1)} %get-tuple-element.96.refs_1_), channel_id=1, source_target_pairs={{0,3},{1,2},{2,1},{3,0},{4,7},{5,6},{6,5},{7,4},{8,11},{9,10},{10,... | collective-permute-start | bytes 589832 | tf_op jit(solution)/shard_map/ppermute | solution.py:68
  138.9 10.7 %collective-permute-start.30 = (bf16[128,768]{1,0:T(8,128)(2,1)S(1)}, bf16[128,768]{1,0:T(8,128)(2,1)S(1)}, u32[]{:S(2)}, u32[]{:S(2)}) collective-permute-start(bf16[128,768]{1,0:T(8,128)(2,1)S(1)} %get-tuple-element.97), channel_id=1, source_target_pairs={{0,1},{1,0},{2,3},{3,2},{4,5},{5,4},{6,7},{7,6},{8,9},{9,8},{10,11... | collective-permute-start | bytes 589832 | tf_op jit(solution)/shard_map/ppermute | solution.py:68
  150.1 2.0 collective-permute-start.31
  150.3 3.8 %collective-permute-start.32 = (bf16[16,768]{1,0:T(8,128)(2,1)S(1)}, bf16[16,768]{1,0:T(8,128)(2,1)S(1)}, u32[]{:S(2)}, u32[]{:S(2)}) collective-permute-start(bf16[16,768]{1,0:T(8,128)(2,1)S(1)} %get-tuple-element.109.refs_1_), channel_id=1, source_target_pairs={{0,2},{1,3},{2,0},{3,1},{4,6},{5,7},{6,4},{7,5},{8,10},{9,11},{10,... | collective-permute-start | bytes 73736 | tf_op jit(solution)/shard_map/ppermute | solution.py:68
  152.0 3.3 %collective-permute-start.33 = (bf16[16,768]{1,0:T(8,128)(2,1)S(1)}, bf16[16,768]{1,0:T(8,128)(2,1)S(1)}, u32[]{:S(2)}, u32[]{:S(2)}) collective-permute-start(bf16[16,768]{1,0:T(8,128)(2,1)S(1)} %get-tuple-element.109.refs_1_), channel_id=1, source_target_pairs={{0,3},{1,2},{2,1},{3,0},{4,7},{5,6},{6,5},{7,4},{8,11},{9,10},{10,... | collective-permute-start | bytes 73736 | tf_op jit(solution)/shard_map/ppermute | solution.py:68
  156.2 18.6 %all-to-all-start.2 = ((bf16[8,16,768]{2,1,0:T(8,128)(2,1)}), bf16[8,16,768]{2,1,0:T(8,128)(2,1)S(1)}, u32[]{:S(2)}, u32[]{:S(2)}) async-start(bf16[8,16,768]{2,1,0:T(8,128)(2,1)} %spread.1), calls=%async_computation.2 | async-start | bytes 393216 | tf_op jit(solution)/shard_map/all_to_all | solution.py:638
  166.4 49.2 %collective-permute-start.38 = (bf16[4,96,1536]{2,1,0:T(8,128)(2,1)}, bf16[4,96,1536]{2,1,0:T(8,128)(2,1)}, u32[]{:S(2)}, u32[]{:S(2)}) collective-permute-start(bf16[4,96,1536]{2,1,0:T(8,128)(2,1)} %copy-done.10), channel_id=1, source_target_pairs={{0,4},{4,0},{8,12},{12,8},{16,20},{20,16},{24,28},{28,24},{1,5},{5... | collective-permute-start | bytes 3538952 | tf_op jit(solution)/shard_map/ppermute | solution.py:68
  169.3 40.6 %collective-permute-start.34 = (bf16[4,96,768]{2,1,0:T(8,128)(2,1)}, bf16[4,96,768]{2,1,0:T(8,128)(2,1)}, u32[]{:S(2)}, u32[]{:S(2)}) collective-permute-start(bf16[4,96,768]{2,1,0:T(8,128)(2,1)} %copy-done.13), channel_id=1, source_target_pairs={{0,4},{4,0},{8,12},{12,8},{16,20},{20,16},{24,28},{28,24},{1,5},{5... | collective-permute-start | bytes 1769480 | tf_op jit(solution)/shard_map/ppermute | solution.py:68
  175.1 34.2 %copy-start.4 = (bf16[2,768]{1,0:T(2,128)(2,1)S(1)}, bf16[2,768]{1,0:T(2,128)(2,1)}, u32[]{:S(2)}) copy-start(bf16[2,768]{1,0:T(2,128)(2,1)} %refs_0_.1) | copy-start | bytes 9220
  175.9 33.3 %all-to-all-start.3 = ((f32[8,2,96]{2,1,0:T(2,128)}), f32[8,2,96]{2,1,0:T(2,128)S(1)}, u32[]{:S(2)}, u32[]{:S(2)}) async-start(f32[8,2,96]{2,1,0:T(2,128)} %copy.66), calls=%async_computation.3 | async-start | bytes 16384 | tf_op jit(solution)/shard_map/all_to_all | solution.py:641
  211.1 9.9 %collective-permute-start.37 = (bf16[96,768]{1,0:T(8,128)(2,1)S(1)}, bf16[96,768]{1,0:T(8,128)(2,1)S(1)}, u32[]{:S(2)}, u32[]{:S(2)}) collective-permute-start(bf16[96,768]{1,0:T(8,128)(2,1)S(1)} %get-tuple-element.171), channel_id=1, source_target_pairs={{0,24},{4,28},{8,16},{12,20},{16,8},{20,12},{24,0},{28,4},{1,25},{... | collective-permute-start | bytes 442376 | tf_op jit(solution)/shard_map/ppermute | solution.py:68
  214.4 25.8 %collective-permute-start.36 = (bf16[96,768]{1,0:T(8,128)(2,1)S(1)}, bf16[96,768]{1,0:T(8,128)(2,1)S(1)}, u32[]{:S(2)}, u32[]{:S(2)}) collective-permute-start(bf16[96,768]{1,0:T(8,128)(2,1)S(1)} %get-tuple-element.172), channel_id=1, source_target_pairs={{0,16},{4,20},{8,24},{12,28},{16,0},{20,4},{24,8},{28,12},{1,17},{... | collective-permute-start | bytes 442376 | tf_op jit(solution)/shard_map/ppermute | solution.py:68
  214.4 25.8 %collective-permute-start.35 = (bf16[96,768]{1,0:T(8,128)(2,1)S(1)}, bf16[96,768]{1,0:T(8,128)(2,1)S(1)}, u32[]{:S(2)}, u32[]{:S(2)}) collective-permute-start(bf16[96,768]{1,0:T(8,128)(2,1)S(1)} %get-tuple-element.170), channel_id=1, source_target_pairs={{0,8},{4,12},{8,0},{12,4},{16,24},{20,28},{24,16},{28,20},{1,9},{5... | collective-permute-start | bytes 442376 | tf_op jit(solution)/shard_map/ppermute | solution.py:68
  217.7 25.5 %collective-permute-start.41 = (bf16[96,1536]{1,0:T(8,128)(2,1)}, bf16[96,1536]{1,0:T(8,128)(2,1)S(1)}, u32[]{:S(2)}, u32[]{:S(2)}) collective-permute-start(bf16[96,1536]{1,0:T(8,128)(2,1)} %get-tuple-element.168), channel_id=1, source_target_pairs={{0,24},{4,28},{8,16},{12,20},{16,8},{20,12},{24,0},{28,4},{1,25},{... | collective-permute-start | bytes 884744 | tf_op jit(solution)/shard_map/ppermute | solution.py:68
  221.0 30.9 %collective-permute-start.40 = (bf16[96,1536]{1,0:T(8,128)(2,1)}, bf16[96,1536]{1,0:T(8,128)(2,1)}, u32[]{:S(2)}, u32[]{:S(2)}) collective-permute-start(bf16[96,1536]{1,0:T(8,128)(2,1)} %get-tuple-element.169), channel_id=1, source_target_pairs={{0,16},{4,20},{8,24},{12,28},{16,0},{20,4},{24,8},{28,12},{1,17},{... | collective-permute-start | bytes 884744 | tf_op jit(solution)/shard_map/ppermute | solution.py:68
  221.0 30.9 %collective-permute-start.39 = (bf16[96,1536]{1,0:T(8,128)(2,1)S(1)}, bf16[96,1536]{1,0:T(8,128)(2,1)}, u32[]{:S(2)}, u32[]{:S(2)}) collective-permute-start(bf16[96,1536]{1,0:T(8,128)(2,1)S(1)} %get-tuple-element.167), channel_id=1, source_target_pairs={{0,8},{4,12},{8,0},{12,4},{16,24},{20,28},{24,16},{28,20},{1,9},{5... | collective-permute-start | bytes 884744 | tf_op jit(solution)/shard_map/ppermute | solution.py:68
  (40 other events, 245.1 us)
Sparse Core Ops, SparseCore 0:
  10.8 68.7 all-gather.1

commit v3 on v2

v3 whole, which is shorter than its diff:
```python
import functools
import math

import jax
import jax.numpy as jnp
from jax import lax
from jax.experimental import pallas as pl
from jax.experimental.pallas import tpu as pltpu
from jax.sharding import PartitionSpec as P

HEAD = 64
EPS = 1e-06
BF = jnp.bfloat16
F32 = jnp.float32
FACTOR = 1.0 / math.sqrt(HEAD)
CURVE = math.sqrt(2.0 / math.pi)
CUBIC = 0.044715


def origin(ndim, step):
    return (0,) * ndim


def call(kernel, name, outs, args, scalars=(), scratch=(), ordered=(), flops=1, blocked=False):
    in_specs = (
        [pl.BlockSpec(memory_space=pltpu.SMEM)] * len(scalars)
        + [pl.BlockSpec(memory_space=pl.ANY)] * len(ordered)
        + (
            [pl.BlockSpec(a.shape, functools.partial(origin, a.ndim)) for a in args]
            if blocked
            else [pl.BlockSpec(memory_space=pltpu.VMEM)] * len(args)
        )
    )
    skip = len(scalars)

    def body(*refs):
        kernel(*refs[:skip], *refs[skip + len(ordered) :])

    shapes = [jax.ShapeDtypeStruct(shape, dtype) for shape, dtype in outs]
    return pl.pallas_call(
        body,
        out_shape=shapes,
        grid=(1,) if blocked else (),
        in_specs=in_specs,
        out_specs=[pl.BlockSpec(memory_space=pltpu.VMEM)] * len(outs),
        scratch_shapes=list(scratch),
        compiler_params=pltpu.CompilerParams(vmem_limit_bytes=14 * 1024 * 1024),
        cost_estimate=pl.CostEstimate(flops=int(flops), bytes_accessed=1, transcendentals=0),
        name=name,
    )(*[s.reshape(1).astype(jnp.int32) for s in scalars], *ordered, *args)


def dot(a, b, over=(1, 0)):
    return lax.dot_general(
        a, b, (((over[0],), (over[1],)), ((), ())), preferred_element_type=F32
    )


def normed(v):
    centered = v - jnp.mean(v, axis=-1, keepdims=True)
    scale = lax.rsqrt(jnp.mean(centered * centered, axis=-1, keepdims=True) + EPS)
    return centered * scale, scale


def norm_back(n, scale, grad):
    mean = jnp.mean(grad, axis=-1, keepdims=True)
    along = jnp.mean(grad * n, axis=-1, keepdims=True)
    return (grad - mean - n * along) * scale


def swap(block, axis, offset):
    count = lax.axis_size(axis)
    return lax.ppermute(block, axis, [(i, i ^ offset) for i in range(count)])


def tp_gather(rows):
    far = swap(rows, "tp", 2)
    near = swap(rows, "tp", 1)
    return [rows, near, far, swap(far, "tp", 1)]


def near_rows_kernel(keep, got, own, out):
    rows = own.shape[0]
    own[...] = keep[:rows].astype(F32) + got[:rows].astype(F32)
    out[...] = (keep[rows:].astype(F32) + got[rows:].astype(F32)).astype(BF)


def tp_scatter(keep, send, ordered=()):
    got = swap(send, "tp", 1)
    rows, cols = keep.shape
    own, out = call(
        near_rows_kernel,
        "near_rows",
        [((rows // 2, cols), F32), ((rows // 2, cols), BF)],
        [keep, got],
        ordered=ordered,
    )
    return [own, swap(out, "tp", 2)]


def put_piece(rank, k, value, keep, send):
    to = jnp.bitwise_xor(rank[0], k)

    @pl.when(to % 2 == 0)
    def _():
        keep[to // 2] = value

    @pl.when(to % 2 == 1)
    def _():
        send[to // 2] = value


def pack_kernel(rank, cond, qv, proj, second, hidden, keep, send, scr):
    count = 2 * keep.shape[0]
    feat = qv.shape[1]
    latents = cond.shape[0]
    value = cond[...].astype(F32)
    act = (value / (1.0 + jnp.exp(-value))).astype(BF).astype(F32)
    tail = hidden[...].astype(F32)
    rows = [qv[...].astype(F32), proj[...].astype(F32), second[...].astype(F32)]
    rows += [tail[:, r * feat : (r + 1) * feat] for r in range(tail.shape[1] // feat)]
    scr[...] = jnp.zeros_like(scr)
    at = latents
    for row in rows:
        scr[at : at + row.shape[0], 0:feat] = row
        at += row.shape[0]
    for k in range(count):
        scr[0:latents, 0:feat] = act[:, k * feat : (k + 1) * feat]
        put_piece(rank, k, scr[...], keep, send)


def pair_kernel(keep, got, *outs):
    for z, out in enumerate(outs):
        out[0] = keep[z]
        out[1] = got[z]


def exchange(keep, send, ordered=()):
    size = keep.shape[0]
    piece = keep.shape[1:]
    if size != 4:
        count = 2 * size
        order = jnp.bitwise_xor(jnp.arange(count), lax.axis_index("fsdp"))
        whole = jnp.stack([keep, send], axis=1).reshape(count, *piece)
        got = lax.all_to_all(
            jnp.take(whole, order, axis=0), "fsdp", split_axis=0, concat_axis=0, tiled=True
        )
        return [jnp.take(got, order, axis=0)]
    got = swap(send, "fsdp", 1)
    pairs = call(
        pair_kernel, "pairs", [((2, *piece), keep.dtype)] * size, [keep, got], ordered=ordered
    )
    return [pairs[0]] + [swap(pairs[z], "fsdp", 2 * z) for z in range(1, size)]


def pick(arrays, k):
    per = arrays[0].shape[0]
    return arrays[k // per].at[k % per]


def attn_own_kernel(qkv, proj, out):
    cols = qkv.shape[2]
    for j in range(3):
        out[:, j * cols : (j + 1) * cols] = qkv[j]
    out[:, 3 * cols :] = proj[...].T


def copy_kernel(value, out):
    out[...] = value[...]


def join_kernel(a, b, out):
    half = out.shape[0] // 2
    if len(a.shape) == 2:
        out[0] = a[...]
        out[1] = b[...]
    else:
        out[:half] = a[...]
        out[half:] = b[...]


def join(a, b, ordered=()):
    size = 1 if a.ndim == 2 else a.shape[0]
    shape = (2 * size, *a.shape[-2:])
    return call(join_kernel, "join", [(shape, a.dtype)], [a, b], ordered=ordered)[0]


def gather_steps(own, ordered=((), ())):
    two = join(own, swap(own, "fsdp", 4), ordered[0])
    four = join(two, swap(two, "fsdp", 2), ordered[1])
    return two, four, swap(four, "fsdp", 1)


def mod_kernel(*refs):
    *got, ada, bias, keep, send, cols_out, scr, pieces = refs
    count = pieces.shape[0]
    feat = ada.shape[0]
    latents = scr.shape[0] // count
    for k in range(count):
        scr[k * latents : (k + 1) * latents, :] = pick(got, k)[0:latents, :]
    cols = scr[:, 0:feat].astype(BF)
    cols_out[...] = cols
    width = ada.shape[1] // 6
    pieces[...] = jnp.zeros_like(pieces)
    for j in range(6):
        at = slice(j * width, (j + 1) * width)
        part = dot(cols, ada[:, at]) + bias[:, at]
        for k in range(count):
            for l in range(latents):
                pieces[k, 6 * l + j : 6 * l + j + 1, :] = part[k * latents + l : k * latents + l + 1]
    for z in range(count // 2):
        keep[z] = pieces[2 * z].astype(BF)
        send[z] = pieces[2 * z + 1].astype(BF)


def bias_kernel(rank, tp_rank, *refs, latents, feat, tp):
    *got, qkv_out, proj_out, second_out, hidden_out, scr = refs
    count = scr.shape[0]
    for k in range(count):
        scr[jnp.bitwise_xor(rank[0], k)] = pick(got, k)[...]
    per = count // tp
    first = tp_rank[0] * per
    cols = per * feat
    qkv_out[...] = jnp.zeros_like(qkv_out)
    at = latents
    for i in range(per):
        f = first + i
        here = slice(i * feat, (i + 1) * feat)
        qkv_out[0:1, here] = scr[f, at : at + 1, 0:feat]
        qkv_out[0:1, 2 * cols + i * feat : 2 * cols + (i + 1) * feat] = scr[
            f, at + 1 : at + 2, 0:feat
        ]
        for r in range(tp):
            lane = (i * tp + r) * feat
            hidden_out[0:1, lane : lane + feat] = scr[f, at + 4 + r : at + 5 + r, 0:feat]
    for f in range(count):
        here = slice(f * feat, (f + 1) * feat)
        proj_out[0:1, here] = scr[f, at + 2 : at + 3, 0:feat]
        second_out[0:1, here] = scr[f, at + 3 : at + 4, 0:feat]


def assemble_kernel(rank, mine, other, *outs):
    rows = mine.shape[1]
    for i, z in enumerate((0, 2, 1, 3)):
        for x, blocks in enumerate((mine, other)):
            at = jnp.bitwise_xor(rank[0], 2 * z + x) * rows
            at = pl.ds(pl.multiple_of(at, rows), rows)
            lane = 0
            for out in outs:
                out[at, :] = blocks[i, :, lane : lane + out.shape[1]]
                lane += out.shape[1]


def first_norm_kernel(x0, x1, x2, x3, *refs):
    *got, mod_out, out = refs
    mod = got[0][...].astype(F32)
    for part in got[1:]:
        mod = mod + part[...].astype(F32)
    mod_out[...] = mod[0 : mod_out.shape[0]]
    latents = mod_out.shape[0] // 6
    part = x0.shape[0] // (2 * latents)
    whole = out.shape[0] // latents
    for b, block in enumerate((x0, x1, x2, x3)):
        for l in range(latents):
            n, _ = normed(block[l * part : (l + 1) * part, :].astype(F32))
            shift, scale = mod[6 * l : 6 * l + 1], mod[6 * l + 1 : 6 * l + 2]
            out[l * whole + b * part : l * whole + (b + 1) * part, :] = (
                n * (1.0 + scale) + shift
            ).astype(BF)


def gate_grad_kernel(x0, x1, x2, x3, mod, out, bias_out):
    latents = mod.shape[0] // 6
    rows = x0.shape[0] // 2
    part = rows // latents
    total = jnp.zeros((1, mod.shape[1]), F32)
    for b, block in enumerate((x0, x1, x2, x3)):
        for l in range(latents):
            cot = block[rows + l * part : rows + (l + 1) * part, :].astype(F32)
            value = (cot * mod[6 * l + 5 : 6 * l + 6, :]).astype(BF)
            out[b * rows + l * part : b * rows + (l + 1) * part, :] = value
            if b == 0:
                total = total + jnp.sum(value.astype(F32), axis=0, keepdims=True)
    bias_out[...] = total


def unpack_rows(blocks, rows, latents):
    part = blocks[0].shape[0] // latents
    whole = part * len(blocks)
    for b, block in enumerate(blocks):
        for l in range(latents):
            rows[l * whole + b * part : l * whole + (b + 1) * part, :] = block[
                l * part : (l + 1) * part, :
            ]


def put_parts(value, keep, send, latent):
    part = value.shape[0] // 4
    rows = keep.shape[0] // 2
    for b in range(4):
        out = send if b % 2 else keep
        at = (b // 2) * rows + latent * part
        out[at : at + part, :] = value[b * part : (b + 1) * part]


def softmax(q, k):
    scores = dot(q, k, (1, 1)) * FACTOR
    weights = jnp.exp(scores - jnp.max(scores, axis=-1, keepdims=True))
    return weights * (1.0 / jnp.sum(weights, axis=-1, keepdims=True))


def attn_kernel(rows, qkv_w, proj_w, bias, qkv, att, keep, send, *, latents):
    cols = proj_w.shape[1]
    size = rows.shape[0] // latents
    for l in range(latents):
        here = slice(l * size, (l + 1) * size)
        projected = (dot(rows[here, :], qkv_w[...]) + bias[...]).astype(BF)
        qkv[here, :] = projected
        mixed = []
        for h in range(cols // HEAD):
            q, k, v = [
                projected[:, j * cols + h * HEAD : j * cols + (h + 1) * HEAD] for j in range(3)
            ]
            mixed.append(dot(softmax(q, k).astype(BF), v))
        attended = jnp.concatenate(mixed, axis=1).astype(BF)
        att[here, :] = attended
        put_parts(dot(attended, proj_w[...], (1, 1)).astype(BF), keep, send, l)


def middle_kernel(x, p0, p1, bias, mod, branch_out, middle_out, out):
    latents = mod.shape[0] // 6
    rows = out.shape[0] // latents
    for l in range(latents):
        here = slice(l * rows, (l + 1) * rows)
        branch = bias[...] + p0[here, :] + p1[here, :].astype(F32)
        branch_out[here, :] = branch
        gate = mod[6 * l + 2 : 6 * l + 3, :]
        middle = x[here, :].astype(F32) + gate * branch
        middle_out[here, :] = middle
        n, _ = normed(middle)
        shift = mod[6 * l + 3 : 6 * l + 4, :]
        scale = mod[6 * l + 4 : 6 * l + 5, :]
        out[here, :] = (n * (1.0 + scale) + shift).astype(BF)


def mlp_kernel(
    x0, x1, x2, x3, grads, first, second, bias, act_out, pre_out, x_out, keep, send
):
    rows = x0.shape[0]
    for b, x in enumerate((x0, x1, x2, x3)):
        here = slice(b * rows, (b + 1) * rows)
        x_out[here, :] = x[...]
        v = dot(x[...], first[...]) + bias[...]
        square = v * v
        t = jnp.tanh(CURVE * v * (1.0 + CUBIC * square))
        act_out[here, :] = (0.5 * v * (1.0 + t)).astype(BF)
        slope = 0.5 * (1.0 + t) + 0.5 * v * (1.0 - t * t) * CURVE * (1.0 + 3.0 * CUBIC * square)
        pre = (dot(grads[here, :], second[...]) * slope).astype(BF)
        pre_out[here, :] = pre
        at = (b // 2) * rows
        out = send if b % 2 else keep
        out[at : at + rows, :] = dot(pre, first[...], (1, 1)).astype(BF)


def store_grad(rank, product, keep, send, cols):
    rows = keep.shape[1]
    place = rank[0] // 2
    for mine in range(2):

        @pl.when(rank[0] % 2 == mine)
        def _():
            for z in range(keep.shape[0]):
                to = jnp.bitwise_xor(place, z)
                keep[to, :, cols] = product[(2 * z + mine) * rows : (2 * z + mine + 1) * rows]
                send[to, :, cols] = product[
                    (2 * z + 1 - mine) * rows : (2 * z + 2 - mine) * rows
                ]


def mlp_grad_kernel(rank, x, g, act, pre, keep_b, send_b, keep_c, send_c, bias_out):
    hidden = act.shape[1]
    for left, right, keep, send in ((x, pre, keep_b, send_b), (g, act, keep_c, send_c)):
        for at in range(0, hidden, 256):
            product = dot(left[...], right[:, at : at + 256], (0, 0)).astype(BF)
            store_grad(rank, product, keep, send, slice(at, at + 256))
    bias_out[...] = jnp.sum(pre[...].astype(F32), axis=0, keepdims=True)


def mlp_out_kernel(act, second, keep, send):
    rows = keep.shape[0] // 2
    for b in range(4):
        at = (b // 2) * rows
        out = send if b % 2 else keep
        value = dot(act[b * rows : (b + 1) * rows, :], second[...], (1, 1))
        out[at : at + rows, :] = value.astype(BF)


def output_kernel(middle, x, p0, p1, bias, mod, out, sums):
    latents = mod.shape[0] // 6
    size = middle.shape[0]
    rows = size // latents
    for l in range(latents):
        here = slice(l * rows, (l + 1) * rows)
        branch = bias[...] + p0[here, :] + p1[here, :].astype(F32)
        cot = x[size + l * rows : size + (l + 1) * rows, :].astype(F32)
        out[here, :] = (middle[here, :] + mod[6 * l + 5 : 6 * l + 6, :] * branch).astype(BF)
        sums[l : l + 1, :] = jnp.sum(cot * branch, axis=0, keepdims=True)


def middle_back_kernel(x, middle, branch, p0, p1, mod, grad_out, out, sums):
    latents = mod.shape[0] // 6
    width = middle.shape[1]
    size = middle.shape[0]
    rows = size // latents
    total = jnp.zeros((1, width), F32)
    for l in range(latents):
        here = slice(l * rows, (l + 1) * rows)
        grad = p0[here, :] + p1[here, :].astype(F32)
        cot = x[size + l * rows : size + (l + 1) * rows, :].astype(F32)
        n, scale = normed(middle[here, :])
        sums[3 * l + 1 : 3 * l + 2, :] = jnp.sum(grad, axis=0, keepdims=True)
        sums[3 * l + 2 : 3 * l + 3, :] = jnp.sum(grad * n, axis=0, keepdims=True)
        factor = 1.0 + mod[6 * l + 4 : 6 * l + 5, :]
        whole = cot + norm_back(n, scale, grad * factor)
        grad_out[here, :] = whole
        sums[3 * l : 3 * l + 1, :] = jnp.sum(whole * branch[here, :], axis=0, keepdims=True)
        low = (whole * mod[6 * l + 2 : 6 * l + 3, :]).astype(BF)
        out[here, :] = low
        total = total + jnp.sum(low.astype(F32), axis=0, keepdims=True)
    sums[3 * latents : 3 * latents + 1, :] = total


def attn_back_kernel(
    g0, g1, g2, g3, qkv_w, proj_w, qkv, rows, grads, keep, send, *, latents
):
    unpack_rows([g0, g1, g2, g3], rows, latents)
    cols = proj_w.shape[1]
    size = rows.shape[0] // latents
    for l in range(latents):
        here = slice(l * size, (l + 1) * size)
        back = dot(rows[here, :], proj_w[...]).astype(BF)
        projected = qkv[here, :]
        found = [[], [], []]
        for h in range(cols // HEAD):
            q, k, v = [
                projected[:, j * cols + h * HEAD : j * cols + (h + 1) * HEAD] for j in range(3)
            ]
            up = back[:, h * HEAD : (h + 1) * HEAD]
            probs = softmax(q, k)
            grad_probs = dot(up, v, (1, 1))
            inner = jnp.sum(probs * grad_probs, axis=-1, keepdims=True)
            scores = (probs * (grad_probs - inner)).astype(BF)
            found[0].append(dot(scores, k) * FACTOR)
            found[1].append(dot(scores, q, (0, 0)) * FACTOR)
            found[2].append(dot(probs.astype(BF), up, (0, 0)))
        grad = jnp.concatenate(found[0] + found[1] + found[2], axis=1).astype(BF)
        grads[here, :] = grad
        put_parts(dot(grad, qkv_w[...], (1, 1)).astype(BF), keep, send, l)


def attn_grad_kernel(rank, rows, grads, back, att, keep, send, bias_out):
    cols = att.shape[1]
    for at in range(0, 3 * cols, cols):
        product = dot(rows[...], grads[:, at : at + cols], (0, 0)).astype(BF)
        store_grad(rank, product, keep, send, slice(at, at + cols))
    product = dot(back[...], att[...], (0, 0)).astype(BF)
    store_grad(rank, product, keep, send, slice(3 * cols, 4 * cols))
    bias_out[...] = jnp.sum(grads[...].astype(F32), axis=0, keepdims=True)


def input_back_kernel(
    x, grad_middle, p0, p1, mod, sums, gates, fc2, fc1, qkv, out, pack, scr
):
    latents = mod.shape[0] // 6
    rows = out.shape[0] // latents
    cols = qkv.shape[1] // 3
    scr[...] = jnp.zeros_like(scr)
    for l in range(latents):
        here = slice(l * rows, (l + 1) * rows)
        grad = p0[here, :] + p1[here, :].astype(F32)
        n, scale = normed(x[here, :].astype(F32))
        scr[6 * l : 6 * l + 1, :] = jnp.sum(grad, axis=0, keepdims=True)
        scr[6 * l + 1 : 6 * l + 2, :] = jnp.sum(grad * n, axis=0, keepdims=True)
        scr[6 * l + 2 : 6 * l + 5, :] = sums[3 * l : 3 * l + 3, :]
        scr[6 * l + 5 : 6 * l + 6, :] = gates[l : l + 1, :]
        factor = 1.0 + mod[6 * l + 1 : 6 * l + 2, :]
        out[here, :] = grad_middle[here, :] + norm_back(n, scale, grad * factor)
    at = 6 * latents
    scr[at : at + 1, :] = sums[3 * latents : 3 * latents + 1, :]
    scr[at + 1 : at + 2, :] = fc2[...]
    scr[at + 2 : at + 3, :] = fc1[...]
    scr[at + 3 : at + 4, 0:cols] = qkv[:, 0:cols]
    scr[at + 3 : at + 4, cols : 2 * cols] = qkv[:, 2 * cols :]
    pack[...] = scr[...].astype(BF)


def spread_kernel(
    rank, tp_rank, k0, k1, k2, k3, keep, send, parts, total, *, latents, feat
):
    count = 2 * keep.shape[0]
    packs = (k0, k1, k2, k3)
    per = count // len(packs)
    cols = per * feat
    mods = 6 * latents
    summed = jnp.zeros(k0.shape, F32)
    for d, pack in enumerate(packs):
        value = pack[...].astype(F32)
        parts[jnp.bitwise_xor(tp_rank[0], d)] = value
        summed = summed + value
    total[...] = summed
    row = slice(mods, mods + 1)
    total[row, :] = jnp.zeros((1, k0.shape[1]), F32)
    for k in range(count):
        t, i = k // per, k % per
        here = slice(k * feat, (k + 1) * feat)
        total[row, 0:feat] = parts[t, mods + 3 : mods + 4, i * feat : (i + 1) * feat]
        total[row, feat : 2 * feat] = parts[
            t, mods + 3 : mods + 4, cols + i * feat : cols + (i + 1) * feat
        ]
        total[row, 2 * feat : 3 * feat] = summed[mods : mods + 1, here]
        total[row, 3 * feat : 4 * feat] = summed[mods + 1 : mods + 2, here]
        total[row, 4 * feat : 8 * feat] = parts[
            t, mods + 2 : mods + 3, 4 * i * feat : 4 * (i + 1) * feat
        ]
        put_piece(rank, k, total[...].astype(BF), keep, send)


def silu_kernel(*refs, latents):
    *got, ada, keep, send, grads, bias_out, scr, out_scr = refs
    width = ada.shape[1] // 6
    feat = ada.shape[0]
    count = scr.shape[1] // latents
    mods = 6 * latents
    bias = jnp.zeros((1, width), F32)
    for k in range(count):
        value = pick(got, k)[...].astype(F32)
        bias = bias + value[mods : mods + 1]
        for l in range(latents):
            for j in range(6):
                scr[j, k * latents + l : k * latents + l + 1, :] = value[6 * l + j : 6 * l + j + 1]
    bias_out[...] = bias
    total = jnp.zeros((count * latents, feat), F32)
    for j in range(6):
        at = slice(j * width, (j + 1) * width)
        rows = scr[j].astype(BF)
        grads[:, at] = rows
        total = total + dot(rows, ada[:, at], (1, 1))
    out_scr[...] = jnp.zeros_like(out_scr)
    for k in range(count):
        out_scr[k, 0:latents, 0:feat] = total[k * latents : (k + 1) * latents]
    for z in range(count // 2):
        keep[z] = out_scr[2 * z]
        send[z] = out_scr[2 * z + 1]


def cond_kernel(rank, *refs, latents, feat):
    *got, cond, out, scr = refs
    count = scr.shape[0]
    for k in range(count):
        scr[jnp.bitwise_xor(rank[0], k)] = pick(got, k)[...]
    value = cond[...].astype(F32)
    gate = 1.0 / (1.0 + jnp.exp(-value))
    slope = gate * (1.0 + value * (1.0 - gate))
    for k in range(count):
        here = slice(k * feat, (k + 1) * feat)
        out[:, here] = scr[k, 0:latents, 0:feat] * slope[:, here]


def scatter_pieces(keep, send):
    count = 2 * keep.shape[0]
    order = jnp.bitwise_xor(jnp.arange(count), lax.axis_index("fsdp"))
    whole = jnp.stack([keep, send], axis=1).reshape(count, *keep.shape[1:]).astype(F32)
    whole = jnp.take(whole, order, axis=0)
    return lax.psum_scatter(whole, "fsdp", scatter_dimension=0, tiled=False)


def halve_four_kernel(keep, got, own, out):
    for z in range(2):
        own[z] = keep[2 * z].astype(F32) + got[2 * z].astype(F32)
        out[z] = (keep[2 * z + 1].astype(F32) + got[2 * z + 1].astype(F32)).astype(BF)


def halve_two_kernel(keep, got, own, out):
    own[...] = keep[0] + got[0].astype(F32)
    out[...] = (keep[1] + got[1].astype(F32)).astype(BF)


def halve_four(keep, send):
    shape = (2, *keep.shape[1:])
    got = swap(send, "fsdp", 1)
    return call(halve_four_kernel, "halve_four", [(shape, F32), (shape, BF)], [keep, got])


def halve_two(keep, send, ordered=()):
    shape = keep.shape[1:]
    got = swap(send, "fsdp", 2)
    outs = [(shape, F32), (shape, BF)]
    return call(halve_two_kernel, "halve_two", outs, [keep, got], ordered=ordered)


def add_kernel(own, got, out):
    out[...] = own[...] + got[...].astype(F32)


def halve_one(own, out):
    got = swap(out, "fsdp", 4)
    return call(add_kernel, "last_sum", [(own.shape, F32)], [own, got])[0]


def attn_add_kernel(own, got, qkv, proj):
    cols = qkv.shape[2]
    for j in range(3):
        here = slice(j * cols, (j + 1) * cols)
        qkv[j] = own[:, here] + got[:, here].astype(F32)
    here = slice(3 * cols, 4 * cols)
    proj[...] = (own[:, here] + got[:, here].astype(F32)).T


def shards(
    inputs,
    conditioning,
    ada_weight,
    ada_bias,
    query_key_value_weight,
    qv_bias,
    attention_output_weight,
    attention_output_bias,
    expand_weight,
    hidden_layer_bias,
    contract_weight,
    contract_bias,
    out_cotangent,
):
    tp_rank = lax.axis_index("tp")
    tp_count = lax.axis_size("tp")
    rank = lax.axis_index("fsdp")
    count = lax.axis_size("fsdp")
    positions, latents, width = inputs.shape
    feat = ada_weight.shape[0]
    cols = query_key_value_weight.shape[2]
    hidden = expand_weight.shape[1]
    hidden_part = hidden_layer_bias.shape[0]
    mod_part = ada_bias.shape[0]
    rows = positions * latents
    tokens = rows * tp_count
    mods = 6 * latents
    direct = count == 8
    block = ((rows, width), BF)
    block_f32 = ((rows, width), F32)

    half = count // 2
    cond_keep, cond_send = call(
        pack_kernel,
        "pack_conditioning",
        [((half, 16, 128), F32)] * 2,
        [
            conditioning,
            qv_bias,
            attention_output_bias.reshape(1, feat),
            contract_bias.reshape(1, feat),
            hidden_layer_bias.reshape(1, hidden_part),
        ],
        [rank],
        scratch=[pltpu.VMEM((16, 128), F32)],
        blocked=True,
    )
    cond_got = exchange(cond_keep, cond_send)

    bias_row = lax.dynamic_update_slice(
        jnp.zeros((1, mod_part * count), F32),
        ada_bias.astype(F32).reshape(1, mod_part),
        (0, rank * mod_part),
    )
    mod_keep, mod_send, cond_cols = call(
        mod_kernel,
        "modulation",
        [((half, 16, width), BF)] * 2 + [((count * latents, feat), BF)],
        [*cond_got, ada_weight, bias_row],
        scratch=[
            pltpu.VMEM((count * latents, 128), F32),
            pltpu.VMEM((count, 16, width), F32),
        ],
    )
    x_own = jnp.stack([inputs.transpose(1, 0, 2), out_cotangent.transpose(1, 0, 2)])
    x_own = x_own.reshape(2 * rows, width)
    x_own = call(
        copy_kernel, "tokens", [((2 * rows, width), BF)], [x_own], ordered=cond_got
    )[0]
    x_blocks = tp_gather(x_own)

    qkv_own = query_key_value_weight.transpose(1, 0, 2)
    if direct:
        attn_own = call(
            attn_own_kernel,
            "attn_own",
            [((feat, 4 * cols), BF)],
            [qkv_own, attention_output_weight],
            ordered=[cond_got[0]],
            blocked=True,
        )[0]
        mod_half = halve_four(mod_keep, mod_send)
        mod_own, mod_out = halve_two(*mod_half)
        mod_parts = [mod_own, swap(mod_out, "fsdp", 4)]
        attn_two, attn_four, attn_other = gather_steps(attn_own, ([mod_half[1]], [mod_own]))
        first_own = call(
            copy_kernel,
            "first_own",
            [((feat, hidden), BF)],
            [expand_weight],
            ordered=[attn_four],
            blocked=True,
        )[0]
        first_two, first_four, first_other = gather_steps(first_own)
        second_own = call(
            copy_kernel,
            "second_own",
            [((feat, hidden), BF)],
            [contract_weight.T],
            ordered=[first_two],
            blocked=True,
        )[0]
        second_two, second_four, second_other = gather_steps(second_own)
        qkv_full, proj_full = call(
            assemble_kernel,
            "attn_weights",
            [((width, 3 * cols), BF), ((width, cols), BF)],
            [attn_four, attn_other],
            [rank],
        )
        first_full = call(
            assemble_kernel,
            "first_weights",
            [((width, hidden), BF)],
            [first_four, first_other],
            [rank],
        )[0]
        second_full = call(
            assemble_kernel,
            "second_weights",
            [((width, hidden), BF)],
            [second_four, second_other],
            [rank],
        )[0]
        steps = [[attn_four], [first_two], [first_four, second_two], [second_four]]
    else:
        steps = [[]] * 4
        mod_parts = [scatter_pieces(mod_keep, mod_send)]
        qkv_full = lax.all_gather(
            query_key_value_weight.reshape(feat, 3 * cols), "fsdp", axis=0, tiled=True
        )
        proj_full = lax.all_gather(attention_output_weight.T, "fsdp", axis=0, tiled=True)
        first_full = lax.all_gather(expand_weight, "fsdp", axis=0, tiled=True)
        second_full = lax.all_gather(contract_weight.T, "fsdp", axis=0, tiled=True)

    qkv_bias, proj_bias, second_bias, hidden_bias = call(
        functools.partial(bias_kernel, latents=latents, feat=feat, tp=tp_count),
        "biases",
        [((1, 3 * cols), F32), ((1, width), F32), ((1, width), F32), ((1, hidden), F32)],
        cond_got,
        [rank, tp_rank],
        scratch=[pltpu.VMEM((count, 16, 128), F32)],
        ordered=[mod_send],
        flops=1e9,
    )
    mod, attn_rows = call(
        first_norm_kernel,
        "first_norm",
        [((mods, width), F32), ((tokens, width), BF)],
        [*x_blocks, *mod_parts],
        ordered=[hidden_bias, *steps[0]],
    )
    pair = ((2 * rows, width), BF)
    qkv, att, keep, send = call(
        functools.partial(attn_kernel, latents=latents),
        "attention",
        [((tokens, 3 * cols), BF), ((tokens, cols), BF), pair, pair],
        [attn_rows, qkv_full, proj_full, qkv_bias],
        ordered=steps[1],
    )
    branch_parts = tp_scatter(keep, send)
    grad_rows, fc2_part = call(
        gate_grad_kernel,
        "gate_grad",
        [((tokens, width), BF), ((1, width), F32)],
        [*x_blocks, mod],
        ordered=[branch_parts[0], *steps[2]],
        flops=1e9,
    )
    branch, middle, mlp_in = call(
        middle_kernel,
        "middle",
        [block_f32, block_f32, block],
        [x_own, *branch_parts, proj_bias, mod],
        ordered=[fc2_part, *steps[3]],
    )
    m_blocks = tp_gather(mlp_in)
    act, pre, mlp_rows, keep, send = call(
        mlp_kernel,
        "mlp",
        [((tokens, hidden), BF)] * 2 + [((tokens, width), BF), pair, pair],
        [*m_blocks, grad_rows, first_full, second_full, hidden_bias],
    )
    out_keep, out_send = call(
        mlp_out_kernel, "mlp_out", [pair, pair], [act, second_full], ordered=[send], flops=1.5e9
    )
    grad_in = tp_scatter(keep, send, [out_send])
    if direct:
        first_keep, first_send, second_keep, second_send, fc1_part = call(
            mlp_grad_kernel,
            "mlp_weight_grad",
            [((half, feat, hidden), BF)] * 4 + [((1, hidden), F32)],
            [mlp_rows, grad_rows, act, pre],
            [rank],
            ordered=[grad_in[0]],
            flops=4e9,
        )
        first_half = halve_four(first_keep, first_send)
        first_one = halve_two(*first_half)
        first_sum = halve_one(*first_one)
        second_half = halve_four(second_keep, second_send)
        second_one = halve_two(*second_half)
        second_sum = halve_one(*second_one)
        steps = [[first_half[1]], [second_half[1], first_one[1]], [second_one[1]]]
    else:
        first_sum = lax.psum_scatter(
            dot(mlp_rows, pre, (0, 0)), "fsdp", scatter_dimension=0, tiled=True
        )
        second_sum = lax.psum_scatter(
            dot(grad_rows, act, (0, 0)), "fsdp", scatter_dimension=0, tiled=True
        )
        fc1_part = jnp.sum(pre.astype(F32), axis=0, keepdims=True)
        steps = [[]] * 3

    grad_middle, grad_attn, sums = call(
        middle_back_kernel,
        "middle_back",
        [block_f32, block, ((8, width), F32)],
        [x_own, middle, branch, *grad_in, mod],
        ordered=[fc1_part] if direct else [],
    )
    a_blocks = tp_gather(grad_attn)
    mlp_parts = tp_scatter(out_keep, out_send, [a_blocks[2]])
    back_rows, grads, keep, send = call(
        functools.partial(attn_back_kernel, latents=latents),
        "attention_back",
        [((tokens, width), BF), ((tokens, 3 * cols), BF), pair, pair],
        [*a_blocks, qkv_full, proj_full, qkv],
        ordered=[mlp_parts[0], *steps[0]],
    )
    grad_in = tp_scatter(keep, send)
    output, gates = call(
        output_kernel,
        "output",
        [block, ((8, width), F32)],
        [middle, x_own, *mlp_parts, second_bias, mod],
    )
    if direct:
        attn_keep, attn_send, qkv_part = call(
            attn_grad_kernel,
            "attn_weight_grad",
            [((half, feat, 4 * cols), BF)] * 2 + [((1, 3 * cols), F32)],
            [attn_rows, grads, back_rows, att],
            [rank],
            ordered=[grad_in[0], gates, *steps[1]],
            flops=6e9,
        )
        attn_half = halve_four(attn_keep, attn_send)
        own, out = halve_two(*attn_half)
        tail = [[attn_half[1]], [out]]
        qkv_sum, proj_sum = call(
            attn_add_kernel,
            "attn_sum",
            [((3, feat, cols), F32), ((cols, feat), F32)],
            [own, swap(out, "fsdp", 4)],
        )
        qkv_sum = qkv_sum.transpose(1, 0, 2)
    else:
        tail = [[]] * 2
        qkv_sum = lax.psum_scatter(
            dot(attn_rows, grads, (0, 0)), "fsdp", scatter_dimension=0, tiled=True
        ).reshape(feat, 3, cols)
        proj_sum = lax.psum_scatter(
            dot(back_rows, att, (0, 0)), "fsdp", scatter_dimension=0, tiled=True
        ).T
        qkv_part = jnp.sum(grads.astype(F32), axis=0, keepdims=True)

    inputs_grad, pack = call(
        input_back_kernel,
        "input_back",
        [block_f32, ((16, width), BF)],
        [x_own, grad_middle, *grad_in, mod, sums, gates, fc2_part, fc1_part, qkv_part],
        scratch=[pltpu.VMEM((16, width), F32)],
    )
    packs = [pack] + [swap(pack, "tp", d) for d in range(1, tp_count)]
    spread_keep, spread_send = call(
        functools.partial(spread_kernel, latents=latents, feat=feat),
        "spread",
        [((half, 16, width), BF)] * 2,
        packs,
        [rank, tp_rank],
        scratch=[pltpu.VMEM((tp_count, 16, width), F32), pltpu.VMEM((16, width), F32)],
        ordered=steps[2],
    )
    silu_keep, silu_send, grad_mod_all, bias_grads = call(
        functools.partial(silu_kernel, latents=latents),
        "silu_columns",
        [((half, 8, 128), F32)] * 2
        + [((count * latents, 6 * width), BF), ((1, width), F32)],
        [*exchange(spread_keep, spread_send), ada_weight],
        scratch=[
            pltpu.VMEM((6, count * latents, width), F32),
            pltpu.VMEM((count, 8, 128), F32),
        ],
        ordered=tail[0],
    )
    cond_grad = call(
        functools.partial(cond_kernel, latents=latents, feat=feat),
        "cond_grad",
        [((latents, width), F32)],
        [*exchange(silu_keep, silu_send), conditioning],
        [rank],
        scratch=[pltpu.VMEM((count, 8, 128), F32)],
        ordered=tail[1],
    )[0]
    ada_weight_grad = dot(cond_cols, grad_mod_all, (0, 0))
    bias_grads = bias_grads.reshape(width)
    ada_bias_grad = jnp.sum(
        lax.dynamic_slice_in_dim(grad_mod_all, rank * mod_part, mod_part, 1).astype(F32), axis=0
    )

    return (
        output.reshape(latents, positions, width).transpose(1, 0, 2),
        inputs_grad.reshape(latents, positions, width).transpose(1, 0, 2),
        cond_grad,
        ada_weight_grad,
        ada_bias_grad,
        qkv_sum,
        bias_grads[: 2 * feat].reshape(2, feat),
        proj_sum,
        bias_grads[2 * feat : 3 * feat],
        first_sum,
        bias_grads[4 * feat : 4 * feat + hidden_part],
        second_sum.T,
        bias_grads[3 * feat : 4 * feat],
    )


def solution(mesh):
    return jax.shard_map(
        shards,
        mesh=mesh,
        in_specs=(
            P("tp", "fsdp", None),
            P("fsdp", None),
            P("fsdp", None),
            P("fsdp"),
            P("fsdp", None, "tp"),
            P(None, "fsdp"),
            P("tp", "fsdp"),
            P("fsdp"),
            P("fsdp", "tp"),
            P("fsdp"),
            P("tp", "fsdp"),
            P("fsdp"),
            P("tp", "fsdp", None),
        ),
        out_specs=(
            P("tp", "fsdp", None),
            P("tp", "fsdp", None),
            P("fsdp", None),
            P("fsdp", None),
            P("fsdp"),
            P("fsdp", None, "tp"),
            P(None, "fsdp"),
            P("tp", "fsdp"),
            P("fsdp"),
            P("fsdp", "tp"),
            P("fsdp"),
            P("tp", "fsdp"),
            P("fsdp"),
        ),
        check_vma=False,
    )
```

time: 262 us -> 185 us (0.71)
  starting transfers between devices: 76.6 us -> 54.3 us
  waiting for transfers between devices: 108 us -> 87.8 us
  local copies, waits for them, and re-layouts: 26.3 us -> 10.9 us
  between operations: 14.5 us -> 1.16 us
  other arithmetic: 8.86 us -> 1.24 us
  Pallas kernels: 24.9 us -> 28 us
    all_to_all x4 -> x0, waiting for transfers between devices: 46.4 us -> none  [the longest x1 25.8 us: shards(): lax.all_to_all(silu_cols.reshape(count, latents, feat), 'fsdp', split_axi...]
    ppermute x42 -> x53, waiting for transfers between devices: 61.5 us -> 87.8 us  [swap(): return lax.ppermute(block, axis, [(i, i ^ offset) for i in range(count)])]
    all_to_all x4 -> x0, starting transfers between devices: 24.3 us -> none  [the longest x2 17.5 us: shards(): got = lax.all_to_all(sent, 'fsdp', split_axis=0, concat_axis=0, tiled=True)]
    unnamed x86 -> x26, local copies, waits for them, and re-layouts: 18.6 us -> 5.55 us
    convert_element_type x2 -> x0, other arithmetic: 3.32 us -> none  [scatter_two(): (keep[d].astype(F32) + got[d].astype(F32)).astype(BF)]
    pallas_call x17 -> x49, Pallas kernels: 24.9 us -> 28 us  [call(): pl.pallas_call(body, out_shape=shapes, grid=(1,) if blocked else (), in_s...]
    ppermute x42 -> x53, starting transfers between devices: 52.3 us -> 54.3 us  [swap(): return lax.ppermute(block, axis, [(i, i ^ offset) for i in range(count)])]
  transfers between devices with their start and end apart: 47 -> 53, of which waited for: 21 -> 28; matrix products, arithmetic and copies ran while one was open for 6% -> 4% of each run, Pallas kernels for 8% -> 11%
where the time goes in v3:
time: 185 us
  waiting for transfers between devices  87.8 us (47%)
  starting transfers between devices  54.3 us (29%)
  Pallas kernels  28 us (15%)
  local copies, waits for them, and re-layouts  10.9 us (6%)
    ppermute x53, waiting for transfers between devices, swap(): return lax.ppermute(block, axis, [(i, i ^ offset) for i in range(count)])  87.8 us
    ppermute x53, starting transfers between devices, swap(): return lax.ppermute(block, axis, [(i, i ^ offset) for i in range(count)])  54.3 us
    pallas_call x49, Pallas kernels, call(): pl.pallas_call(body, out_shape=shapes, grid=(1,) if blocked else (), in_s...  28 us
    unnamed x26, local copies, waits for them, and re-layouts  5.55 us
  transfers between devices with their start and end apart: 53, of which 28 were waited for; matrix products, arithmetic and copies ran while one was open for 4% of the time, Pallas kernels for 11%

profile of v3, /device:TPU:0, one launch (start us, length us, event | category | flops | bytes accessed | tf_op | source)
XLA Modules:
  0.0 185.1 jit_solution(2627488353217845478)
XLA Ops:
  4.5 2.9 %collective-permute-start = (f32[4,16,128]{2,1,0:T(8,128)S(1)}, f32[4,16,128]{2,1,0:T(8,128)S(1)}, u32[]{:S(2)}, u32[]{:S(2)}) collective-permute-start(f32[4,16,128]{2,1,0:T(8,128)S(1)} %get-tuple-element.106), channel_id=1, source_target_pairs={{0,4},{4,0},{8,12},{12,8},{16,20},{20,16},{24,28},{28,24},{1,5},{5... | collective-permute-start | bytes 98312 | tf_op jit(solution)/shard_map/ppermute | solution.py:73
  7.5 1.9 %collective-permute-done.refs_1_ = f32[4,16,128]{2,1,0:T(8,128)S(1)} collective-permute-done((f32[4,16,128]{2,1,0:T(8,128)S(1)}, f32[4,16,128]{2,1,0:T(8,128)S(1)}, u32[]{:S(2)}, u32[]{:S(2)}) %collective-permute-start) | collective-permute-done | bytes 32800 | tf_op jit(solution)/shard_map/ppermute | solution.py:73
  11.2 3.2 %collective-permute-start.6 = (bf16[96,768]{1,0:T(8,128)(2,1)S(1)}, bf16[96,768]{1,0:T(8,128)(2,1)S(1)}, u32[]{:S(2)}, u32[]{:S(2)}) collective-permute-start(bf16[96,768]{1,0:T(8,128)(2,1)S(1)} %attn_own.1.refs_1_), channel_id=1, source_target_pairs={{0,16},{4,20},{8,24},{12,28},{16,0},{20,4},{24,8},{28,12},{1,17},{... | collective-permute-start | bytes 442376 | tf_op jit(solution)/shard_map/ppermute | solution.py:73
  14.4 1.6 collective-permute-start.1
  16.3 2.5 %collective-permute-start.3 = (f32[2,16,128]{2,1,0:T(8,128)S(1)}, f32[2,16,128]{2,1,0:T(8,128)S(1)}, u32[]{:S(2)}, u32[]{:S(2)}) collective-permute-start(f32[2,16,128]{2,1,0:T(8,128)S(1)} %get-tuple-element.110), channel_id=1, source_target_pairs={{0,24},{4,28},{8,16},{12,20},{16,8},{20,12},{24,0},{28,4},{1,25},{... | collective-permute-start | bytes 49160 | tf_op jit(solution)/shard_map/ppermute | solution.py:73
  19.7 1.6 collective-permute-done.2.refs_2_.refs_5_
  23.3 1.6 collective-permute-start.4
  24.9 3.1 %collective-permute-done.4.refs_1_ = bf16[4,16,768]{2,1,0:T(8,128)(2,1)S(1)} collective-permute-done((bf16[4,16,768]{2,1,0:T(8,128)(2,1)S(1)}, bf16[4,16,768]{2,1,0:T(8,128)(2,1)S(1)}, u32[]{:S(2)}, u32[]{:S(2)}) %collective-permute-start.4) | collective-permute-done | bytes 98336 | tf_op jit(solution)/shard_map/ppermute | solution.py:73
  29.3 1.6 collective-permute-start.10
  30.9 1.5 collective-permute-start.5
  32.4 3.0 %collective-permute-done.5.refs_1_ = bf16[2,16,768]{2,1,0:T(8,128)(2,1)S(1)} collective-permute-done((bf16[2,16,768]{2,1,0:T(8,128)(2,1)S(1)}, bf16[2,16,768]{2,1,0:T(8,128)(2,1)S(1)}, u32[]{:S(2)}, u32[]{:S(2)}) %collective-permute-start.5) | collective-permute-done | bytes 49184 | tf_op jit(solution)/shard_map/ppermute | solution.py:73
  35.4 1.6 collective-permute-start.13
  38.3 3.2 %collective-permute-start.8 = (bf16[96,768]{1,0:T(8,128)(2,1)S(1)}, bf16[96,768]{1,0:T(8,128)(2,1)S(1)}, u32[]{:S(2)}, u32[]{:S(2)}) collective-permute-start(bf16[96,768]{1,0:T(8,128)(2,1)S(1)} %first_own.1.refs_0_), channel_id=1, source_target_pairs={{0,16},{4,20},{8,24},{12,28},{16,0},{20,4},{24,8},{28,12},{1,17},{... | collective-permute-start | bytes 442376 | tf_op jit(solution)/shard_map/ppermute | solution.py:73
  41.5 8.3 %collective-permute-done.8.refs_1_ = bf16[96,768]{1,0:T(8,128)(2,1)S(1)} collective-permute-done((bf16[96,768]{1,0:T(8,128)(2,1)S(1)}, bf16[96,768]{1,0:T(8,128)(2,1)S(1)}, u32[]{:S(2)}, u32[]{:S(2)}) %collective-permute-start.8) | collective-permute-done | bytes 147488 | tf_op jit(solution)/shard_map/ppermute | solution.py:73
  51.0 2.5 %attention.1 = (bf16[512,576]{1,0:T(8,128)(2,1)S(1)}, bf16[512,192]{1,0:T(8,128)(2,1)S(1)}, bf16[256,768]{1,0:T(8,128)(2,1)S(1)}, bf16[256,768]{1,0:T(8,128)(2,1)S(1)}) custom-call(bf16[2,96,768]{2,1,0:T(8,128)(2,1)S(1)} %join.8.refs_0_, bf16[512,768]{1,0:T(8,128)(2,1)S(1)} %get-tuple-element.118.refs_1_.refs_5_, ...), custom_call_target="tpu_custom_call" | custom-call | flops 1 | bytes 1 | tf_op jit(solution)/shard_map/attention/pallas_call | solution.py:40
  53.6 3.5 %collective-permute-start.15 = (bf16[2,96,768]{2,1,0:T(8,128)(2,1)S(1)}, bf16[2,96,768]{2,1,0:T(8,128)(2,1)S(1)}, u32[]{:S(2)}, u32[]{:S(2)}) collective-permute-start(bf16[2,96,768]{2,1,0:T(8,128)(2,1)S(1)} %join.8.refs_0_), channel_id=1, source_target_pairs={{0,8},{4,12},{8,0},{12,4},{16,24},{20,28},{24,16},{28,20},{1,9},{5... | collective-permute-start | bytes 884744 | tf_op jit(solution)/shard_map/ppermute | solution.py:73
  57.1 2.5 %collective-permute-done.16.refs_1_ = bf16[96,768]{1,0:T(8,128)(2,1)S(1)} collective-permute-done((bf16[96,768]{1,0:T(8,128)(2,1)S(1)}, bf16[96,768]{1,0:T(8,128)(2,1)S(1)}, u32[]{:S(2)}, u32[]{:S(2)}) %collective-permute-start.16) | collective-permute-done | bytes 147488 | tf_op jit(solution)/shard_map/ppermute | solution.py:73
  59.7 6.1 %collective-permute-done.15.refs_1_ = bf16[2,96,768]{2,1,0:T(8,128)(2,1)S(1)} collective-permute-done((bf16[2,96,768]{2,1,0:T(8,128)(2,1)S(1)}, bf16[2,96,768]{2,1,0:T(8,128)(2,1)S(1)}, u32[]{:S(2)}, u32[]{:S(2)}) %collective-permute-start.15) | collective-permute-done | bytes 294944 | tf_op jit(solution)/shard_map/ppermute | solution.py:73
  66.0 1.6 collective-permute-start.18
  67.6 1.5 collective-permute-start.22
  69.1 3.1 %collective-permute-done.17.refs_1_ = bf16[2,96,768]{2,1,0:T(8,128)(2,1)S(1)} collective-permute-done((bf16[2,96,768]{2,1,0:T(8,128)(2,1)S(1)}, bf16[2,96,768]{2,1,0:T(8,128)(2,1)S(1)}, u32[]{:S(2)}, u32[]{:S(2)}) %collective-permute-start.17) | collective-permute-done | bytes 294944 | tf_op jit(solution)/shard_map/ppermute | solution.py:73
  72.2 1.6 collective-permute-start.23
  74.2 1.6 collective-permute-start.20
  75.8 5.1 %collective-permute-done.20.refs_2_ = bf16[128,768]{1,0:T(8,128)(2,1)S(1)} collective-permute-done((bf16[128,768]{1,0:T(8,128)(2,1)S(1)}, bf16[128,768]{1,0:T(8,128)(2,1)S(1)}, u32[]{:S(2)}, u32[]{:S(2)}) %collective-permute-start.20) | collective-permute-done | bytes 196640 | tf_op jit(solution)/shard_map/ppermute | solution.py:73
  80.9 2.9 %collective-permute-done.22.refs_2_ = bf16[4,96,768]{2,1,0:T(8,128)(2,1)S(1)} collective-permute-done((bf16[4,96,768]{2,1,0:T(8,128)(2,1)S(1)}, bf16[4,96,768]{2,1,0:T(8,128)(2,1)S(1)}, u32[]{:S(2)}, u32[]{:S(2)}) %collective-permute-start.22) | collective-permute-done | bytes 589856 | tf_op jit(solution)/shard_map/ppermute | solution.py:73
  83.9 11.4 %collective-permute-done.23.refs_2_ = bf16[4,96,768]{2,1,0:T(8,128)(2,1)S(1)} collective-permute-done((bf16[4,96,768]{2,1,0:T(8,128)(2,1)S(1)}, bf16[4,96,768]{2,1,0:T(8,128)(2,1)S(1)}, u32[]{:S(2)}, u32[]{:S(2)}) %collective-permute-start.23) | collective-permute-done | bytes 589856 | tf_op jit(solution)/shard_map/ppermute | solution.py:73
  95.3 3.1 %mlp.1 = (bf16[512,768]{1,0:T(8,128)(2,1)S(1)}, bf16[512,768]{1,0:T(8,128)(2,1)S(1)}, bf16[512,768]{1,0:T(8,128)(2,1)S(1)}, bf16[256,768]{1,0:T(8,128)(2,1)S(1)}, bf16[256,768]{1,0:T(8,128)(2,1)S(1)}) custom-call(bf16[128,768]{1,0:T(8,128)(2,1)S(1)} %get-tuple-element.130.refs_0_, bf16[128,768]{1,0:T(8,128)(2,1)S(1)} %collective-permute-done.19.refs_1_, ...), custom_call_target="tpu_custom_call" | custom-call | flops 1 | bytes 1 | tf_op jit(solution)/shard_map/mlp/pallas_call | solution.py:40
  98.5 1.6 mlp_out.1
  100.9 4.0 %mlp_weight_grad.1 = (bf16[4,96,768]{2,1,0:T(8,128)(2,1)S(1)}, bf16[4,96,768]{2,1,0:T(8,128)(2,1)S(1)}, bf16[4,96,768]{2,1,0:T(8,128)(2,1)S(1)}, bf16[4,96,768]{2,1,0:T(8,128)(2,1)S(1)}, f32[1,768]{1,0:T(1,128)S(1)}) custom-call(s32[1]{0:T(128)} %bitcast.refs_0_, f32[128,768]{1,0:T(8,128)S(1)} %get-tuple-element.136.refs_1_.refs_4_, ...), custom_call_target="tpu_custom_call" | custom-call | flops 4000000000 | bytes 1 | tf_op jit(solution)/shard_map/mlp_weight_grad/pallas_call | solution.py:40
  104.9 1.5 collective-permute-start.29
  108.7 1.5 collective-permute-start.34
  110.2 4.5 %collective-permute-done.26.refs_0_.refs_4_ = bf16[128,768]{1,0:T(8,128)(2,1)S(1)} collective-permute-done((bf16[128,768]{1,0:T(8,128)(2,1)S(1)}, bf16[128,768]{1,0:T(8,128)(2,1)S(1)}, u32[]{:S(2)}, u32[]{:S(2)}) %collective-permute-start.26) | collective-permute-done | bytes 196640 | tf_op jit(solution)/shard_map/ppermute | solution.py:73
  114.8 6.4 %collective-permute-done.29.refs_1_ = bf16[4,96,768]{2,1,0:T(8,128)(2,1)S(1)} collective-permute-done((bf16[4,96,768]{2,1,0:T(8,128)(2,1)S(1)}, bf16[4,96,768]{2,1,0:T(8,128)(2,1)S(1)}, u32[]{:S(2)}, u32[]{:S(2)}) %collective-permute-start.29) | collective-permute-done | bytes 589856 | tf_op jit(solution)/shard_map/ppermute | solution.py:73
  121.3 4.7 %attention_back.1 = (bf16[512,768]{1,0:T(8,128)(2,1)S(1)}, bf16[512,576]{1,0:T(8,128)(2,1)S(1)}, bf16[256,768]{1,0:T(8,128)(2,1)S(1)}, bf16[256,768]{1,0:T(8,128)(2,1)S(1)}) custom-call(f32[128,768]{1,0:T(8,128)S(1)} %get-tuple-element.144.refs_2_.refs_0_, bf16[2,96,768]{2,1,0:T(8,128)(2,1)S(1)} %get-tuple-element.151.refs_1_, ...), custom_call_target="tpu_custom_call" | custom-call | flops 1 | bytes 1 | tf_op jit(solution)/shard_map/attention_back/pallas_call | solution.py:40
  126.4 1.5 collective-permute-start.28
  127.9 5.1 %collective-permute-done.34.refs_1_ = bf16[4,96,768]{2,1,0:T(8,128)(2,1)S(1)} collective-permute-done((bf16[4,96,768]{2,1,0:T(8,128)(2,1)S(1)}, bf16[4,96,768]{2,1,0:T(8,128)(2,1)S(1)}, u32[]{:S(2)}, u32[]{:S(2)}) %collective-permute-start.34) | collective-permute-done | bytes 589856 | tf_op jit(solution)/shard_map/ppermute | solution.py:73
  133.5 2.0 %collective-permute-done.35.refs_1_ = bf16[2,96,768]{2,1,0:T(8,128)(2,1)S(1)} collective-permute-done((bf16[2,96,768]{2,1,0:T(8,128)(2,1)S(1)}, bf16[2,96,768]{2,1,0:T(8,128)(2,1)S(1)}, u32[]{:S(2)}, u32[]{:S(2)}) %collective-permute-start.35) | collective-permute-done | bytes 294944 | tf_op jit(solution)/shard_map/ppermute | solution.py:73
  135.7 2.9 %attn_weight_grad.1 = (bf16[4,96,768]{2,1,0:T(8,128)(2,1)S(1)}, bf16[4,96,768]{2,1,0:T(8,128)(2,1)S(1)}, f32[1,576]{1,0:T(1,128)S(1)}) custom-call(s32[1]{0:T(128)} %bitcast.refs_0_, f32[128,768]{1,0:T(8,128)S(1)} %get-tuple-element.155.refs_1_.refs_2_, f32[8,768]{1,0:T(8,128)S(1)} %get-tuple-element.158.refs_2_.refs_6_, ...), custom_call_target="tpu_custom_call" | custom-call | flops 6000000000 | bytes 1 | tf_op jit(solution)/shard_map/attn_weight_grad/pallas_call | solution.py:40
  138.6 1.5 collective-permute-start.36
  140.4 1.5 collective-permute-start.33
  143.3 3.0 %collective-permute-done.33.refs_3_ = bf16[128,768]{1,0:T(8,128)(2,1)S(1)} collective-permute-done((bf16[128,768]{1,0:T(8,128)(2,1)S(1)}, bf16[128,768]{1,0:T(8,128)(2,1)S(1)}, u32[]{:S(2)}, u32[]{:S(2)}) %collective-permute-start.33) | collective-permute-done | bytes 196640 | tf_op jit(solution)/shard_map/ppermute | solution.py:73
  146.8 1.6 collective-permute-start.40
  148.4 3.2 %collective-permute-done.38.refs_1_ = bf16[2,96,768]{2,1,0:T(8,128)(2,1)S(1)} collective-permute-done((bf16[2,96,768]{2,1,0:T(8,128)(2,1)S(1)}, bf16[2,96,768]{2,1,0:T(8,128)(2,1)S(1)}, u32[]{:S(2)}, u32[]{:S(2)}) %collective-permute-start.38) | collective-permute-done | bytes 294944 | tf_op jit(solution)/shard_map/ppermute | solution.py:73
  154.2 4.3 %collective-permute-done.42.refs_1_ = bf16[4,16,768]{2,1,0:T(8,128)(2,1)S(1)} collective-permute-done((bf16[4,16,768]{2,1,0:T(8,128)(2,1)S(1)}, bf16[4,16,768]{2,1,0:T(8,128)(2,1)S(1)}, u32[]{:S(2)}, u32[]{:S(2)}) %collective-permute-start.42) | collective-permute-done | bytes 98336 | tf_op jit(solution)/shard_map/ppermute | solution.py:73
  160.6 2.4 %collective-permute-start.45 = (bf16[2,16,768]{2,1,0:T(8,128)(2,1)S(1)}, bf16[2,16,768]{2,1,0:T(8,128)(2,1)S(1)}, u32[]{:S(2)}, u32[]{:S(2)}) collective-permute-start(bf16[2,16,768]{2,1,0:T(8,128)(2,1)S(1)} %get-tuple-element.182), channel_id=1, source_target_pairs={{0,24},{4,28},{8,16},{12,20},{16,8},{20,12},{24,0},{28,4},{1,25},{... | collective-permute-start | bytes 147464 | tf_op jit(solution)/shard_map/ppermute | solution.py:73
  168.3 1.6 fusion
  169.9 4.2 %collective-permute-done.37.refs_1_ = bf16[2,96,768]{2,1,0:T(8,128)(2,1)S(1)} collective-permute-done((bf16[2,96,768]{2,1,0:T(8,128)(2,1)S(1)}, bf16[2,96,768]{2,1,0:T(8,128)(2,1)S(1)}, u32[]{:S(2)}, u32[]{:S(2)}) %collective-permute-start.37) | collective-permute-done | bytes 294944 | tf_op jit(solution)/shard_map/ppermute | solution.py:73
  178.0 2.3 %collective-permute-start.49 = (f32[2,8,128]{2,1,0:T(8,128)S(1)}, f32[2,8,128]{2,1,0:T(8,128)S(1)}, u32[]{:S(2)}, u32[]{:S(2)}) collective-permute-start(f32[2,8,128]{2,1,0:T(8,128)S(1)} %get-tuple-element.188), channel_id=1, source_target_pairs={{0,24},{4,28},{8,16},{12,20},{16,8},{20,12},{24,0},{28,4},{1,25},{... | collective-permute-start | bytes 24584 | tf_op jit(solution)/shard_map/ppermute | solution.py:73
  (147 shorter events, 38.8 us)
Async XLA Ops:
  11.2 16.8 %collective-permute-start.6 = (bf16[96,768]{1,0:T(8,128)(2,1)S(1)}, bf16[96,768]{1,0:T(8,128)(2,1)S(1)}, u32[]{:S(2)}, u32[]{:S(2)}) collective-permute-start(bf16[96,768]{1,0:T(8,128)(2,1)S(1)} %attn_own.1.refs_1_), channel_id=1, source_target_pairs={{0,16},{4,20},{8,24},{12,28},{16,0},{20,4},{24,8},{28,12},{1,17},{... | collective-permute-start | bytes 442376 | tf_op jit(solution)/shard_map/ppermute | solution.py:73
  14.4 5.3 %collective-permute-start.1 = (f32[2,16,128]{2,1,0:T(8,128)S(1)}, f32[2,16,128]{2,1,0:T(8,128)S(1)}, u32[]{:S(2)}, u32[]{:S(2)}) collective-permute-start(f32[2,16,128]{2,1,0:T(8,128)S(1)} %get-tuple-element.108), channel_id=1, source_target_pairs={{0,8},{4,12},{8,0},{12,4},{16,24},{20,28},{24,16},{28,20},{1,9},{5... | collective-permute-start | bytes 49160 | tf_op jit(solution)/shard_map/ppermute | solution.py:73
  16.0 5.3 %collective-permute-start.2 = (f32[2,16,128]{2,1,0:T(8,128)S(1)}, f32[2,16,128]{2,1,0:T(8,128)S(1)}, u32[]{:S(2)}, u32[]{:S(2)}) collective-permute-start(f32[2,16,128]{2,1,0:T(8,128)S(1)} %get-tuple-element.109), channel_id=1, source_target_pairs={{0,16},{4,20},{8,24},{12,28},{16,0},{20,4},{24,8},{28,12},{1,17},{... | collective-permute-start | bytes 49160 | tf_op jit(solution)/shard_map/ppermute | solution.py:73
  16.3 5.5 %collective-permute-start.3 = (f32[2,16,128]{2,1,0:T(8,128)S(1)}, f32[2,16,128]{2,1,0:T(8,128)S(1)}, u32[]{:S(2)}, u32[]{:S(2)}) collective-permute-start(f32[2,16,128]{2,1,0:T(8,128)S(1)} %get-tuple-element.110), channel_id=1, source_target_pairs={{0,24},{4,28},{8,16},{12,20},{16,8},{20,12},{24,0},{28,4},{1,25},{... | collective-permute-start | bytes 49160 | tf_op jit(solution)/shard_map/ppermute | solution.py:73
  28.1 7.3 %collective-permute-start.7 = (bf16[2,96,768]{2,1,0:T(8,128)(2,1)S(1)}, bf16[2,96,768]{2,1,0:T(8,128)(2,1)S(1)}, u32[]{:S(2)}, u32[]{:S(2)}) collective-permute-start(bf16[2,96,768]{2,1,0:T(8,128)(2,1)S(1)} %join.6.refs_1_), channel_id=1, source_target_pairs={{0,8},{4,12},{8,0},{12,4},{16,24},{20,28},{24,16},{28,20},{1,9},{5... | collective-permute-start | bytes 884744 | tf_op jit(solution)/shard_map/ppermute | solution.py:73
  29.3 8.9 %collective-permute-start.10 = (bf16[256,768]{1,0:T(8,128)(2,1)S(1)}, bf16[256,768]{1,0:T(8,128)(2,1)S(1)}, u32[]{:S(2)}, u32[]{:S(2)}) collective-permute-start(bf16[256,768]{1,0:T(8,128)(2,1)S(1)} %tokens.1.refs_2_.refs_3_.refs_1_.refs_0_), channel_id=1, source_target_pairs={{0,2},{1,3},{2,0},{3,1},{4,6},{5,7},{6,4},{7,5},{8,10},{9,11},{10,... | collective-permute-start | bytes 1179656 | tf_op jit(solution)/shard_map/ppermute | solution.py:73
  35.4 15.3 %collective-permute-start.13 = (bf16[4,96,768]{2,1,0:T(8,128)(2,1)S(1)}, bf16[4,96,768]{2,1,0:T(8,128)(2,1)S(1)}, u32[]{:S(2)}, u32[]{:S(2)}) collective-permute-start(bf16[4,96,768]{2,1,0:T(8,128)(2,1)S(1)} %join.7.refs_0_.refs_1_), channel_id=1, source_target_pairs={{0,4},{4,0},{8,12},{12,8},{16,20},{20,16},{24,28},{28,24},{1,5},{5... | collective-permute-start | bytes 1769480 | tf_op jit(solution)/shard_map/ppermute | solution.py:73
  37.0 13.2 %collective-permute-start.9 = (bf16[256,768]{1,0:T(8,128)(2,1)S(1)}, bf16[256,768]{1,0:T(8,128)(2,1)S(1)}, u32[]{:S(2)}, u32[]{:S(2)}) collective-permute-start(bf16[256,768]{1,0:T(8,128)(2,1)S(1)} %tokens.1.refs_2_.refs_3_.refs_1_.refs_0_), channel_id=1, source_target_pairs={{0,1},{1,0},{2,3},{3,2},{4,5},{5,4},{6,7},{7,6},{8,9},{9,8},{10,11... | collective-permute-start | bytes 1179656 | tf_op jit(solution)/shard_map/ppermute | solution.py:73
  38.2 11.9 %collective-permute-start.11 = (bf16[256,768]{1,0:T(8,128)(2,1)S(1)}, bf16[256,768]{1,0:T(8,128)(2,1)S(1)}, u32[]{:S(2)}, u32[]{:S(2)}) collective-permute-start(bf16[256,768]{1,0:T(8,128)(2,1)S(1)} %collective-permute-done.10.refs_4_.refs_5_), channel_id=1, source_target_pairs={{0,1},{1,0},{2,3},{3,2},{4,5},{5,4},{6,7},{7,6},{8,9},{9,8},{10,11... | collective-permute-start | bytes 1179656 | tf_op jit(solution)/shard_map/ppermute | solution.py:73
  38.3 11.6 %collective-permute-start.8 = (bf16[96,768]{1,0:T(8,128)(2,1)S(1)}, bf16[96,768]{1,0:T(8,128)(2,1)S(1)}, u32[]{:S(2)}, u32[]{:S(2)}) collective-permute-start(bf16[96,768]{1,0:T(8,128)(2,1)S(1)} %first_own.1.refs_0_), channel_id=1, source_target_pairs={{0,16},{4,20},{8,24},{12,28},{16,0},{20,4},{24,8},{28,12},{1,17},{... | collective-permute-start | bytes 442376 | tf_op jit(solution)/shard_map/ppermute | solution.py:73
  41.4 8.7 %collective-permute-start.12 = (bf16[16,768]{1,0:T(8,128)(2,1)S(1)}, bf16[16,768]{1,0:T(8,128)(2,1)S(1)}, u32[]{:S(2)}, u32[]{:S(2)}) collective-permute-start(bf16[16,768]{1,0:T(8,128)(2,1)S(1)} %get-tuple-element.117), channel_id=1, source_target_pairs={{0,16},{4,20},{8,24},{12,28},{16,0},{20,4},{24,8},{28,12},{1,17},{... | collective-permute-start | bytes 73736 | tf_op jit(solution)/shard_map/ppermute | solution.py:73
  49.9 9.7 %collective-permute-start.16 = (bf16[96,768]{1,0:T(8,128)(2,1)S(1)}, bf16[96,768]{1,0:T(8,128)(2,1)S(1)}, u32[]{:S(2)}, u32[]{:S(2)}) collective-permute-start(bf16[96,768]{1,0:T(8,128)(2,1)S(1)} %second_own.1.refs_0_), channel_id=1, source_target_pairs={{0,16},{4,20},{8,24},{12,28},{16,0},{20,4},{24,8},{28,12},{1,17},{... | collective-permute-start | bytes 442376 | tf_op jit(solution)/shard_map/ppermute | solution.py:73
  53.5 12.3 %collective-permute-start.14 = (bf16[256,768]{1,0:T(8,128)(2,1)S(1)}, bf16[256,768]{1,0:T(8,128)(2,1)S(1)}, u32[]{:S(2)}, u32[]{:S(2)}) collective-permute-start(bf16[256,768]{1,0:T(8,128)(2,1)S(1)} %get-tuple-element.123), channel_id=1, source_target_pairs={{0,1},{1,0},{2,3},{3,2},{4,5},{5,4},{6,7},{7,6},{8,9},{9,8},{10,11... | collective-permute-start | bytes 1179656 | tf_op jit(solution)/shard_map/ppermute | solution.py:73
  53.6 12.2 %collective-permute-start.15 = (bf16[2,96,768]{2,1,0:T(8,128)(2,1)S(1)}, bf16[2,96,768]{2,1,0:T(8,128)(2,1)S(1)}, u32[]{:S(2)}, u32[]{:S(2)}) collective-permute-start(bf16[2,96,768]{2,1,0:T(8,128)(2,1)S(1)} %join.8.refs_0_), channel_id=1, source_target_pairs={{0,8},{4,12},{8,0},{12,4},{16,24},{20,28},{24,16},{28,20},{1,9},{5... | collective-permute-start | bytes 884744 | tf_op jit(solution)/shard_map/ppermute | solution.py:73
  59.6 12.5 %collective-permute-start.17 = (bf16[2,96,768]{2,1,0:T(8,128)(2,1)S(1)}, bf16[2,96,768]{2,1,0:T(8,128)(2,1)S(1)}, u32[]{:S(2)}, u32[]{:S(2)}) collective-permute-start(bf16[2,96,768]{2,1,0:T(8,128)(2,1)S(1)} %join.10.refs_2_.refs_0_), channel_id=1, source_target_pairs={{0,8},{4,12},{8,0},{12,4},{16,24},{20,28},{24,16},{28,20},{1,9},{5... | collective-permute-start | bytes 884744 | tf_op jit(solution)/shard_map/ppermute | solution.py:73
  66.0 7.9 %collective-permute-start.18 = (bf16[128,768]{1,0:T(8,128)(2,1)S(1)}, bf16[128,768]{1,0:T(8,128)(2,1)S(1)}, u32[]{:S(2)}, u32[]{:S(2)}) collective-permute-start(bf16[128,768]{1,0:T(8,128)(2,1)S(1)} %get-tuple-element.127), channel_id=1, source_target_pairs={{0,2},{1,3},{2,0},{3,1},{4,6},{5,7},{6,4},{7,5},{8,10},{9,11},{10,... | collective-permute-start | bytes 589832 | tf_op jit(solution)/shard_map/ppermute | solution.py:73
  67.6 16.2 %collective-permute-start.22 = (bf16[4,96,768]{2,1,0:T(8,128)(2,1)S(1)}, bf16[4,96,768]{2,1,0:T(8,128)(2,1)S(1)}, u32[]{:S(2)}, u32[]{:S(2)}) collective-permute-start(bf16[4,96,768]{2,1,0:T(8,128)(2,1)S(1)} %join.9.refs_1_), channel_id=1, source_target_pairs={{0,4},{4,0},{8,12},{12,8},{16,20},{20,16},{24,28},{28,24},{1,5},{5... | collective-permute-start | bytes 1769480 | tf_op jit(solution)/shard_map/ppermute | solution.py:73
  72.2 23.1 %collective-permute-start.23 = (bf16[4,96,768]{2,1,0:T(8,128)(2,1)S(1)}, bf16[4,96,768]{2,1,0:T(8,128)(2,1)S(1)}, u32[]{:S(2)}, u32[]{:S(2)}) collective-permute-start(bf16[4,96,768]{2,1,0:T(8,128)(2,1)S(1)} %join.11.refs_1_), channel_id=1, source_target_pairs={{0,4},{4,0},{8,12},{12,8},{16,20},{20,16},{24,28},{28,24},{1,5},{5... | collective-permute-start | bytes 1769480 | tf_op jit(solution)/shard_map/ppermute | solution.py:73
  74.2 6.7 %collective-permute-start.20 = (bf16[128,768]{1,0:T(8,128)(2,1)S(1)}, bf16[128,768]{1,0:T(8,128)(2,1)S(1)}, u32[]{:S(2)}, u32[]{:S(2)}) collective-permute-start(bf16[128,768]{1,0:T(8,128)(2,1)S(1)} %get-tuple-element.130.refs_0_), channel_id=1, source_target_pairs={{0,2},{1,3},{2,0},{3,1},{4,6},{5,7},{6,4},{7,5},{8,10},{9,11},{10,... | collective-permute-start | bytes 589832 | tf_op jit(solution)/shard_map/ppermute | solution.py:73
  75.8 19.5 %collective-permute-start.19 = (bf16[128,768]{1,0:T(8,128)(2,1)S(1)}, bf16[128,768]{1,0:T(8,128)(2,1)S(1)}, u32[]{:S(2)}, u32[]{:S(2)}) collective-permute-start(bf16[128,768]{1,0:T(8,128)(2,1)S(1)} %get-tuple-element.130.refs_0_), channel_id=1, source_target_pairs={{0,1},{1,0},{2,3},{3,2},{4,5},{5,4},{6,7},{7,6},{8,9},{9,8},{10,11... | collective-permute-start | bytes 589832 | tf_op jit(solution)/shard_map/ppermute | solution.py:73
  80.9 14.4 %collective-permute-start.21 = (bf16[128,768]{1,0:T(8,128)(2,1)S(1)}, bf16[128,768]{1,0:T(8,128)(2,1)S(1)}, u32[]{:S(2)}, u32[]{:S(2)}) collective-permute-start(bf16[128,768]{1,0:T(8,128)(2,1)S(1)} %collective-permute-done.20.refs_2_), channel_id=1, source_target_pairs={{0,1},{1,0},{2,3},{3,2},{4,5},{5,4},{6,7},{7,6},{8,9},{9,8},{10,11... | collective-permute-start | bytes 589832 | tf_op jit(solution)/shard_map/ppermute | solution.py:73
  100.3 7.3 %collective-permute-start.25 = (bf16[128,768]{1,0:T(8,128)(2,1)S(1)}, bf16[128,768]{1,0:T(8,128)(2,1)S(1)}, u32[]{:S(2)}, u32[]{:S(2)}) collective-permute-start(bf16[128,768]{1,0:T(8,128)(2,1)S(1)} %get-tuple-element.141), channel_id=1, source_target_pairs={{0,2},{1,3},{2,0},{3,1},{4,6},{5,7},{6,4},{7,5},{8,10},{9,11},{10,... | collective-permute-start | bytes 589832 | tf_op jit(solution)/shard_map/ppermute | solution.py:73
  104.9 16.2 %collective-permute-start.29 = (bf16[4,96,768]{2,1,0:T(8,128)(2,1)S(1)}, bf16[4,96,768]{2,1,0:T(8,128)(2,1)S(1)}, u32[]{:S(2)}, u32[]{:S(2)}) collective-permute-start(bf16[4,96,768]{2,1,0:T(8,128)(2,1)S(1)} %get-tuple-element.150), channel_id=1, source_target_pairs={{0,4},{4,0},{8,12},{12,8},{16,20},{20,16},{24,28},{28,24},{1,5},{5... | collective-permute-start | bytes 1769480 | tf_op jit(solution)/shard_map/ppermute | solution.py:73
  106.4 8.2 %collective-permute-start.27 = (bf16[256,768]{1,0:T(8,128)(2,1)S(1)}, bf16[256,768]{1,0:T(8,128)(2,1)S(1)}, u32[]{:S(2)}, u32[]{:S(2)}) collective-permute-start(bf16[256,768]{1,0:T(8,128)(2,1)S(1)} %get-tuple-element.134.refs_0_), channel_id=1, source_target_pairs={{0,1},{1,0},{2,3},{3,2},{4,5},{5,4},{6,7},{7,6},{8,9},{9,8},{10,11... | collective-permute-start | bytes 1179656 | tf_op jit(solution)/shard_map/ppermute | solution.py:73
  108.1 6.5 %collective-permute-start.26 = (bf16[128,768]{1,0:T(8,128)(2,1)S(1)}, bf16[128,768]{1,0:T(8,128)(2,1)S(1)}, u32[]{:S(2)}, u32[]{:S(2)}) collective-permute-start(bf16[128,768]{1,0:T(8,128)(2,1)S(1)} %get-tuple-element.142.refs_2_), channel_id=1, source_target_pairs={{0,2},{1,3},{2,0},{3,1},{4,6},{5,7},{6,4},{7,5},{8,10},{9,11},{10,... | collective-permute-start | bytes 589832 | tf_op jit(solution)/shard_map/ppermute | solution.py:73
  108.7 24.3 %collective-permute-start.34 = (bf16[4,96,768]{2,1,0:T(8,128)(2,1)S(1)}, bf16[4,96,768]{2,1,0:T(8,128)(2,1)S(1)}, u32[]{:S(2)}, u32[]{:S(2)}) collective-permute-start(bf16[4,96,768]{2,1,0:T(8,128)(2,1)S(1)} %get-tuple-element.160), channel_id=1, source_target_pairs={{0,4},{4,0},{8,12},{12,8},{16,20},{20,16},{24,28},{28,24},{1,5},{5... | collective-permute-start | bytes 1769480 | tf_op jit(solution)/shard_map/ppermute | solution.py:73
  110.2 11.1 %collective-permute-start.30 = (bf16[128,768]{1,0:T(8,128)(2,1)S(1)}, bf16[128,768]{1,0:T(8,128)(2,1)S(1)}, u32[]{:S(2)}, u32[]{:S(2)}) collective-permute-start(bf16[128,768]{1,0:T(8,128)(2,1)S(1)} %get-tuple-element.142.refs_2_), channel_id=1, source_target_pairs={{0,1},{1,0},{2,3},{3,2},{4,5},{5,4},{6,7},{7,6},{8,9},{9,8},{10,11... | collective-permute-start | bytes 589832 | tf_op jit(solution)/shard_map/ppermute | solution.py:73
  114.7 6.6 %collective-permute-start.31 = (bf16[128,768]{1,0:T(8,128)(2,1)S(1)}, bf16[128,768]{1,0:T(8,128)(2,1)S(1)}, u32[]{:S(2)}, u32[]{:S(2)}) collective-permute-start(bf16[128,768]{1,0:T(8,128)(2,1)S(1)} %collective-permute-done.26.refs_0_.refs_4_), channel_id=1, source_target_pairs={{0,1},{1,0},{2,3},{3,2},{4,5},{5,4},{6,7},{7,6},{8,9},{9,8},{10,11... | collective-permute-start | bytes 589832 | tf_op jit(solution)/shard_map/ppermute | solution.py:73
  126.0 9.6 %collective-permute-start.32 = (bf16[256,768]{1,0:T(8,128)(2,1)S(1)}, bf16[256,768]{1,0:T(8,128)(2,1)S(1)}, u32[]{:S(2)}, u32[]{:S(2)}) collective-permute-start(bf16[256,768]{1,0:T(8,128)(2,1)S(1)} %get-tuple-element.154), channel_id=1, source_target_pairs={{0,1},{1,0},{2,3},{3,2},{4,5},{5,4},{6,7},{7,6},{8,9},{9,8},{10,11... | collective-permute-start | bytes 1179656 | tf_op jit(solution)/shard_map/ppermute | solution.py:73
  126.1 9.4 %collective-permute-start.35 = (bf16[2,96,768]{2,1,0:T(8,128)(2,1)S(1)}, bf16[2,96,768]{2,1,0:T(8,128)(2,1)S(1)}, u32[]{:S(2)}, u32[]{:S(2)}) collective-permute-start(bf16[2,96,768]{2,1,0:T(8,128)(2,1)S(1)} %get-tuple-element.151.refs_1_), channel_id=1, source_target_pairs={{0,8},{4,12},{8,0},{12,4},{16,24},{20,28},{24,16},{28,20},{1,9},{5... | collective-permute-start | bytes 884744 | tf_op jit(solution)/shard_map/ppermute | solution.py:73
  126.4 7.0 %collective-permute-start.28 = (bf16[128,768]{1,0:T(8,128)(2,1)S(1)}, bf16[128,768]{1,0:T(8,128)(2,1)S(1)}, u32[]{:S(2)}, u32[]{:S(2)}) collective-permute-start(bf16[128,768]{1,0:T(8,128)(2,1)S(1)} %get-tuple-element.145), channel_id=1, source_target_pairs={{0,2},{1,3},{2,0},{3,1},{4,6},{5,7},{6,4},{7,5},{8,10},{9,11},{10,... | collective-permute-start | bytes 589832 | tf_op jit(solution)/shard_map/ppermute | solution.py:73
  138.6 27.9 %collective-permute-start.36 = (bf16[4,96,768]{2,1,0:T(8,128)(2,1)S(1)}, bf16[4,96,768]{2,1,0:T(8,128)(2,1)S(1)}, u32[]{:S(2)}, u32[]{:S(2)}) collective-permute-start(bf16[4,96,768]{2,1,0:T(8,128)(2,1)S(1)} %get-tuple-element.170), channel_id=1, source_target_pairs={{0,4},{4,0},{8,12},{12,8},{16,20},{20,16},{24,28},{28,24},{1,5},{5... | collective-permute-start | bytes 1769480 | tf_op jit(solution)/shard_map/ppermute | solution.py:73
  140.1 11.5 %collective-permute-start.38 = (bf16[2,96,768]{2,1,0:T(8,128)(2,1)S(1)}, bf16[2,96,768]{2,1,0:T(8,128)(2,1)S(1)}, u32[]{:S(2)}, u32[]{:S(2)}) collective-permute-start(bf16[2,96,768]{2,1,0:T(8,128)(2,1)S(1)} %get-tuple-element.161.refs_3_), channel_id=1, source_target_pairs={{0,8},{4,12},{8,0},{12,4},{16,24},{20,28},{24,16},{28,20},{1,9},{5... | collective-permute-start | bytes 884744 | tf_op jit(solution)/shard_map/ppermute | solution.py:73
  140.4 6.0 %collective-permute-start.33 = (bf16[128,768]{1,0:T(8,128)(2,1)S(1)}, bf16[128,768]{1,0:T(8,128)(2,1)S(1)}, u32[]{:S(2)}, u32[]{:S(2)}) collective-permute-start(bf16[128,768]{1,0:T(8,128)(2,1)S(1)} %get-tuple-element.156), channel_id=1, source_target_pairs={{0,2},{1,3},{2,0},{3,1},{4,6},{5,7},{6,4},{7,5},{8,10},{9,11},{10,... | collective-permute-start | bytes 589832 | tf_op jit(solution)/shard_map/ppermute | solution.py:73
  141.9 18.7 %collective-permute-start.51 = (bf16[96,768]{1,0:T(8,128)(2,1)S(1)}, bf16[96,768]{1,0:T(8,128)(2,1)S(1)}, u32[]{:S(2)}, u32[]{:S(2)}) collective-permute-start(bf16[96,768]{1,0:T(8,128)(2,1)S(1)} %get-tuple-element.163.refs_4_), channel_id=1, source_target_pairs={{0,16},{4,20},{8,24},{12,28},{16,0},{20,4},{24,8},{28,12},{1,17},{... | collective-permute-start | bytes 442376 | tf_op jit(solution)/shard_map/ppermute | solution.py:73
  146.7 4.9 %collective-permute-start.41 = (bf16[16,768]{1,0:T(8,128)(2,1)S(1)}, bf16[16,768]{1,0:T(8,128)(2,1)S(1)}, u32[]{:S(2)}, u32[]{:S(2)}) collective-permute-start(bf16[16,768]{1,0:T(8,128)(2,1)S(1)} %get-tuple-element.176.refs_3_), channel_id=1, source_target_pairs={{0,3},{1,2},{2,1},{3,0},{4,7},{5,6},{6,5},{7,4},{8,11},{9,10},{10,... | collective-permute-start | bytes 73736 | tf_op jit(solution)/shard_map/ppermute | solution.py:73
  146.8 4.9 %collective-permute-start.40 = (bf16[16,768]{1,0:T(8,128)(2,1)S(1)}, bf16[16,768]{1,0:T(8,128)(2,1)S(1)}, u32[]{:S(2)}, u32[]{:S(2)}) collective-permute-start(bf16[16,768]{1,0:T(8,128)(2,1)S(1)} %get-tuple-element.176.refs_3_), channel_id=1, source_target_pairs={{0,2},{1,3},{2,0},{3,1},{4,6},{5,7},{6,4},{7,5},{8,10},{9,11},{10,... | collective-permute-start | bytes 73736 | tf_op jit(solution)/shard_map/ppermute | solution.py:73
  151.6 13.0 %collective-permute-start.52 = (bf16[96,768]{1,0:T(8,128)(2,1)S(1)}, bf16[96,768]{1,0:T(8,128)(2,1)S(1)}, u32[]{:S(2)}, u32[]{:S(2)}) collective-permute-start(bf16[96,768]{1,0:T(8,128)(2,1)S(1)} %get-tuple-element.175.refs_2_), channel_id=1, source_target_pairs={{0,16},{4,20},{8,24},{12,28},{16,0},{20,4},{24,8},{28,12},{1,17},{... | collective-permute-start | bytes 442376 | tf_op jit(solution)/shard_map/ppermute | solution.py:73
  153.6 4.9 %collective-permute-start.42 = (bf16[4,16,768]{2,1,0:T(8,128)(2,1)S(1)}, bf16[4,16,768]{2,1,0:T(8,128)(2,1)S(1)}, u32[]{:S(2)}, u32[]{:S(2)}) collective-permute-start(bf16[4,16,768]{2,1,0:T(8,128)(2,1)S(1)} %get-tuple-element.178), channel_id=1, source_target_pairs={{0,4},{4,0},{8,12},{12,8},{16,20},{20,16},{24,28},{28,24},{1,5},{5... | collective-permute-start | bytes 294920 | tf_op jit(solution)/shard_map/ppermute | solution.py:73
  158.5 8.1 %collective-permute-start.43 = (bf16[2,16,768]{2,1,0:T(8,128)(2,1)S(1)}, bf16[2,16,768]{2,1,0:T(8,128)(2,1)S(1)}, u32[]{:S(2)}, u32[]{:S(2)}) collective-permute-start(bf16[2,16,768]{2,1,0:T(8,128)(2,1)S(1)} %get-tuple-element.180), channel_id=1, source_target_pairs={{0,8},{4,12},{8,0},{12,4},{16,24},{20,28},{24,16},{28,20},{1,9},{5... | collective-permute-start | bytes 147464 | tf_op jit(solution)/shard_map/ppermute | solution.py:73
  159.3 7.3 %collective-permute-start.44 = (bf16[2,16,768]{2,1,0:T(8,128)(2,1)S(1)}, bf16[2,16,768]{2,1,0:T(8,128)(2,1)S(1)}, u32[]{:S(2)}, u32[]{:S(2)}) collective-permute-start(bf16[2,16,768]{2,1,0:T(8,128)(2,1)S(1)} %get-tuple-element.181), channel_id=1, source_target_pairs={{0,16},{4,20},{8,24},{12,28},{16,0},{20,4},{24,8},{28,12},{1,17},{... | collective-permute-start | bytes 147464 | tf_op jit(solution)/shard_map/ppermute | solution.py:73
  160.6 6.0 %collective-permute-start.45 = (bf16[2,16,768]{2,1,0:T(8,128)(2,1)S(1)}, bf16[2,16,768]{2,1,0:T(8,128)(2,1)S(1)}, u32[]{:S(2)}, u32[]{:S(2)}) collective-permute-start(bf16[2,16,768]{2,1,0:T(8,128)(2,1)S(1)} %get-tuple-element.182), channel_id=1, source_target_pairs={{0,24},{4,28},{8,16},{12,20},{16,8},{20,12},{24,0},{28,4},{1,25},{... | collective-permute-start | bytes 147464 | tf_op jit(solution)/shard_map/ppermute | solution.py:73
  166.6 7.5 %collective-permute-start.37 = (bf16[2,96,768]{2,1,0:T(8,128)(2,1)S(1)}, bf16[2,96,768]{2,1,0:T(8,128)(2,1)S(1)}, u32[]{:S(2)}, u32[]{:S(2)}) collective-permute-start(bf16[2,96,768]{2,1,0:T(8,128)(2,1)S(1)} %get-tuple-element.172.refs_0_), channel_id=1, source_target_pairs={{0,8},{4,12},{8,0},{12,4},{16,24},{20,28},{24,16},{28,20},{1,9},{5... | collective-permute-start | bytes 884744 | tf_op jit(solution)/shard_map/ppermute | solution.py:73
  167.7 8.2 %collective-permute-start.46 = (f32[4,8,128]{2,1,0:T(8,128)S(1)}, f32[4,8,128]{2,1,0:T(8,128)S(1)}, u32[]{:S(2)}, u32[]{:S(2)}) collective-permute-start(f32[4,8,128]{2,1,0:T(8,128)S(1)} %get-tuple-element.184), channel_id=1, source_target_pairs={{0,4},{4,0},{8,12},{12,8},{16,20},{20,16},{24,28},{28,24},{1,5},{5... | collective-permute-start | bytes 49160 | tf_op jit(solution)/shard_map/ppermute | solution.py:73
  174.1 10.1 %collective-permute-start.50 = (bf16[96,768]{1,0:T(8,128)(2,1)S(1)}, bf16[96,768]{1,0:T(8,128)(2,1)S(1)}, u32[]{:S(2)}, u32[]{:S(2)}) collective-permute-start(bf16[96,768]{1,0:T(8,128)(2,1)S(1)} %get-tuple-element.173.refs_1_), channel_id=1, source_target_pairs={{0,16},{4,20},{8,24},{12,28},{16,0},{20,4},{24,8},{28,12},{1,17},{... | collective-permute-start | bytes 442376 | tf_op jit(solution)/shard_map/ppermute | solution.py:73
  175.9 5.7 %collective-permute-start.47 = (f32[2,8,128]{2,1,0:T(8,128)S(1)}, f32[2,8,128]{2,1,0:T(8,128)S(1)}, u32[]{:S(2)}, u32[]{:S(2)}) collective-permute-start(f32[2,8,128]{2,1,0:T(8,128)S(1)} %get-tuple-element.186), channel_id=1, source_target_pairs={{0,8},{4,12},{8,0},{12,4},{16,24},{20,28},{24,16},{28,20},{1,9},{5... | collective-permute-start | bytes 24584 | tf_op jit(solution)/shard_map/ppermute | solution.py:73
  177.1 4.9 %collective-permute-start.48 = (f32[2,8,128]{2,1,0:T(8,128)S(1)}, f32[2,8,128]{2,1,0:T(8,128)S(1)}, u32[]{:S(2)}, u32[]{:S(2)}) collective-permute-start(f32[2,8,128]{2,1,0:T(8,128)S(1)} %get-tuple-element.187), channel_id=1, source_target_pairs={{0,16},{4,20},{8,24},{12,28},{16,0},{20,4},{24,8},{28,12},{1,17},{... | collective-permute-start | bytes 24584 | tf_op jit(solution)/shard_map/ppermute | solution.py:73
  178.0 5.4 %collective-permute-start.49 = (f32[2,8,128]{2,1,0:T(8,128)S(1)}, f32[2,8,128]{2,1,0:T(8,128)S(1)}, u32[]{:S(2)}, u32[]{:S(2)}) collective-permute-start(f32[2,8,128]{2,1,0:T(8,128)S(1)} %get-tuple-element.188), channel_id=1, source_target_pairs={{0,24},{4,28},{8,16},{12,20},{16,8},{20,12},{24,0},{28,4},{1,25},{... | collective-permute-start | bytes 24584 | tf_op jit(solution)/shard_map/ppermute | solution.py:73
  (18 other events, 107.0 us)

commit v4 on v3

--- a/solution.py
+++ b/solution.py
@@ -17,33 +17,42 @@
 CUBIC = 0.044715
 
 
-def origin(ndim, step):
-    return (0,) * ndim
-
-
-def call(kernel, name, outs, args, scalars=(), scratch=(), ordered=(), flops=1, blocked=False):
+def call(kernel, name, outs, args, scalars=(), scratch=(), ordered=(), flops=1, fetch=False):
+    space = pltpu.HBM if fetch else pltpu.VMEM
     in_specs = (
         [pl.BlockSpec(memory_space=pltpu.SMEM)] * len(scalars)
         + [pl.BlockSpec(memory_space=pl.ANY)] * len(ordered)
-        + (
-            [pl.BlockSpec(a.shape, functools.partial(origin, a.ndim)) for a in args]
-            if blocked
-            else [pl.BlockSpec(memory_space=pltpu.VMEM)] * len(args)
-        )
+        + [pl.BlockSpec(memory_space=space)] * len(args)
     )
     skip = len(scalars)
+    first = skip + len(ordered)
 
     def body(*refs):
-        kernel(*refs[:skip], *refs[skip + len(ordered) :])
-
-    shapes = [jax.ShapeDtypeStruct(shape, dtype) for shape, dtype in outs]
+        if not fetch:
+            kernel(*refs[:skip], *refs[first:])
+            return
+        *refs, sems = refs
+        held = refs[len(refs) - len(args) :]
+        copies = [
+            pltpu.make_async_copy(source, target, sems.at[i])
+            for i, (source, target) in enumerate(zip(refs[first : first + len(args)], held))
+        ]
+        for copy in copies:
+            copy.start()
+        for copy in copies:
+            copy.wait()
+        kernel(*refs[:skip], *held, *refs[first + len(args) : len(refs) - len(args)])
+
+    extra = []
+    if fetch:
+        extra = [pltpu.VMEM(a.shape, a.dtype) for a in args]
+        extra.append(pltpu.SemaphoreType.DMA((len(args),)))
     return pl.pallas_call(
         body,
-        out_shape=shapes,
-        grid=(1,) if blocked else (),
+        out_shape=[jax.ShapeDtypeStruct(shape, dtype) for shape, dtype in outs],
         in_specs=in_specs,
         out_specs=[pl.BlockSpec(memory_space=pltpu.VMEM)] * len(outs),
-        scratch_shapes=list(scratch),
+        scratch_shapes=[*scratch, *extra],
         compiler_params=pltpu.CompilerParams(vmem_limit_bytes=14 * 1024 * 1024),
         cost_estimate=pl.CostEstimate(flops=int(flops), bytes_accessed=1, transcendentals=0),
         name=name,
@@ -110,20 +119,16 @@
         send[to // 2] = value
 
 
-def pack_kernel(rank, cond, qv, proj, second, hidden, keep, send, scr):
+def pack_kernel(rank, cond, bias, keep, send, scr):
     count = 2 * keep.shape[0]
-    feat = qv.shape[1]
     latents = cond.shape[0]
+    feat = cond.shape[1] // count
     value = cond[...].astype(F32)
     act = (value / (1.0 + jnp.exp(-value))).astype(BF).astype(F32)
-    tail = hidden[...].astype(F32)
-    rows = [qv[...].astype(F32), proj[...].astype(F32), second[...].astype(F32)]
-    rows += [tail[:, r * feat : (r + 1) * feat] for r in range(tail.shape[1] // feat)]
+    row = bias[...].astype(F32).reshape(1, bias.shape[0])
     scr[...] = jnp.zeros_like(scr)
-    at = latents
-    for row in rows:
-        scr[at : at + row.shape[0], 0:feat] = row
-        at += row.shape[0]
+    for r in range(bias.shape[0] // feat):
+        scr[latents + r : latents + r + 1, 0:feat] = row[:, r * feat : (r + 1) * feat]
     for k in range(count):
         scr[0:latents, 0:feat] = act[:, k * feat : (k + 1) * feat]
         put_piece(rank, k, scr[...], keep, send)
@@ -185,9 +190,9 @@
     return call(join_kernel, "join", [(shape, a.dtype)], [a, b], ordered=ordered)[0]
 
 
-def gather_steps(own, ordered=((), ())):
-    two = join(own, swap(own, "fsdp", 4), ordered[0])
-    four = join(two, swap(two, "fsdp", 2), ordered[1])
+def gather_steps(own):
+    two = join(own, swap(own, "fsdp", 4))
+    four = join(two, swap(two, "fsdp", 2))
     return two, four, swap(four, "fsdp", 1)
 
 
@@ -208,9 +213,9 @@
         for k in range(count):
             for l in range(latents):
                 pieces[k, 6 * l + j : 6 * l + j + 1, :] = part[k * latents + l : k * latents + l + 1]
-    for z in range(count // 2):
-        keep[z] = pieces[2 * z].astype(BF)
-        send[z] = pieces[2 * z + 1].astype(BF)
+    for place, z in enumerate((0, 2, 1, 3) if count == 8 else range(count // 2)):
+        keep[place] = pieces[2 * z].astype(BF)
+        send[place] = pieces[2 * z + 1].astype(BF)
 
 
 def bias_kernel(rank, tp_rank, *refs, latents, feat, tp):
@@ -256,6 +261,7 @@
     mod = got[0][...].astype(F32)
     for part in got[1:]:
         mod = mod + part[...].astype(F32)
+    mod = mod.reshape(mod.shape[-2:])
     mod_out[...] = mod[0 : mod_out.shape[0]]
     latents = mod_out.shape[0] // 6
     part = x0.shape[0] // (2 * latents)
@@ -362,28 +368,27 @@
         out[at : at + rows, :] = dot(pre, first[...], (1, 1)).astype(BF)
 
 
-def store_grad(rank, product, keep, send, cols):
+def store_grad(rank, product, keep, send, cols, step):
     rows = keep.shape[1]
-    place = rank[0] // 2
-    for mine in range(2):
-
-        @pl.when(rank[0] % 2 == mine)
-        def _():
-            for z in range(keep.shape[0]):
-                to = jnp.bitwise_xor(place, z)
-                keep[to, :, cols] = product[(2 * z + mine) * rows : (2 * z + mine + 1) * rows]
-                send[to, :, cols] = product[
-                    (2 * z + 1 - mine) * rows : (2 * z + 2 - mine) * rows
-                ]
-
-
-def mlp_grad_kernel(rank, x, g, act, pre, keep_b, send_b, keep_c, send_c, bias_out):
-    hidden = act.shape[1]
-    for left, right, keep, send in ((x, pre, keep_b, send_b), (g, act, keep_c, send_c)):
-        for at in range(0, hidden, 256):
-            product = dot(left[...], right[:, at : at + 256], (0, 0)).astype(BF)
-            store_grad(rank, product, keep, send, slice(at, at + 256))
-    bias_out[...] = jnp.sum(pre[...].astype(F32), axis=0, keepdims=True)
+    for half in range(2):
+
+        @pl.when((rank[0] // step) % 2 == half)
+        def _(half=half):
+            for k in range(2 * keep.shape[0]):
+                to = jnp.bitwise_xor(rank[0], k)
+                if step == 1:
+                    place = (to // 2 % 2) * 2 + to // 4
+                else:
+                    place = (to // 4) * 2 + to % 2
+                target = keep if (k // step) % 2 == half else send
+                target[place, :, cols] = product[k * rows : (k + 1) * rows]
+
+
+def mlp_grad_kernel(rank, left, right, keep, send, *bias_out, step):
+    product = dot(left[...], right[...], (0, 0)).astype(BF)
+    store_grad(rank, product, keep, send, slice(0, right.shape[1]), step)
+    if bias_out:
+        bias_out[0][...] = jnp.sum(right[...].astype(F32), axis=0, keepdims=True)
 
 
 def mlp_out_kernel(act, second, keep, send):
@@ -431,7 +436,7 @@
 
 
 def attn_back_kernel(
-    g0, g1, g2, g3, qkv_w, proj_w, qkv, rows, grads, keep, send, *, latents
+    g0, g1, g2, g3, qkv_w, proj_w, qkv, rows, grads, keep, send, bias_out, *, latents
 ):
     unpack_rows([g0, g1, g2, g3], rows, latents)
     cols = proj_w.shape[1]
@@ -455,17 +460,18 @@
             found[2].append(dot(probs.astype(BF), up, (0, 0)))
         grad = jnp.concatenate(found[0] + found[1] + found[2], axis=1).astype(BF)
         grads[here, :] = grad
+        part = jnp.sum(grad.astype(F32), axis=0, keepdims=True)
+        total = part if l == 0 else total + part
         put_parts(dot(grad, qkv_w[...], (1, 1)).astype(BF), keep, send, l)
-
-
-def attn_grad_kernel(rank, rows, grads, back, att, keep, send, bias_out):
-    cols = att.shape[1]
-    for at in range(0, 3 * cols, cols):
-        product = dot(rows[...], grads[:, at : at + cols], (0, 0)).astype(BF)
-        store_grad(rank, product, keep, send, slice(at, at + cols))
+    bias_out[...] = total
+
+
+def attn_grad_kernel(rank, rows, grads, back, att, keep, send):
+    cut = grads.shape[1]
+    product = dot(rows[...], grads[...], (0, 0)).astype(BF)
+    store_grad(rank, product, keep, send, slice(0, cut), 1)
     product = dot(back[...], att[...], (0, 0)).astype(BF)
-    store_grad(rank, product, keep, send, slice(3 * cols, 4 * cols))
-    bias_out[...] = jnp.sum(grads[...].astype(F32), axis=0, keepdims=True)
+    store_grad(rank, product, keep, send, slice(cut, keep.shape[2]), 1)
 
 
 def input_back_kernel(
@@ -574,46 +580,37 @@
     return lax.psum_scatter(whole, "fsdp", scatter_dimension=0, tiled=False)
 
 
-def halve_four_kernel(keep, got, own, out):
-    for z in range(2):
-        own[z] = keep[2 * z].astype(F32) + got[2 * z].astype(F32)
-        out[z] = (keep[2 * z + 1].astype(F32) + got[2 * z + 1].astype(F32)).astype(BF)
-
-
-def halve_two_kernel(keep, got, own, out):
-    own[...] = keep[0] + got[0].astype(F32)
-    out[...] = (keep[1] + got[1].astype(F32)).astype(BF)
-
-
-def halve_four(keep, send):
-    shape = (2, *keep.shape[1:])
-    got = swap(send, "fsdp", 1)
-    return call(halve_four_kernel, "halve_four", [(shape, F32), (shape, BF)], [keep, got])
-
-
-def halve_two(keep, send, ordered=()):
-    shape = keep.shape[1:]
-    got = swap(send, "fsdp", 2)
+def halve_kernel(keep, got, own, out):
+    half = own.shape[0]
+    for i in range(half):
+        own[i] = keep[i].astype(F32) + got[i].astype(F32)
+        out[i] = (keep[half + i].astype(F32) + got[half + i].astype(F32)).astype(BF)
+
+
+def halve(keep, send, offset, ordered=()):
+    got = swap(send, "fsdp", offset)
+    shape = (keep.shape[0] // 2, *keep.shape[1:])
     outs = [(shape, F32), (shape, BF)]
-    return call(halve_two_kernel, "halve_two", outs, [keep, got], ordered=ordered)
+    return call(halve_kernel, "halve", outs, [keep, got], ordered=ordered)
 
 
 def add_kernel(own, got, out):
     out[...] = own[...] + got[...].astype(F32)
 
 
-def halve_one(own, out):
-    got = swap(out, "fsdp", 4)
-    return call(add_kernel, "last_sum", [(own.shape, F32)], [own, got])[0]
+def last_sum(own, out, offset):
+    got = swap(out, "fsdp", offset)
+    total = call(add_kernel, "last_sum", [(own.shape, F32)], [own, got])[0]
+    return total.reshape(own.shape[1:])
 
 
 def attn_add_kernel(own, got, qkv, proj):
     cols = qkv.shape[2]
     for j in range(3):
         here = slice(j * cols, (j + 1) * cols)
-        qkv[j] = own[:, here] + got[:, here].astype(F32)
+        qkv[j] = own[0, :, here] + got[0, :, here].astype(F32)
     here = slice(3 * cols, 4 * cols)
-    proj[...] = (own[:, here] + got[:, here].astype(F32)).T
+    proj[...] = (own[0, :, here] + got[0, :, here].astype(F32)).T
 
 
 def shards(
@@ -648,23 +645,33 @@
     block = ((rows, width), BF)
     block_f32 = ((rows, width), F32)
 
+    qkv_own = query_key_value_weight.transpose(1, 0, 2)
+    first_ops = []
+    if direct:
+        attn_own = call(
+            attn_own_kernel,
+            "attn_own",
+            [((feat, 4 * cols), BF)],
+            [qkv_own, attention_output_weight],
+            fetch=True,
+        )[0]
+        first_ops = [attn_own]
+        attn_two = join(attn_own, swap(attn_own, "fsdp", 4))
+
     half = count // 2
+    bias_own = jnp.concatenate(
+        [qv_bias.reshape(-1), attention_output_bias, contract_bias, hidden_layer_bias]
+    )
     cond_keep, cond_send = call(
         pack_kernel,
         "pack_conditioning",
         [((half, 16, 128), F32)] * 2,
-        [
-            conditioning,
-            qv_bias,
-            attention_output_bias.reshape(1, feat),
-            contract_bias.reshape(1, feat),
-            hidden_layer_bias.reshape(1, hidden_part),
-        ],
+        [conditioning, bias_own],
         [rank],
         scratch=[pltpu.VMEM((16, 128), F32)],
-        blocked=True,
-    )
-    cond_got = exchange(cond_keep, cond_send)
+        ordered=first_ops,
+    )
+    cond_got = exchange(cond_keep, cond_send, [attn_two] if direct else ())
 
     bias_row = lax.dynamic_update_slice(
         jnp.zeros((1, mod_part * count), F32),
@@ -688,27 +695,16 @@
     )[0]
     x_blocks = tp_gather(x_own)
 
-    qkv_own = query_key_value_weight.transpose(1, 0, 2)
     if direct:
-        attn_own = call(
-            attn_own_kernel,
-            "attn_own",
-            [((feat, 4 * cols), BF)],
-            [qkv_own, attention_output_weight],
-            ordered=[cond_got[0]],
-            blocked=True,
-        )[0]
-        mod_half = halve_four(mod_keep, mod_send)
-        mod_own, mod_out = halve_two(*mod_half)
-        mod_parts = [mod_own, swap(mod_out, "fsdp", 4)]
-        attn_two, attn_four, attn_other = gather_steps(attn_own, ([mod_half[1]], [mod_own]))
+        attn_four = join(attn_two, swap(attn_two, "fsdp", 2), [mod_send])
+        attn_other = swap(attn_four, "fsdp", 1)
         first_own = call(
             copy_kernel,
             "first_own",
             [((feat, hidden), BF)],
             [expand_weight],
             ordered=[attn_four],
-            blocked=True,
+            fetch=True,
         )[0]
         first_two, first_four, first_other = gather_steps(first_own)
         second_own = call(
@@ -716,8 +712,8 @@
             "second_own",
             [((feat, hidden), BF)],
             [contract_weight.T],
-            ordered=[first_two],
-            blocked=True,
+            ordered=[first_four],
+            fetch=True,
         )[0]
         second_two, second_four, second_other = gather_steps(second_own)
         qkv_full, proj_full = call(
@@ -741,7 +737,10 @@
             [second_four, second_other],
             [rank],
         )[0]
-        steps = [[attn_four], [first_two], [first_four, second_two], [second_four]]
+        steps = [[first_four], [], [second_two, first_full], [second_four]]
+        half_one = halve(mod_keep, mod_send, 1)
+        half_two = halve(*half_one, 2, [first_two])
+        mod_parts = [half_two[0], swap(half_two[1], "fsdp", 4)]
     else:
         steps = [[]] * 4
         mod_parts = [scatter_pieces(mod_keep, mod_send)]
@@ -777,13 +776,13 @@
         [attn_rows, qkv_full, proj_full, qkv_bias],
         ordered=steps[1],
     )
-    branch_parts = tp_scatter(keep, send)
+    branch_parts = tp_scatter(keep, send, steps[2])
     grad_rows, fc2_part = call(
         gate_grad_kernel,
         "gate_grad",
         [((tokens, width), BF), ((1, width), F32)],
         [*x_blocks, mod],
-        ordered=[branch_parts[0], *steps[2]],
+        ordered=[branch_parts[0]],
         flops=1e9,
     )
     branch, middle, mlp_in = call(
@@ -800,27 +799,45 @@
         [((tokens, hidden), BF)] * 2 + [((tokens, width), BF), pair, pair],
         [*m_blocks, grad_rows, first_full, second_full, hidden_bias],
     )
+    first_done = []
+    if direct:
+        blocks = [((half, feat, hidden), BF)] * 2
+        first_keep, first_send, fc1_part = call(
+            functools.partial(mlp_grad_kernel, step=1),
+            "first_grad",
+            blocks + [((1, hidden), F32)],
+            [mlp_rows, pre],
+            [rank],
+            ordered=[send],
+            flops=2e9,
+        )
+        first_done = [fc1_part]
+    grad_in = tp_scatter(keep, send, first_done)
     out_keep, out_send = call(
-        mlp_out_kernel, "mlp_out", [pair, pair], [act, second_full], ordered=[send], flops=1.5e9
-    )
-    grad_in = tp_scatter(keep, send, [out_send])
+        mlp_out_kernel,
+        "mlp_out",
+        [pair, pair],
+        [act, second_full],
+        ordered=[grad_in[0]],
+        flops=1.5e9,
+    )
     if direct:
-        first_keep, first_send, second_keep, second_send, fc1_part = call(
-            mlp_grad_kernel,
-            "mlp_weight_grad",
-            [((half, feat, hidden), BF)] * 4 + [((1, hidden), F32)],
-            [mlp_rows, grad_rows, act, pre],
+        second_keep, second_send = call(
+            functools.partial(mlp_grad_kernel, step=2),
+            "second_grad",
+            blocks,
+            [grad_rows, act],
             [rank],
-            ordered=[grad_in[0]],
-            flops=4e9,
+            ordered=[out_send],
+            flops=2e9,
         )
-        first_half = halve_four(first_keep, first_send)
-        first_one = halve_two(*first_half)
-        first_sum = halve_one(*first_one)
-        second_half = halve_four(second_keep, second_send)
-        second_one = halve_two(*second_half)
-        second_sum = halve_one(*second_one)
-        steps = [[first_half[1]], [second_half[1], first_one[1]], [second_one[1]]]
+        first_half = halve(first_keep, first_send, 1)
+        first_one = halve(*first_half, 2)
+        first_sum = last_sum(*first_one, 4)
+        second_half = halve(second_keep, second_send, 2)
+        second_one = halve(*second_half, 4)
+        second_sum = last_sum(*second_one, 1)
+        steps = [[first_half[1]], [second_half[1]], [first_one[1]], [second_one[1]]]
     else:
         first_sum = lax.psum_scatter(
             dot(mlp_rows, pre, (0, 0)), "fsdp", scatter_dimension=0, tiled=True
@@ -829,43 +846,44 @@
             dot(grad_rows, act, (0, 0)), "fsdp", scatter_dimension=0, tiled=True
         )
         fc1_part = jnp.sum(pre.astype(F32), axis=0, keepdims=True)
-        steps = [[]] * 3
+        steps = [[]] * 4
+        second_keep = fc1_part
 
     grad_middle, grad_attn, sums = call(
         middle_back_kernel,
         "middle_back",
         [block_f32, block, ((8, width), F32)],
         [x_own, middle, branch, *grad_in, mod],
-        ordered=[fc1_part] if direct else [],
+        ordered=[second_keep],
     )
     a_blocks = tp_gather(grad_attn)
     mlp_parts = tp_scatter(out_keep, out_send, [a_blocks[2]])
-    back_rows, grads, keep, send = call(
+    back_rows, grads, keep, send, qkv_part = call(
         functools.partial(attn_back_kernel, latents=latents),
         "attention_back",
-        [((tokens, width), BF), ((tokens, 3 * cols), BF), pair, pair],
+        [((tokens, width), BF), ((tokens, 3 * cols), BF), pair, pair, ((1, 3 * cols), F32)],
         [*a_blocks, qkv_full, proj_full, qkv],
         ordered=[mlp_parts[0], *steps[0]],
     )
-    grad_in = tp_scatter(keep, send)
     output, gates = call(
         output_kernel,
         "output",
         [block, ((8, width), F32)],
         [middle, x_own, *mlp_parts, second_bias, mod],
     )
+    grad_in = tp_scatter(keep, send, [*steps[1], gates])
     if direct:
-        attn_keep, attn_send, qkv_part = call(
+        attn_keep, attn_send = call(
             attn_grad_kernel,
             "attn_weight_grad",
-            [((half, feat, 4 * cols), BF)] * 2 + [((1, 3 * cols), F32)],
+            [((half, feat, 4 * cols), BF)] * 2,
             [attn_rows, grads, back_rows, att],
             [rank],
-            ordered=[grad_in[0], gates, *steps[1]],
+            ordered=[grad_in[0]],
             flops=6e9,
         )
-        attn_half = halve_four(attn_keep, attn_send)
-        own, out = halve_two(*attn_half)
+        attn_half = halve(attn_keep, attn_send, 1)
+        own, out = halve(*attn_half, 2)
         tail = [[attn_half[1]], [out]]
         qkv_sum, proj_sum = call(
             attn_add_kernel,
@@ -882,7 +900,6 @@
         proj_sum = lax.psum_scatter(
             dot(back_rows, att, (0, 0)), "fsdp", scatter_dimension=0, tiled=True
         ).T
-        qkv_part = jnp.sum(grads.astype(F32), axis=0, keepdims=True)
 
     inputs_grad, pack = call(
         input_back_kernel,
@@ -890,6 +907,7 @@
         [block_f32, ((16, width), BF)],
         [x_own, grad_middle, *grad_in, mod, sums, gates, fc2_part, fc1_part, qkv_part],
         scratch=[pltpu.VMEM((16, width), F32)],
+        ordered=steps[2],
     )
     packs = [pack] + [swap(pack, "tp", d) for d in range(1, tp_count)]
     spread_keep, spread_send = call(
@@ -899,19 +917,17 @@
         packs,
         [rank, tp_rank],
         scratch=[pltpu.VMEM((tp_count, 16, width), F32), pltpu.VMEM((16, width), F32)],
-        ordered=steps[2],
     )
     silu_keep, silu_send, grad_mod_all, bias_grads = call(
         functools.partial(silu_kernel, latents=latents),
         "silu_columns",
         [((half, 8, 128), F32)] * 2
         + [((count * latents, 6 * width), BF), ((1, width), F32)],
-        [*exchange(spread_keep, spread_send), ada_weight],
+        [*exchange(spread_keep, spread_send, [*steps[3], *tail[0]]), ada_weight],
         scratch=[
             pltpu.VMEM((6, count * latents, width), F32),
             pltpu.VMEM((count, 8, 128), F32),
         ],
-        ordered=tail[0],
     )
     cond_grad = call(
         functools.partial(cond_kernel, latents=latents, feat=feat),

time: 185 us -> 180 us (0.973)
  starting transfers between devices: 54.3 us -> 45.3 us
  Pallas kernels: 28 us -> 30.8 us
    ppermute x53, starting transfers between devices: 54.3 us -> 45.3 us  [swap(): return lax.ppermute(block, axis, [(i, i ^ offset) for i in range(count)])]
    pallas_call x49 -> x50, Pallas kernels: 28 us -> 30.8 us  [call(): pl.pallas_call(body, out_shape=[jax.ShapeDtypeStruct(shape, dtype) for sh...]
    unnamed x26 -> x28, local copies, waits for them, and re-layouts: 5.55 us -> 4.85 us
  transfers between devices with their start and end apart: 53 -> 53, of which waited for: 28 -> 24; matrix products, arithmetic and copies ran while one was open for 4% -> 5% of each run, Pallas kernels for 11% -> 14%
where the time goes in v4:
time: 180 us; the launch traced here: 179 us
  waiting for transfers between devices  87.7 us (49%)
  starting transfers between devices  45.3 us (25%)
  Pallas kernels  30.8 us (17%)
  local copies, waits for them, and re-layouts  9.6 us (5%)
  other arithmetic  3.07 us (2%)
    ppermute x53, waiting for transfers between devices, swap(): return lax.ppermute(block, axis, [(i, i ^ offset) for i in range(count)])  87.7 us
    ppermute x53, starting transfers between devices, swap(): return lax.ppermute(block, axis, [(i, i ^ offset) for i in range(count)])  45.3 us
    pallas_call x50, Pallas kernels, call(): pl.pallas_call(body, out_shape=[jax.ShapeDtypeStruct(shape, dtype) for sh...  30.8 us
    unnamed x28, local copies, waits for them, and re-layouts  4.85 us
  transfers between devices with their start and end apart: 53, of which 24 were waited for; matrix products, arithmetic and copies ran while one was open for 5% of the time, Pallas kernels for 14%

profile of v4, /device:TPU:0, one launch (start us, length us, event | category | flops | bytes accessed | tf_op | source)
XLA Modules:
  0.0 179.2 jit_solution(9379736376812136404)
XLA Ops:
  2.7 4.1 %collective-permute-start = (bf16[96,768]{1,0:T(8,128)(2,1)S(1)}, bf16[96,768]{1,0:T(8,128)(2,1)S(1)}, u32[]{:S(2)}, u32[]{:S(2)}) collective-permute-start(bf16[96,768]{1,0:T(8,128)(2,1)S(1)} %attn_own.1.refs_0_.refs_1_), channel_id=1, source_target_pairs={{0,16},{4,20},{8,24},{12,28},{16,0},{20,4},{24,8},{28,12},{1,17},{... | collective-permute-start | bytes 442376 | tf_op jit(solution)/shard_map/ppermute | solution.py:82
  9.6 1.5 collective-permute-start.1
  11.1 2.8 %collective-permute-done.refs_1_ = bf16[96,768]{1,0:T(8,128)(2,1)S(1)} collective-permute-done((bf16[96,768]{1,0:T(8,128)(2,1)S(1)}, bf16[96,768]{1,0:T(8,128)(2,1)S(1)}, u32[]{:S(2)}, u32[]{:S(2)}) %collective-permute-start) | collective-permute-done | bytes 147488 | tf_op jit(solution)/shard_map/ppermute | solution.py:82
  14.7 1.3 collective-permute-start.2
  16.0 2.2 %collective-permute-start.3 = (f32[2,16,128]{2,1,0:T(8,128)S(1)}, f32[2,16,128]{2,1,0:T(8,128)S(1)}, u32[]{:S(2)}, u32[]{:S(2)}) collective-permute-start(f32[2,16,128]{2,1,0:T(8,128)S(1)} %get-tuple-element.109), channel_id=1, source_target_pairs={{0,16},{4,20},{8,24},{12,28},{16,0},{20,4},{24,8},{28,12},{1,17},{... | collective-permute-start | bytes 49160 | tf_op jit(solution)/shard_map/ppermute | solution.py:82
  18.2 1.4 collective-permute-start.4
  19.6 1.6 pad_maximum_fusion
  21.3 1.6 collective-permute-done.2.refs_1_.refs_4_
  22.8 2.9 %collective-permute-done.4.refs_3_.refs_6_ = f32[2,16,128]{2,1,0:T(8,128)S(1)} collective-permute-done((f32[2,16,128]{2,1,0:T(8,128)S(1)}, f32[2,16,128]{2,1,0:T(8,128)S(1)}, u32[]{:S(2)}, u32[]{:S(2)}) %collective-permute-start.4) | collective-permute-done | bytes 16416 | tf_op jit(solution)/shard_map/ppermute | solution.py:82
  25.7 1.6 collective-permute-start.11
  28.4 1.6 collective-permute-start.16
  30.1 6.5 %collective-permute-done.6.refs_1_ = bf16[96,768]{1,0:T(8,128)(2,1)S(1)} collective-permute-done((bf16[96,768]{1,0:T(8,128)(2,1)S(1)}, bf16[96,768]{1,0:T(8,128)(2,1)S(1)}, u32[]{:S(2)}, u32[]{:S(2)}) %collective-permute-start.6) | collective-permute-done | bytes 147488 | tf_op jit(solution)/shard_map/ppermute | solution.py:82
  37.3 1.6 collective-permute-start.13
  38.9 6.0 %collective-permute-done.7.refs_1_ = bf16[2,96,768]{2,1,0:T(8,128)(2,1)S(1)} collective-permute-done((bf16[2,96,768]{2,1,0:T(8,128)(2,1)S(1)}, bf16[2,96,768]{2,1,0:T(8,128)(2,1)S(1)}, u32[]{:S(2)}, u32[]{:S(2)}) %collective-permute-start.7) | collective-permute-done | bytes 294944 | tf_op jit(solution)/shard_map/ppermute | solution.py:82
  45.0 1.7 collective-permute-start.9
  48.2 4.1 %collective-permute-done.14.refs_2_ = bf16[2,16,768]{2,1,0:T(8,128)(2,1)} collective-permute-done((bf16[2,16,768]{2,1,0:T(8,128)(2,1)}, bf16[2,16,768]{2,1,0:T(8,128)(2,1)}, u32[]{:S(2)}, u32[]{:S(2)}) %collective-permute-start.14) | collective-permute-done | bytes 49184 | tf_op jit(solution)/shard_map/ppermute | solution.py:82
  55.0 2.3 %collective-permute-start.8 = (bf16[96,768]{1,0:T(8,128)(2,1)S(1)}, bf16[96,768]{1,0:T(8,128)(2,1)S(1)}, u32[]{:S(2)}, u32[]{:S(2)}) collective-permute-start(bf16[96,768]{1,0:T(8,128)(2,1)S(1)} %second_own.1.refs_0_), channel_id=1, source_target_pairs={{0,16},{4,20},{8,24},{12,28},{16,0},{20,4},{24,8},{28,12},{1,17},{... | collective-permute-start | bytes 442376 | tf_op jit(solution)/shard_map/ppermute | solution.py:82
  58.3 1.3 collective-permute-done.15.refs_7_
  59.6 1.8 %first_norm.1 = (f32[12,768]{1,0:T(8,128)S(1)}, bf16[512,768]{1,0:T(8,128)(2,1)S(1)}) custom-call(f32[1,768]{1,0:T(1,128)S(1)} %get-tuple-element.112.refs_0_.refs_7_, bf16[4,96,768]{2,1,0:T(8,128)(2,1)S(1)} %join.9.refs_0_.refs_1_, bf16[256,768]{1,0:T(8,128)(2,1)S(1)} %tokens.1.refs_2_.refs_1_, bf16[256,768]{1,0:T(8,128)(2,1)} %collective-permute-done.10.refs_3_.refs_2_, ...), custom_call_target="tpu_custom_call" | custom-call | flops 1 | bytes 1 | tf_op jit(solution)/shard_map/first_norm/pallas_call | solution.py:50
  61.4 1.3 attn_weights.1
  62.8 2.5 %attention.1 = (bf16[512,576]{1,0:T(8,128)(2,1)S(1)}, bf16[512,192]{1,0:T(8,128)(2,1)S(1)}, bf16[256,768]{1,0:T(8,128)(2,1)S(1)}, bf16[256,768]{1,0:T(8,128)(2,1)S(1)}) custom-call(bf16[512,768]{1,0:T(8,128)(2,1)S(1)} %get-tuple-element.118.refs_0_.refs_2_, bf16[768,576]{1,0:T(8,128)(2,1)S(1)} %get-tuple-element.119.refs_1_.refs_6_, ...), custom_call_target="tpu_custom_call" | custom-call | flops 1 | bytes 1 | tf_op jit(solution)/shard_map/attention/pallas_call | solution.py:50
  65.6 1.5 collective-permute-done.17.refs_3_
  67.8 7.1 %collective-permute-done.18.refs_1_ = bf16[2,96,768]{2,1,0:T(8,128)(2,1)S(1)} collective-permute-done((bf16[2,96,768]{2,1,0:T(8,128)(2,1)S(1)}, bf16[2,96,768]{2,1,0:T(8,128)(2,1)S(1)}, u32[]{:S(2)}, u32[]{:S(2)}) %collective-permute-start.18) | collective-permute-done | bytes 294944 | tf_op jit(solution)/shard_map/ppermute | solution.py:82
  75.2 1.4 gate_grad.1
  77.5 5.8 %collective-permute-done.21.refs_2_ = bf16[128,768]{1,0:T(8,128)(2,1)S(1)} collective-permute-done((bf16[128,768]{1,0:T(8,128)(2,1)S(1)}, bf16[128,768]{1,0:T(8,128)(2,1)S(1)}, u32[]{:S(2)}, u32[]{:S(2)}) %collective-permute-start.21) | collective-permute-done | bytes 196640 | tf_op jit(solution)/shard_map/ppermute | solution.py:82
  83.3 6.6 %collective-permute-done.23.refs_2_ = bf16[4,96,768]{2,1,0:T(8,128)(2,1)S(1)} collective-permute-done((bf16[4,96,768]{2,1,0:T(8,128)(2,1)S(1)}, bf16[4,96,768]{2,1,0:T(8,128)(2,1)S(1)}, u32[]{:S(2)}, u32[]{:S(2)}) %collective-permute-start.23) | collective-permute-done | bytes 589856 | tf_op jit(solution)/shard_map/ppermute | solution.py:82
  90.0 3.1 %mlp.1 = (bf16[512,768]{1,0:T(8,128)(2,1)S(1)}, bf16[512,768]{1,0:T(8,128)(2,1)S(1)}, bf16[512,768]{1,0:T(8,128)(2,1)S(1)}, bf16[256,768]{1,0:T(8,128)(2,1)S(1)}, bf16[256,768]{1,0:T(8,128)(2,1)S(1)}) custom-call(bf16[128,768]{1,0:T(8,128)(2,1)S(1)} %get-tuple-element.130.refs_0_, bf16[128,768]{1,0:T(8,128)(2,1)S(1)} %collective-permute-done.20.refs_1_, ...), custom_call_target="tpu_custom_call" | custom-call | flops 1 | bytes 1 | tf_op jit(solution)/shard_map/mlp/pallas_call | solution.py:50
  93.2 1.3 first_grad.1
  95.6 1.6 mlp_out.1
  98.2 3.8 %collective-permute-done.25.refs_5_ = bf16[128,768]{1,0:T(8,128)(2,1)S(1)} collective-permute-done((bf16[128,768]{1,0:T(8,128)(2,1)S(1)}, bf16[128,768]{1,0:T(8,128)(2,1)S(1)}, u32[]{:S(2)}, u32[]{:S(2)}) %collective-permute-start.25) | collective-permute-done | bytes 196640 | tf_op jit(solution)/shard_map/ppermute | solution.py:82
  103.1 5.6 %collective-permute-done.26.refs_0_.refs_4_ = bf16[128,768]{1,0:T(8,128)(2,1)S(1)} collective-permute-done((bf16[128,768]{1,0:T(8,128)(2,1)S(1)}, bf16[128,768]{1,0:T(8,128)(2,1)S(1)}, u32[]{:S(2)}, u32[]{:S(2)}) %collective-permute-start.26) | collective-permute-done | bytes 196640 | tf_op jit(solution)/shard_map/ppermute | solution.py:82
  110.5 4.7 %attention_back.1 = (bf16[512,768]{1,0:T(8,128)(2,1)S(1)}, bf16[512,576]{1,0:T(8,128)(2,1)S(1)}, bf16[256,768]{1,0:T(8,128)(2,1)S(1)}, bf16[256,768]{1,0:T(8,128)(2,1)S(1)}, f32[1,576]{1,0:T(1,128)S(1)}) custom-call(f32[128,768]{1,0:T(8,128)S(1)} %get-tuple-element.145.refs_2_.refs_0_, bf16[2,96,768]{2,1,0:T(8,128)(2,1)S(1)} %get-tuple-element.152.refs_1_, ...), custom_call_target="tpu_custom_call" | custom-call | flops 1 | bytes 1 | tf_op jit(solution)/shard_map/attention_back/pallas_call | solution.py:50
  115.9 8.6 %collective-permute-done.31.refs_1_ = bf16[4,96,768]{2,1,0:T(8,128)(2,1)S(1)} collective-permute-done((bf16[4,96,768]{2,1,0:T(8,128)(2,1)S(1)}, bf16[4,96,768]{2,1,0:T(8,128)(2,1)S(1)}, u32[]{:S(2)}, u32[]{:S(2)}) %collective-permute-start.31) | collective-permute-done | bytes 589856 | tf_op jit(solution)/shard_map/ppermute | solution.py:82
  124.9 1.9 %attn_weight_grad.1 = (bf16[4,96,768]{2,1,0:T(8,128)(2,1)S(1)}, bf16[4,96,768]{2,1,0:T(8,128)(2,1)S(1)}) custom-call(s32[1]{0:T(128)} %bitcast.1.refs_0_, f32[128,768]{1,0:T(8,128)S(1)} %get-tuple-element.161.refs_3_.refs_1_, bf16[512,768]{1,0:T(8,128)(2,1)S(1)} %get-tuple-element.118.refs_0_.refs_2_, bf16[512,576]{1,0:T(8,128)(2,1)S(1)} %get-tuple-element.166.refs_3_, ...), custom_call_target="tpu_custom_call" | custom-call | flops 6000000000 | bytes 1 | tf_op jit(solution)/shard_map/attn_weight_grad/pallas_call | solution.py:50
  126.8 1.8 %collective-permute-start.36 = (bf16[4,96,768]{2,1,0:T(8,128)(2,1)S(1)}, bf16[4,96,768]{2,1,0:T(8,128)(2,1)S(1)}, u32[]{:S(2)}, u32[]{:S(2)}) collective-permute-start(bf16[4,96,768]{2,1,0:T(8,128)(2,1)S(1)} %get-tuple-element.170), channel_id=1, source_target_pairs={{0,4},{4,0},{8,12},{12,8},{16,20},{20,16},{24,28},{28,24},{1,5},{5... | collective-permute-start | bytes 1769480 | tf_op jit(solution)/shard_map/ppermute | solution.py:82
  129.1 1.6 collective-permute-start.38
  131.3 11.0 %collective-permute-done.30.refs_1_ = bf16[2,96,768]{2,1,0:T(8,128)(2,1)S(1)} collective-permute-done((bf16[2,96,768]{2,1,0:T(8,128)(2,1)S(1)}, bf16[2,96,768]{2,1,0:T(8,128)(2,1)S(1)}, u32[]{:S(2)}, u32[]{:S(2)}) %collective-permute-start.30) | collective-permute-done | bytes 294944 | tf_op jit(solution)/shard_map/ppermute | solution.py:82
  143.4 1.3 collective-permute-start.39
  148.4 1.3 collective-permute-start.52
  149.8 3.6 %collective-permute-done.42.refs_3_ = bf16[4,16,768]{2,1,0:T(8,128)(2,1)S(1)} collective-permute-done((bf16[4,16,768]{2,1,0:T(8,128)(2,1)S(1)}, bf16[4,16,768]{2,1,0:T(8,128)(2,1)S(1)}, u32[]{:S(2)}, u32[]{:S(2)}) %collective-permute-start.42) | collective-permute-done | bytes 98336 | tf_op jit(solution)/shard_map/ppermute | solution.py:82
  154.3 2.0 %collective-permute-start.44 = (bf16[2,16,768]{2,1,0:T(8,128)(2,1)S(1)}, bf16[2,16,768]{2,1,0:T(8,128)(2,1)S(1)}, u32[]{:S(2)}, u32[]{:S(2)}) collective-permute-start(bf16[2,16,768]{2,1,0:T(8,128)(2,1)S(1)} %get-tuple-element.181), channel_id=1, source_target_pairs={{0,16},{4,20},{8,24},{12,28},{16,0},{20,4},{24,8},{28,12},{1,17},{... | collective-permute-start | bytes 147464 | tf_op jit(solution)/shard_map/ppermute | solution.py:82
  156.3 1.6 collective-permute-start.45
  161.3 1.4 collective-permute-done.45.refs_3_
  163.6 1.6 fusion
  165.3 3.2 %collective-permute-done.37.refs_1_ = bf16[2,96,768]{2,1,0:T(8,128)(2,1)S(1)} collective-permute-done((bf16[2,96,768]{2,1,0:T(8,128)(2,1)S(1)}, bf16[2,96,768]{2,1,0:T(8,128)(2,1)S(1)}, u32[]{:S(2)}, u32[]{:S(2)}) %collective-permute-start.37) | collective-permute-done | bytes 294944 | tf_op jit(solution)/shard_map/ppermute | solution.py:82
  170.3 1.4 collective-permute-start.47
  172.2 2.5 %collective-permute-start.49 = (f32[2,8,128]{2,1,0:T(8,128)S(1)}, f32[2,8,128]{2,1,0:T(8,128)S(1)}, u32[]{:S(2)}, u32[]{:S(2)}) collective-permute-start(f32[2,8,128]{2,1,0:T(8,128)S(1)} %get-tuple-element.188), channel_id=1, source_target_pairs={{0,24},{4,28},{8,16},{12,20},{16,8},{20,12},{24,0},{28,4},{1,25},{... | collective-permute-start | bytes 24584 | tf_op jit(solution)/shard_map/ppermute | solution.py:82
  176.3 1.3 collective-permute-done.49.refs_5_
  (151 shorter events, 37.7 us)
Async XLA Ops:
  2.7 11.1 %collective-permute-start = (bf16[96,768]{1,0:T(8,128)(2,1)S(1)}, bf16[96,768]{1,0:T(8,128)(2,1)S(1)}, u32[]{:S(2)}, u32[]{:S(2)}) collective-permute-start(bf16[96,768]{1,0:T(8,128)(2,1)S(1)} %attn_own.1.refs_0_.refs_1_), channel_id=1, source_target_pairs={{0,16},{4,20},{8,24},{12,28},{16,0},{20,4},{24,8},{28,12},{1,17},{... | collective-permute-start | bytes 442376 | tf_op jit(solution)/shard_map/ppermute | solution.py:82
  9.6 5.1 %collective-permute-start.1 = (f32[4,16,128]{2,1,0:T(8,128)S(1)}, f32[4,16,128]{2,1,0:T(8,128)S(1)}, u32[]{:S(2)}, u32[]{:S(2)}) collective-permute-start(f32[4,16,128]{2,1,0:T(8,128)S(1)} %get-tuple-element.106), channel_id=1, source_target_pairs={{0,4},{4,0},{8,12},{12,8},{16,20},{20,16},{24,28},{28,24},{1,5},{5... | collective-permute-start | bytes 98312 | tf_op jit(solution)/shard_map/ppermute | solution.py:82
  13.9 14.0 %collective-permute-start.5 = (bf16[2,96,768]{2,1,0:T(8,128)(2,1)S(1)}, bf16[2,96,768]{2,1,0:T(8,128)(2,1)S(1)}, u32[]{:S(2)}, u32[]{:S(2)}) collective-permute-start(bf16[2,96,768]{2,1,0:T(8,128)(2,1)S(1)} %join.6.refs_0_.refs_1_), channel_id=1, source_target_pairs={{0,8},{4,12},{8,0},{12,4},{16,24},{20,28},{24,16},{28,20},{1,9},{5... | collective-permute-start | bytes 884744 | tf_op jit(solution)/shard_map/ppermute | solution.py:82
  14.7 8.1 %collective-permute-start.2 = (f32[2,16,128]{2,1,0:T(8,128)S(1)}, f32[2,16,128]{2,1,0:T(8,128)S(1)}, u32[]{:S(2)}, u32[]{:S(2)}) collective-permute-start(f32[2,16,128]{2,1,0:T(8,128)S(1)} %get-tuple-element.108), channel_id=1, source_target_pairs={{0,8},{4,12},{8,0},{12,4},{16,24},{20,28},{24,16},{28,20},{1,9},{5... | collective-permute-start | bytes 49160 | tf_op jit(solution)/shard_map/ppermute | solution.py:82
  16.0 6.8 %collective-permute-start.3 = (f32[2,16,128]{2,1,0:T(8,128)S(1)}, f32[2,16,128]{2,1,0:T(8,128)S(1)}, u32[]{:S(2)}, u32[]{:S(2)}) collective-permute-start(f32[2,16,128]{2,1,0:T(8,128)S(1)} %get-tuple-element.109), channel_id=1, source_target_pairs={{0,16},{4,20},{8,24},{12,28},{16,0},{20,4},{24,8},{28,12},{1,17},{... | collective-permute-start | bytes 49160 | tf_op jit(solution)/shard_map/ppermute | solution.py:82
  18.2 7.5 %collective-permute-start.4 = (f32[2,16,128]{2,1,0:T(8,128)S(1)}, f32[2,16,128]{2,1,0:T(8,128)S(1)}, u32[]{:S(2)}, u32[]{:S(2)}) collective-permute-start(f32[2,16,128]{2,1,0:T(8,128)S(1)} %get-tuple-element.110), channel_id=1, source_target_pairs={{0,24},{4,28},{8,16},{12,20},{16,8},{20,12},{24,0},{28,4},{1,25},{... | collective-permute-start | bytes 49160 | tf_op jit(solution)/shard_map/ppermute | solution.py:82
  25.7 11.0 %collective-permute-start.11 = (bf16[256,768]{1,0:T(8,128)(2,1)S(1)}, bf16[256,768]{1,0:T(8,128)(2,1)}, u32[]{:S(2)}, u32[]{:S(2)}) collective-permute-start(bf16[256,768]{1,0:T(8,128)(2,1)S(1)} %tokens.1.refs_2_.refs_1_), channel_id=1, source_target_pairs={{0,2},{1,3},{2,0},{3,1},{4,6},{5,7},{6,4},{7,5},{8,10},{9,11},{10,... | collective-permute-start | bytes 1179656 | tf_op jit(solution)/shard_map/ppermute | solution.py:82
  28.2 8.4 %collective-permute-start.6 = (bf16[96,768]{1,0:T(8,128)(2,1)S(1)}, bf16[96,768]{1,0:T(8,128)(2,1)S(1)}, u32[]{:S(2)}, u32[]{:S(2)}) collective-permute-start(bf16[96,768]{1,0:T(8,128)(2,1)S(1)} %first_own.1.refs_0_), channel_id=1, source_target_pairs={{0,16},{4,20},{8,24},{12,28},{16,0},{20,4},{24,8},{28,12},{1,17},{... | collective-permute-start | bytes 442376 | tf_op jit(solution)/shard_map/ppermute | solution.py:82
  28.4 33.0 %collective-permute-start.16 = (bf16[4,96,768]{2,1,0:T(8,128)(2,1)S(1)}, bf16[4,96,768]{2,1,0:T(8,128)(2,1)}, u32[]{:S(2)}, u32[]{:S(2)}) collective-permute-start(bf16[4,96,768]{2,1,0:T(8,128)(2,1)S(1)} %join.7.refs_0_.refs_1_), channel_id=1, source_target_pairs={{0,4},{4,0},{8,12},{12,8},{16,20},{20,16},{24,28},{28,24},{1,5},{5... | collective-permute-start | bytes 1769480 | tf_op jit(solution)/shard_map/ppermute | solution.py:82
  36.6 8.3 %collective-permute-start.7 = (bf16[2,96,768]{2,1,0:T(8,128)(2,1)S(1)}, bf16[2,96,768]{2,1,0:T(8,128)(2,1)S(1)}, u32[]{:S(2)}, u32[]{:S(2)}) collective-permute-start(bf16[2,96,768]{2,1,0:T(8,128)(2,1)S(1)} %join.8.refs_0_), channel_id=1, source_target_pairs={{0,8},{4,12},{8,0},{12,4},{16,24},{20,28},{24,16},{28,20},{1,9},{5... | collective-permute-start | bytes 884744 | tf_op jit(solution)/shard_map/ppermute | solution.py:82
  36.7 18.3 %collective-permute-start.10 = (bf16[256,768]{1,0:T(8,128)(2,1)S(1)}, bf16[256,768]{1,0:T(8,128)(2,1)}, u32[]{:S(2)}, u32[]{:S(2)}) collective-permute-start(bf16[256,768]{1,0:T(8,128)(2,1)S(1)} %tokens.1.refs_2_.refs_1_), channel_id=1, source_target_pairs={{0,1},{1,0},{2,3},{3,2},{4,5},{5,4},{6,7},{7,6},{8,9},{9,8},{10,11... | collective-permute-start | bytes 1179656 | tf_op jit(solution)/shard_map/ppermute | solution.py:82
  36.8 22.8 %collective-permute-start.12 = (bf16[256,768]{1,0:T(8,128)(2,1)}, bf16[256,768]{1,0:T(8,128)(2,1)}, u32[]{:S(2)}, u32[]{:S(2)}) collective-permute-start(bf16[256,768]{1,0:T(8,128)(2,1)} %collective-permute-done.11.refs_4_.refs_3_), channel_id=1, source_target_pairs={{0,1},{1,0},{2,3},{3,2},{4,5},{5,4},{6,7},{7,6},{8,9},{9,8},{10,11... | collective-permute-start | bytes 1179656 | tf_op jit(solution)/shard_map/ppermute | solution.py:82
  37.3 9.4 %collective-permute-start.13 = (bf16[4,16,768]{2,1,0:T(8,128)(2,1)S(1)}, bf16[4,16,768]{2,1,0:T(8,128)(2,1)S(1)}, u32[]{:S(2)}, u32[]{:S(2)}) collective-permute-start(bf16[4,16,768]{2,1,0:T(8,128)(2,1)S(1)} %get-tuple-element.111.refs_0_.refs_2_), channel_id=1, source_target_pairs={{0,4},{4,0},{8,12},{12,8},{16,20},{20,16},{24,28},{28,24},{1,5},{5... | collective-permute-start | bytes 294920 | tf_op jit(solution)/shard_map/ppermute | solution.py:82
  45.0 20.5 %collective-permute-start.9 = (bf16[4,96,768]{2,1,0:T(8,128)(2,1)S(1)}, bf16[4,96,768]{2,1,0:T(8,128)(2,1)S(1)}, u32[]{:S(2)}, u32[]{:S(2)}) collective-permute-start(bf16[4,96,768]{2,1,0:T(8,128)(2,1)S(1)} %join.9.refs_0_.refs_1_), channel_id=1, source_target_pairs={{0,4},{4,0},{8,12},{12,8},{16,20},{20,16},{24,28},{28,24},{1,5},{5... | collective-permute-start | bytes 1769480 | tf_op jit(solution)/shard_map/ppermute | solution.py:82
  47.9 4.4 %collective-permute-start.14 = (bf16[2,16,768]{2,1,0:T(8,128)(2,1)}, bf16[2,16,768]{2,1,0:T(8,128)(2,1)}, u32[]{:S(2)}, u32[]{:S(2)}) collective-permute-start(bf16[2,16,768]{2,1,0:T(8,128)(2,1)} %get-tuple-element.115), channel_id=1, source_target_pairs={{0,8},{4,12},{8,0},{12,4},{16,24},{20,28},{24,16},{28,20},{1,9},{5... | collective-permute-start | bytes 147464 | tf_op jit(solution)/shard_map/ppermute | solution.py:82
  54.1 5.6 %collective-permute-start.15 = (bf16[1,16,768]{2,1,0:T(8,128)(2,1)S(1)}, bf16[1,16,768]{2,1,0:T(8,128)(2,1)S(1)}, u32[]{:S(2)}, u32[]{:S(2)}) collective-permute-start(bf16[1,16,768]{2,1,0:T(8,128)(2,1)S(1)} %get-tuple-element.117), channel_id=1, source_target_pairs={{0,16},{4,20},{8,24},{12,28},{16,0},{20,4},{24,8},{28,12},{1,17},{... | collective-permute-start | bytes 73736 | tf_op jit(solution)/shard_map/ppermute | solution.py:82
  55.0 10.3 %collective-permute-start.8 = (bf16[96,768]{1,0:T(8,128)(2,1)S(1)}, bf16[96,768]{1,0:T(8,128)(2,1)S(1)}, u32[]{:S(2)}, u32[]{:S(2)}) collective-permute-start(bf16[96,768]{1,0:T(8,128)(2,1)S(1)} %second_own.1.refs_0_), channel_id=1, source_target_pairs={{0,16},{4,20},{8,24},{12,28},{16,0},{20,4},{24,8},{28,12},{1,17},{... | collective-permute-start | bytes 442376 | tf_op jit(solution)/shard_map/ppermute | solution.py:82
  65.4 9.5 %collective-permute-start.18 = (bf16[2,96,768]{2,1,0:T(8,128)(2,1)S(1)}, bf16[2,96,768]{2,1,0:T(8,128)(2,1)S(1)}, u32[]{:S(2)}, u32[]{:S(2)}) collective-permute-start(bf16[2,96,768]{2,1,0:T(8,128)(2,1)S(1)} %join.10.refs_0_), channel_id=1, source_target_pairs={{0,8},{4,12},{8,0},{12,4},{16,24},{20,28},{24,16},{28,20},{1,9},{5... | collective-permute-start | bytes 884744 | tf_op jit(solution)/shard_map/ppermute | solution.py:82
  67.2 9.4 %collective-permute-start.19 = (bf16[128,768]{1,0:T(8,128)(2,1)S(1)}, bf16[128,768]{1,0:T(8,128)(2,1)S(1)}, u32[]{:S(2)}, u32[]{:S(2)}) collective-permute-start(bf16[128,768]{1,0:T(8,128)(2,1)S(1)} %get-tuple-element.127), channel_id=1, source_target_pairs={{0,2},{1,3},{2,0},{3,1},{4,6},{5,7},{6,4},{7,5},{8,10},{9,11},{10,... | collective-permute-start | bytes 589832 | tf_op jit(solution)/shard_map/ppermute | solution.py:82
  74.9 15.0 %collective-permute-start.23 = (bf16[4,96,768]{2,1,0:T(8,128)(2,1)S(1)}, bf16[4,96,768]{2,1,0:T(8,128)(2,1)S(1)}, u32[]{:S(2)}, u32[]{:S(2)}) collective-permute-start(bf16[4,96,768]{2,1,0:T(8,128)(2,1)S(1)} %join.11.refs_1_), channel_id=1, source_target_pairs={{0,4},{4,0},{8,12},{12,8},{16,20},{20,16},{24,28},{28,24},{1,5},{5... | collective-permute-start | bytes 1769480 | tf_op jit(solution)/shard_map/ppermute | solution.py:82
  76.9 6.4 %collective-permute-start.21 = (bf16[128,768]{1,0:T(8,128)(2,1)S(1)}, bf16[128,768]{1,0:T(8,128)(2,1)S(1)}, u32[]{:S(2)}, u32[]{:S(2)}) collective-permute-start(bf16[128,768]{1,0:T(8,128)(2,1)S(1)} %get-tuple-element.130.refs_0_), channel_id=1, source_target_pairs={{0,2},{1,3},{2,0},{3,1},{4,6},{5,7},{6,4},{7,5},{8,10},{9,11},{10,... | collective-permute-start | bytes 589832 | tf_op jit(solution)/shard_map/ppermute | solution.py:82
  77.5 12.5 %collective-permute-start.20 = (bf16[128,768]{1,0:T(8,128)(2,1)S(1)}, bf16[128,768]{1,0:T(8,128)(2,1)S(1)}, u32[]{:S(2)}, u32[]{:S(2)}) collective-permute-start(bf16[128,768]{1,0:T(8,128)(2,1)S(1)} %get-tuple-element.130.refs_0_), channel_id=1, source_target_pairs={{0,1},{1,0},{2,3},{3,2},{4,5},{5,4},{6,7},{7,6},{8,9},{9,8},{10,11... | collective-permute-start | bytes 589832 | tf_op jit(solution)/shard_map/ppermute | solution.py:82
  83.3 6.7 %collective-permute-start.22 = (bf16[128,768]{1,0:T(8,128)(2,1)S(1)}, bf16[128,768]{1,0:T(8,128)(2,1)S(1)}, u32[]{:S(2)}, u32[]{:S(2)}) collective-permute-start(bf16[128,768]{1,0:T(8,128)(2,1)S(1)} %collective-permute-done.21.refs_2_), channel_id=1, source_target_pairs={{0,1},{1,0},{2,3},{3,2},{4,5},{5,4},{6,7},{7,6},{8,9},{9,8},{10,11... | collective-permute-start | bytes 589832 | tf_op jit(solution)/shard_map/ppermute | solution.py:82
  94.5 15.8 %collective-permute-start.29 = (bf16[4,96,768]{2,1,0:T(8,128)(2,1)S(1)}, bf16[4,96,768]{2,1,0:T(8,128)(2,1)S(1)}, u32[]{:S(2)}, u32[]{:S(2)}) collective-permute-start(bf16[4,96,768]{2,1,0:T(8,128)(2,1)S(1)} %get-tuple-element.150), channel_id=1, source_target_pairs={{0,4},{4,0},{8,12},{12,8},{16,20},{20,16},{24,28},{28,24},{1,5},{5... | collective-permute-start | bytes 1769480 | tf_op jit(solution)/shard_map/ppermute | solution.py:82
  95.0 7.0 %collective-permute-start.25 = (bf16[128,768]{1,0:T(8,128)(2,1)S(1)}, bf16[128,768]{1,0:T(8,128)(2,1)S(1)}, u32[]{:S(2)}, u32[]{:S(2)}) collective-permute-start(bf16[128,768]{1,0:T(8,128)(2,1)S(1)} %get-tuple-element.142), channel_id=1, source_target_pairs={{0,2},{1,3},{2,0},{3,1},{4,6},{5,7},{6,4},{7,5},{8,10},{9,11},{10,... | collective-permute-start | bytes 589832 | tf_op jit(solution)/shard_map/ppermute | solution.py:82
  97.2 13.2 %collective-permute-start.27 = (bf16[256,768]{1,0:T(8,128)(2,1)S(1)}, bf16[256,768]{1,0:T(8,128)(2,1)S(1)}, u32[]{:S(2)}, u32[]{:S(2)}) collective-permute-start(bf16[256,768]{1,0:T(8,128)(2,1)S(1)} %get-tuple-element.139.refs_1_), channel_id=1, source_target_pairs={{0,1},{1,0},{2,3},{3,2},{4,5},{5,4},{6,7},{7,6},{8,9},{9,8},{10,11... | collective-permute-start | bytes 1179656 | tf_op jit(solution)/shard_map/ppermute | solution.py:82
  102.5 6.2 %collective-permute-start.26 = (bf16[128,768]{1,0:T(8,128)(2,1)S(1)}, bf16[128,768]{1,0:T(8,128)(2,1)S(1)}, u32[]{:S(2)}, u32[]{:S(2)}) collective-permute-start(bf16[128,768]{1,0:T(8,128)(2,1)S(1)} %get-tuple-element.143.refs_2_), channel_id=1, source_target_pairs={{0,2},{1,3},{2,0},{3,1},{4,6},{5,7},{6,4},{7,5},{8,10},{9,11},{10,... | collective-permute-start | bytes 589832 | tf_op jit(solution)/shard_map/ppermute | solution.py:82
  103.1 7.4 %collective-permute-start.32 = (bf16[128,768]{1,0:T(8,128)(2,1)S(1)}, bf16[128,768]{1,0:T(8,128)(2,1)S(1)}, u32[]{:S(2)}, u32[]{:S(2)}) collective-permute-start(bf16[128,768]{1,0:T(8,128)(2,1)S(1)} %get-tuple-element.143.refs_2_), channel_id=1, source_target_pairs={{0,1},{1,0},{2,3},{3,2},{4,5},{5,4},{6,7},{7,6},{8,9},{9,8},{10,11... | collective-permute-start | bytes 589832 | tf_op jit(solution)/shard_map/ppermute | solution.py:82
  108.8 15.7 %collective-permute-start.31 = (bf16[4,96,768]{2,1,0:T(8,128)(2,1)S(1)}, bf16[4,96,768]{2,1,0:T(8,128)(2,1)S(1)}, u32[]{:S(2)}, u32[]{:S(2)}) collective-permute-start(bf16[4,96,768]{2,1,0:T(8,128)(2,1)S(1)} %get-tuple-element.155), channel_id=1, source_target_pairs={{0,8},{4,12},{8,0},{12,4},{16,24},{20,28},{24,16},{28,20},{1,9},{5... | collective-permute-start | bytes 1769480 | tf_op jit(solution)/shard_map/ppermute | solution.py:82
  115.2 9.5 %collective-permute-start.34 = (bf16[256,768]{1,0:T(8,128)(2,1)S(1)}, bf16[256,768]{1,0:T(8,128)(2,1)S(1)}, u32[]{:S(2)}, u32[]{:S(2)}) collective-permute-start(bf16[256,768]{1,0:T(8,128)(2,1)S(1)} %get-tuple-element.160), channel_id=1, source_target_pairs={{0,1},{1,0},{2,3},{3,2},{4,5},{5,4},{6,7},{7,6},{8,9},{9,8},{10,11... | collective-permute-start | bytes 1179656 | tf_op jit(solution)/shard_map/ppermute | solution.py:82
  115.3 9.3 %collective-permute-start.28 = (bf16[128,768]{1,0:T(8,128)(2,1)S(1)}, bf16[128,768]{1,0:T(8,128)(2,1)S(1)}, u32[]{:S(2)}, u32[]{:S(2)}) collective-permute-start(bf16[128,768]{1,0:T(8,128)(2,1)S(1)} %get-tuple-element.146), channel_id=1, source_target_pairs={{0,2},{1,3},{2,0},{3,1},{4,6},{5,7},{6,4},{7,5},{8,10},{9,11},{10,... | collective-permute-start | bytes 589832 | tf_op jit(solution)/shard_map/ppermute | solution.py:82
  126.8 22.9 %collective-permute-start.36 = (bf16[4,96,768]{2,1,0:T(8,128)(2,1)S(1)}, bf16[4,96,768]{2,1,0:T(8,128)(2,1)S(1)}, u32[]{:S(2)}, u32[]{:S(2)}) collective-permute-start(bf16[4,96,768]{2,1,0:T(8,128)(2,1)S(1)} %get-tuple-element.170), channel_id=1, source_target_pairs={{0,4},{4,0},{8,12},{12,8},{16,20},{20,16},{24,28},{28,24},{1,5},{5... | collective-permute-start | bytes 1769480 | tf_op jit(solution)/shard_map/ppermute | solution.py:82
  128.6 13.7 %collective-permute-start.30 = (bf16[2,96,768]{2,1,0:T(8,128)(2,1)S(1)}, bf16[2,96,768]{2,1,0:T(8,128)(2,1)S(1)}, u32[]{:S(2)}, u32[]{:S(2)}) collective-permute-start(bf16[2,96,768]{2,1,0:T(8,128)(2,1)S(1)} %get-tuple-element.152.refs_1_), channel_id=1, source_target_pairs={{0,8},{4,12},{8,0},{12,4},{16,24},{20,28},{24,16},{28,20},{1,9},{5... | collective-permute-start | bytes 884744 | tf_op jit(solution)/shard_map/ppermute | solution.py:82
  129.1 15.6 %collective-permute-start.38 = (bf16[2,96,768]{2,1,0:T(8,128)(2,1)S(1)}, bf16[2,96,768]{2,1,0:T(8,128)(2,1)S(1)}, u32[]{:S(2)}, u32[]{:S(2)}) collective-permute-start(bf16[2,96,768]{2,1,0:T(8,128)(2,1)S(1)} %get-tuple-element.156.refs_0_), channel_id=1, source_target_pairs={{0,16},{4,20},{8,24},{12,28},{16,0},{20,4},{24,8},{28,12},{1,17},{... | collective-permute-start | bytes 884744 | tf_op jit(solution)/shard_map/ppermute | solution.py:82
  130.8 11.6 %collective-permute-start.35 = (bf16[128,768]{1,0:T(8,128)(2,1)S(1)}, bf16[128,768]{1,0:T(8,128)(2,1)S(1)}, u32[]{:S(2)}, u32[]{:S(2)}) collective-permute-start(bf16[128,768]{1,0:T(8,128)(2,1)S(1)} %get-tuple-element.162), channel_id=1, source_target_pairs={{0,2},{1,3},{2,0},{3,1},{4,6},{5,7},{6,4},{7,5},{8,10},{9,11},{10,... | collective-permute-start | bytes 589832 | tf_op jit(solution)/shard_map/ppermute | solution.py:82
  142.9 3.9 %collective-permute-start.40 = (bf16[16,768]{1,0:T(8,128)(2,1)S(1)}, bf16[16,768]{1,0:T(8,128)(2,1)S(1)}, u32[]{:S(2)}, u32[]{:S(2)}) collective-permute-start(bf16[16,768]{1,0:T(8,128)(2,1)S(1)} %get-tuple-element.176.refs_2_), channel_id=1, source_target_pairs={{0,2},{1,3},{2,0},{3,1},{4,6},{5,7},{6,4},{7,5},{8,10},{9,11},{10,... | collective-permute-start | bytes 73736 | tf_op jit(solution)/shard_map/ppermute | solution.py:82
  144.7 14.0 %collective-permute-start.51 = (bf16[1,96,768]{2,1,0:T(8,128)(2,1)S(1)}, bf16[1,96,768]{2,1,0:T(8,128)(2,1)S(1)}, u32[]{:S(2)}, u32[]{:S(2)}) collective-permute-start(bf16[1,96,768]{2,1,0:T(8,128)(2,1)S(1)} %get-tuple-element.153.refs_0_), channel_id=1, source_target_pairs={{0,16},{4,20},{8,24},{12,28},{16,0},{20,4},{24,8},{28,12},{1,17},{... | collective-permute-start | bytes 442376 | tf_op jit(solution)/shard_map/ppermute | solution.py:82
  147.6 5.8 %collective-permute-start.42 = (bf16[4,16,768]{2,1,0:T(8,128)(2,1)S(1)}, bf16[4,16,768]{2,1,0:T(8,128)(2,1)S(1)}, u32[]{:S(2)}, u32[]{:S(2)}) collective-permute-start(bf16[4,16,768]{2,1,0:T(8,128)(2,1)S(1)} %get-tuple-element.178), channel_id=1, source_target_pairs={{0,4},{4,0},{8,12},{12,8},{16,20},{20,16},{24,28},{28,24},{1,5},{5... | collective-permute-start | bytes 294920 | tf_op jit(solution)/shard_map/ppermute | solution.py:82
  148.4 11.1 %collective-permute-start.52 = (bf16[1,96,768]{2,1,0:T(8,128)(2,1)S(1)}, bf16[1,96,768]{2,1,0:T(8,128)(2,1)S(1)}, u32[]{:S(2)}, u32[]{:S(2)}) collective-permute-start(bf16[1,96,768]{2,1,0:T(8,128)(2,1)S(1)} %get-tuple-element.175.refs_0_), channel_id=1, source_target_pairs={{0,4},{4,0},{8,12},{12,8},{16,20},{20,16},{24,28},{28,24},{1,5},{5... | collective-permute-start | bytes 442376 | tf_op jit(solution)/shard_map/ppermute | solution.py:82
  153.4 7.9 %collective-permute-start.43 = (bf16[2,16,768]{2,1,0:T(8,128)(2,1)S(1)}, bf16[2,16,768]{2,1,0:T(8,128)(2,1)S(1)}, u32[]{:S(2)}, u32[]{:S(2)}) collective-permute-start(bf16[2,16,768]{2,1,0:T(8,128)(2,1)S(1)} %get-tuple-element.180), channel_id=1, source_target_pairs={{0,8},{4,12},{8,0},{12,4},{16,24},{20,28},{24,16},{28,20},{1,9},{5... | collective-permute-start | bytes 147464 | tf_op jit(solution)/shard_map/ppermute | solution.py:82
  154.3 7.0 %collective-permute-start.44 = (bf16[2,16,768]{2,1,0:T(8,128)(2,1)S(1)}, bf16[2,16,768]{2,1,0:T(8,128)(2,1)S(1)}, u32[]{:S(2)}, u32[]{:S(2)}) collective-permute-start(bf16[2,16,768]{2,1,0:T(8,128)(2,1)S(1)} %get-tuple-element.181), channel_id=1, source_target_pairs={{0,16},{4,20},{8,24},{12,28},{16,0},{20,4},{24,8},{28,12},{1,17},{... | collective-permute-start | bytes 147464 | tf_op jit(solution)/shard_map/ppermute | solution.py:82
  156.3 6.4 %collective-permute-start.45 = (bf16[2,16,768]{2,1,0:T(8,128)(2,1)S(1)}, bf16[2,16,768]{2,1,0:T(8,128)(2,1)S(1)}, u32[]{:S(2)}, u32[]{:S(2)}) collective-permute-start(bf16[2,16,768]{2,1,0:T(8,128)(2,1)S(1)} %get-tuple-element.182), channel_id=1, source_target_pairs={{0,24},{4,28},{8,16},{12,20},{16,8},{20,12},{24,0},{28,4},{1,25},{... | collective-permute-start | bytes 147464 | tf_op jit(solution)/shard_map/ppermute | solution.py:82
  161.3 7.2 %collective-permute-start.37 = (bf16[2,96,768]{2,1,0:T(8,128)(2,1)S(1)}, bf16[2,96,768]{2,1,0:T(8,128)(2,1)S(1)}, u32[]{:S(2)}, u32[]{:S(2)}) collective-permute-start(bf16[2,96,768]{2,1,0:T(8,128)(2,1)S(1)} %get-tuple-element.172.refs_1_), channel_id=1, source_target_pairs={{0,8},{4,12},{8,0},{12,4},{16,24},{20,28},{24,16},{28,20},{1,9},{5... | collective-permute-start | bytes 884744 | tf_op jit(solution)/shard_map/ppermute | solution.py:82
  163.6 6.7 %collective-permute-start.46 = (f32[4,8,128]{2,1,0:T(8,128)S(1)}, f32[4,8,128]{2,1,0:T(8,128)S(1)}, u32[]{:S(2)}, u32[]{:S(2)}) collective-permute-start(f32[4,8,128]{2,1,0:T(8,128)S(1)} %get-tuple-element.184), channel_id=1, source_target_pairs={{0,4},{4,0},{8,12},{12,8},{16,20},{20,16},{24,28},{28,24},{1,5},{5... | collective-permute-start | bytes 49160 | tf_op jit(solution)/shard_map/ppermute | solution.py:82
  168.5 9.9 %collective-permute-start.50 = (bf16[1,96,768]{2,1,0:T(8,128)(2,1)S(1)}, bf16[1,96,768]{2,1,0:T(8,128)(2,1)S(1)}, u32[]{:S(2)}, u32[]{:S(2)}) collective-permute-start(bf16[1,96,768]{2,1,0:T(8,128)(2,1)S(1)} %get-tuple-element.173.refs_1_), channel_id=1, source_target_pairs={{0,16},{4,20},{8,24},{12,28},{16,0},{20,4},{24,8},{28,12},{1,17},{... | collective-permute-start | bytes 442376 | tf_op jit(solution)/shard_map/ppermute | solution.py:82
  170.3 5.7 %collective-permute-start.47 = (f32[2,8,128]{2,1,0:T(8,128)S(1)}, f32[2,8,128]{2,1,0:T(8,128)S(1)}, u32[]{:S(2)}, u32[]{:S(2)}) collective-permute-start(f32[2,8,128]{2,1,0:T(8,128)S(1)} %get-tuple-element.186), channel_id=1, source_target_pairs={{0,8},{4,12},{8,0},{12,4},{16,24},{20,28},{24,16},{28,20},{1,9},{5... | collective-permute-start | bytes 24584 | tf_op jit(solution)/shard_map/ppermute | solution.py:82
  171.7 4.6 %collective-permute-start.48 = (f32[2,8,128]{2,1,0:T(8,128)S(1)}, f32[2,8,128]{2,1,0:T(8,128)S(1)}, u32[]{:S(2)}, u32[]{:S(2)}) collective-permute-start(f32[2,8,128]{2,1,0:T(8,128)S(1)} %get-tuple-element.187), channel_id=1, source_target_pairs={{0,16},{4,20},{8,24},{12,28},{16,0},{20,4},{24,8},{28,12},{1,17},{... | collective-permute-start | bytes 24584 | tf_op jit(solution)/shard_map/ppermute | solution.py:82
  172.2 5.4 %collective-permute-start.49 = (f32[2,8,128]{2,1,0:T(8,128)S(1)}, f32[2,8,128]{2,1,0:T(8,128)S(1)}, u32[]{:S(2)}, u32[]{:S(2)}) collective-permute-start(f32[2,8,128]{2,1,0:T(8,128)S(1)} %get-tuple-element.188), channel_id=1, source_target_pairs={{0,24},{4,28},{8,16},{12,20},{16,8},{20,12},{24,0},{28,4},{1,25},{... | collective-permute-start | bytes 24584 | tf_op jit(solution)/shard_map/ppermute | solution.py:82
  (19 other events, 141.3 us)

commit v5 on v4

--- a/solution.py
+++ b/solution.py
@@ -696,6 +696,9 @@
     x_blocks = tp_gather(x_own)
 
     if direct:
+        half_one = halve(mod_keep, mod_send, 1)
+        half_two = halve(*half_one, 2)
+        mod_parts = [half_two[0], swap(half_two[1], "fsdp", 4)]
         attn_four = join(attn_two, swap(attn_two, "fsdp", 2), [mod_send])
         attn_other = swap(attn_four, "fsdp", 1)
         first_own = call(
@@ -703,7 +706,7 @@
             "first_own",
             [((feat, hidden), BF)],
             [expand_weight],
-            ordered=[attn_four],
+            ordered=[half_two[1]],
             fetch=True,
         )[0]
         first_two, first_four, first_other = gather_steps(first_own)
@@ -737,12 +740,9 @@
             [second_four, second_other],
             [rank],
         )[0]
-        steps = [[first_four], [], [second_two, first_full], [second_four]]
-        half_one = halve(mod_keep, mod_send, 1)
-        half_two = halve(*half_one, 2, [first_two])
-        mod_parts = [half_two[0], swap(half_two[1], "fsdp", 4)]
+        steps = [[attn_four], [first_two], [first_four], [second_two], [second_four, first_full]]
     else:
-        steps = [[]] * 4
+        steps = [[]] * 5
         mod_parts = [scatter_pieces(mod_keep, mod_send)]
         qkv_full = lax.all_gather(
             query_key_value_weight.reshape(feat, 3 * cols), "fsdp", axis=0, tiled=True
@@ -782,7 +782,7 @@
         "gate_grad",
         [((tokens, width), BF), ((1, width), F32)],
         [*x_blocks, mod],
-        ordered=[branch_parts[0]],
+        ordered=[branch_parts[0], *steps[3]],
         flops=1e9,
     )
     branch, middle, mlp_in = call(
@@ -790,7 +790,7 @@
         "middle",
         [block_f32, block_f32, block],
         [x_own, *branch_parts, proj_bias, mod],
-        ordered=[fc2_part, *steps[3]],
+        ordered=[fc2_part, *steps[4]],
     )
     m_blocks = tp_gather(mlp_in)
     act, pre, mlp_rows, keep, send = call(
@@ -823,7 +823,7 @@
     )
     if direct:
         second_keep, second_send = call(
-            functools.partial(mlp_grad_kernel, step=2),
+            functools.partial(mlp_grad_kernel, step=1),
             "second_grad",
             blocks,
             [grad_rows, act],
@@ -832,12 +832,10 @@
             flops=2e9,
         )
         first_half = halve(first_keep, first_send, 1)
-        first_one = halve(*first_half, 2)
-        first_sum = last_sum(*first_one, 4)
-        second_half = halve(second_keep, second_send, 2)
-        second_one = halve(*second_half, 4)
-        second_sum = last_sum(*second_one, 1)
-        steps = [[first_half[1]], [second_half[1]], [first_one[1]], [second_one[1]]]
+        second_sent = call(
+            copy_kernel, "second_sent", blocks[:1], [second_send], ordered=[first_half[1]]
+        )[0]
+        steps = [[first_half[1], second_sent]]
     else:
         first_sum = lax.psum_scatter(
             dot(mlp_rows, pre, (0, 0)), "fsdp", scatter_dimension=0, tiled=True
@@ -846,7 +844,7 @@
             dot(grad_rows, act, (0, 0)), "fsdp", scatter_dimension=0, tiled=True
         )
         fc1_part = jnp.sum(pre.astype(F32), axis=0, keepdims=True)
-        steps = [[]] * 4
+        steps = [[]]
         second_keep = fc1_part
 
     grad_middle, grad_attn, sums = call(
@@ -871,7 +869,7 @@
         [block, ((8, width), F32)],
         [middle, x_own, *mlp_parts, second_bias, mod],
     )
-    grad_in = tp_scatter(keep, send, [*steps[1], gates])
+    grad_in = tp_scatter(keep, send, [gates])
     if direct:
         attn_keep, attn_send = call(
             attn_grad_kernel,
@@ -882,18 +880,7 @@
             ordered=[grad_in[0]],
             flops=6e9,
         )
-        attn_half = halve(attn_keep, attn_send, 1)
-        own, out = halve(*attn_half, 2)
-        tail = [[attn_half[1]], [out]]
-        qkv_sum, proj_sum = call(
-            attn_add_kernel,
-            "attn_sum",
-            [((3, feat, cols), F32), ((cols, feat), F32)],
-            [own, swap(out, "fsdp", 4)],
-        )
-        qkv_sum = qkv_sum.transpose(1, 0, 2)
     else:
-        tail = [[]] * 2
         qkv_sum = lax.psum_scatter(
             dot(attn_rows, grads, (0, 0)), "fsdp", scatter_dimension=0, tiled=True
         ).reshape(feat, 3, cols)
@@ -907,8 +894,13 @@
         [block_f32, ((16, width), BF)],
         [x_own, grad_middle, *grad_in, mod, sums, gates, fc2_part, fc1_part, qkv_part],
         scratch=[pltpu.VMEM((16, width), F32)],
-        ordered=steps[2],
-    )
+    )
+    tail = [[]] * 3
+    if direct:
+        first_one = halve(*first_half, 2, [pack])
+        first_sum = last_sum(*first_one, 4)
+        second_half = halve(second_keep, second_sent, 1, [pack])
+        tail[0] = [first_one[1], second_half[1]]
     packs = [pack] + [swap(pack, "tp", d) for d in range(1, tp_count)]
     spread_keep, spread_send = call(
         functools.partial(spread_kernel, latents=latents, feat=feat),
@@ -917,13 +909,28 @@
         packs,
         [rank, tp_rank],
         scratch=[pltpu.VMEM((tp_count, 16, width), F32), pltpu.VMEM((16, width), F32)],
-    )
+        ordered=tail[0],
+    )
+    if direct:
+        attn_half = halve(attn_keep, attn_send, 1, [spread_send])
+        attn_own_sum, attn_out = halve(*attn_half, 2)
+        qkv_sum, proj_sum = call(
+            attn_add_kernel,
+            "attn_sum",
+            [((3, feat, cols), F32), ((cols, feat), F32)],
+            [attn_own_sum, swap(attn_out, "fsdp", 4)],
+        )
+        qkv_sum = qkv_sum.transpose(1, 0, 2)
+        second_one = halve(*second_half, 2, [spread_send])
+        second_sum = last_sum(*second_one, 4)
+        tail[1] = [attn_half[1], second_one[1]]
+        tail[2] = [attn_out]
     silu_keep, silu_send, grad_mod_all, bias_grads = call(
         functools.partial(silu_kernel, latents=latents),
         "silu_columns",
         [((half, 8, 128), F32)] * 2
         + [((count * latents, 6 * width), BF), ((1, width), F32)],
-        [*exchange(spread_keep, spread_send, [*steps[3], *tail[0]]), ada_weight],
+        [*exchange(spread_keep, spread_send, tail[1]), ada_weight],
         scratch=[
             pltpu.VMEM((6, count * latents, width), F32),
             pltpu.VMEM((count, 8, 128), F32),
@@ -933,10 +940,9 @@
         functools.partial(cond_kernel, latents=latents, feat=feat),
         "cond_grad",
         [((latents, width), F32)],
-        [*exchange(silu_keep, silu_send), conditioning],
+        [*exchange(silu_keep, silu_send, tail[2]), conditioning],
         [rank],
         scratch=[pltpu.VMEM((count, 8, 128), F32)],
-        ordered=tail[1],
     )[0]
     ada_weight_grad = dot(cond_cols, grad_mod_all, (0, 0))
     bias_grads = bias_grads.reshape(width)

time: 180 us -> 176 us (0.978)
  waiting for transfers between devices: 87.7 us -> 79.1 us
  starting transfers between devices: 45.3 us -> 50.9 us
    ppermute x53, waiting for transfers between devices: 87.7 us -> 79.1 us  [swap(): return lax.ppermute(block, axis, [(i, i ^ offset) for i in range(count)])]
    ppermute x53, starting transfers between devices: 45.3 us -> 50.9 us  [swap(): return lax.ppermute(block, axis, [(i, i ^ offset) for i in range(count)])]
    pallas_call x50 -> x51, Pallas kernels: 30.8 us -> 29.4 us  [call(): pl.pallas_call(body, out_shape=[jax.ShapeDtypeStruct(shape, dtype) for sh...]
    unnamed x28 -> x40, local copies, waits for them, and re-layouts: 4.85 us -> 5.22 us
  transfers between devices with their start and end apart: 53 -> 53, of which waited for: 24 -> 24; matrix products, arithmetic and copies ran while one was open for 5% -> 5% of each run, Pallas kernels for 14% -> 12%
where the time goes in v5:
time: 176 us; the launch traced here: 175 us
  waiting for transfers between devices  79.1 us (45%)
  starting transfers between devices  50.9 us (29%)
  Pallas kernels  29.4 us (17%)
  local copies, waits for them, and re-layouts  9.97 us (6%)
  other arithmetic  3.07 us (2%)
    ppermute x53, waiting for transfers between devices, swap(): return lax.ppermute(block, axis, [(i, i ^ offset) for i in range(count)])  79.1 us
    ppermute x53, starting transfers between devices, swap(): return lax.ppermute(block, axis, [(i, i ^ offset) for i in range(count)])  50.9 us
    pallas_call x51, Pallas kernels, call(): pl.pallas_call(body, out_shape=[jax.ShapeDtypeStruct(shape, dtype) for sh...  29.4 us
    unnamed x40, local copies, waits for them, and re-layouts  5.22 us
  transfers between devices with their start and end apart: 53, of which 24 were waited for; matrix products, arithmetic and copies ran while one was open for 5% of the time, Pallas kernels for 12%

profile of v5, /device:TPU:0, one launch (start us, length us, event | category | flops | bytes accessed | tf_op | source)
XLA Modules:
  0.0 175.2 jit_solution(6125113259581425452)
XLA Ops:
  2.7 4.1 %collective-permute-start = (bf16[96,768]{1,0:T(8,128)(2,1)S(1)}, bf16[96,768]{1,0:T(8,128)(2,1)S(1)}, u32[]{:S(2)}, u32[]{:S(2)}) collective-permute-start(bf16[96,768]{1,0:T(8,128)(2,1)S(1)} %attn_own.1.refs_0_.refs_1_), channel_id=1, source_target_pairs={{0,16},{4,20},{8,24},{12,28},{16,0},{20,4},{24,8},{28,12},{1,17},{... | collective-permute-start | bytes 442376 | tf_op jit(solution)/shard_map/ppermute | solution.py:82
  9.6 1.5 collective-permute-start.1
  11.1 2.8 %collective-permute-done.refs_1_ = bf16[96,768]{1,0:T(8,128)(2,1)S(1)} collective-permute-done((bf16[96,768]{1,0:T(8,128)(2,1)S(1)}, bf16[96,768]{1,0:T(8,128)(2,1)S(1)}, u32[]{:S(2)}, u32[]{:S(2)}) %collective-permute-start) | collective-permute-done | bytes 147488 | tf_op jit(solution)/shard_map/ppermute | solution.py:82
  14.7 1.3 collective-permute-start.2
  16.0 2.2 %collective-permute-start.3 = (f32[2,16,128]{2,1,0:T(8,128)S(1)}, f32[2,16,128]{2,1,0:T(8,128)S(1)}, u32[]{:S(2)}, u32[]{:S(2)}) collective-permute-start(f32[2,16,128]{2,1,0:T(8,128)S(1)} %get-tuple-element.109), channel_id=1, source_target_pairs={{0,16},{4,20},{8,24},{12,28},{16,0},{20,4},{24,8},{28,12},{1,17},{... | collective-permute-start | bytes 49160 | tf_op jit(solution)/shard_map/ppermute | solution.py:82
  18.2 1.4 collective-permute-start.4
  19.6 1.6 pad_maximum_fusion
  21.3 1.6 collective-permute-done.2.refs_1_.refs_4_
  22.8 2.9 %collective-permute-done.4.refs_3_.refs_6_ = f32[2,16,128]{2,1,0:T(8,128)S(1)} collective-permute-done((f32[2,16,128]{2,1,0:T(8,128)S(1)}, f32[2,16,128]{2,1,0:T(8,128)S(1)}, u32[]{:S(2)}, u32[]{:S(2)}) %collective-permute-start.4) | collective-permute-done | bytes 16416 | tf_op jit(solution)/shard_map/ppermute | solution.py:82
  25.7 1.6 collective-permute-start.11
  28.4 1.6 collective-permute-start.5
  30.6 3.4 %collective-permute-done.5.refs_1_ = bf16[4,16,768]{2,1,0:T(8,128)(2,1)S(1)} collective-permute-done((bf16[4,16,768]{2,1,0:T(8,128)(2,1)S(1)}, bf16[4,16,768]{2,1,0:T(8,128)(2,1)S(1)}, u32[]{:S(2)}, u32[]{:S(2)}) %collective-permute-start.5) | collective-permute-done | bytes 98336 | tf_op jit(solution)/shard_map/ppermute | solution.py:82
  34.5 3.7 %collective-permute-done.6.refs_1_ = bf16[2,16,768]{2,1,0:T(8,128)(2,1)S(1)} collective-permute-done((bf16[2,16,768]{2,1,0:T(8,128)(2,1)S(1)}, bf16[2,16,768]{2,1,0:T(8,128)(2,1)S(1)}, u32[]{:S(2)}, u32[]{:S(2)}) %collective-permute-start.6) | collective-permute-done | bytes 49184 | tf_op jit(solution)/shard_map/ppermute | solution.py:82
  40.6 7.0 %collective-permute-done.7.refs_1_ = bf16[96,768]{1,0:T(8,128)(2,1)S(1)} collective-permute-done((bf16[96,768]{1,0:T(8,128)(2,1)S(1)}, bf16[96,768]{1,0:T(8,128)(2,1)S(1)}, u32[]{:S(2)}, u32[]{:S(2)}) %collective-permute-start.7) | collective-permute-done | bytes 147488 | tf_op jit(solution)/shard_map/ppermute | solution.py:82
  47.7 1.9 %collective-permute-start.13 = (bf16[1,16,768]{2,1,0:T(8,128)(2,1)}, bf16[1,16,768]{2,1,0:T(8,128)(2,1)}, u32[]{:S(2)}, u32[]{:S(2)}) collective-permute-start(bf16[1,16,768]{2,1,0:T(8,128)(2,1)} %get-tuple-element.115.refs_0_), channel_id=1, source_target_pairs={{0,16},{4,20},{8,24},{12,28},{16,0},{20,4},{24,8},{28,12},{1,17},{... | collective-permute-start | bytes 73736 | tf_op jit(solution)/shard_map/ppermute | solution.py:82
  49.6 5.1 %collective-permute-done.8.refs_1_ = bf16[2,96,768]{2,1,0:T(8,128)(2,1)} collective-permute-done((bf16[2,96,768]{2,1,0:T(8,128)(2,1)S(1)}, bf16[2,96,768]{2,1,0:T(8,128)(2,1)}, u32[]{:S(2)}, u32[]{:S(2)}) %collective-permute-start.8) | collective-permute-done | bytes 294944 | tf_op jit(solution)/shard_map/ppermute | solution.py:82
  55.8 1.8 %collective-permute-start.18 = (bf16[4,96,768]{2,1,0:T(8,128)(2,1)S(1)}, bf16[4,96,768]{2,1,0:T(8,128)(2,1)S(1)}, u32[]{:S(2)}, u32[]{:S(2)}) collective-permute-start(bf16[4,96,768]{2,1,0:T(8,128)(2,1)S(1)} %join.8.refs_0_.refs_1_), channel_id=1, source_target_pairs={{0,4},{4,0},{8,12},{12,8},{16,20},{20,16},{24,28},{28,24},{1,5},{5... | collective-permute-start | bytes 1769480 | tf_op jit(solution)/shard_map/ppermute | solution.py:82
  59.6 1.6 first_norm.1
  61.4 2.5 %attention.1 = (bf16[512,576]{1,0:T(8,128)(2,1)S(1)}, bf16[512,192]{1,0:T(8,128)(2,1)S(1)}, bf16[256,768]{1,0:T(8,128)(2,1)S(1)}, bf16[256,768]{1,0:T(8,128)(2,1)S(1)}) custom-call(bf16[2,96,768]{2,1,0:T(8,128)(2,1)S(1)} %join.7.refs_0_, bf16[512,768]{1,0:T(8,128)(2,1)S(1)} %get-tuple-element.118.refs_1_.refs_2_, ...), custom_call_target="tpu_custom_call" | custom-call | flops 1 | bytes 1 | tf_op jit(solution)/shard_map/attention/pallas_call | solution.py:50
  64.0 1.5 collective-permute-done.16.refs_1_
  66.7 7.0 %collective-permute-done.17.refs_1_ = bf16[2,96,768]{2,1,0:T(8,128)(2,1)S(1)} collective-permute-done((bf16[2,96,768]{2,1,0:T(8,128)(2,1)S(1)}, bf16[2,96,768]{2,1,0:T(8,128)(2,1)S(1)}, u32[]{:S(2)}, u32[]{:S(2)}) %collective-permute-start.17) | collective-permute-done | bytes 294944 | tf_op jit(solution)/shard_map/ppermute | solution.py:82
  76.2 5.2 %collective-permute-done.21.refs_2_ = bf16[128,768]{1,0:T(8,128)(2,1)S(1)} collective-permute-done((bf16[128,768]{1,0:T(8,128)(2,1)S(1)}, bf16[128,768]{1,0:T(8,128)(2,1)S(1)}, u32[]{:S(2)}, u32[]{:S(2)}) %collective-permute-start.21) | collective-permute-done | bytes 196640 | tf_op jit(solution)/shard_map/ppermute | solution.py:82
  81.4 6.6 %collective-permute-done.23.refs_2_ = bf16[4,96,768]{2,1,0:T(8,128)(2,1)S(1)} collective-permute-done((bf16[4,96,768]{2,1,0:T(8,128)(2,1)S(1)}, bf16[4,96,768]{2,1,0:T(8,128)(2,1)S(1)}, u32[]{:S(2)}, u32[]{:S(2)}) %collective-permute-start.23) | collective-permute-done | bytes 589856 | tf_op jit(solution)/shard_map/ppermute | solution.py:82
  88.1 3.1 %mlp.1 = (bf16[512,768]{1,0:T(8,128)(2,1)S(1)}, bf16[512,768]{1,0:T(8,128)(2,1)S(1)}, bf16[512,768]{1,0:T(8,128)(2,1)S(1)}, bf16[256,768]{1,0:T(8,128)(2,1)S(1)}, bf16[256,768]{1,0:T(8,128)(2,1)S(1)}) custom-call(bf16[128,768]{1,0:T(8,128)(2,1)S(1)} %get-tuple-element.130.refs_0_, bf16[128,768]{1,0:T(8,128)(2,1)S(1)} %collective-permute-done.20.refs_1_, ...), custom_call_target="tpu_custom_call" | custom-call | flops 1 | bytes 1 | tf_op jit(solution)/shard_map/mlp/pallas_call | solution.py:50
  93.6 1.6 mlp_out.1
  96.3 3.8 %collective-permute-done.25.refs_5_ = bf16[128,768]{1,0:T(8,128)(2,1)S(1)} collective-permute-done((bf16[128,768]{1,0:T(8,128)(2,1)S(1)}, bf16[128,768]{1,0:T(8,128)(2,1)S(1)}, u32[]{:S(2)}, u32[]{:S(2)}) %collective-permute-start.25) | collective-permute-done | bytes 196640 | tf_op jit(solution)/shard_map/ppermute | solution.py:82
  101.2 5.6 %collective-permute-done.26.refs_0_.refs_5_ = bf16[128,768]{1,0:T(8,128)(2,1)S(1)} collective-permute-done((bf16[128,768]{1,0:T(8,128)(2,1)S(1)}, bf16[128,768]{1,0:T(8,128)(2,1)S(1)}, u32[]{:S(2)}, u32[]{:S(2)}) %collective-permute-start.26) | collective-permute-done | bytes 196640 | tf_op jit(solution)/shard_map/ppermute | solution.py:82
  106.8 1.5 collective-permute-done.29.refs_1_
  108.7 4.7 %attention_back.1 = (bf16[512,768]{1,0:T(8,128)(2,1)S(1)}, bf16[512,576]{1,0:T(8,128)(2,1)S(1)}, bf16[256,768]{1,0:T(8,128)(2,1)S(1)}, bf16[256,768]{1,0:T(8,128)(2,1)S(1)}, f32[1,576]{1,0:T(1,128)S(1)}) custom-call(f32[128,768]{1,0:T(8,128)S(1)} %get-tuple-element.145.refs_2_.refs_0_, bf16[2,96,768]{2,1,0:T(8,128)(2,1)S(1)} %get-tuple-element.153.refs_0_.refs_1_, ...), custom_call_target="tpu_custom_call" | custom-call | flops 1 | bytes 1 | tf_op jit(solution)/shard_map/attention_back/pallas_call | solution.py:50
  114.0 1.4 collective-permute-start.35
  115.5 5.3 %collective-permute-done.28.refs_3_ = bf16[128,768]{1,0:T(8,128)(2,1)S(1)} collective-permute-done((bf16[128,768]{1,0:T(8,128)(2,1)S(1)}, bf16[128,768]{1,0:T(8,128)(2,1)S(1)}, u32[]{:S(2)}, u32[]{:S(2)}) %collective-permute-start.28) | collective-permute-done | bytes 196640 | tf_op jit(solution)/shard_map/ppermute | solution.py:82
  121.0 1.9 %attn_weight_grad.1 = (bf16[4,96,768]{2,1,0:T(8,128)(2,1)S(1)}, bf16[4,96,768]{2,1,0:T(8,128)(2,1)S(1)}) custom-call(s32[1]{0:T(128)} %bitcast.1.refs_0_, f32[128,768]{1,0:T(8,128)S(1)} %get-tuple-element.158.refs_2_.refs_1_, bf16[512,768]{1,0:T(8,128)(2,1)S(1)} %get-tuple-element.118.refs_1_.refs_2_, bf16[512,576]{1,0:T(8,128)(2,1)S(1)} %get-tuple-element.168.refs_3_, ...), custom_call_target="tpu_custom_call" | custom-call | flops 6000000000 | bytes 1 | tf_op jit(solution)/shard_map/attn_weight_grad/pallas_call | solution.py:50
  122.9 1.4 collective-permute-start.39
  124.8 2.5 %collective-permute-start.34 = (bf16[2,96,768]{2,1,0:T(8,128)(2,1)S(1)}, bf16[2,96,768]{2,1,0:T(8,128)(2,1)S(1)}, u32[]{:S(2)}, u32[]{:S(2)}) collective-permute-start(bf16[2,96,768]{2,1,0:T(8,128)(2,1)S(1)} %get-tuple-element.153.refs_0_.refs_1_), channel_id=1, source_target_pairs={{0,8},{4,12},{8,0},{12,4},{16,24},{20,28},{24,16},{28,20},{1,9},{5... | collective-permute-start | bytes 884744 | tf_op jit(solution)/shard_map/ppermute | solution.py:82
  127.3 3.1 %collective-permute-done.33.refs_3_ = bf16[128,768]{1,0:T(8,128)(2,1)S(1)} collective-permute-done((bf16[128,768]{1,0:T(8,128)(2,1)S(1)}, bf16[128,768]{1,0:T(8,128)(2,1)S(1)}, u32[]{:S(2)}, u32[]{:S(2)}) %collective-permute-start.33) | collective-permute-done | bytes 196640 | tf_op jit(solution)/shard_map/ppermute | solution.py:82
  130.9 2.5 %collective-permute-start.41 = (bf16[2,96,768]{2,1,0:T(8,128)(2,1)S(1)}, bf16[2,96,768]{2,1,0:T(8,128)(2,1)S(1)}, u32[]{:S(2)}, u32[]{:S(2)}) collective-permute-start(bf16[2,96,768]{2,1,0:T(8,128)(2,1)S(1)} %get-tuple-element.166.refs_3_), channel_id=1, source_target_pairs={{0,8},{4,12},{8,0},{12,4},{16,24},{20,28},{24,16},{28,20},{1,9},{5... | collective-permute-start | bytes 884744 | tf_op jit(solution)/shard_map/ppermute | solution.py:82
  135.4 1.3 collective-permute-done.38.refs_7_
  140.3 2.5 %collective-permute-done.39.refs_2_ = bf16[4,96,768]{2,1,0:T(8,128)(2,1)S(1)} collective-permute-done((bf16[4,96,768]{2,1,0:T(8,128)(2,1)S(1)}, bf16[4,96,768]{2,1,0:T(8,128)(2,1)S(1)}, u32[]{:S(2)}, u32[]{:S(2)}) %collective-permute-start.39) | collective-permute-done | bytes 589856 | tf_op jit(solution)/shard_map/ppermute | solution.py:82
  144.2 2.5 %collective-permute-start.43 = (bf16[2,16,768]{2,1,0:T(8,128)(2,1)S(1)}, bf16[2,16,768]{2,1,0:T(8,128)(2,1)S(1)}, u32[]{:S(2)}, u32[]{:S(2)}) collective-permute-start(bf16[2,16,768]{2,1,0:T(8,128)(2,1)S(1)} %get-tuple-element.180), channel_id=1, source_target_pairs={{0,8},{4,12},{8,0},{12,4},{16,24},{20,28},{24,16},{28,20},{1,9},{5... | collective-permute-start | bytes 147464 | tf_op jit(solution)/shard_map/ppermute | solution.py:82
  147.8 1.4 collective-permute-start.45
  151.9 2.0 %collective-permute-start.52 = (bf16[1,96,768]{2,1,0:T(8,128)(2,1)S(1)}, bf16[1,96,768]{2,1,0:T(8,128)(2,1)S(1)}, u32[]{:S(2)}, u32[]{:S(2)}) collective-permute-start(bf16[1,96,768]{2,1,0:T(8,128)(2,1)S(1)} %get-tuple-element.177.refs_1_), channel_id=1, source_target_pairs={{0,16},{4,20},{8,24},{12,28},{16,0},{20,4},{24,8},{28,12},{1,17},{... | collective-permute-start | bytes 442376 | tf_op jit(solution)/shard_map/ppermute | solution.py:82
  155.9 1.4 collective-permute-start.46
  157.2 1.6 fusion
  158.8 5.0 %collective-permute-done.40.refs_1_ = bf16[2,96,768]{2,1,0:T(8,128)(2,1)S(1)} collective-permute-done((bf16[2,96,768]{2,1,0:T(8,128)(2,1)S(1)}, bf16[2,96,768]{2,1,0:T(8,128)(2,1)S(1)}, u32[]{:S(2)}, u32[]{:S(2)}) %collective-permute-start.40) | collective-permute-done | bytes 294944 | tf_op jit(solution)/shard_map/ppermute | solution.py:82
  165.1 1.7 collective-permute-start.47
  166.8 1.3 collective-permute-start.48
  168.2 1.4 collective-permute-start.49
  172.0 1.6 collective-permute-done.49.refs_4_
  (164 shorter events, 41.9 us)
Async XLA Ops:
  2.7 11.1 %collective-permute-start = (bf16[96,768]{1,0:T(8,128)(2,1)S(1)}, bf16[96,768]{1,0:T(8,128)(2,1)S(1)}, u32[]{:S(2)}, u32[]{:S(2)}) collective-permute-start(bf16[96,768]{1,0:T(8,128)(2,1)S(1)} %attn_own.1.refs_0_.refs_1_), channel_id=1, source_target_pairs={{0,16},{4,20},{8,24},{12,28},{16,0},{20,4},{24,8},{28,12},{1,17},{... | collective-permute-start | bytes 442376 | tf_op jit(solution)/shard_map/ppermute | solution.py:82
  9.6 5.1 %collective-permute-start.1 = (f32[4,16,128]{2,1,0:T(8,128)S(1)}, f32[4,16,128]{2,1,0:T(8,128)S(1)}, u32[]{:S(2)}, u32[]{:S(2)}) collective-permute-start(f32[4,16,128]{2,1,0:T(8,128)S(1)} %get-tuple-element.106), channel_id=1, source_target_pairs={{0,4},{4,0},{8,12},{12,8},{16,20},{20,16},{24,28},{28,24},{1,5},{5... | collective-permute-start | bytes 98312 | tf_op jit(solution)/shard_map/ppermute | solution.py:82
  13.9 16.2 %collective-permute-start.9 = (bf16[2,96,768]{2,1,0:T(8,128)(2,1)S(1)}, bf16[2,96,768]{2,1,0:T(8,128)(2,1)S(1)}, u32[]{:S(2)}, u32[]{:S(2)}) collective-permute-start(bf16[2,96,768]{2,1,0:T(8,128)(2,1)S(1)} %join.6.refs_0_.refs_1_), channel_id=1, source_target_pairs={{0,8},{4,12},{8,0},{12,4},{16,24},{20,28},{24,16},{28,20},{1,9},{5... | collective-permute-start | bytes 884744 | tf_op jit(solution)/shard_map/ppermute | solution.py:82
  14.7 8.1 %collective-permute-start.2 = (f32[2,16,128]{2,1,0:T(8,128)S(1)}, f32[2,16,128]{2,1,0:T(8,128)S(1)}, u32[]{:S(2)}, u32[]{:S(2)}) collective-permute-start(f32[2,16,128]{2,1,0:T(8,128)S(1)} %get-tuple-element.108), channel_id=1, source_target_pairs={{0,8},{4,12},{8,0},{12,4},{16,24},{20,28},{24,16},{28,20},{1,9},{5... | collective-permute-start | bytes 49160 | tf_op jit(solution)/shard_map/ppermute | solution.py:82
  16.0 6.8 %collective-permute-start.3 = (f32[2,16,128]{2,1,0:T(8,128)S(1)}, f32[2,16,128]{2,1,0:T(8,128)S(1)}, u32[]{:S(2)}, u32[]{:S(2)}) collective-permute-start(f32[2,16,128]{2,1,0:T(8,128)S(1)} %get-tuple-element.109), channel_id=1, source_target_pairs={{0,16},{4,20},{8,24},{12,28},{16,0},{20,4},{24,8},{28,12},{1,17},{... | collective-permute-start | bytes 49160 | tf_op jit(solution)/shard_map/ppermute | solution.py:82
  18.2 7.5 %collective-permute-start.4 = (f32[2,16,128]{2,1,0:T(8,128)S(1)}, f32[2,16,128]{2,1,0:T(8,128)S(1)}, u32[]{:S(2)}, u32[]{:S(2)}) collective-permute-start(f32[2,16,128]{2,1,0:T(8,128)S(1)} %get-tuple-element.110), channel_id=1, source_target_pairs={{0,24},{4,28},{8,16},{12,20},{16,8},{20,12},{24,0},{28,4},{1,25},{... | collective-permute-start | bytes 49160 | tf_op jit(solution)/shard_map/ppermute | solution.py:82
  25.7 14.3 %collective-permute-start.11 = (bf16[256,768]{1,0:T(8,128)(2,1)S(1)}, bf16[256,768]{1,0:T(8,128)(2,1)S(1)}, u32[]{:S(2)}, u32[]{:S(2)}) collective-permute-start(bf16[256,768]{1,0:T(8,128)(2,1)S(1)} %tokens.1.refs_2_.refs_3_.refs_1_.refs_0_), channel_id=1, source_target_pairs={{0,2},{1,3},{2,0},{3,1},{4,6},{5,7},{6,4},{7,5},{8,10},{9,11},{10,... | collective-permute-start | bytes 1179656 | tf_op jit(solution)/shard_map/ppermute | solution.py:82
  28.4 5.6 %collective-permute-start.5 = (bf16[4,16,768]{2,1,0:T(8,128)(2,1)S(1)}, bf16[4,16,768]{2,1,0:T(8,128)(2,1)S(1)}, u32[]{:S(2)}, u32[]{:S(2)}) collective-permute-start(bf16[4,16,768]{2,1,0:T(8,128)(2,1)S(1)} %get-tuple-element.112.refs_2_.refs_0_), channel_id=1, source_target_pairs={{0,4},{4,0},{8,12},{12,8},{16,20},{20,16},{24,28},{28,24},{1,5},{5... | collective-permute-start | bytes 294920 | tf_op jit(solution)/shard_map/ppermute | solution.py:82
  30.1 31.0 %collective-permute-start.14 = (bf16[4,96,768]{2,1,0:T(8,128)(2,1)S(1)}, bf16[4,96,768]{2,1,0:T(8,128)(2,1)S(1)}, u32[]{:S(2)}, u32[]{:S(2)}) collective-permute-start(bf16[4,96,768]{2,1,0:T(8,128)(2,1)S(1)} %join.9.refs_1_), channel_id=1, source_target_pairs={{0,4},{4,0},{8,12},{12,8},{16,20},{20,16},{24,28},{28,24},{1,5},{5... | collective-permute-start | bytes 1769480 | tf_op jit(solution)/shard_map/ppermute | solution.py:82
  34.1 4.2 %collective-permute-start.6 = (bf16[2,16,768]{2,1,0:T(8,128)(2,1)S(1)}, bf16[2,16,768]{2,1,0:T(8,128)(2,1)S(1)}, u32[]{:S(2)}, u32[]{:S(2)}) collective-permute-start(bf16[2,16,768]{2,1,0:T(8,128)(2,1)S(1)} %get-tuple-element.114), channel_id=1, source_target_pairs={{0,8},{4,12},{8,0},{12,4},{16,24},{20,28},{24,16},{28,20},{1,9},{5... | collective-permute-start | bytes 147464 | tf_op jit(solution)/shard_map/ppermute | solution.py:82
  39.6 7.9 %collective-permute-start.7 = (bf16[96,768]{1,0:T(8,128)(2,1)S(1)}, bf16[96,768]{1,0:T(8,128)(2,1)S(1)}, u32[]{:S(2)}, u32[]{:S(2)}) collective-permute-start(bf16[96,768]{1,0:T(8,128)(2,1)S(1)} %first_own.1.refs_0_), channel_id=1, source_target_pairs={{0,16},{4,20},{8,24},{12,28},{16,0},{20,4},{24,8},{28,12},{1,17},{... | collective-permute-start | bytes 442376 | tf_op jit(solution)/shard_map/ppermute | solution.py:82
  40.1 18.9 %collective-permute-start.10 = (bf16[256,768]{1,0:T(8,128)(2,1)S(1)}, bf16[256,768]{1,0:T(8,128)(2,1)S(1)}, u32[]{:S(2)}, u32[]{:S(2)}) collective-permute-start(bf16[256,768]{1,0:T(8,128)(2,1)S(1)} %tokens.1.refs_2_.refs_3_.refs_1_.refs_0_), channel_id=1, source_target_pairs={{0,1},{1,0},{2,3},{3,2},{4,5},{5,4},{6,7},{7,6},{8,9},{9,8},{10,11... | collective-permute-start | bytes 1179656 | tf_op jit(solution)/shard_map/ppermute | solution.py:82
  40.1 18.9 %collective-permute-start.12 = (bf16[256,768]{1,0:T(8,128)(2,1)S(1)}, bf16[256,768]{1,0:T(8,128)(2,1)}, u32[]{:S(2)}, u32[]{:S(2)}) collective-permute-start(bf16[256,768]{1,0:T(8,128)(2,1)S(1)} %collective-permute-done.11.refs_4_), channel_id=1, source_target_pairs={{0,1},{1,0},{2,3},{3,2},{4,5},{5,4},{6,7},{7,6},{8,9},{9,8},{10,11... | collective-permute-start | bytes 1179656 | tf_op jit(solution)/shard_map/ppermute | solution.py:82
  47.6 7.2 %collective-permute-start.8 = (bf16[2,96,768]{2,1,0:T(8,128)(2,1)S(1)}, bf16[2,96,768]{2,1,0:T(8,128)(2,1)}, u32[]{:S(2)}, u32[]{:S(2)}) collective-permute-start(bf16[2,96,768]{2,1,0:T(8,128)(2,1)S(1)} %join.7.refs_0_), channel_id=1, source_target_pairs={{0,8},{4,12},{8,0},{12,4},{16,24},{20,28},{24,16},{28,20},{1,9},{5... | collective-permute-start | bytes 884744 | tf_op jit(solution)/shard_map/ppermute | solution.py:82
  47.7 11.0 %collective-permute-start.13 = (bf16[1,16,768]{2,1,0:T(8,128)(2,1)}, bf16[1,16,768]{2,1,0:T(8,128)(2,1)}, u32[]{:S(2)}, u32[]{:S(2)}) collective-permute-start(bf16[1,16,768]{2,1,0:T(8,128)(2,1)} %get-tuple-element.115.refs_0_), channel_id=1, source_target_pairs={{0,16},{4,20},{8,24},{12,28},{16,0},{20,4},{24,8},{28,12},{1,17},{... | collective-permute-start | bytes 73736 | tf_op jit(solution)/shard_map/ppermute | solution.py:82
  55.8 18.3 %collective-permute-start.18 = (bf16[4,96,768]{2,1,0:T(8,128)(2,1)S(1)}, bf16[4,96,768]{2,1,0:T(8,128)(2,1)S(1)}, u32[]{:S(2)}, u32[]{:S(2)}) collective-permute-start(bf16[4,96,768]{2,1,0:T(8,128)(2,1)S(1)} %join.8.refs_0_.refs_1_), channel_id=1, source_target_pairs={{0,4},{4,0},{8,12},{12,8},{16,20},{20,16},{24,28},{28,24},{1,5},{5... | collective-permute-start | bytes 1769480 | tf_op jit(solution)/shard_map/ppermute | solution.py:82
  58.7 6.9 %collective-permute-start.16 = (bf16[96,768]{1,0:T(8,128)(2,1)S(1)}, bf16[96,768]{1,0:T(8,128)(2,1)S(1)}, u32[]{:S(2)}, u32[]{:S(2)}) collective-permute-start(bf16[96,768]{1,0:T(8,128)(2,1)S(1)} %second_own.1.refs_0_), channel_id=1, source_target_pairs={{0,16},{4,20},{8,24},{12,28},{16,0},{20,4},{24,8},{28,12},{1,17},{... | collective-permute-start | bytes 442376 | tf_op jit(solution)/shard_map/ppermute | solution.py:82
  65.6 8.1 %collective-permute-start.17 = (bf16[2,96,768]{2,1,0:T(8,128)(2,1)S(1)}, bf16[2,96,768]{2,1,0:T(8,128)(2,1)S(1)}, u32[]{:S(2)}, u32[]{:S(2)}) collective-permute-start(bf16[2,96,768]{2,1,0:T(8,128)(2,1)S(1)} %join.10.refs_1_.refs_0_), channel_id=1, source_target_pairs={{0,8},{4,12},{8,0},{12,4},{16,24},{20,28},{24,16},{28,20},{1,9},{5... | collective-permute-start | bytes 884744 | tf_op jit(solution)/shard_map/ppermute | solution.py:82
  66.1 9.2 %collective-permute-start.19 = (bf16[128,768]{1,0:T(8,128)(2,1)S(1)}, bf16[128,768]{1,0:T(8,128)(2,1)S(1)}, u32[]{:S(2)}, u32[]{:S(2)}) collective-permute-start(bf16[128,768]{1,0:T(8,128)(2,1)S(1)} %get-tuple-element.127), channel_id=1, source_target_pairs={{0,2},{1,3},{2,0},{3,1},{4,6},{5,7},{6,4},{7,5},{8,10},{9,11},{10,... | collective-permute-start | bytes 589832 | tf_op jit(solution)/shard_map/ppermute | solution.py:82
  73.7 14.3 %collective-permute-start.23 = (bf16[4,96,768]{2,1,0:T(8,128)(2,1)S(1)}, bf16[4,96,768]{2,1,0:T(8,128)(2,1)S(1)}, u32[]{:S(2)}, u32[]{:S(2)}) collective-permute-start(bf16[4,96,768]{2,1,0:T(8,128)(2,1)S(1)} %join.11.refs_1_), channel_id=1, source_target_pairs={{0,4},{4,0},{8,12},{12,8},{16,20},{20,16},{24,28},{28,24},{1,5},{5... | collective-permute-start | bytes 1769480 | tf_op jit(solution)/shard_map/ppermute | solution.py:82
  75.6 5.7 %collective-permute-start.21 = (bf16[128,768]{1,0:T(8,128)(2,1)S(1)}, bf16[128,768]{1,0:T(8,128)(2,1)S(1)}, u32[]{:S(2)}, u32[]{:S(2)}) collective-permute-start(bf16[128,768]{1,0:T(8,128)(2,1)S(1)} %get-tuple-element.130.refs_0_), channel_id=1, source_target_pairs={{0,2},{1,3},{2,0},{3,1},{4,6},{5,7},{6,4},{7,5},{8,10},{9,11},{10,... | collective-permute-start | bytes 589832 | tf_op jit(solution)/shard_map/ppermute | solution.py:82
  76.2 11.8 %collective-permute-start.20 = (bf16[128,768]{1,0:T(8,128)(2,1)S(1)}, bf16[128,768]{1,0:T(8,128)(2,1)S(1)}, u32[]{:S(2)}, u32[]{:S(2)}) collective-permute-start(bf16[128,768]{1,0:T(8,128)(2,1)S(1)} %get-tuple-element.130.refs_0_), channel_id=1, source_target_pairs={{0,1},{1,0},{2,3},{3,2},{4,5},{5,4},{6,7},{7,6},{8,9},{9,8},{10,11... | collective-permute-start | bytes 589832 | tf_op jit(solution)/shard_map/ppermute | solution.py:82
  81.4 6.7 %collective-permute-start.22 = (bf16[128,768]{1,0:T(8,128)(2,1)S(1)}, bf16[128,768]{1,0:T(8,128)(2,1)S(1)}, u32[]{:S(2)}, u32[]{:S(2)}) collective-permute-start(bf16[128,768]{1,0:T(8,128)(2,1)S(1)} %collective-permute-done.21.refs_2_), channel_id=1, source_target_pairs={{0,1},{1,0},{2,3},{3,2},{4,5},{5,4},{6,7},{7,6},{8,9},{9,8},{10,11... | collective-permute-start | bytes 589832 | tf_op jit(solution)/shard_map/ppermute | solution.py:82
  92.5 15.8 %collective-permute-start.29 = (bf16[4,96,768]{2,1,0:T(8,128)(2,1)S(1)}, bf16[4,96,768]{2,1,0:T(8,128)(2,1)S(1)}, u32[]{:S(2)}, u32[]{:S(2)}) collective-permute-start(bf16[4,96,768]{2,1,0:T(8,128)(2,1)S(1)} %get-tuple-element.152), channel_id=1, source_target_pairs={{0,4},{4,0},{8,12},{12,8},{16,20},{20,16},{24,28},{28,24},{1,5},{5... | collective-permute-start | bytes 1769480 | tf_op jit(solution)/shard_map/ppermute | solution.py:82
  93.1 7.0 %collective-permute-start.25 = (bf16[128,768]{1,0:T(8,128)(2,1)S(1)}, bf16[128,768]{1,0:T(8,128)(2,1)S(1)}, u32[]{:S(2)}, u32[]{:S(2)}) collective-permute-start(bf16[128,768]{1,0:T(8,128)(2,1)S(1)} %get-tuple-element.142), channel_id=1, source_target_pairs={{0,2},{1,3},{2,0},{3,1},{4,6},{5,7},{6,4},{7,5},{8,10},{9,11},{10,... | collective-permute-start | bytes 589832 | tf_op jit(solution)/shard_map/ppermute | solution.py:82
  95.3 13.3 %collective-permute-start.27 = (bf16[256,768]{1,0:T(8,128)(2,1)S(1)}, bf16[256,768]{1,0:T(8,128)(2,1)S(1)}, u32[]{:S(2)}, u32[]{:S(2)}) collective-permute-start(bf16[256,768]{1,0:T(8,128)(2,1)S(1)} %get-tuple-element.139.refs_1_), channel_id=1, source_target_pairs={{0,1},{1,0},{2,3},{3,2},{4,5},{5,4},{6,7},{7,6},{8,9},{9,8},{10,11... | collective-permute-start | bytes 1179656 | tf_op jit(solution)/shard_map/ppermute | solution.py:82
  100.6 6.2 %collective-permute-start.26 = (bf16[128,768]{1,0:T(8,128)(2,1)S(1)}, bf16[128,768]{1,0:T(8,128)(2,1)S(1)}, u32[]{:S(2)}, u32[]{:S(2)}) collective-permute-start(bf16[128,768]{1,0:T(8,128)(2,1)S(1)} %get-tuple-element.143.refs_3_), channel_id=1, source_target_pairs={{0,2},{1,3},{2,0},{3,1},{4,6},{5,7},{6,4},{7,5},{8,10},{9,11},{10,... | collective-permute-start | bytes 589832 | tf_op jit(solution)/shard_map/ppermute | solution.py:82
  101.2 7.5 %collective-permute-start.30 = (bf16[128,768]{1,0:T(8,128)(2,1)S(1)}, bf16[128,768]{1,0:T(8,128)(2,1)S(1)}, u32[]{:S(2)}, u32[]{:S(2)}) collective-permute-start(bf16[128,768]{1,0:T(8,128)(2,1)S(1)} %get-tuple-element.143.refs_3_), channel_id=1, source_target_pairs={{0,1},{1,0},{2,3},{3,2},{4,5},{5,4},{6,7},{7,6},{8,9},{9,8},{10,11... | collective-permute-start | bytes 589832 | tf_op jit(solution)/shard_map/ppermute | solution.py:82
  113.4 7.5 %collective-permute-start.32 = (bf16[256,768]{1,0:T(8,128)(2,1)S(1)}, bf16[256,768]{1,0:T(8,128)(2,1)S(1)}, u32[]{:S(2)}, u32[]{:S(2)}) collective-permute-start(bf16[256,768]{1,0:T(8,128)(2,1)S(1)} %get-tuple-element.157), channel_id=1, source_target_pairs={{0,1},{1,0},{2,3},{3,2},{4,5},{5,4},{6,7},{7,6},{8,9},{9,8},{10,11... | collective-permute-start | bytes 1179656 | tf_op jit(solution)/shard_map/ppermute | solution.py:82
  113.4 7.3 %collective-permute-start.28 = (bf16[128,768]{1,0:T(8,128)(2,1)S(1)}, bf16[128,768]{1,0:T(8,128)(2,1)S(1)}, u32[]{:S(2)}, u32[]{:S(2)}) collective-permute-start(bf16[128,768]{1,0:T(8,128)(2,1)S(1)} %get-tuple-element.146), channel_id=1, source_target_pairs={{0,2},{1,3},{2,0},{3,1},{4,6},{5,7},{6,4},{7,5},{8,10},{9,11},{10,... | collective-permute-start | bytes 589832 | tf_op jit(solution)/shard_map/ppermute | solution.py:82
  114.0 16.8 %collective-permute-start.35 = (bf16[4,96,768]{2,1,0:T(8,128)(2,1)S(1)}, bf16[4,96,768]{2,1,0:T(8,128)(2,1)S(1)}, u32[]{:S(2)}, u32[]{:S(2)}) collective-permute-start(bf16[4,96,768]{2,1,0:T(8,128)(2,1)S(1)} %second_sent.1.refs_2_), channel_id=1, source_target_pairs={{0,4},{4,0},{8,12},{12,8},{16,20},{20,16},{24,28},{28,24},{1,5},{5... | collective-permute-start | bytes 1769480 | tf_op jit(solution)/shard_map/ppermute | solution.py:82
  122.9 19.9 %collective-permute-start.39 = (bf16[4,96,768]{2,1,0:T(8,128)(2,1)S(1)}, bf16[4,96,768]{2,1,0:T(8,128)(2,1)S(1)}, u32[]{:S(2)}, u32[]{:S(2)}) collective-permute-start(bf16[4,96,768]{2,1,0:T(8,128)(2,1)S(1)} %get-tuple-element.172), channel_id=1, source_target_pairs={{0,4},{4,0},{8,12},{12,8},{16,20},{20,16},{24,28},{28,24},{1,5},{5... | collective-permute-start | bytes 1769480 | tf_op jit(solution)/shard_map/ppermute | solution.py:82
  124.3 6.1 %collective-permute-start.33 = (bf16[128,768]{1,0:T(8,128)(2,1)S(1)}, bf16[128,768]{1,0:T(8,128)(2,1)S(1)}, u32[]{:S(2)}, u32[]{:S(2)}) collective-permute-start(bf16[128,768]{1,0:T(8,128)(2,1)S(1)} %get-tuple-element.159), channel_id=1, source_target_pairs={{0,2},{1,3},{2,0},{3,1},{4,6},{5,7},{6,4},{7,5},{8,10},{9,11},{10,... | collective-permute-start | bytes 589832 | tf_op jit(solution)/shard_map/ppermute | solution.py:82
  124.8 9.6 %collective-permute-start.34 = (bf16[2,96,768]{2,1,0:T(8,128)(2,1)S(1)}, bf16[2,96,768]{2,1,0:T(8,128)(2,1)S(1)}, u32[]{:S(2)}, u32[]{:S(2)}) collective-permute-start(bf16[2,96,768]{2,1,0:T(8,128)(2,1)S(1)} %get-tuple-element.153.refs_0_.refs_1_), channel_id=1, source_target_pairs={{0,8},{4,12},{8,0},{12,4},{16,24},{20,28},{24,16},{28,20},{1,9},{5... | collective-permute-start | bytes 884744 | tf_op jit(solution)/shard_map/ppermute | solution.py:82
  130.9 9.3 %collective-permute-start.41 = (bf16[2,96,768]{2,1,0:T(8,128)(2,1)S(1)}, bf16[2,96,768]{2,1,0:T(8,128)(2,1)S(1)}, u32[]{:S(2)}, u32[]{:S(2)}) collective-permute-start(bf16[2,96,768]{2,1,0:T(8,128)(2,1)S(1)} %get-tuple-element.166.refs_3_), channel_id=1, source_target_pairs={{0,8},{4,12},{8,0},{12,4},{16,24},{20,28},{24,16},{28,20},{1,9},{5... | collective-permute-start | bytes 884744 | tf_op jit(solution)/shard_map/ppermute | solution.py:82
  133.5 4.1 %collective-permute-start.37 = (bf16[16,768]{1,0:T(8,128)(2,1)S(1)}, bf16[16,768]{1,0:T(8,128)(2,1)S(1)}, u32[]{:S(2)}, u32[]{:S(2)}) collective-permute-start(bf16[16,768]{1,0:T(8,128)(2,1)S(1)} %get-tuple-element.163.refs_0_.refs_4_), channel_id=1, source_target_pairs={{0,2},{1,3},{2,0},{3,1},{4,6},{5,7},{6,4},{7,5},{8,10},{9,11},{10,... | collective-permute-start | bytes 73736 | tf_op jit(solution)/shard_map/ppermute | solution.py:82
  138.4 5.7 %collective-permute-start.42 = (bf16[4,16,768]{2,1,0:T(8,128)(2,1)S(1)}, bf16[4,16,768]{2,1,0:T(8,128)(2,1)S(1)}, u32[]{:S(2)}, u32[]{:S(2)}) collective-permute-start(bf16[4,16,768]{2,1,0:T(8,128)(2,1)S(1)} %get-tuple-element.167.refs_0_), channel_id=1, source_target_pairs={{0,4},{4,0},{8,12},{12,8},{16,20},{20,16},{24,28},{28,24},{1,5},{5... | collective-permute-start | bytes 294920 | tf_op jit(solution)/shard_map/ppermute | solution.py:82
  139.1 12.0 %collective-permute-start.51 = (bf16[1,96,768]{2,1,0:T(8,128)(2,1)S(1)}, bf16[1,96,768]{2,1,0:T(8,128)(2,1)S(1)}, u32[]{:S(2)}, u32[]{:S(2)}) collective-permute-start(bf16[1,96,768]{2,1,0:T(8,128)(2,1)S(1)} %get-tuple-element.165.refs_2_), channel_id=1, source_target_pairs={{0,16},{4,20},{8,24},{12,28},{16,0},{20,4},{24,8},{28,12},{1,17},{... | collective-permute-start | bytes 442376 | tf_op jit(solution)/shard_map/ppermute | solution.py:82
  144.2 10.7 %collective-permute-start.43 = (bf16[2,16,768]{2,1,0:T(8,128)(2,1)S(1)}, bf16[2,16,768]{2,1,0:T(8,128)(2,1)S(1)}, u32[]{:S(2)}, u32[]{:S(2)}) collective-permute-start(bf16[2,16,768]{2,1,0:T(8,128)(2,1)S(1)} %get-tuple-element.180), channel_id=1, source_target_pairs={{0,8},{4,12},{8,0},{12,4},{16,24},{20,28},{24,16},{28,20},{1,9},{5... | collective-permute-start | bytes 147464 | tf_op jit(solution)/shard_map/ppermute | solution.py:82
  146.7 8.1 %collective-permute-start.44 = (bf16[2,16,768]{2,1,0:T(8,128)(2,1)S(1)}, bf16[2,16,768]{2,1,0:T(8,128)(2,1)S(1)}, u32[]{:S(2)}, u32[]{:S(2)}) collective-permute-start(bf16[2,16,768]{2,1,0:T(8,128)(2,1)S(1)} %get-tuple-element.181), channel_id=1, source_target_pairs={{0,16},{4,20},{8,24},{12,28},{16,0},{20,4},{24,8},{28,12},{1,17},{... | collective-permute-start | bytes 147464 | tf_op jit(solution)/shard_map/ppermute | solution.py:82
  147.8 7.1 %collective-permute-start.45 = (bf16[2,16,768]{2,1,0:T(8,128)(2,1)S(1)}, bf16[2,16,768]{2,1,0:T(8,128)(2,1)S(1)}, u32[]{:S(2)}, u32[]{:S(2)}) collective-permute-start(bf16[2,16,768]{2,1,0:T(8,128)(2,1)S(1)} %get-tuple-element.182), channel_id=1, source_target_pairs={{0,24},{4,28},{8,16},{12,20},{16,8},{20,12},{24,0},{28,4},{1,25},{... | collective-permute-start | bytes 147464 | tf_op jit(solution)/shard_map/ppermute | solution.py:82
  151.9 19.0 %collective-permute-start.52 = (bf16[1,96,768]{2,1,0:T(8,128)(2,1)S(1)}, bf16[1,96,768]{2,1,0:T(8,128)(2,1)S(1)}, u32[]{:S(2)}, u32[]{:S(2)}) collective-permute-start(bf16[1,96,768]{2,1,0:T(8,128)(2,1)S(1)} %get-tuple-element.177.refs_1_), channel_id=1, source_target_pairs={{0,16},{4,20},{8,24},{12,28},{16,0},{20,4},{24,8},{28,12},{1,17},{... | collective-permute-start | bytes 442376 | tf_op jit(solution)/shard_map/ppermute | solution.py:82
  153.9 10.0 %collective-permute-start.40 = (bf16[2,96,768]{2,1,0:T(8,128)(2,1)S(1)}, bf16[2,96,768]{2,1,0:T(8,128)(2,1)S(1)}, u32[]{:S(2)}, u32[]{:S(2)}) collective-permute-start(bf16[2,96,768]{2,1,0:T(8,128)(2,1)S(1)} %get-tuple-element.174.refs_0_), channel_id=1, source_target_pairs={{0,8},{4,12},{8,0},{12,4},{16,24},{20,28},{24,16},{28,20},{1,9},{5... | collective-permute-start | bytes 884744 | tf_op jit(solution)/shard_map/ppermute | solution.py:82
  155.9 9.3 %collective-permute-start.46 = (f32[4,8,128]{2,1,0:T(8,128)S(1)}, f32[4,8,128]{2,1,0:T(8,128)S(1)}, u32[]{:S(2)}, u32[]{:S(2)}) collective-permute-start(f32[4,8,128]{2,1,0:T(8,128)S(1)} %get-tuple-element.184), channel_id=1, source_target_pairs={{0,4},{4,0},{8,12},{12,8},{16,20},{20,16},{24,28},{28,24},{1,5},{5... | collective-permute-start | bytes 49160 | tf_op jit(solution)/shard_map/ppermute | solution.py:82
  164.0 10.4 %collective-permute-start.50 = (bf16[1,96,768]{2,1,0:T(8,128)(2,1)S(1)}, bf16[1,96,768]{2,1,0:T(8,128)(2,1)S(1)}, u32[]{:S(2)}, u32[]{:S(2)}) collective-permute-start(bf16[1,96,768]{2,1,0:T(8,128)(2,1)S(1)} %get-tuple-element.175.refs_0_), channel_id=1, source_target_pairs={{0,16},{4,20},{8,24},{12,28},{16,0},{20,4},{24,8},{28,12},{1,17},{... | collective-permute-start | bytes 442376 | tf_op jit(solution)/shard_map/ppermute | solution.py:82
  165.1 6.5 %collective-permute-start.47 = (f32[2,8,128]{2,1,0:T(8,128)S(1)}, f32[2,8,128]{2,1,0:T(8,128)S(1)}, u32[]{:S(2)}, u32[]{:S(2)}) collective-permute-start(f32[2,8,128]{2,1,0:T(8,128)S(1)} %get-tuple-element.186), channel_id=1, source_target_pairs={{0,8},{4,12},{8,0},{12,4},{16,24},{20,28},{24,16},{28,20},{1,9},{5... | collective-permute-start | bytes 24584 | tf_op jit(solution)/shard_map/ppermute | solution.py:82
  166.8 5.2 %collective-permute-start.48 = (f32[2,8,128]{2,1,0:T(8,128)S(1)}, f32[2,8,128]{2,1,0:T(8,128)S(1)}, u32[]{:S(2)}, u32[]{:S(2)}) collective-permute-start(f32[2,8,128]{2,1,0:T(8,128)S(1)} %get-tuple-element.187), channel_id=1, source_target_pairs={{0,16},{4,20},{8,24},{12,28},{16,0},{20,4},{24,8},{28,12},{1,17},{... | collective-permute-start | bytes 24584 | tf_op jit(solution)/shard_map/ppermute | solution.py:82
  168.2 5.4 %collective-permute-start.49 = (f32[2,8,128]{2,1,0:T(8,128)S(1)}, f32[2,8,128]{2,1,0:T(8,128)S(1)}, u32[]{:S(2)}, u32[]{:S(2)}) collective-permute-start(f32[2,8,128]{2,1,0:T(8,128)S(1)} %get-tuple-element.188), channel_id=1, source_target_pairs={{0,24},{4,28},{8,16},{12,20},{16,8},{20,12},{24,0},{28,4},{1,25},{... | collective-permute-start | bytes 24584 | tf_op jit(solution)/shard_map/ppermute | solution.py:82
  (25 other events, 176.5 us)

commit v6 on v5

--- a/solution.py
+++ b/solution.py
@@ -140,7 +140,7 @@
         out[1] = got[z]
 
 
-def exchange(keep, send, ordered=()):
+def exchange(keep, send, ordered=(), got=None):
     size = keep.shape[0]
     piece = keep.shape[1:]
     if size != 4:
@@ -151,7 +151,7 @@
             jnp.take(whole, order, axis=0), "fsdp", split_axis=0, concat_axis=0, tiled=True
         )
         return [jnp.take(got, order, axis=0)]
-    got = swap(send, "fsdp", 1)
+    got = swap(send, "fsdp", 1) if got is None else got
     pairs = call(
         pair_kernel, "pairs", [((2, *piece), keep.dtype)] * size, [keep, got], ordered=ordered
     )
@@ -163,11 +163,22 @@
     return arrays[k // per].at[k % per]
 
 
-def attn_own_kernel(qkv, proj, out):
+def both_own_kernel(qkv, proj, first, out):
     cols = qkv.shape[2]
     for j in range(3):
         out[:, j * cols : (j + 1) * cols] = qkv[j]
-    out[:, 3 * cols :] = proj[...].T
+    out[:, 3 * cols : 4 * cols] = proj[...].T
+    out[:, 4 * cols :] = first[...]
+
+
+def join_split_kernel(a, b, *outs):
+    half = a.shape[0]
+    lane = 0
+    for out in outs:
+        here = slice(lane, lane + out.shape[2])
+        out[:half] = a[:, :, here]
+        out[half:] = b[:, :, here]
+        lane += out.shape[2]
 
 
 def copy_kernel(value, out):
@@ -391,25 +402,31 @@
         bias_out[0][...] = jnp.sum(right[...].astype(F32), axis=0, keepdims=True)
 
 
-def mlp_out_kernel(act, second, keep, send):
+def mlp_out_kernel(act, second, x0, x1, x2, x3, bias, keep, send, sums, *, latents):
     rows = keep.shape[0] // 2
-    for b in range(4):
+    part = rows // latents
+    sums[...] = jnp.zeros_like(sums)
+    for b, x in enumerate((x0, x1, x2, x3)):
         at = (b // 2) * rows
         out = send if b % 2 else keep
         value = dot(act[b * rows : (b + 1) * rows, :], second[...], (1, 1))
         out[at : at + rows, :] = value.astype(BF)
-
-
-def output_kernel(middle, x, p0, p1, bias, mod, out, sums):
+        if b == 0:
+            value = value + bias[...]
+        grad = value * x[rows:, :].astype(F32)
+        for l in range(latents):
+            sums[l : l + 1, :] += jnp.sum(
+                grad[l * part : (l + 1) * part], axis=0, keepdims=True
+            )
+
+
+def output_kernel(middle, p0, p1, bias, mod, out):
     latents = mod.shape[0] // 6
-    size = middle.shape[0]
-    rows = size // latents
+    rows = middle.shape[0] // latents
     for l in range(latents):
         here = slice(l * rows, (l + 1) * rows)
         branch = bias[...] + p0[here, :] + p1[here, :].astype(F32)
-        cot = x[size + l * rows : size + (l + 1) * rows, :].astype(F32)
         out[here, :] = (middle[here, :] + mod[6 * l + 5 : 6 * l + 6, :] * branch).astype(BF)
-        sums[l : l + 1, :] = jnp.sum(cot * branch, axis=0, keepdims=True)
 
 
 def middle_back_kernel(x, middle, branch, p0, p1, mod, grad_out, out, sums):
@@ -648,15 +665,15 @@
     qkv_own = query_key_value_weight.transpose(1, 0, 2)
     first_ops = []
     if direct:
-        attn_own = call(
-            attn_own_kernel,
-            "attn_own",
-            [((feat, 4 * cols), BF)],
-            [qkv_own, attention_output_weight],
+        both_own = call(
+            both_own_kernel,
+            "both_own",
+            [((feat, 4 * cols + hidden), BF)],
+            [qkv_own, attention_output_weight, expand_weight],
             fetch=True,
         )[0]
-        first_ops = [attn_own]
-        attn_two = join(attn_own, swap(attn_own, "fsdp", 4))
+        first_ops = [both_own]
+        both_far = swap(both_own, "fsdp", 4)
 
     half = count // 2
     bias_own = jnp.concatenate(
@@ -671,7 +688,9 @@
         scratch=[pltpu.VMEM((16, 128), F32)],
         ordered=first_ops,
     )
-    cond_got = exchange(cond_keep, cond_send, [attn_two] if direct else ())
+    if direct:
+        both_two = join(both_own, both_far, [cond_send])
+    cond_got = exchange(cond_keep, cond_send, [both_two] if direct else ())
 
     bias_row = lax.dynamic_update_slice(
         jnp.zeros((1, mod_part * count), F32),
@@ -691,7 +710,7 @@
     x_own = jnp.stack([inputs.transpose(1, 0, 2), out_cotangent.transpose(1, 0, 2)])
     x_own = x_own.reshape(2 * rows, width)
     x_own = call(
-        copy_kernel, "tokens", [((2 * rows, width), BF)], [x_own], ordered=cond_got
+        copy_kernel, "tokens", [((2 * rows, width), BF)], [x_own], ordered=cond_got[:1]
     )[0]
     x_blocks = tp_gather(x_own)
 
@@ -699,23 +718,28 @@
         half_one = halve(mod_keep, mod_send, 1)
         half_two = halve(*half_one, 2)
         mod_parts = [half_two[0], swap(half_two[1], "fsdp", 4)]
-        attn_four = join(attn_two, swap(attn_two, "fsdp", 2), [mod_send])
+        attn_four, first_early = call(
+            join_split_kernel,
+            "join_split",
+            [((4, feat, 4 * cols), BF), ((4, feat, hidden), BF)],
+            [both_two, swap(both_two, "fsdp", 2)],
+            ordered=[half_one[1]],
+        )
         attn_other = swap(attn_four, "fsdp", 1)
-        first_own = call(
+        first_four = call(
             copy_kernel,
-            "first_own",
-            [((feat, hidden), BF)],
-            [expand_weight],
-            ordered=[half_two[1]],
-            fetch=True,
+            "first_sent",
+            [((4, feat, hidden), BF)],
+            [first_early],
+            ordered=[attn_other],
         )[0]
-        first_two, first_four, first_other = gather_steps(first_own)
+        first_other = swap(first_four, "fsdp", 1)
         second_own = call(
             copy_kernel,
             "second_own",
             [((feat, hidden), BF)],
             [contract_weight.T],
-            ordered=[first_four],
+            ordered=[mod_parts[1]],
             fetch=True,
         )[0]
         second_two, second_four, second_other = gather_steps(second_own)
@@ -740,7 +764,7 @@
             [second_four, second_other],
             [rank],
         )[0]
-        steps = [[attn_four], [first_two], [first_four], [second_two], [second_four, first_full]]
+        steps = [[attn_four], [first_four], [second_two], [], [second_four, first_full]]
     else:
         steps = [[]] * 5
         mod_parts = [scatter_pieces(mod_keep, mod_send)]
@@ -813,11 +837,11 @@
         )
         first_done = [fc1_part]
     grad_in = tp_scatter(keep, send, first_done)
-    out_keep, out_send = call(
-        mlp_out_kernel,
+    out_keep, out_send, gates = call(
+        functools.partial(mlp_out_kernel, latents=latents),
         "mlp_out",
-        [pair, pair],
-        [act, second_full],
+        [pair, pair, ((8, width), F32)],
+        [act, second_full, *x_blocks, second_bias],
         ordered=[grad_in[0]],
         flops=1.5e9,
     )
@@ -855,21 +879,14 @@
         ordered=[second_keep],
     )
     a_blocks = tp_gather(grad_attn)
-    mlp_parts = tp_scatter(out_keep, out_send, [a_blocks[2]])
     back_rows, grads, keep, send, qkv_part = call(
         functools.partial(attn_back_kernel, latents=latents),
         "attention_back",
         [((tokens, width), BF), ((tokens, 3 * cols), BF), pair, pair, ((1, 3 * cols), F32)],
         [*a_blocks, qkv_full, proj_full, qkv],
-        ordered=[mlp_parts[0], *steps[0]],
-    )
-    output, gates = call(
-        output_kernel,
-        "output",
-        [block, ((8, width), F32)],
-        [middle, x_own, *mlp_parts, second_bias, mod],
-    )
-    grad_in = tp_scatter(keep, send, [gates])
+        ordered=steps[0],
+    )
+    grad_in = tp_scatter(keep, send)
     if direct:
         attn_keep, attn_send = call(
             attn_grad_kernel,
@@ -911,8 +928,10 @@
         scratch=[pltpu.VMEM((tp_count, 16, width), F32), pltpu.VMEM((16, width), F32)],
         ordered=tail[0],
     )
+    spread_got = None
     if direct:
-        attn_half = halve(attn_keep, attn_send, 1, [spread_send])
+        spread_got = swap(spread_send, "fsdp", 1)
+        attn_half = halve(attn_keep, attn_send, 1, [spread_got])
         attn_own_sum, attn_out = halve(*attn_half, 2)
         qkv_sum, proj_sum = call(
             attn_add_kernel,
@@ -921,7 +940,7 @@
             [attn_own_sum, swap(attn_out, "fsdp", 4)],
         )
         qkv_sum = qkv_sum.transpose(1, 0, 2)
-        second_one = halve(*second_half, 2, [spread_send])
+        second_one = halve(*second_half, 2, [spread_got])
         second_sum = last_sum(*second_one, 4)
         tail[1] = [attn_half[1], second_one[1]]
         tail[2] = [attn_out]
@@ -930,17 +949,22 @@
         "silu_columns",
         [((half, 8, 128), F32)] * 2
         + [((count * latents, 6 * width), BF), ((1, width), F32)],
-        [*exchange(spread_keep, spread_send, tail[1]), ada_weight],
+        [*exchange(spread_keep, spread_send, tail[1], spread_got), ada_weight],
         scratch=[
             pltpu.VMEM((6, count * latents, width), F32),
             pltpu.VMEM((count, 8, 128), F32),
         ],
-    )
+        ordered=tail[2],
+    )
+    mlp_parts = tp_scatter(out_keep, out_send, [silu_send])
+    output = call(
+        output_kernel, "output", [block], [middle, *mlp_parts, second_bias, mod]
+    )[0]
     cond_grad = call(
         functools.partial(cond_kernel, latents=latents, feat=feat),
         "cond_grad",
         [((latents, width), F32)],
-        [*exchange(silu_keep, silu_send, tail[2]), conditioning],
+        [*exchange(silu_keep, silu_send), conditioning],
         [rank],
         scratch=[pltpu.VMEM((count, 8, 128), F32)],
     )[0]

time: 176 us -> 195 us (1.11)
  starting transfers between devices: 50.9 us -> 60.6 us
  waiting for transfers between devices: 79.1 us -> 85.4 us
  local copies, waits for them, and re-layouts: 9.97 us -> 13.8 us
    ppermute x53 -> x51, starting transfers between devices: 50.9 us -> 60.6 us  [swap(): return lax.ppermute(block, axis, [(i, i ^ offset) for i in range(count)])]
    ppermute x53 -> x51, waiting for transfers between devices: 79.1 us -> 85.4 us  [swap(): return lax.ppermute(block, axis, [(i, i ^ offset) for i in range(count)])]
    unnamed x40 -> x36, local copies, waits for them, and re-layouts: 5.22 us -> 9.02 us
    pallas_call x51 -> x49, Pallas kernels: 29.4 us -> 29.7 us  [call(): pl.pallas_call(body, out_shape=[jax.ShapeDtypeStruct(shape, dtype) for sh...]
  transfers between devices with their start and end apart: 53 -> 51, of which waited for: 24 -> 23; matrix products, arithmetic and copies ran while one was open for 5% -> 4% of each run, Pallas kernels for 12% -> 11%
where the time goes in v6:
time: 195 us; the launch traced here: 194 us
  waiting for transfers between devices  85.4 us (44%)
  starting transfers between devices  60.6 us (31%)
  Pallas kernels  29.7 us (15%)
  local copies, waits for them, and re-layouts  13.8 us (7%)
  other arithmetic  2.01 us (1%)
    ppermute x51, waiting for transfers between devices, swap(): return lax.ppermute(block, axis, [(i, i ^ offset) for i in range(count)])  85.4 us
    ppermute x51, starting transfers between devices, swap(): return lax.ppermute(block, axis, [(i, i ^ offset) for i in range(count)])  60.6 us
    pallas_call x49, Pallas kernels, call(): pl.pallas_call(body, out_shape=[jax.ShapeDtypeStruct(shape, dtype) for sh...  29.7 us
    unnamed x36, local copies, waits for them, and re-layouts  9.02 us
  transfers between devices with their start and end apart: 51, of which 23 were waited for; matrix products, arithmetic and copies ran while one was open for 4% of the time, Pallas kernels for 11%

profile of v6, /device:TPU:0, one launch (start us, length us, event | category | flops | bytes accessed | tf_op | source)
XLA Modules:
  0.0 194.2 jit_solution(4445205299388825515)
XLA Ops:
  3.9 4.1 %collective-permute-start = (bf16[96,1536]{1,0:T(8,128)(2,1)S(1)}, bf16[96,1536]{1,0:T(8,128)(2,1)S(1)}, u32[]{:S(2)}, u32[]{:S(2)}) collective-permute-start(bf16[96,1536]{1,0:T(8,128)(2,1)S(1)} %both_own.1.refs_1_), channel_id=1, source_target_pairs={{0,16},{4,20},{8,24},{12,28},{16,0},{20,4},{24,8},{28,12},{1,17},{... | collective-permute-start | bytes 884744 | tf_op jit(solution)/shard_map/ppermute | solution.py:82
  10.7 10.6 %collective-permute-done.refs_2_ = bf16[96,1536]{1,0:T(8,128)(2,1)S(1)} collective-permute-done((bf16[96,1536]{1,0:T(8,128)(2,1)S(1)}, bf16[96,1536]{1,0:T(8,128)(2,1)S(1)}, u32[]{:S(2)}, u32[]{:S(2)}) %collective-permute-start) | collective-permute-done | bytes 294944 | tf_op jit(solution)/shard_map/ppermute | solution.py:82
  24.3 1.8 collective-permute-done.1.refs_2_
  26.1 1.6 collective-permute-start.12
  29.1 2.1 %collective-permute-start.3 = (f32[2,16,128]{2,1,0:T(8,128)S(1)}, f32[2,16,128]{2,1,0:T(8,128)S(1)}, u32[]{:S(2)}, u32[]{:S(2)}) collective-permute-start(f32[2,16,128]{2,1,0:T(8,128)S(1)} %get-tuple-element.110), channel_id=1, source_target_pairs={{0,16},{4,20},{8,24},{12,28},{16,0},{20,4},{24,8},{28,12},{1,17},{... | collective-permute-start | bytes 49160 | tf_op jit(solution)/shard_map/ppermute | solution.py:82
  32.7 3.9 %collective-permute-done.2.refs_1_.refs_4_ = f32[2,16,128]{2,1,0:T(8,128)S(1)} collective-permute-done((f32[2,16,128]{2,1,0:T(8,128)S(1)}, f32[2,16,128]{2,1,0:T(8,128)S(1)}, u32[]{:S(2)}, u32[]{:S(2)}) %collective-permute-start.2) | collective-permute-done | bytes 16416 | tf_op jit(solution)/shard_map/ppermute | solution.py:82
  36.7 2.9 %collective-permute-done.4.refs_3_.refs_6_ = f32[2,16,128]{2,1,0:T(8,128)S(1)} collective-permute-done((f32[2,16,128]{2,1,0:T(8,128)S(1)}, f32[2,16,128]{2,1,0:T(8,128)S(1)}, u32[]{:S(2)}, u32[]{:S(2)}) %collective-permute-start.4) | collective-permute-done | bytes 16416 | tf_op jit(solution)/shard_map/ppermute | solution.py:82
  39.8 1.6 collective-permute-start.5
  41.4 3.1 %collective-permute-done.5.refs_1_ = bf16[4,16,768]{2,1,0:T(8,128)(2,1)S(1)} collective-permute-done((bf16[4,16,768]{2,1,0:T(8,128)(2,1)S(1)}, bf16[4,16,768]{2,1,0:T(8,128)(2,1)S(1)}, u32[]{:S(2)}, u32[]{:S(2)}) %collective-permute-start.5) | collective-permute-done | bytes 98336 | tf_op jit(solution)/shard_map/ppermute | solution.py:82
  46.5 1.6 collective-permute-start.10
  49.0 3.7 %collective-permute-done.6.refs_1_ = bf16[2,16,768]{2,1,0:T(8,128)(2,1)S(1)} collective-permute-done((bf16[2,16,768]{2,1,0:T(8,128)(2,1)S(1)}, bf16[2,16,768]{2,1,0:T(8,128)(2,1)S(1)}, u32[]{:S(2)}, u32[]{:S(2)}) %collective-permute-start.6) | collective-permute-done | bytes 49184 | tf_op jit(solution)/shard_map/ppermute | solution.py:82
  54.2 4.7 %collective-permute-done.7.refs_0_.refs_7_ = bf16[1,16,768]{2,1,0:T(8,128)(2,1)S(1)} collective-permute-done((bf16[1,16,768]{2,1,0:T(8,128)(2,1)}, bf16[1,16,768]{2,1,0:T(8,128)(2,1)S(1)}, u32[]{:S(2)}, u32[]{:S(2)}) %collective-permute-start.7) | collective-permute-done | bytes 24608 | tf_op jit(solution)/shard_map/ppermute | solution.py:82
  62.7 1.7 first_norm.1
  64.7 2.5 %attention.1 = (bf16[512,576]{1,0:T(8,128)(2,1)S(1)}, bf16[512,192]{1,0:T(8,128)(2,1)S(1)}, bf16[256,768]{1,0:T(8,128)(2,1)S(1)}, bf16[256,768]{1,0:T(8,128)(2,1)S(1)}) custom-call(bf16[4,96,768]{2,1,0:T(8,128)(2,1)S(1)} %first_sent.1.refs_0_.refs_1_, bf16[512,768]{1,0:T(8,128)(2,1)S(1)} %get-tuple-element.121.refs_1_.refs_2_, ...), custom_call_target="tpu_custom_call" | custom-call | flops 1 | bytes 1 | tf_op jit(solution)/shard_map/attention/pallas_call | solution.py:50
  68.0 2.1 %collective-permute-start.15 = (bf16[2,96,768]{2,1,0:T(8,128)(2,1)S(1)}, bf16[2,96,768]{2,1,0:T(8,128)(2,1)S(1)}, u32[]{:S(2)}, u32[]{:S(2)}) collective-permute-start(bf16[2,96,768]{2,1,0:T(8,128)(2,1)S(1)} %join.4.refs_0_), channel_id=1, source_target_pairs={{0,8},{4,12},{8,0},{12,4},{16,24},{20,28},{24,16},{28,20},{1,9},{5... | collective-permute-start | bytes 884744 | tf_op jit(solution)/shard_map/ppermute | solution.py:82
  70.1 1.6 collective-permute-start.17
  71.7 5.7 %collective-permute-done.15.refs_1_ = bf16[2,96,768]{2,1,0:T(8,128)(2,1)S(1)} collective-permute-done((bf16[2,96,768]{2,1,0:T(8,128)(2,1)S(1)}, bf16[2,96,768]{2,1,0:T(8,128)(2,1)S(1)}, u32[]{:S(2)}, u32[]{:S(2)}) %collective-permute-start.15) | collective-permute-done | bytes 294944 | tf_op jit(solution)/shard_map/ppermute | solution.py:82
  77.4 1.6 collective-permute-start.21
  80.3 3.2 %collective-permute-done.16.refs_2_ = bf16[4,96,768]{2,1,0:T(8,128)(2,1)S(1)} collective-permute-done((bf16[4,96,768]{2,1,0:T(8,128)(2,1)S(1)}, bf16[4,96,768]{2,1,0:T(8,128)(2,1)S(1)}, u32[]{:S(2)}, u32[]{:S(2)}) %collective-permute-start.16) | collective-permute-done | bytes 589856 | tf_op jit(solution)/shard_map/ppermute | solution.py:82
  83.9 1.6 collective-permute-start.19
  85.5 4.5 %collective-permute-done.19.refs_2_ = bf16[128,768]{1,0:T(8,128)(2,1)S(1)} collective-permute-done((bf16[128,768]{1,0:T(8,128)(2,1)S(1)}, bf16[128,768]{1,0:T(8,128)(2,1)S(1)}, u32[]{:S(2)}, u32[]{:S(2)}) %collective-permute-start.19) | collective-permute-done | bytes 196640 | tf_op jit(solution)/shard_map/ppermute | solution.py:82
  90.0 5.7 %collective-permute-done.21.refs_2_ = bf16[4,96,768]{2,1,0:T(8,128)(2,1)S(1)} collective-permute-done((bf16[4,96,768]{2,1,0:T(8,128)(2,1)S(1)}, bf16[4,96,768]{2,1,0:T(8,128)(2,1)S(1)}, u32[]{:S(2)}, u32[]{:S(2)}) %collective-permute-start.21) | collective-permute-done | bytes 589856 | tf_op jit(solution)/shard_map/ppermute | solution.py:82
  95.8 3.1 %mlp.1 = (bf16[512,768]{1,0:T(8,128)(2,1)S(1)}, bf16[512,768]{1,0:T(8,128)(2,1)S(1)}, bf16[512,768]{1,0:T(8,128)(2,1)S(1)}, bf16[256,768]{1,0:T(8,128)(2,1)S(1)}, bf16[256,768]{1,0:T(8,128)(2,1)S(1)}) custom-call(bf16[128,768]{1,0:T(8,128)(2,1)S(1)} %get-tuple-element.133.refs_0_, bf16[128,768]{1,0:T(8,128)(2,1)S(1)} %collective-permute-done.18.refs_1_, ...), custom_call_target="tpu_custom_call" | custom-call | flops 1 | bytes 1 | tf_op jit(solution)/shard_map/mlp/pallas_call | solution.py:50
  101.0 1.6 collective-permute-start.23
  102.6 2.8 %mlp_out.1 = (bf16[256,768]{1,0:T(8,128)(2,1)S(1)}, bf16[256,768]{1,0:T(8,128)(2,1)S(1)}, f32[8,768]{1,0:T(8,128)S(1)}) custom-call(f32[128,768]{1,0:T(8,128)S(1)} %get-tuple-element.140.refs_0_.refs_4_, bf16[512,768]{1,0:T(8,128)(2,1)S(1)} %get-tuple-element.141.refs_1_.refs_3_, bf16[768,768]{1,0:T(8,128)(2,1)S(1)} %second_weights.1.refs_6_.refs_2_, ...), custom_call_target="tpu_custom_call" | custom-call | flops 1500000000 | bytes 1 | tf_op jit(solution)/shard_map/mlp_out/pallas_call | solution.py:50
  106.3 1.7 collective-permute-done.23.refs_5_
  108.5 1.6 collective-permute-start.26
  110.1 4.7 %collective-permute-done.26.refs_4_ = bf16[128,768]{1,0:T(8,128)(2,1)S(1)} collective-permute-done((bf16[128,768]{1,0:T(8,128)(2,1)S(1)}, bf16[128,768]{1,0:T(8,128)(2,1)S(1)}, u32[]{:S(2)}, u32[]{:S(2)}) %collective-permute-start.26) | collective-permute-done | bytes 196640 | tf_op jit(solution)/shard_map/ppermute | solution.py:82
  116.3 4.7 %attention_back.1 = (bf16[512,768]{1,0:T(8,128)(2,1)S(1)}, bf16[512,576]{1,0:T(8,128)(2,1)S(1)}, bf16[256,768]{1,0:T(8,128)(2,1)S(1)}, bf16[256,768]{1,0:T(8,128)(2,1)S(1)}, f32[1,576]{1,0:T(1,128)S(1)}) custom-call(bf16[2,96,768]{2,1,0:T(8,128)(2,1)S(1)} %get-tuple-element.150.refs_0_, bf16[4,96,768]{2,1,0:T(8,128)(2,1)S(1)} %second_sent.1.refs_1_, ...), custom_call_target="tpu_custom_call" | custom-call | flops 1 | bytes 1 | tf_op jit(solution)/shard_map/attention_back/pallas_call | solution.py:50
  122.9 1.9 attn_weight_grad.1
  124.8 1.5 collective-permute-start.36
  126.3 2.0 %collective-permute-start.30 = (bf16[2,96,768]{2,1,0:T(8,128)(2,1)S(1)}, bf16[2,96,768]{2,1,0:T(8,128)(2,1)S(1)}, u32[]{:S(2)}, u32[]{:S(2)}) collective-permute-start(bf16[2,96,768]{2,1,0:T(8,128)(2,1)S(1)} %get-tuple-element.150.refs_0_), channel_id=1, source_target_pairs={{0,8},{4,12},{8,0},{12,4},{16,24},{20,28},{24,16},{28,20},{1,9},{5... | collective-permute-start | bytes 884744 | tf_op jit(solution)/shard_map/ppermute | solution.py:82
  129.8 4.9 %collective-permute-done.29.refs_3_ = bf16[128,768]{1,0:T(8,128)(2,1)S(1)} collective-permute-done((bf16[128,768]{1,0:T(8,128)(2,1)S(1)}, bf16[128,768]{1,0:T(8,128)(2,1)S(1)}, u32[]{:S(2)}, u32[]{:S(2)}) %collective-permute-start.29) | collective-permute-done | bytes 196640 | tf_op jit(solution)/shard_map/ppermute | solution.py:82
  135.1 2.2 %collective-permute-done.31.refs_2_ = bf16[4,96,768]{2,1,0:T(8,128)(2,1)S(1)} collective-permute-done((bf16[4,96,768]{2,1,0:T(8,128)(2,1)S(1)}, bf16[4,96,768]{2,1,0:T(8,128)(2,1)S(1)}, u32[]{:S(2)}, u32[]{:S(2)}) %collective-permute-start.31) | collective-permute-done | bytes 589856 | tf_op jit(solution)/shard_map/ppermute | solution.py:82
  137.5 2.1 %collective-permute-start.38 = (bf16[2,96,768]{2,1,0:T(8,128)(2,1)S(1)}, bf16[2,96,768]{2,1,0:T(8,128)(2,1)S(1)}, u32[]{:S(2)}, u32[]{:S(2)}) collective-permute-start(bf16[2,96,768]{2,1,0:T(8,128)(2,1)S(1)} %get-tuple-element.164.refs_3_), channel_id=1, source_target_pairs={{0,8},{4,12},{8,0},{12,4},{16,24},{20,28},{24,16},{28,20},{1,9},{5... | collective-permute-start | bytes 884744 | tf_op jit(solution)/shard_map/ppermute | solution.py:82
  139.6 1.5 collective-permute-start.33
  144.3 1.5 collective-permute-start.35
  145.8 5.7 %collective-permute-done.35.refs_0_.refs_3_ = bf16[4,16,768]{2,1,0:T(8,128)(2,1)S(1)} collective-permute-done((bf16[4,16,768]{2,1,0:T(8,128)(2,1)S(1)}, bf16[4,16,768]{2,1,0:T(8,128)(2,1)S(1)}, u32[]{:S(2)}, u32[]{:S(2)}) %collective-permute-start.35) | collective-permute-done | bytes 98336 | tf_op jit(solution)/shard_map/ppermute | solution.py:82
  151.7 2.1 %collective-permute-start.37 = (bf16[2,96,768]{2,1,0:T(8,128)(2,1)S(1)}, bf16[2,96,768]{2,1,0:T(8,128)(2,1)S(1)}, u32[]{:S(2)}, u32[]{:S(2)}) collective-permute-start(bf16[2,96,768]{2,1,0:T(8,128)(2,1)S(1)} %get-tuple-element.172.refs_0_), channel_id=1, source_target_pairs={{0,8},{4,12},{8,0},{12,4},{16,24},{20,28},{24,16},{28,20},{1,9},{5... | collective-permute-start | bytes 884744 | tf_op jit(solution)/shard_map/ppermute | solution.py:82
  154.9 2.0 %collective-permute-start.50 = (bf16[1,96,768]{2,1,0:T(8,128)(2,1)S(1)}, bf16[1,96,768]{2,1,0:T(8,128)(2,1)S(1)}, u32[]{:S(2)}, u32[]{:S(2)}) collective-permute-start(bf16[1,96,768]{2,1,0:T(8,128)(2,1)S(1)} %get-tuple-element.175.refs_1_), channel_id=1, source_target_pairs={{0,16},{4,20},{8,24},{12,28},{16,0},{20,4},{24,8},{28,12},{1,17},{... | collective-permute-start | bytes 442376 | tf_op jit(solution)/shard_map/ppermute | solution.py:82
  157.0 7.4 %collective-permute-done.49.refs_1_ = bf16[1,96,768]{2,1,0:T(8,128)(2,1)S(1)} collective-permute-done((bf16[1,96,768]{2,1,0:T(8,128)(2,1)S(1)}, bf16[1,96,768]{2,1,0:T(8,128)(2,1)S(1)}, u32[]{:S(2)}, u32[]{:S(2)}) %collective-permute-start.49) | collective-permute-done | bytes 147488 | tf_op jit(solution)/shard_map/ppermute | solution.py:82
  164.4 3.4 %collective-permute-start.40 = (bf16[2,16,768]{2,1,0:T(8,128)(2,1)S(1)}, bf16[2,16,768]{2,1,0:T(8,128)(2,1)S(1)}, u32[]{:S(2)}, u32[]{:S(2)}) collective-permute-start(bf16[2,16,768]{2,1,0:T(8,128)(2,1)S(1)} %get-tuple-element.179), channel_id=1, source_target_pairs={{0,16},{4,20},{8,24},{12,28},{16,0},{20,4},{24,8},{28,12},{1,17},{... | collective-permute-start | bytes 147464 | tf_op jit(solution)/shard_map/ppermute | solution.py:82
  167.9 2.6 %collective-permute-done.50.refs_1_ = bf16[1,96,768]{2,1,0:T(8,128)(2,1)S(1)} collective-permute-done((bf16[1,96,768]{2,1,0:T(8,128)(2,1)S(1)}, bf16[1,96,768]{2,1,0:T(8,128)(2,1)S(1)}, u32[]{:S(2)}, u32[]{:S(2)}) %collective-permute-start.50) | collective-permute-done | bytes 147488 | tf_op jit(solution)/shard_map/ppermute | solution.py:82
  170.4 3.6 %collective-permute-start.41 = (bf16[2,16,768]{2,1,0:T(8,128)(2,1)S(1)}, bf16[2,16,768]{2,1,0:T(8,128)(2,1)S(1)}, u32[]{:S(2)}, u32[]{:S(2)}) collective-permute-start(bf16[2,16,768]{2,1,0:T(8,128)(2,1)S(1)} %get-tuple-element.180), channel_id=1, source_target_pairs={{0,24},{4,28},{8,16},{12,20},{16,8},{20,12},{24,0},{28,4},{1,25},{... | collective-permute-start | bytes 147464 | tf_op jit(solution)/shard_map/ppermute | solution.py:82
  179.2 1.6 collective-permute-start.43
  180.7 1.6 fusion
  184.1 2.0 %collective-permute-start.46 = (f32[2,8,128]{2,1,0:T(8,128)S(1)}, f32[2,8,128]{2,1,0:T(8,128)S(1)}, u32[]{:S(2)}, u32[]{:S(2)}) collective-permute-start(f32[2,8,128]{2,1,0:T(8,128)S(1)} %get-tuple-element.189), channel_id=1, source_target_pairs={{0,16},{4,20},{8,24},{12,28},{16,0},{20,4},{24,8},{28,12},{1,17},{... | collective-permute-start | bytes 24584 | tf_op jit(solution)/shard_map/ppermute | solution.py:82
  188.7 2.9 %collective-permute-done.47.refs_4_ = f32[2,8,128]{2,1,0:T(8,128)S(1)} collective-permute-done((f32[2,8,128]{2,1,0:T(8,128)S(1)}, f32[2,8,128]{2,1,0:T(8,128)S(1)}, u32[]{:S(2)}, u32[]{:S(2)}) %collective-permute-start.47) | collective-permute-done | bytes 8224 | tf_op jit(solution)/shard_map/ppermute | solution.py:82
  (154 shorter events, 48.5 us)
Async XLA Ops:
  3.9 17.4 %collective-permute-start = (bf16[96,1536]{1,0:T(8,128)(2,1)S(1)}, bf16[96,1536]{1,0:T(8,128)(2,1)S(1)}, u32[]{:S(2)}, u32[]{:S(2)}) collective-permute-start(bf16[96,1536]{1,0:T(8,128)(2,1)S(1)} %both_own.1.refs_1_), channel_id=1, source_target_pairs={{0,16},{4,20},{8,24},{12,28},{16,0},{20,4},{24,8},{28,12},{1,17},{... | collective-permute-start | bytes 884744 | tf_op jit(solution)/shard_map/ppermute | solution.py:82
  21.4 23.2 %collective-permute-start.9 = (bf16[2,96,1536]{2,1,0:T(8,128)(2,1)S(1)}, bf16[2,96,1536]{2,1,0:T(8,128)(2,1)S(1)}, u32[]{:S(2)}, u32[]{:S(2)}) collective-permute-start(bf16[2,96,1536]{2,1,0:T(8,128)(2,1)S(1)} %join.3.refs_0_.refs_1_), channel_id=1, source_target_pairs={{0,8},{4,12},{8,0},{12,4},{16,24},{20,28},{24,16},{28,20},{1,9},{5... | collective-permute-start | bytes 1769480 | tf_op jit(solution)/shard_map/ppermute | solution.py:82
  22.2 3.9 %collective-permute-start.1 = (f32[4,16,128]{2,1,0:T(8,128)S(1)}, f32[4,16,128]{2,1,0:T(8,128)S(1)}, u32[]{:S(2)}, u32[]{:S(2)}) collective-permute-start(f32[4,16,128]{2,1,0:T(8,128)S(1)} %get-tuple-element.106.refs_0_), channel_id=1, source_target_pairs={{0,4},{4,0},{8,12},{12,8},{16,20},{20,16},{24,28},{28,24},{1,5},{5... | collective-permute-start | bytes 98312 | tf_op jit(solution)/shard_map/ppermute | solution.py:82
  26.1 22.0 %collective-permute-start.12 = (bf16[256,768]{1,0:T(8,128)(2,1)S(1)}, bf16[256,768]{1,0:T(8,128)(2,1)S(1)}, u32[]{:S(2)}, u32[]{:S(2)}) collective-permute-start(bf16[256,768]{1,0:T(8,128)(2,1)S(1)} %tokens.1.refs_2_.refs_1_.refs_3_.refs_0_), channel_id=1, source_target_pairs={{0,2},{1,3},{2,0},{3,1},{4,6},{5,7},{6,4},{7,5},{8,10},{9,11},{10,... | collective-permute-start | bytes 1179656 | tf_op jit(solution)/shard_map/ppermute | solution.py:82
  27.7 9.0 %collective-permute-start.2 = (f32[2,16,128]{2,1,0:T(8,128)S(1)}, f32[2,16,128]{2,1,0:T(8,128)S(1)}, u32[]{:S(2)}, u32[]{:S(2)}) collective-permute-start(f32[2,16,128]{2,1,0:T(8,128)S(1)} %get-tuple-element.109), channel_id=1, source_target_pairs={{0,8},{4,12},{8,0},{12,4},{16,24},{20,28},{24,16},{28,20},{1,9},{5... | collective-permute-start | bytes 49160 | tf_op jit(solution)/shard_map/ppermute | solution.py:82
  29.1 7.6 %collective-permute-start.3 = (f32[2,16,128]{2,1,0:T(8,128)S(1)}, f32[2,16,128]{2,1,0:T(8,128)S(1)}, u32[]{:S(2)}, u32[]{:S(2)}) collective-permute-start(f32[2,16,128]{2,1,0:T(8,128)S(1)} %get-tuple-element.110), channel_id=1, source_target_pairs={{0,16},{4,20},{8,24},{12,28},{16,0},{20,4},{24,8},{28,12},{1,17},{... | collective-permute-start | bytes 49160 | tf_op jit(solution)/shard_map/ppermute | solution.py:82
  31.2 8.4 %collective-permute-start.4 = (f32[2,16,128]{2,1,0:T(8,128)S(1)}, f32[2,16,128]{2,1,0:T(8,128)S(1)}, u32[]{:S(2)}, u32[]{:S(2)}) collective-permute-start(f32[2,16,128]{2,1,0:T(8,128)S(1)} %get-tuple-element.111), channel_id=1, source_target_pairs={{0,24},{4,28},{8,16},{12,20},{16,8},{20,12},{24,0},{28,4},{1,25},{... | collective-permute-start | bytes 49160 | tf_op jit(solution)/shard_map/ppermute | solution.py:82
  39.8 4.7 %collective-permute-start.5 = (bf16[4,16,768]{2,1,0:T(8,128)(2,1)S(1)}, bf16[4,16,768]{2,1,0:T(8,128)(2,1)S(1)}, u32[]{:S(2)}, u32[]{:S(2)}) collective-permute-start(bf16[4,16,768]{2,1,0:T(8,128)(2,1)S(1)} %get-tuple-element.113.refs_2_), channel_id=1, source_target_pairs={{0,4},{4,0},{8,12},{12,8},{16,20},{20,16},{24,28},{28,24},{1,5},{5... | collective-permute-start | bytes 294920 | tf_op jit(solution)/shard_map/ppermute | solution.py:82
  46.5 17.9 %collective-permute-start.10 = (bf16[4,96,768]{2,1,0:T(8,128)(2,1)S(1)}, bf16[4,96,768]{2,1,0:T(8,128)(2,1)S(1)}, u32[]{:S(2)}, u32[]{:S(2)}) collective-permute-start(bf16[4,96,768]{2,1,0:T(8,128)(2,1)S(1)} %get-tuple-element.117.refs_1_), channel_id=1, source_target_pairs={{0,4},{4,0},{8,12},{12,8},{16,20},{20,16},{24,28},{28,24},{1,5},{5... | collective-permute-start | bytes 1769480 | tf_op jit(solution)/shard_map/ppermute | solution.py:82
  48.1 14.0 %collective-permute-start.11 = (bf16[256,768]{1,0:T(8,128)(2,1)S(1)}, bf16[256,768]{1,0:T(8,128)(2,1)}, u32[]{:S(2)}, u32[]{:S(2)}) collective-permute-start(bf16[256,768]{1,0:T(8,128)(2,1)S(1)} %tokens.1.refs_2_.refs_1_.refs_3_.refs_0_), channel_id=1, source_target_pairs={{0,1},{1,0},{2,3},{3,2},{4,5},{5,4},{6,7},{7,6},{8,9},{9,8},{10,11... | collective-permute-start | bytes 1179656 | tf_op jit(solution)/shard_map/ppermute | solution.py:82
  48.1 14.0 %collective-permute-start.13 = (bf16[256,768]{1,0:T(8,128)(2,1)S(1)}, bf16[256,768]{1,0:T(8,128)(2,1)}, u32[]{:S(2)}, u32[]{:S(2)}) collective-permute-start(bf16[256,768]{1,0:T(8,128)(2,1)S(1)} %collective-permute-done.12.refs_4_.refs_3_.refs_5_), channel_id=1, source_target_pairs={{0,1},{1,0},{2,3},{3,2},{4,5},{5,4},{6,7},{7,6},{8,9},{9,8},{10,11... | collective-permute-start | bytes 1179656 | tf_op jit(solution)/shard_map/ppermute | solution.py:82
  48.6 4.1 %collective-permute-start.6 = (bf16[2,16,768]{2,1,0:T(8,128)(2,1)S(1)}, bf16[2,16,768]{2,1,0:T(8,128)(2,1)S(1)}, u32[]{:S(2)}, u32[]{:S(2)}) collective-permute-start(bf16[2,16,768]{2,1,0:T(8,128)(2,1)S(1)} %get-tuple-element.115.refs_0_), channel_id=1, source_target_pairs={{0,8},{4,12},{8,0},{12,4},{16,24},{20,28},{24,16},{28,20},{1,9},{5... | collective-permute-start | bytes 147464 | tf_op jit(solution)/shard_map/ppermute | solution.py:82
  53.9 5.0 %collective-permute-start.7 = (bf16[1,16,768]{2,1,0:T(8,128)(2,1)}, bf16[1,16,768]{2,1,0:T(8,128)(2,1)S(1)}, u32[]{:S(2)}, u32[]{:S(2)}) collective-permute-start(bf16[1,16,768]{2,1,0:T(8,128)(2,1)} %get-tuple-element.116), channel_id=1, source_target_pairs={{0,16},{4,20},{8,24},{12,28},{16,0},{20,4},{24,8},{28,12},{1,17},{... | collective-permute-start | bytes 73736 | tf_op jit(solution)/shard_map/ppermute | solution.py:82
  60.1 7.9 %collective-permute-start.8 = (bf16[96,768]{1,0:T(8,128)(2,1)S(1)}, bf16[96,768]{1,0:T(8,128)(2,1)S(1)}, u32[]{:S(2)}, u32[]{:S(2)}) collective-permute-start(bf16[96,768]{1,0:T(8,128)(2,1)S(1)} %second_own.1.refs_0_), channel_id=1, source_target_pairs={{0,16},{4,20},{8,24},{12,28},{16,0},{20,4},{24,8},{28,12},{1,17},{... | collective-permute-start | bytes 442376 | tf_op jit(solution)/shard_map/ppermute | solution.py:82
  67.3 2.8 %collective-permute-start.14 = (bf16[256,768]{1,0:T(8,128)(2,1)S(1)}, bf16[256,768]{1,0:T(8,128)(2,1)S(1)}, u32[]{:S(2)}, u32[]{:S(2)}) collective-permute-start(bf16[256,768]{1,0:T(8,128)(2,1)S(1)} %get-tuple-element.126), channel_id=1, source_target_pairs={{0,1},{1,0},{2,3},{3,2},{4,5},{5,4},{6,7},{7,6},{8,9},{9,8},{10,11... | collective-permute-start | bytes 1179656 | tf_op jit(solution)/shard_map/ppermute | solution.py:82
  67.3 16.2 %collective-permute-start.16 = (bf16[4,96,768]{2,1,0:T(8,128)(2,1)S(1)}, bf16[4,96,768]{2,1,0:T(8,128)(2,1)S(1)}, u32[]{:S(2)}, u32[]{:S(2)}) collective-permute-start(bf16[4,96,768]{2,1,0:T(8,128)(2,1)S(1)} %first_sent.1.refs_0_.refs_1_), channel_id=1, source_target_pairs={{0,4},{4,0},{8,12},{12,8},{16,20},{20,16},{24,28},{28,24},{1,5},{5... | collective-permute-start | bytes 1769480 | tf_op jit(solution)/shard_map/ppermute | solution.py:82
  68.0 9.4 %collective-permute-start.15 = (bf16[2,96,768]{2,1,0:T(8,128)(2,1)S(1)}, bf16[2,96,768]{2,1,0:T(8,128)(2,1)S(1)}, u32[]{:S(2)}, u32[]{:S(2)}) collective-permute-start(bf16[2,96,768]{2,1,0:T(8,128)(2,1)S(1)} %join.4.refs_0_), channel_id=1, source_target_pairs={{0,8},{4,12},{8,0},{12,4},{16,24},{20,28},{24,16},{28,20},{1,9},{5... | collective-permute-start | bytes 884744 | tf_op jit(solution)/shard_map/ppermute | solution.py:82
  70.1 13.5 %collective-permute-start.17 = (bf16[128,768]{1,0:T(8,128)(2,1)S(1)}, bf16[128,768]{1,0:T(8,128)(2,1)S(1)}, u32[]{:S(2)}, u32[]{:S(2)}) collective-permute-start(bf16[128,768]{1,0:T(8,128)(2,1)S(1)} %get-tuple-element.130), channel_id=1, source_target_pairs={{0,2},{1,3},{2,0},{3,1},{4,6},{5,7},{6,4},{7,5},{8,10},{9,11},{10,... | collective-permute-start | bytes 589832 | tf_op jit(solution)/shard_map/ppermute | solution.py:82
  77.4 18.3 %collective-permute-start.21 = (bf16[4,96,768]{2,1,0:T(8,128)(2,1)S(1)}, bf16[4,96,768]{2,1,0:T(8,128)(2,1)S(1)}, u32[]{:S(2)}, u32[]{:S(2)}) collective-permute-start(bf16[4,96,768]{2,1,0:T(8,128)(2,1)S(1)} %join.5.refs_1_), channel_id=1, source_target_pairs={{0,4},{4,0},{8,12},{12,8},{16,20},{20,16},{24,28},{28,24},{1,5},{5... | collective-permute-start | bytes 1769480 | tf_op jit(solution)/shard_map/ppermute | solution.py:82
  83.9 6.1 %collective-permute-start.19 = (bf16[128,768]{1,0:T(8,128)(2,1)S(1)}, bf16[128,768]{1,0:T(8,128)(2,1)S(1)}, u32[]{:S(2)}, u32[]{:S(2)}) collective-permute-start(bf16[128,768]{1,0:T(8,128)(2,1)S(1)} %get-tuple-element.133.refs_0_), channel_id=1, source_target_pairs={{0,2},{1,3},{2,0},{3,1},{4,6},{5,7},{6,4},{7,5},{8,10},{9,11},{10,... | collective-permute-start | bytes 589832 | tf_op jit(solution)/shard_map/ppermute | solution.py:82
  85.5 10.3 %collective-permute-start.18 = (bf16[128,768]{1,0:T(8,128)(2,1)S(1)}, bf16[128,768]{1,0:T(8,128)(2,1)S(1)}, u32[]{:S(2)}, u32[]{:S(2)}) collective-permute-start(bf16[128,768]{1,0:T(8,128)(2,1)S(1)} %get-tuple-element.133.refs_0_), channel_id=1, source_target_pairs={{0,1},{1,0},{2,3},{3,2},{4,5},{5,4},{6,7},{7,6},{8,9},{9,8},{10,11... | collective-permute-start | bytes 589832 | tf_op jit(solution)/shard_map/ppermute | solution.py:82
  90.0 5.8 %collective-permute-start.20 = (bf16[128,768]{1,0:T(8,128)(2,1)S(1)}, bf16[128,768]{1,0:T(8,128)(2,1)S(1)}, u32[]{:S(2)}, u32[]{:S(2)}) collective-permute-start(bf16[128,768]{1,0:T(8,128)(2,1)S(1)} %collective-permute-done.19.refs_2_), channel_id=1, source_target_pairs={{0,1},{1,0},{2,3},{3,2},{4,5},{5,4},{6,7},{7,6},{8,9},{9,8},{10,11... | collective-permute-start | bytes 589832 | tf_op jit(solution)/shard_map/ppermute | solution.py:82
  100.3 15.8 %collective-permute-start.24 = (bf16[4,96,768]{2,1,0:T(8,128)(2,1)S(1)}, bf16[4,96,768]{2,1,0:T(8,128)(2,1)S(1)}, u32[]{:S(2)}, u32[]{:S(2)}) collective-permute-start(bf16[4,96,768]{2,1,0:T(8,128)(2,1)S(1)} %get-tuple-element.149), channel_id=1, source_target_pairs={{0,4},{4,0},{8,12},{12,8},{16,20},{20,16},{24,28},{28,24},{1,5},{5... | collective-permute-start | bytes 1769480 | tf_op jit(solution)/shard_map/ppermute | solution.py:82
  101.0 7.1 %collective-permute-start.23 = (bf16[128,768]{1,0:T(8,128)(2,1)S(1)}, bf16[128,768]{1,0:T(8,128)(2,1)S(1)}, u32[]{:S(2)}, u32[]{:S(2)}) collective-permute-start(bf16[128,768]{1,0:T(8,128)(2,1)S(1)} %get-tuple-element.146), channel_id=1, source_target_pairs={{0,2},{1,3},{2,0},{3,1},{4,6},{5,7},{6,4},{7,5},{8,10},{9,11},{10,... | collective-permute-start | bytes 589832 | tf_op jit(solution)/shard_map/ppermute | solution.py:82
  108.5 6.3 %collective-permute-start.26 = (bf16[128,768]{1,0:T(8,128)(2,1)S(1)}, bf16[128,768]{1,0:T(8,128)(2,1)S(1)}, u32[]{:S(2)}, u32[]{:S(2)}) collective-permute-start(bf16[128,768]{1,0:T(8,128)(2,1)S(1)} %get-tuple-element.152.refs_2_), channel_id=1, source_target_pairs={{0,2},{1,3},{2,0},{3,1},{4,6},{5,7},{6,4},{7,5},{8,10},{9,11},{10,... | collective-permute-start | bytes 589832 | tf_op jit(solution)/shard_map/ppermute | solution.py:82
  110.1 6.1 %collective-permute-start.25 = (bf16[128,768]{1,0:T(8,128)(2,1)S(1)}, bf16[128,768]{1,0:T(8,128)(2,1)S(1)}, u32[]{:S(2)}, u32[]{:S(2)}) collective-permute-start(bf16[128,768]{1,0:T(8,128)(2,1)S(1)} %get-tuple-element.152.refs_2_), channel_id=1, source_target_pairs={{0,1},{1,0},{2,3},{3,2},{4,5},{5,4},{6,7},{7,6},{8,9},{9,8},{10,11... | collective-permute-start | bytes 589832 | tf_op jit(solution)/shard_map/ppermute | solution.py:82
  121.2 16.2 %collective-permute-start.31 = (bf16[4,96,768]{2,1,0:T(8,128)(2,1)S(1)}, bf16[4,96,768]{2,1,0:T(8,128)(2,1)S(1)}, u32[]{:S(2)}, u32[]{:S(2)}) collective-permute-start(bf16[4,96,768]{2,1,0:T(8,128)(2,1)S(1)} %second_sent.1.refs_1_), channel_id=1, source_target_pairs={{0,4},{4,0},{8,12},{12,8},{16,20},{20,16},{24,28},{28,24},{1,5},{5... | collective-permute-start | bytes 1769480 | tf_op jit(solution)/shard_map/ppermute | solution.py:82
  124.8 26.8 %collective-permute-start.36 = (bf16[4,96,768]{2,1,0:T(8,128)(2,1)S(1)}, bf16[4,96,768]{2,1,0:T(8,128)(2,1)S(1)}, u32[]{:S(2)}, u32[]{:S(2)}) collective-permute-start(bf16[4,96,768]{2,1,0:T(8,128)(2,1)S(1)} %get-tuple-element.170), channel_id=1, source_target_pairs={{0,4},{4,0},{8,12},{12,8},{16,20},{20,16},{24,28},{28,24},{1,5},{5... | collective-permute-start | bytes 1769480 | tf_op jit(solution)/shard_map/ppermute | solution.py:82
  126.3 14.8 %collective-permute-start.30 = (bf16[2,96,768]{2,1,0:T(8,128)(2,1)S(1)}, bf16[2,96,768]{2,1,0:T(8,128)(2,1)S(1)}, u32[]{:S(2)}, u32[]{:S(2)}) collective-permute-start(bf16[2,96,768]{2,1,0:T(8,128)(2,1)S(1)} %get-tuple-element.150.refs_0_), channel_id=1, source_target_pairs={{0,8},{4,12},{8,0},{12,4},{16,24},{20,28},{24,16},{28,20},{1,9},{5... | collective-permute-start | bytes 884744 | tf_op jit(solution)/shard_map/ppermute | solution.py:82
  128.3 6.4 %collective-permute-start.29 = (bf16[128,768]{1,0:T(8,128)(2,1)S(1)}, bf16[128,768]{1,0:T(8,128)(2,1)S(1)}, u32[]{:S(2)}, u32[]{:S(2)}) collective-permute-start(bf16[128,768]{1,0:T(8,128)(2,1)S(1)} %get-tuple-element.157), channel_id=1, source_target_pairs={{0,2},{1,3},{2,0},{3,1},{4,6},{5,7},{6,4},{7,5},{8,10},{9,11},{10,... | collective-permute-start | bytes 589832 | tf_op jit(solution)/shard_map/ppermute | solution.py:82
  137.5 17.3 %collective-permute-start.38 = (bf16[2,96,768]{2,1,0:T(8,128)(2,1)S(1)}, bf16[2,96,768]{2,1,0:T(8,128)(2,1)S(1)}, u32[]{:S(2)}, u32[]{:S(2)}) collective-permute-start(bf16[2,96,768]{2,1,0:T(8,128)(2,1)S(1)} %get-tuple-element.164.refs_3_), channel_id=1, source_target_pairs={{0,8},{4,12},{8,0},{12,4},{16,24},{20,28},{24,16},{28,20},{1,9},{5... | collective-permute-start | bytes 884744 | tf_op jit(solution)/shard_map/ppermute | solution.py:82
  139.6 3.4 %collective-permute-start.34 = (bf16[16,768]{1,0:T(8,128)(2,1)S(1)}, bf16[16,768]{1,0:T(8,128)(2,1)S(1)}, u32[]{:S(2)}, u32[]{:S(2)}) collective-permute-start(bf16[16,768]{1,0:T(8,128)(2,1)S(1)} %get-tuple-element.161.refs_0_.refs_4_), channel_id=1, source_target_pairs={{0,3},{1,2},{2,1},{3,0},{4,7},{5,6},{6,5},{7,4},{8,11},{9,10},{10,... | collective-permute-start | bytes 73736 | tf_op jit(solution)/shard_map/ppermute | solution.py:82
  139.6 3.9 %collective-permute-start.33 = (bf16[16,768]{1,0:T(8,128)(2,1)S(1)}, bf16[16,768]{1,0:T(8,128)(2,1)S(1)}, u32[]{:S(2)}, u32[]{:S(2)}) collective-permute-start(bf16[16,768]{1,0:T(8,128)(2,1)S(1)} %get-tuple-element.161.refs_0_.refs_4_), channel_id=1, source_target_pairs={{0,2},{1,3},{2,0},{3,1},{4,6},{5,7},{6,4},{7,5},{8,10},{9,11},{10,... | collective-permute-start | bytes 73736 | tf_op jit(solution)/shard_map/ppermute | solution.py:82
  141.1 2.3 %collective-permute-start.32 = (bf16[16,768]{1,0:T(8,128)(2,1)S(1)}, bf16[16,768]{1,0:T(8,128)(2,1)S(1)}, u32[]{:S(2)}, u32[]{:S(2)}) collective-permute-start(bf16[16,768]{1,0:T(8,128)(2,1)S(1)} %get-tuple-element.161.refs_0_.refs_4_), channel_id=1, source_target_pairs={{0,1},{1,0},{2,3},{3,2},{4,5},{5,4},{6,7},{7,6},{8,9},{9,8},{10,11... | collective-permute-start | bytes 73736 | tf_op jit(solution)/shard_map/ppermute | solution.py:82
  144.3 7.3 %collective-permute-start.35 = (bf16[4,16,768]{2,1,0:T(8,128)(2,1)S(1)}, bf16[4,16,768]{2,1,0:T(8,128)(2,1)S(1)}, u32[]{:S(2)}, u32[]{:S(2)}) collective-permute-start(bf16[4,16,768]{2,1,0:T(8,128)(2,1)S(1)} %get-tuple-element.165), channel_id=1, source_target_pairs={{0,4},{4,0},{8,12},{12,8},{16,20},{20,16},{24,28},{28,24},{1,5},{5... | collective-permute-start | bytes 294920 | tf_op jit(solution)/shard_map/ppermute | solution.py:82
  151.7 24.9 %collective-permute-start.37 = (bf16[2,96,768]{2,1,0:T(8,128)(2,1)S(1)}, bf16[2,96,768]{2,1,0:T(8,128)(2,1)S(1)}, u32[]{:S(2)}, u32[]{:S(2)}) collective-permute-start(bf16[2,96,768]{2,1,0:T(8,128)(2,1)S(1)} %get-tuple-element.172.refs_0_), channel_id=1, source_target_pairs={{0,8},{4,12},{8,0},{12,4},{16,24},{20,28},{24,16},{28,20},{1,9},{5... | collective-permute-start | bytes 884744 | tf_op jit(solution)/shard_map/ppermute | solution.py:82
  153.8 10.7 %collective-permute-start.49 = (bf16[1,96,768]{2,1,0:T(8,128)(2,1)S(1)}, bf16[1,96,768]{2,1,0:T(8,128)(2,1)S(1)}, u32[]{:S(2)}, u32[]{:S(2)}) collective-permute-start(bf16[1,96,768]{2,1,0:T(8,128)(2,1)S(1)} %get-tuple-element.163.refs_2_), channel_id=1, source_target_pairs={{0,16},{4,20},{8,24},{12,28},{16,0},{20,4},{24,8},{28,12},{1,17},{... | collective-permute-start | bytes 442376 | tf_op jit(solution)/shard_map/ppermute | solution.py:82
  154.9 15.6 %collective-permute-start.50 = (bf16[1,96,768]{2,1,0:T(8,128)(2,1)S(1)}, bf16[1,96,768]{2,1,0:T(8,128)(2,1)S(1)}, u32[]{:S(2)}, u32[]{:S(2)}) collective-permute-start(bf16[1,96,768]{2,1,0:T(8,128)(2,1)S(1)} %get-tuple-element.175.refs_1_), channel_id=1, source_target_pairs={{0,16},{4,20},{8,24},{12,28},{16,0},{20,4},{24,8},{28,12},{1,17},{... | collective-permute-start | bytes 442376 | tf_op jit(solution)/shard_map/ppermute | solution.py:82
  156.8 22.2 %collective-permute-start.42 = (bf16[256,768]{1,0:T(8,128)(2,1)S(1)}, bf16[256,768]{1,0:T(8,128)(2,1)S(1)}, u32[]{:S(2)}, u32[]{:S(2)}) collective-permute-start(bf16[256,768]{1,0:T(8,128)(2,1)S(1)} %get-tuple-element.143.refs_1_), channel_id=1, source_target_pairs={{0,1},{1,0},{2,3},{3,2},{4,5},{5,4},{6,7},{7,6},{8,9},{9,8},{10,11... | collective-permute-start | bytes 1179656 | tf_op jit(solution)/shard_map/ppermute | solution.py:82
  156.8 19.9 %collective-permute-start.39 = (bf16[2,16,768]{2,1,0:T(8,128)(2,1)S(1)}, bf16[2,16,768]{2,1,0:T(8,128)(2,1)S(1)}, u32[]{:S(2)}, u32[]{:S(2)}) collective-permute-start(bf16[2,16,768]{2,1,0:T(8,128)(2,1)S(1)} %get-tuple-element.178), channel_id=1, source_target_pairs={{0,8},{4,12},{8,0},{12,4},{16,24},{20,28},{24,16},{28,20},{1,9},{5... | collective-permute-start | bytes 147464 | tf_op jit(solution)/shard_map/ppermute | solution.py:82
  164.4 12.3 %collective-permute-start.40 = (bf16[2,16,768]{2,1,0:T(8,128)(2,1)S(1)}, bf16[2,16,768]{2,1,0:T(8,128)(2,1)S(1)}, u32[]{:S(2)}, u32[]{:S(2)}) collective-permute-start(bf16[2,16,768]{2,1,0:T(8,128)(2,1)S(1)} %get-tuple-element.179), channel_id=1, source_target_pairs={{0,16},{4,20},{8,24},{12,28},{16,0},{20,4},{24,8},{28,12},{1,17},{... | collective-permute-start | bytes 147464 | tf_op jit(solution)/shard_map/ppermute | solution.py:82
  170.4 6.3 %collective-permute-start.41 = (bf16[2,16,768]{2,1,0:T(8,128)(2,1)S(1)}, bf16[2,16,768]{2,1,0:T(8,128)(2,1)S(1)}, u32[]{:S(2)}, u32[]{:S(2)}) collective-permute-start(bf16[2,16,768]{2,1,0:T(8,128)(2,1)S(1)} %get-tuple-element.180), channel_id=1, source_target_pairs={{0,24},{4,28},{8,16},{12,20},{16,8},{20,12},{24,0},{28,4},{1,25},{... | collective-permute-start | bytes 147464 | tf_op jit(solution)/shard_map/ppermute | solution.py:82
  176.6 15.8 %collective-permute-start.48 = (bf16[1,96,768]{2,1,0:T(8,128)(2,1)S(1)}, bf16[1,96,768]{2,1,0:T(8,128)(2,1)S(1)}, u32[]{:S(2)}, u32[]{:S(2)}) collective-permute-start(bf16[1,96,768]{2,1,0:T(8,128)(2,1)S(1)} %get-tuple-element.173.refs_0_), channel_id=1, source_target_pairs={{0,16},{4,20},{8,24},{12,28},{16,0},{20,4},{24,8},{28,12},{1,17},{... | collective-permute-start | bytes 442376 | tf_op jit(solution)/shard_map/ppermute | solution.py:82
  177.2 5.8 %collective-permute-start.44 = (f32[4,8,128]{2,1,0:T(8,128)S(1)}, f32[4,8,128]{2,1,0:T(8,128)S(1)}, u32[]{:S(2)}, u32[]{:S(2)}) collective-permute-start(f32[4,8,128]{2,1,0:T(8,128)S(1)} %get-tuple-element.181.refs_0_), channel_id=1, source_target_pairs={{0,4},{4,0},{8,12},{12,8},{16,20},{20,16},{24,28},{28,24},{1,5},{5... | collective-permute-start | bytes 49160 | tf_op jit(solution)/shard_map/ppermute | solution.py:82
  179.2 14.1 %collective-permute-start.43 = (bf16[128,768]{1,0:T(8,128)(2,1)S(1)}, bf16[128,768]{1,0:T(8,128)(2,1)S(1)}, u32[]{:S(2)}, u32[]{:S(2)}) collective-permute-start(bf16[128,768]{1,0:T(8,128)(2,1)S(1)} %get-tuple-element.184), channel_id=1, source_target_pairs={{0,2},{1,3},{2,0},{3,1},{4,6},{5,7},{6,4},{7,5},{8,10},{9,11},{10,... | collective-permute-start | bytes 589832 | tf_op jit(solution)/shard_map/ppermute | solution.py:82
  183.0 5.7 %collective-permute-start.45 = (f32[2,8,128]{2,1,0:T(8,128)S(1)}, f32[2,8,128]{2,1,0:T(8,128)S(1)}, u32[]{:S(2)}, u32[]{:S(2)}) collective-permute-start(f32[2,8,128]{2,1,0:T(8,128)S(1)} %get-tuple-element.188), channel_id=1, source_target_pairs={{0,8},{4,12},{8,0},{12,4},{16,24},{20,28},{24,16},{28,20},{1,9},{5... | collective-permute-start | bytes 24584 | tf_op jit(solution)/shard_map/ppermute | solution.py:82
  184.1 4.6 %collective-permute-start.46 = (f32[2,8,128]{2,1,0:T(8,128)S(1)}, f32[2,8,128]{2,1,0:T(8,128)S(1)}, u32[]{:S(2)}, u32[]{:S(2)}) collective-permute-start(f32[2,8,128]{2,1,0:T(8,128)S(1)} %get-tuple-element.189), channel_id=1, source_target_pairs={{0,16},{4,20},{8,24},{12,28},{16,0},{20,4},{24,8},{28,12},{1,17},{... | collective-permute-start | bytes 24584 | tf_op jit(solution)/shard_map/ppermute | solution.py:82
  186.2 5.4 %collective-permute-start.47 = (f32[2,8,128]{2,1,0:T(8,128)S(1)}, f32[2,8,128]{2,1,0:T(8,128)S(1)}, u32[]{:S(2)}, u32[]{:S(2)}) collective-permute-start(f32[2,8,128]{2,1,0:T(8,128)S(1)} %get-tuple-element.190), channel_id=1, source_target_pairs={{0,24},{4,28},{8,16},{12,20},{16,8},{20,12},{24,0},{28,4},{1,25},{... | collective-permute-start | bytes 24584 | tf_op jit(solution)/shard_map/ppermute | solution.py:82
  (21 other events, 117.9 us)

commit v7 on v5

--- a/solution.py
+++ b/solution.py
@@ -140,7 +140,7 @@
         out[1] = got[z]
 
 
-def exchange(keep, send, ordered=()):
+def exchange(keep, send, ordered=(), got=None):
     size = keep.shape[0]
     piece = keep.shape[1:]
     if size != 4:
@@ -151,7 +151,7 @@
             jnp.take(whole, order, axis=0), "fsdp", split_axis=0, concat_axis=0, tiled=True
         )
         return [jnp.take(got, order, axis=0)]
-    got = swap(send, "fsdp", 1)
+    got = swap(send, "fsdp", 1) if got is None else got
     pairs = call(
         pair_kernel, "pairs", [((2, *piece), keep.dtype)] * size, [keep, got], ordered=ordered
     )
@@ -190,9 +190,9 @@
     return call(join_kernel, "join", [(shape, a.dtype)], [a, b], ordered=ordered)[0]
 
 
-def gather_steps(own):
-    two = join(own, swap(own, "fsdp", 4))
-    four = join(two, swap(two, "fsdp", 2))
+def gather_steps(own, ordered=((), ())):
+    two = join(own, swap(own, "fsdp", 4), ordered[0])
+    four = join(two, swap(two, "fsdp", 2), ordered[1])
     return two, four, swap(four, "fsdp", 1)
 
 
@@ -391,25 +391,31 @@
         bias_out[0][...] = jnp.sum(right[...].astype(F32), axis=0, keepdims=True)
 
 
-def mlp_out_kernel(act, second, keep, send):
+def mlp_out_kernel(act, second, x0, x1, x2, x3, bias, keep, send, sums, *, latents):
     rows = keep.shape[0] // 2
-    for b in range(4):
+    part = rows // latents
+    sums[...] = jnp.zeros_like(sums)
+    for b, x in enumerate((x0, x1, x2, x3)):
         at = (b // 2) * rows
         out = send if b % 2 else keep
         value = dot(act[b * rows : (b + 1) * rows, :], second[...], (1, 1))
         out[at : at + rows, :] = value.astype(BF)
-
-
-def output_kernel(middle, x, p0, p1, bias, mod, out, sums):
+        if b == 0:
+            value = value + bias[...]
+        grad = value * x[rows:, :].astype(F32)
+        for l in range(latents):
+            sums[l : l + 1, :] += jnp.sum(
+                grad[l * part : (l + 1) * part], axis=0, keepdims=True
+            )
+
+
+def output_kernel(middle, p0, p1, bias, mod, out):
     latents = mod.shape[0] // 6
-    size = middle.shape[0]
-    rows = size // latents
+    rows = middle.shape[0] // latents
     for l in range(latents):
         here = slice(l * rows, (l + 1) * rows)
         branch = bias[...] + p0[here, :] + p1[here, :].astype(F32)
-        cot = x[size + l * rows : size + (l + 1) * rows, :].astype(F32)
         out[here, :] = (middle[here, :] + mod[6 * l + 5 : 6 * l + 6, :] * branch).astype(BF)
-        sums[l : l + 1, :] = jnp.sum(cot * branch, axis=0, keepdims=True)
 
 
 def middle_back_kernel(x, middle, branch, p0, p1, mod, grad_out, out, sums):
@@ -706,10 +712,10 @@
             "first_own",
             [((feat, hidden), BF)],
             [expand_weight],
-            ordered=[half_two[1]],
+            ordered=[mod_send],
             fetch=True,
         )[0]
-        first_two, first_four, first_other = gather_steps(first_own)
+        first_two, first_four, first_other = gather_steps(first_own, ([half_two[1]], [mod_parts[1]]))
         second_own = call(
             copy_kernel,
             "second_own",
@@ -740,7 +746,7 @@
             [second_four, second_other],
             [rank],
         )[0]
-        steps = [[attn_four], [first_two], [first_four], [second_two], [second_four, first_full]]
+        steps = [[attn_four], [first_four], [second_two], [], [second_four, first_full]]
     else:
         steps = [[]] * 5
         mod_parts = [scatter_pieces(mod_keep, mod_send)]
@@ -758,7 +764,7 @@
         cond_got,
         [rank, tp_rank],
         scratch=[pltpu.VMEM((count, 16, 128), F32)],
-        ordered=[mod_send],
+        ordered=[cond_cols],
         flops=1e9,
     )
     mod, attn_rows = call(
@@ -813,11 +819,11 @@
         )
         first_done = [fc1_part]
     grad_in = tp_scatter(keep, send, first_done)
-    out_keep, out_send = call(
-        mlp_out_kernel,
+    out_keep, out_send, gates = call(
+        functools.partial(mlp_out_kernel, latents=latents),
         "mlp_out",
-        [pair, pair],
-        [act, second_full],
+        [pair, pair, ((8, width), F32)],
+        [act, second_full, *x_blocks, second_bias],
         ordered=[grad_in[0]],
         flops=1.5e9,
     )
@@ -863,13 +869,10 @@
         [*a_blocks, qkv_full, proj_full, qkv],
         ordered=[mlp_parts[0], *steps[0]],
     )
-    output, gates = call(
-        output_kernel,
-        "output",
-        [block, ((8, width), F32)],
-        [middle, x_own, *mlp_parts, second_bias, mod],
-    )
-    grad_in = tp_scatter(keep, send, [gates])
+    output = call(
+        output_kernel, "output", [block], [middle, *mlp_parts, second_bias, mod]
+    )[0]
+    grad_in = tp_scatter(keep, send)
     if direct:
         attn_keep, attn_send = call(
             attn_grad_kernel,
@@ -877,7 +880,7 @@
             [((half, feat, 4 * cols), BF)] * 2,
             [attn_rows, grads, back_rows, att],
             [rank],
-            ordered=[grad_in[0]],
+            ordered=[grad_in[0], output],
             flops=6e9,
         )
     else:
@@ -911,8 +914,10 @@
         scratch=[pltpu.VMEM((tp_count, 16, width), F32), pltpu.VMEM((16, width), F32)],
         ordered=tail[0],
     )
+    spread_got = None
     if direct:
-        attn_half = halve(attn_keep, attn_send, 1, [spread_send])
+        spread_got = swap(spread_send, "fsdp", 1)
+        attn_half = halve(attn_keep, attn_send, 1, [spread_got])
         attn_own_sum, attn_out = halve(*attn_half, 2)
         qkv_sum, proj_sum = call(
             attn_add_kernel,
@@ -921,8 +926,7 @@
             [attn_own_sum, swap(attn_out, "fsdp", 4)],
         )
         qkv_sum = qkv_sum.transpose(1, 0, 2)
-        second_one = halve(*second_half, 2, [spread_send])
-        second_sum = last_sum(*second_one, 4)
+        second_one = halve(*second_half, 2, [spread_got])
         tail[1] = [attn_half[1], second_one[1]]
         tail[2] = [attn_out]
     silu_keep, silu_send, grad_mod_all, bias_grads = call(
@@ -930,17 +934,27 @@
         "silu_columns",
         [((half, 8, 128), F32)] * 2
         + [((count * latents, 6 * width), BF), ((1, width), F32)],
-        [*exchange(spread_keep, spread_send, tail[1]), ada_weight],
+        [*exchange(spread_keep, spread_send, tail[1], spread_got), ada_weight],
         scratch=[
             pltpu.VMEM((6, count * latents, width), F32),
             pltpu.VMEM((count, 8, 128), F32),
         ],
-    )
+        ordered=tail[2],
+    )
+    if direct:
+        second_last = call(
+            copy_kernel,
+            "second_last",
+            [(second_one[1].shape, BF)],
+            [second_one[1]],
+            ordered=[silu_send],
+        )[0]
+        second_sum = last_sum(second_one[0], second_last, 4)
     cond_grad = call(
         functools.partial(cond_kernel, latents=latents, feat=feat),
         "cond_grad",
         [((latents, width), F32)],
-        [*exchange(silu_keep, silu_send, tail[2]), conditioning],
+        [*exchange(silu_keep, silu_send), conditioning],
         [rank],
         scratch=[pltpu.VMEM((count, 8, 128), F32)],
     )[0]

time: 176 us -> 181 us (1.028)
  waiting for transfers between devices: 79.1 us -> 85.4 us
  starting transfers between devices: 50.9 us -> 49 us
    ppermute x53, waiting for transfers between devices: 79.1 us -> 85.4 us  [swap(): return lax.ppermute(block, axis, [(i, i ^ offset) for i in range(count)])]
    ppermute x53, starting transfers between devices: 50.9 us -> 49 us  [swap(): return lax.ppermute(block, axis, [(i, i ^ offset) for i in range(count)])]
    pallas_call x51 -> x52, Pallas kernels: 29.4 us -> 30.3 us  [call(): pl.pallas_call(body, out_shape=[jax.ShapeDtypeStruct(shape, dtype) for sh...]
    unnamed x40 -> x36, local copies, waits for them, and re-layouts: 5.22 us -> 5.18 us
  transfers between devices with their start and end apart: 53 -> 53, of which waited for: 24 -> 25; matrix products, arithmetic and copies ran while one was open for 5% -> 5% of each run, Pallas kernels for 12% -> 12%
where the time goes in v7:
time: 181 us; the launch traced here: 180 us
  waiting for transfers between devices  85.4 us (47%)
  starting transfers between devices  49 us (27%)
  Pallas kernels  30.3 us (17%)
  local copies, waits for them, and re-layouts  9.92 us (5%)
  other arithmetic  3.07 us (2%)
    ppermute x53, waiting for transfers between devices, swap(): return lax.ppermute(block, axis, [(i, i ^ offset) for i in range(count)])  85.4 us
    ppermute x53, starting transfers between devices, swap(): return lax.ppermute(block, axis, [(i, i ^ offset) for i in range(count)])  49 us
    pallas_call x52, Pallas kernels, call(): pl.pallas_call(body, out_shape=[jax.ShapeDtypeStruct(shape, dtype) for sh...  30.3 us
    unnamed x36, local copies, waits for them, and re-layouts  5.18 us
  transfers between devices with their start and end apart: 53, of which 25 were waited for; matrix products, arithmetic and copies ran while one was open for 5% of the time, Pallas kernels for 12%

profile of v7, /device:TPU:0, one launch (start us, length us, event | category | flops | bytes accessed | tf_op | source)
XLA Modules:
  0.0 180.5 jit_solution(12887294329786688956)
XLA Ops:
  2.7 4.1 %collective-permute-start = (bf16[96,768]{1,0:T(8,128)(2,1)S(1)}, bf16[96,768]{1,0:T(8,128)(2,1)S(1)}, u32[]{:S(2)}, u32[]{:S(2)}) collective-permute-start(bf16[96,768]{1,0:T(8,128)(2,1)S(1)} %attn_own.1.refs_0_.refs_1_), channel_id=1, source_target_pairs={{0,16},{4,20},{8,24},{12,28},{16,0},{20,4},{24,8},{28,12},{1,17},{... | collective-permute-start | bytes 442376 | tf_op jit(solution)/shard_map/ppermute | solution.py:82
  9.6 1.5 collective-permute-start.1
  11.1 2.8 %collective-permute-done.refs_1_ = bf16[96,768]{1,0:T(8,128)(2,1)S(1)} collective-permute-done((bf16[96,768]{1,0:T(8,128)(2,1)S(1)}, bf16[96,768]{1,0:T(8,128)(2,1)S(1)}, u32[]{:S(2)}, u32[]{:S(2)}) %collective-permute-start) | collective-permute-done | bytes 147488 | tf_op jit(solution)/shard_map/ppermute | solution.py:82
  14.7 1.3 collective-permute-start.2
  16.0 2.2 %collective-permute-start.3 = (f32[2,16,128]{2,1,0:T(8,128)S(1)}, f32[2,16,128]{2,1,0:T(8,128)S(1)}, u32[]{:S(2)}, u32[]{:S(2)}) collective-permute-start(f32[2,16,128]{2,1,0:T(8,128)S(1)} %get-tuple-element.108), channel_id=1, source_target_pairs={{0,16},{4,20},{8,24},{12,28},{16,0},{20,4},{24,8},{28,12},{1,17},{... | collective-permute-start | bytes 49160 | tf_op jit(solution)/shard_map/ppermute | solution.py:82
  18.2 1.4 collective-permute-start.4
  19.6 1.6 pad_maximum_fusion
  21.3 1.6 collective-permute-done.2.refs_1_.refs_4_
  22.8 2.9 %collective-permute-done.4.refs_3_.refs_6_ = f32[2,16,128]{2,1,0:T(8,128)S(1)} collective-permute-done((f32[2,16,128]{2,1,0:T(8,128)S(1)}, f32[2,16,128]{2,1,0:T(8,128)S(1)}, u32[]{:S(2)}, u32[]{:S(2)}) %collective-permute-start.4) | collective-permute-done | bytes 16416 | tf_op jit(solution)/shard_map/ppermute | solution.py:82
  25.7 1.6 collective-permute-start.13
  28.5 1.7 collective-permute-start.15
  31.1 13.7 %collective-permute-done.5.refs_1_ = bf16[4,16,768]{2,1,0:T(8,128)(2,1)S(1)} collective-permute-done((bf16[4,16,768]{2,1,0:T(8,128)(2,1)S(1)}, bf16[4,16,768]{2,1,0:T(8,128)(2,1)S(1)}, u32[]{:S(2)}, u32[]{:S(2)}) %collective-permute-start.5) | collective-permute-done | bytes 98336 | tf_op jit(solution)/shard_map/ppermute | solution.py:82
  45.6 3.4 %collective-permute-done.6.refs_1_ = bf16[2,16,768]{2,1,0:T(8,128)(2,1)S(1)} collective-permute-done((bf16[2,16,768]{2,1,0:T(8,128)(2,1)S(1)}, bf16[2,16,768]{2,1,0:T(8,128)(2,1)S(1)}, u32[]{:S(2)}, u32[]{:S(2)}) %collective-permute-start.6) | collective-permute-done | bytes 49184 | tf_op jit(solution)/shard_map/ppermute | solution.py:82
  50.5 1.9 %collective-permute-start.7 = (bf16[1,16,768]{2,1,0:T(8,128)(2,1)}, bf16[1,16,768]{2,1,0:T(8,128)(2,1)}, u32[]{:S(2)}, u32[]{:S(2)}) collective-permute-start(bf16[1,16,768]{2,1,0:T(8,128)(2,1)} %get-tuple-element.114.refs_0_), channel_id=1, source_target_pairs={{0,16},{4,20},{8,24},{12,28},{16,0},{20,4},{24,8},{28,12},{1,17},{... | collective-permute-start | bytes 73736 | tf_op jit(solution)/shard_map/ppermute | solution.py:82
  52.4 3.3 %collective-permute-done.7.refs_0_.refs_7_ = bf16[1,16,768]{2,1,0:T(8,128)(2,1)} collective-permute-done((bf16[1,16,768]{2,1,0:T(8,128)(2,1)}, bf16[1,16,768]{2,1,0:T(8,128)(2,1)}, u32[]{:S(2)}, u32[]{:S(2)}) %collective-permute-start.7) | collective-permute-done | bytes 24608 | tf_op jit(solution)/shard_map/ppermute | solution.py:82
  55.7 1.7 collective-permute-done.9.refs_2_
  58.3 1.7 collective-permute-start.18
  61.1 1.9 %collective-permute-start.10 = (bf16[96,768]{1,0:T(8,128)(2,1)S(1)}, bf16[96,768]{1,0:T(8,128)(2,1)S(1)}, u32[]{:S(2)}, u32[]{:S(2)}) collective-permute-start(bf16[96,768]{1,0:T(8,128)(2,1)S(1)} %second_own.1.refs_0_), channel_id=1, source_target_pairs={{0,16},{4,20},{8,24},{12,28},{16,0},{20,4},{24,8},{28,12},{1,17},{... | collective-permute-start | bytes 442376 | tf_op jit(solution)/shard_map/ppermute | solution.py:82
  63.8 1.6 first_norm.1
  65.7 2.5 %attention.1 = (bf16[512,576]{1,0:T(8,128)(2,1)S(1)}, bf16[512,192]{1,0:T(8,128)(2,1)S(1)}, bf16[256,768]{1,0:T(8,128)(2,1)S(1)}, bf16[256,768]{1,0:T(8,128)(2,1)S(1)}) custom-call(bf16[4,96,768]{2,1,0:T(8,128)(2,1)S(1)} %join.8.refs_0_.refs_1_, bf16[512,768]{1,0:T(8,128)(2,1)S(1)} %get-tuple-element.118.refs_1_.refs_3_, ...), custom_call_target="tpu_custom_call" | custom-call | flops 1 | bytes 1 | tf_op jit(solution)/shard_map/attention/pallas_call | solution.py:50
  70.6 7.1 %collective-permute-done.17.refs_1_ = bf16[2,96,768]{2,1,0:T(8,128)(2,1)S(1)} collective-permute-done((bf16[2,96,768]{2,1,0:T(8,128)(2,1)S(1)}, bf16[2,96,768]{2,1,0:T(8,128)(2,1)S(1)}, u32[]{:S(2)}, u32[]{:S(2)}) %collective-permute-start.17) | collective-permute-done | bytes 294944 | tf_op jit(solution)/shard_map/ppermute | solution.py:82
  80.4 5.2 %collective-permute-done.21.refs_2_ = bf16[128,768]{1,0:T(8,128)(2,1)S(1)} collective-permute-done((bf16[128,768]{1,0:T(8,128)(2,1)S(1)}, bf16[128,768]{1,0:T(8,128)(2,1)S(1)}, u32[]{:S(2)}, u32[]{:S(2)}) %collective-permute-start.21) | collective-permute-done | bytes 196640 | tf_op jit(solution)/shard_map/ppermute | solution.py:82
  85.6 6.6 %collective-permute-done.23.refs_2_ = bf16[4,96,768]{2,1,0:T(8,128)(2,1)S(1)} collective-permute-done((bf16[4,96,768]{2,1,0:T(8,128)(2,1)S(1)}, bf16[4,96,768]{2,1,0:T(8,128)(2,1)S(1)}, u32[]{:S(2)}, u32[]{:S(2)}) %collective-permute-start.23) | collective-permute-done | bytes 589856 | tf_op jit(solution)/shard_map/ppermute | solution.py:82
  92.3 3.1 %mlp.1 = (bf16[512,768]{1,0:T(8,128)(2,1)S(1)}, bf16[512,768]{1,0:T(8,128)(2,1)S(1)}, bf16[512,768]{1,0:T(8,128)(2,1)S(1)}, bf16[256,768]{1,0:T(8,128)(2,1)S(1)}, bf16[256,768]{1,0:T(8,128)(2,1)S(1)}) custom-call(bf16[128,768]{1,0:T(8,128)(2,1)S(1)} %get-tuple-element.130.refs_0_, bf16[128,768]{1,0:T(8,128)(2,1)S(1)} %collective-permute-done.20.refs_1_, ...), custom_call_target="tpu_custom_call" | custom-call | flops 1 | bytes 1 | tf_op jit(solution)/shard_map/mlp/pallas_call | solution.py:50
  95.4 1.3 first_grad.1
  97.9 2.7 %mlp_out.1 = (bf16[256,768]{1,0:T(8,128)(2,1)S(1)}, bf16[256,768]{1,0:T(8,128)(2,1)S(1)}, f32[8,768]{1,0:T(8,128)S(1)}) custom-call(f32[128,768]{1,0:T(8,128)S(1)} %get-tuple-element.137.refs_0_.refs_4_, bf16[512,768]{1,0:T(8,128)(2,1)S(1)} %get-tuple-element.138.refs_1_.refs_3_, bf16[768,768]{1,0:T(8,128)(2,1)S(1)} %second_weights.1.refs_6_.refs_2_, ...), custom_call_target="tpu_custom_call" | custom-call | flops 1500000000 | bytes 1 | tf_op jit(solution)/shard_map/mlp_out/pallas_call | solution.py:50
  101.6 2.8 %collective-permute-done.25.refs_5_ = bf16[128,768]{1,0:T(8,128)(2,1)S(1)} collective-permute-done((bf16[128,768]{1,0:T(8,128)(2,1)S(1)}, bf16[128,768]{1,0:T(8,128)(2,1)S(1)}, u32[]{:S(2)}, u32[]{:S(2)}) %collective-permute-start.25) | collective-permute-done | bytes 196640 | tf_op jit(solution)/shard_map/ppermute | solution.py:82
  105.4 5.7 %collective-permute-done.26.refs_0_.refs_5_ = bf16[128,768]{1,0:T(8,128)(2,1)S(1)} collective-permute-done((bf16[128,768]{1,0:T(8,128)(2,1)S(1)}, bf16[128,768]{1,0:T(8,128)(2,1)S(1)}, u32[]{:S(2)}, u32[]{:S(2)}) %collective-permute-start.26) | collective-permute-done | bytes 196640 | tf_op jit(solution)/shard_map/ppermute | solution.py:82
  111.1 1.4 collective-permute-done.29.refs_1_
  112.8 4.7 %attention_back.1 = (bf16[512,768]{1,0:T(8,128)(2,1)S(1)}, bf16[512,576]{1,0:T(8,128)(2,1)S(1)}, bf16[256,768]{1,0:T(8,128)(2,1)S(1)}, bf16[256,768]{1,0:T(8,128)(2,1)S(1)}, f32[1,576]{1,0:T(1,128)S(1)}) custom-call(f32[128,768]{1,0:T(8,128)S(1)} %get-tuple-element.146.refs_1_.refs_0_, bf16[2,96,768]{2,1,0:T(8,128)(2,1)S(1)} %get-tuple-element.151.refs_0_.refs_1_, ...), custom_call_target="tpu_custom_call" | custom-call | flops 1 | bytes 1 | tf_op jit(solution)/shard_map/attention_back/pallas_call | solution.py:50
  118.2 1.4 collective-permute-start.35
  119.6 5.3 %collective-permute-done.28.refs_2_ = bf16[128,768]{1,0:T(8,128)(2,1)S(1)} collective-permute-done((bf16[128,768]{1,0:T(8,128)(2,1)S(1)}, bf16[128,768]{1,0:T(8,128)(2,1)S(1)}, u32[]{:S(2)}, u32[]{:S(2)}) %collective-permute-start.28) | collective-permute-done | bytes 196640 | tf_op jit(solution)/shard_map/ppermute | solution.py:82
  125.1 1.9 %attn_weight_grad.1 = (bf16[4,96,768]{2,1,0:T(8,128)(2,1)S(1)}, bf16[4,96,768]{2,1,0:T(8,128)(2,1)S(1)}) custom-call(s32[1]{0:T(128)} %bitcast.1.refs_0_, f32[128,768]{1,0:T(8,128)S(1)} %get-tuple-element.156.refs_2_.refs_1_, bf16[128,768]{1,0:T(8,128)(2,1)S(1)} %output.1.refs_2_, bf16[512,768]{1,0:T(8,128)(2,1)S(1)} %get-tuple-element.118.refs_1_.refs_3_, ...), custom_call_target="tpu_custom_call" | custom-call | flops 6000000000 | bytes 1 | tf_op jit(solution)/shard_map/attn_weight_grad/pallas_call | solution.py:50
  127.0 1.4 collective-permute-start.40
  129.6 5.3 %collective-permute-done.33.refs_3_ = bf16[128,768]{1,0:T(8,128)(2,1)S(1)} collective-permute-done((bf16[128,768]{1,0:T(8,128)(2,1)S(1)}, bf16[128,768]{1,0:T(8,128)(2,1)S(1)}, u32[]{:S(2)}, u32[]{:S(2)}) %collective-permute-start.33) | collective-permute-done | bytes 196640 | tf_op jit(solution)/shard_map/ppermute | solution.py:82
  136.0 1.3 collective-permute-start.36
  141.0 1.3 collective-permute-start.42
  142.4 6.0 %collective-permute-done.39.refs_0_.refs_3_ = bf16[4,16,768]{2,1,0:T(8,128)(2,1)S(1)} collective-permute-done((bf16[4,16,768]{2,1,0:T(8,128)(2,1)S(1)}, bf16[4,16,768]{2,1,0:T(8,128)(2,1)S(1)}, u32[]{:S(2)}, u32[]{:S(2)}) %collective-permute-start.39) | collective-permute-done | bytes 98336 | tf_op jit(solution)/shard_map/ppermute | solution.py:82
  149.2 1.5 collective-permute-start.51
  150.8 1.7 collective-permute-start.43
  153.7 1.6 collective-permute-start.45
  157.2 2.6 %collective-permute-done.51.refs_1_ = bf16[1,96,768]{2,1,0:T(8,128)(2,1)S(1)} collective-permute-done((bf16[1,96,768]{2,1,0:T(8,128)(2,1)S(1)}, bf16[1,96,768]{2,1,0:T(8,128)(2,1)S(1)}, u32[]{:S(2)}, u32[]{:S(2)}) %collective-permute-start.51) | collective-permute-done | bytes 147488 | tf_op jit(solution)/shard_map/ppermute | solution.py:82
  161.6 2.4 %collective-permute-start.50 = (bf16[1,96,768]{2,1,0:T(8,128)(2,1)S(1)}, bf16[1,96,768]{2,1,0:T(8,128)(2,1)S(1)}, u32[]{:S(2)}, u32[]{:S(2)}) collective-permute-start(bf16[1,96,768]{2,1,0:T(8,128)(2,1)S(1)} %get-tuple-element.174.refs_0_), channel_id=1, source_target_pairs={{0,16},{4,20},{8,24},{12,28},{16,0},{20,4},{24,8},{28,12},{1,17},{... | collective-permute-start | bytes 442376 | tf_op jit(solution)/shard_map/ppermute | solution.py:82
  165.4 1.4 collective-permute-start.46
  167.5 1.6 fusion
  169.7 2.0 %collective-permute-start.47 = (f32[2,8,128]{2,1,0:T(8,128)S(1)}, f32[2,8,128]{2,1,0:T(8,128)S(1)}, u32[]{:S(2)}, u32[]{:S(2)}) collective-permute-start(f32[2,8,128]{2,1,0:T(8,128)S(1)} %get-tuple-element.185), channel_id=1, source_target_pairs={{0,8},{4,12},{8,0},{12,4},{16,24},{20,28},{24,16},{28,20},{1,9},{5... | collective-permute-start | bytes 24584 | tf_op jit(solution)/shard_map/ppermute | solution.py:82
  172.7 1.4 collective-permute-start.49
  175.4 2.0 %collective-permute-done.48.refs_3_ = f32[2,8,128]{2,1,0:T(8,128)S(1)} collective-permute-done((f32[2,8,128]{2,1,0:T(8,128)S(1)}, f32[2,8,128]{2,1,0:T(8,128)S(1)}, u32[]{:S(2)}, u32[]{:S(2)}) %collective-permute-start.48) | collective-permute-done | bytes 8224 | tf_op jit(solution)/shard_map/ppermute | solution.py:82
  (161 shorter events, 42.5 us)
Async XLA Ops:
  2.7 11.1 %collective-permute-start = (bf16[96,768]{1,0:T(8,128)(2,1)S(1)}, bf16[96,768]{1,0:T(8,128)(2,1)S(1)}, u32[]{:S(2)}, u32[]{:S(2)}) collective-permute-start(bf16[96,768]{1,0:T(8,128)(2,1)S(1)} %attn_own.1.refs_0_.refs_1_), channel_id=1, source_target_pairs={{0,16},{4,20},{8,24},{12,28},{16,0},{20,4},{24,8},{28,12},{1,17},{... | collective-permute-start | bytes 442376 | tf_op jit(solution)/shard_map/ppermute | solution.py:82
  9.6 5.1 %collective-permute-start.1 = (f32[4,16,128]{2,1,0:T(8,128)S(1)}, f32[4,16,128]{2,1,0:T(8,128)S(1)}, u32[]{:S(2)}, u32[]{:S(2)}) collective-permute-start(f32[4,16,128]{2,1,0:T(8,128)S(1)} %get-tuple-element.105), channel_id=1, source_target_pairs={{0,4},{4,0},{8,12},{12,8},{16,20},{20,16},{24,28},{28,24},{1,5},{5... | collective-permute-start | bytes 98312 | tf_op jit(solution)/shard_map/ppermute | solution.py:82
  13.9 14.6 %collective-permute-start.11 = (bf16[2,96,768]{2,1,0:T(8,128)(2,1)S(1)}, bf16[2,96,768]{2,1,0:T(8,128)(2,1)S(1)}, u32[]{:S(2)}, u32[]{:S(2)}) collective-permute-start(bf16[2,96,768]{2,1,0:T(8,128)(2,1)S(1)} %join.6.refs_0_.refs_1_), channel_id=1, source_target_pairs={{0,8},{4,12},{8,0},{12,4},{16,24},{20,28},{24,16},{28,20},{1,9},{5... | collective-permute-start | bytes 884744 | tf_op jit(solution)/shard_map/ppermute | solution.py:82
  14.7 8.1 %collective-permute-start.2 = (f32[2,16,128]{2,1,0:T(8,128)S(1)}, f32[2,16,128]{2,1,0:T(8,128)S(1)}, u32[]{:S(2)}, u32[]{:S(2)}) collective-permute-start(f32[2,16,128]{2,1,0:T(8,128)S(1)} %get-tuple-element.107), channel_id=1, source_target_pairs={{0,8},{4,12},{8,0},{12,4},{16,24},{20,28},{24,16},{28,20},{1,9},{5... | collective-permute-start | bytes 49160 | tf_op jit(solution)/shard_map/ppermute | solution.py:82
  16.0 6.8 %collective-permute-start.3 = (f32[2,16,128]{2,1,0:T(8,128)S(1)}, f32[2,16,128]{2,1,0:T(8,128)S(1)}, u32[]{:S(2)}, u32[]{:S(2)}) collective-permute-start(f32[2,16,128]{2,1,0:T(8,128)S(1)} %get-tuple-element.108), channel_id=1, source_target_pairs={{0,16},{4,20},{8,24},{12,28},{16,0},{20,4},{24,8},{28,12},{1,17},{... | collective-permute-start | bytes 49160 | tf_op jit(solution)/shard_map/ppermute | solution.py:82
  18.2 7.5 %collective-permute-start.4 = (f32[2,16,128]{2,1,0:T(8,128)S(1)}, f32[2,16,128]{2,1,0:T(8,128)S(1)}, u32[]{:S(2)}, u32[]{:S(2)}) collective-permute-start(f32[2,16,128]{2,1,0:T(8,128)S(1)} %get-tuple-element.109), channel_id=1, source_target_pairs={{0,24},{4,28},{8,16},{12,20},{16,8},{20,12},{24,0},{28,4},{1,25},{... | collective-permute-start | bytes 49160 | tf_op jit(solution)/shard_map/ppermute | solution.py:82
  25.7 19.4 %collective-permute-start.13 = (bf16[256,768]{1,0:T(8,128)(2,1)S(1)}, bf16[256,768]{1,0:T(8,128)(2,1)S(1)}, u32[]{:S(2)}, u32[]{:S(2)}) collective-permute-start(bf16[256,768]{1,0:T(8,128)(2,1)S(1)} %tokens.1.refs_2_.refs_1_.refs_3_.refs_0_), channel_id=1, source_target_pairs={{0,2},{1,3},{2,0},{3,1},{4,6},{5,7},{6,4},{7,5},{8,10},{9,11},{10,... | collective-permute-start | bytes 1179656 | tf_op jit(solution)/shard_map/ppermute | solution.py:82
  28.5 36.9 %collective-permute-start.15 = (bf16[4,96,768]{2,1,0:T(8,128)(2,1)S(1)}, bf16[4,96,768]{2,1,0:T(8,128)(2,1)S(1)}, u32[]{:S(2)}, u32[]{:S(2)}) collective-permute-start(bf16[4,96,768]{2,1,0:T(8,128)(2,1)S(1)} %join.10.refs_1_), channel_id=1, source_target_pairs={{0,4},{4,0},{8,12},{12,8},{16,20},{20,16},{24,28},{28,24},{1,5},{5... | collective-permute-start | bytes 1769480 | tf_op jit(solution)/shard_map/ppermute | solution.py:82
  30.2 14.6 %collective-permute-start.5 = (bf16[4,16,768]{2,1,0:T(8,128)(2,1)S(1)}, bf16[4,16,768]{2,1,0:T(8,128)(2,1)S(1)}, u32[]{:S(2)}, u32[]{:S(2)}) collective-permute-start(bf16[4,16,768]{2,1,0:T(8,128)(2,1)S(1)} %get-tuple-element.111.refs_0_), channel_id=1, source_target_pairs={{0,4},{4,0},{8,12},{12,8},{16,20},{20,16},{24,28},{28,24},{1,5},{5... | collective-permute-start | bytes 294920 | tf_op jit(solution)/shard_map/ppermute | solution.py:82
  30.8 18.8 %collective-permute-start.8 = (bf16[96,768]{1,0:T(8,128)(2,1)S(1)}, bf16[96,768]{1,0:T(8,128)(2,1)S(1)}, u32[]{:S(2)}, u32[]{:S(2)}) collective-permute-start(bf16[96,768]{1,0:T(8,128)(2,1)S(1)} %first_own.1.refs_1_), channel_id=1, source_target_pairs={{0,16},{4,20},{8,24},{12,28},{16,0},{20,4},{24,8},{28,12},{1,17},{... | collective-permute-start | bytes 442376 | tf_op jit(solution)/shard_map/ppermute | solution.py:82
  44.8 4.2 %collective-permute-start.6 = (bf16[2,16,768]{2,1,0:T(8,128)(2,1)S(1)}, bf16[2,16,768]{2,1,0:T(8,128)(2,1)S(1)}, u32[]{:S(2)}, u32[]{:S(2)}) collective-permute-start(bf16[2,16,768]{2,1,0:T(8,128)(2,1)S(1)} %get-tuple-element.113), channel_id=1, source_target_pairs={{0,8},{4,12},{8,0},{12,4},{16,24},{20,28},{24,16},{28,20},{1,9},{5... | collective-permute-start | bytes 147464 | tf_op jit(solution)/shard_map/ppermute | solution.py:82
  45.1 18.0 %collective-permute-start.12 = (bf16[256,768]{1,0:T(8,128)(2,1)S(1)}, bf16[256,768]{1,0:T(8,128)(2,1)S(1)}, u32[]{:S(2)}, u32[]{:S(2)}) collective-permute-start(bf16[256,768]{1,0:T(8,128)(2,1)S(1)} %tokens.1.refs_2_.refs_1_.refs_3_.refs_0_), channel_id=1, source_target_pairs={{0,1},{1,0},{2,3},{3,2},{4,5},{5,4},{6,7},{7,6},{8,9},{9,8},{10,11... | collective-permute-start | bytes 1179656 | tf_op jit(solution)/shard_map/ppermute | solution.py:82
  45.1 18.0 %collective-permute-start.14 = (bf16[256,768]{1,0:T(8,128)(2,1)S(1)}, bf16[256,768]{1,0:T(8,128)(2,1)}, u32[]{:S(2)}, u32[]{:S(2)}) collective-permute-start(bf16[256,768]{1,0:T(8,128)(2,1)S(1)} %collective-permute-done.13.refs_4_.refs_3_.refs_5_), channel_id=1, source_target_pairs={{0,1},{1,0},{2,3},{3,2},{4,5},{5,4},{6,7},{7,6},{8,9},{9,8},{10,11... | collective-permute-start | bytes 1179656 | tf_op jit(solution)/shard_map/ppermute | solution.py:82
  50.2 7.1 %collective-permute-start.9 = (bf16[2,96,768]{2,1,0:T(8,128)(2,1)S(1)}, bf16[2,96,768]{2,1,0:T(8,128)(2,1)}, u32[]{:S(2)}, u32[]{:S(2)}) collective-permute-start(bf16[2,96,768]{2,1,0:T(8,128)(2,1)S(1)} %join.7.refs_1_), channel_id=1, source_target_pairs={{0,8},{4,12},{8,0},{12,4},{16,24},{20,28},{24,16},{28,20},{1,9},{5... | collective-permute-start | bytes 884744 | tf_op jit(solution)/shard_map/ppermute | solution.py:82
  50.5 5.2 %collective-permute-start.7 = (bf16[1,16,768]{2,1,0:T(8,128)(2,1)}, bf16[1,16,768]{2,1,0:T(8,128)(2,1)}, u32[]{:S(2)}, u32[]{:S(2)}) collective-permute-start(bf16[1,16,768]{2,1,0:T(8,128)(2,1)} %get-tuple-element.114.refs_0_), channel_id=1, source_target_pairs={{0,16},{4,20},{8,24},{12,28},{16,0},{20,4},{24,8},{28,12},{1,17},{... | collective-permute-start | bytes 73736 | tf_op jit(solution)/shard_map/ppermute | solution.py:82
  58.3 19.9 %collective-permute-start.18 = (bf16[4,96,768]{2,1,0:T(8,128)(2,1)S(1)}, bf16[4,96,768]{2,1,0:T(8,128)(2,1)S(1)}, u32[]{:S(2)}, u32[]{:S(2)}) collective-permute-start(bf16[4,96,768]{2,1,0:T(8,128)(2,1)S(1)} %join.8.refs_0_.refs_1_), channel_id=1, source_target_pairs={{0,4},{4,0},{8,12},{12,8},{16,20},{20,16},{24,28},{28,24},{1,5},{5... | collective-permute-start | bytes 1769480 | tf_op jit(solution)/shard_map/ppermute | solution.py:82
  61.1 7.7 %collective-permute-start.10 = (bf16[96,768]{1,0:T(8,128)(2,1)S(1)}, bf16[96,768]{1,0:T(8,128)(2,1)S(1)}, u32[]{:S(2)}, u32[]{:S(2)}) collective-permute-start(bf16[96,768]{1,0:T(8,128)(2,1)S(1)} %second_own.1.refs_0_), channel_id=1, source_target_pairs={{0,16},{4,20},{8,24},{12,28},{16,0},{20,4},{24,8},{28,12},{1,17},{... | collective-permute-start | bytes 442376 | tf_op jit(solution)/shard_map/ppermute | solution.py:82
  68.8 8.9 %collective-permute-start.17 = (bf16[2,96,768]{2,1,0:T(8,128)(2,1)S(1)}, bf16[2,96,768]{2,1,0:T(8,128)(2,1)S(1)}, u32[]{:S(2)}, u32[]{:S(2)}) collective-permute-start(bf16[2,96,768]{2,1,0:T(8,128)(2,1)S(1)} %join.9.refs_0_), channel_id=1, source_target_pairs={{0,8},{4,12},{8,0},{12,4},{16,24},{20,28},{24,16},{28,20},{1,9},{5... | collective-permute-start | bytes 884744 | tf_op jit(solution)/shard_map/ppermute | solution.py:82
  70.1 9.5 %collective-permute-start.19 = (bf16[128,768]{1,0:T(8,128)(2,1)S(1)}, bf16[128,768]{1,0:T(8,128)(2,1)S(1)}, u32[]{:S(2)}, u32[]{:S(2)}) collective-permute-start(bf16[128,768]{1,0:T(8,128)(2,1)S(1)} %get-tuple-element.127), channel_id=1, source_target_pairs={{0,2},{1,3},{2,0},{3,1},{4,6},{5,7},{6,4},{7,5},{8,10},{9,11},{10,... | collective-permute-start | bytes 589832 | tf_op jit(solution)/shard_map/ppermute | solution.py:82
  77.8 14.4 %collective-permute-start.23 = (bf16[4,96,768]{2,1,0:T(8,128)(2,1)S(1)}, bf16[4,96,768]{2,1,0:T(8,128)(2,1)S(1)}, u32[]{:S(2)}, u32[]{:S(2)}) collective-permute-start(bf16[4,96,768]{2,1,0:T(8,128)(2,1)S(1)} %join.11.refs_1_), channel_id=1, source_target_pairs={{0,4},{4,0},{8,12},{12,8},{16,20},{20,16},{24,28},{28,24},{1,5},{5... | collective-permute-start | bytes 1769480 | tf_op jit(solution)/shard_map/ppermute | solution.py:82
  79.8 5.7 %collective-permute-start.21 = (bf16[128,768]{1,0:T(8,128)(2,1)S(1)}, bf16[128,768]{1,0:T(8,128)(2,1)S(1)}, u32[]{:S(2)}, u32[]{:S(2)}) collective-permute-start(bf16[128,768]{1,0:T(8,128)(2,1)S(1)} %get-tuple-element.130.refs_0_), channel_id=1, source_target_pairs={{0,2},{1,3},{2,0},{3,1},{4,6},{5,7},{6,4},{7,5},{8,10},{9,11},{10,... | collective-permute-start | bytes 589832 | tf_op jit(solution)/shard_map/ppermute | solution.py:82
  80.4 11.9 %collective-permute-start.20 = (bf16[128,768]{1,0:T(8,128)(2,1)S(1)}, bf16[128,768]{1,0:T(8,128)(2,1)S(1)}, u32[]{:S(2)}, u32[]{:S(2)}) collective-permute-start(bf16[128,768]{1,0:T(8,128)(2,1)S(1)} %get-tuple-element.130.refs_0_), channel_id=1, source_target_pairs={{0,1},{1,0},{2,3},{3,2},{4,5},{5,4},{6,7},{7,6},{8,9},{9,8},{10,11... | collective-permute-start | bytes 589832 | tf_op jit(solution)/shard_map/ppermute | solution.py:82
  85.6 6.7 %collective-permute-start.22 = (bf16[128,768]{1,0:T(8,128)(2,1)S(1)}, bf16[128,768]{1,0:T(8,128)(2,1)S(1)}, u32[]{:S(2)}, u32[]{:S(2)}) collective-permute-start(bf16[128,768]{1,0:T(8,128)(2,1)S(1)} %collective-permute-done.21.refs_2_), channel_id=1, source_target_pairs={{0,1},{1,0},{2,3},{3,2},{4,5},{5,4},{6,7},{7,6},{8,9},{9,8},{10,11... | collective-permute-start | bytes 589832 | tf_op jit(solution)/shard_map/ppermute | solution.py:82
  96.7 15.8 %collective-permute-start.29 = (bf16[4,96,768]{2,1,0:T(8,128)(2,1)S(1)}, bf16[4,96,768]{2,1,0:T(8,128)(2,1)S(1)}, u32[]{:S(2)}, u32[]{:S(2)}) collective-permute-start(bf16[4,96,768]{2,1,0:T(8,128)(2,1)S(1)} %get-tuple-element.150), channel_id=1, source_target_pairs={{0,4},{4,0},{8,12},{12,8},{16,20},{20,16},{24,28},{28,24},{1,5},{5... | collective-permute-start | bytes 1769480 | tf_op jit(solution)/shard_map/ppermute | solution.py:82
  97.3 7.1 %collective-permute-start.25 = (bf16[128,768]{1,0:T(8,128)(2,1)S(1)}, bf16[128,768]{1,0:T(8,128)(2,1)S(1)}, u32[]{:S(2)}, u32[]{:S(2)}) collective-permute-start(bf16[128,768]{1,0:T(8,128)(2,1)S(1)} %get-tuple-element.143), channel_id=1, source_target_pairs={{0,2},{1,3},{2,0},{3,1},{4,6},{5,7},{6,4},{7,5},{8,10},{9,11},{10,... | collective-permute-start | bytes 589832 | tf_op jit(solution)/shard_map/ppermute | solution.py:82
  100.5 12.2 %collective-permute-start.27 = (bf16[256,768]{1,0:T(8,128)(2,1)S(1)}, bf16[256,768]{1,0:T(8,128)(2,1)S(1)}, u32[]{:S(2)}, u32[]{:S(2)}) collective-permute-start(bf16[256,768]{1,0:T(8,128)(2,1)S(1)} %get-tuple-element.140.refs_1_), channel_id=1, source_target_pairs={{0,1},{1,0},{2,3},{3,2},{4,5},{5,4},{6,7},{7,6},{8,9},{9,8},{10,11... | collective-permute-start | bytes 1179656 | tf_op jit(solution)/shard_map/ppermute | solution.py:82
  104.9 6.3 %collective-permute-start.26 = (bf16[128,768]{1,0:T(8,128)(2,1)S(1)}, bf16[128,768]{1,0:T(8,128)(2,1)S(1)}, u32[]{:S(2)}, u32[]{:S(2)}) collective-permute-start(bf16[128,768]{1,0:T(8,128)(2,1)S(1)} %get-tuple-element.144.refs_3_), channel_id=1, source_target_pairs={{0,2},{1,3},{2,0},{3,1},{4,6},{5,7},{6,4},{7,5},{8,10},{9,11},{10,... | collective-permute-start | bytes 589832 | tf_op jit(solution)/shard_map/ppermute | solution.py:82
  105.4 7.4 %collective-permute-start.30 = (bf16[128,768]{1,0:T(8,128)(2,1)S(1)}, bf16[128,768]{1,0:T(8,128)(2,1)S(1)}, u32[]{:S(2)}, u32[]{:S(2)}) collective-permute-start(bf16[128,768]{1,0:T(8,128)(2,1)S(1)} %get-tuple-element.144.refs_3_), channel_id=1, source_target_pairs={{0,1},{1,0},{2,3},{3,2},{4,5},{5,4},{6,7},{7,6},{8,9},{9,8},{10,11... | collective-permute-start | bytes 589832 | tf_op jit(solution)/shard_map/ppermute | solution.py:82
  117.5 7.5 %collective-permute-start.32 = (bf16[256,768]{1,0:T(8,128)(2,1)S(1)}, bf16[256,768]{1,0:T(8,128)(2,1)S(1)}, u32[]{:S(2)}, u32[]{:S(2)}) collective-permute-start(bf16[256,768]{1,0:T(8,128)(2,1)S(1)} %get-tuple-element.155), channel_id=1, source_target_pairs={{0,1},{1,0},{2,3},{3,2},{4,5},{5,4},{6,7},{7,6},{8,9},{9,8},{10,11... | collective-permute-start | bytes 1179656 | tf_op jit(solution)/shard_map/ppermute | solution.py:82
  117.6 7.3 %collective-permute-start.28 = (bf16[128,768]{1,0:T(8,128)(2,1)S(1)}, bf16[128,768]{1,0:T(8,128)(2,1)S(1)}, u32[]{:S(2)}, u32[]{:S(2)}) collective-permute-start(bf16[128,768]{1,0:T(8,128)(2,1)S(1)} %get-tuple-element.147), channel_id=1, source_target_pairs={{0,2},{1,3},{2,0},{3,1},{4,6},{5,7},{6,4},{7,5},{8,10},{9,11},{10,... | collective-permute-start | bytes 589832 | tf_op jit(solution)/shard_map/ppermute | solution.py:82
  118.2 17.8 %collective-permute-start.35 = (bf16[4,96,768]{2,1,0:T(8,128)(2,1)S(1)}, bf16[4,96,768]{2,1,0:T(8,128)(2,1)S(1)}, u32[]{:S(2)}, u32[]{:S(2)}) collective-permute-start(bf16[4,96,768]{2,1,0:T(8,128)(2,1)S(1)} %second_sent.1.refs_2_), channel_id=1, source_target_pairs={{0,4},{4,0},{8,12},{12,8},{16,20},{20,16},{24,28},{28,24},{1,5},{5... | collective-permute-start | bytes 1769480 | tf_op jit(solution)/shard_map/ppermute | solution.py:82
  127.0 21.3 %collective-permute-start.40 = (bf16[4,96,768]{2,1,0:T(8,128)(2,1)S(1)}, bf16[4,96,768]{2,1,0:T(8,128)(2,1)S(1)}, u32[]{:S(2)}, u32[]{:S(2)}) collective-permute-start(bf16[4,96,768]{2,1,0:T(8,128)(2,1)S(1)} %get-tuple-element.171), channel_id=1, source_target_pairs={{0,4},{4,0},{8,12},{12,8},{16,20},{20,16},{24,28},{28,24},{1,5},{5... | collective-permute-start | bytes 1769480 | tf_op jit(solution)/shard_map/ppermute | solution.py:82
  128.4 9.0 %collective-permute-start.34 = (bf16[2,96,768]{2,1,0:T(8,128)(2,1)S(1)}, bf16[2,96,768]{2,1,0:T(8,128)(2,1)S(1)}, u32[]{:S(2)}, u32[]{:S(2)}) collective-permute-start(bf16[2,96,768]{2,1,0:T(8,128)(2,1)S(1)} %get-tuple-element.151.refs_0_.refs_1_), channel_id=1, source_target_pairs={{0,8},{4,12},{8,0},{12,4},{16,24},{20,28},{24,16},{28,20},{1,9},{5... | collective-permute-start | bytes 884744 | tf_op jit(solution)/shard_map/ppermute | solution.py:82
  129.1 5.8 %collective-permute-start.33 = (bf16[128,768]{1,0:T(8,128)(2,1)S(1)}, bf16[128,768]{1,0:T(8,128)(2,1)S(1)}, u32[]{:S(2)}, u32[]{:S(2)}) collective-permute-start(bf16[128,768]{1,0:T(8,128)(2,1)S(1)} %get-tuple-element.157), channel_id=1, source_target_pairs={{0,2},{1,3},{2,0},{3,1},{4,6},{5,7},{6,4},{7,5},{8,10},{9,11},{10,... | collective-permute-start | bytes 589832 | tf_op jit(solution)/shard_map/ppermute | solution.py:82
  135.4 3.9 %collective-permute-start.37 = (bf16[16,768]{1,0:T(8,128)(2,1)S(1)}, bf16[16,768]{1,0:T(8,128)(2,1)S(1)}, u32[]{:S(2)}, u32[]{:S(2)}) collective-permute-start(bf16[16,768]{1,0:T(8,128)(2,1)S(1)} %get-tuple-element.162.refs_0_.refs_4_), channel_id=1, source_target_pairs={{0,2},{1,3},{2,0},{3,1},{4,6},{5,7},{6,4},{7,5},{8,10},{9,11},{10,... | collective-permute-start | bytes 73736 | tf_op jit(solution)/shard_map/ppermute | solution.py:82
  140.2 8.2 %collective-permute-start.39 = (bf16[4,16,768]{2,1,0:T(8,128)(2,1)S(1)}, bf16[4,16,768]{2,1,0:T(8,128)(2,1)S(1)}, u32[]{:S(2)}, u32[]{:S(2)}) collective-permute-start(bf16[4,16,768]{2,1,0:T(8,128)(2,1)S(1)} %get-tuple-element.166), channel_id=1, source_target_pairs={{0,4},{4,0},{8,12},{12,8},{16,20},{20,16},{24,28},{28,24},{1,5},{5... | collective-permute-start | bytes 294920 | tf_op jit(solution)/shard_map/ppermute | solution.py:82
  141.0 9.7 %collective-permute-start.42 = (bf16[2,96,768]{2,1,0:T(8,128)(2,1)S(1)}, bf16[2,96,768]{2,1,0:T(8,128)(2,1)S(1)}, u32[]{:S(2)}, u32[]{:S(2)}) collective-permute-start(bf16[2,96,768]{2,1,0:T(8,128)(2,1)S(1)} %get-tuple-element.165.refs_3_), channel_id=1, source_target_pairs={{0,8},{4,12},{8,0},{12,4},{16,24},{20,28},{24,16},{28,20},{1,9},{5... | collective-permute-start | bytes 884744 | tf_op jit(solution)/shard_map/ppermute | solution.py:82
  148.5 13.1 %collective-permute-start.41 = (bf16[2,96,768]{2,1,0:T(8,128)(2,1)S(1)}, bf16[2,96,768]{2,1,0:T(8,128)(2,1)S(1)}, u32[]{:S(2)}, u32[]{:S(2)}) collective-permute-start(bf16[2,96,768]{2,1,0:T(8,128)(2,1)S(1)} %get-tuple-element.173.refs_0_), channel_id=1, source_target_pairs={{0,8},{4,12},{8,0},{12,4},{16,24},{20,28},{24,16},{28,20},{1,9},{5... | collective-permute-start | bytes 884744 | tf_op jit(solution)/shard_map/ppermute | solution.py:82
  149.2 10.5 %collective-permute-start.51 = (bf16[1,96,768]{2,1,0:T(8,128)(2,1)S(1)}, bf16[1,96,768]{2,1,0:T(8,128)(2,1)S(1)}, u32[]{:S(2)}, u32[]{:S(2)}) collective-permute-start(bf16[1,96,768]{2,1,0:T(8,128)(2,1)S(1)} %get-tuple-element.164.refs_2_), channel_id=1, source_target_pairs={{0,16},{4,20},{8,24},{12,28},{16,0},{20,4},{24,8},{28,12},{1,17},{... | collective-permute-start | bytes 442376 | tf_op jit(solution)/shard_map/ppermute | solution.py:82
  150.8 13.2 %collective-permute-start.43 = (bf16[2,16,768]{2,1,0:T(8,128)(2,1)S(1)}, bf16[2,16,768]{2,1,0:T(8,128)(2,1)S(1)}, u32[]{:S(2)}, u32[]{:S(2)}) collective-permute-start(bf16[2,16,768]{2,1,0:T(8,128)(2,1)S(1)} %get-tuple-element.179), channel_id=1, source_target_pairs={{0,8},{4,12},{8,0},{12,4},{16,24},{20,28},{24,16},{28,20},{1,9},{5... | collective-permute-start | bytes 147464 | tf_op jit(solution)/shard_map/ppermute | solution.py:82
  152.5 11.5 %collective-permute-start.44 = (bf16[2,16,768]{2,1,0:T(8,128)(2,1)S(1)}, bf16[2,16,768]{2,1,0:T(8,128)(2,1)S(1)}, u32[]{:S(2)}, u32[]{:S(2)}) collective-permute-start(bf16[2,16,768]{2,1,0:T(8,128)(2,1)S(1)} %get-tuple-element.180), channel_id=1, source_target_pairs={{0,16},{4,20},{8,24},{12,28},{16,0},{20,4},{24,8},{28,12},{1,17},{... | collective-permute-start | bytes 147464 | tf_op jit(solution)/shard_map/ppermute | solution.py:82
  153.7 11.3 %collective-permute-start.45 = (bf16[2,16,768]{2,1,0:T(8,128)(2,1)S(1)}, bf16[2,16,768]{2,1,0:T(8,128)(2,1)S(1)}, u32[]{:S(2)}, u32[]{:S(2)}) collective-permute-start(bf16[2,16,768]{2,1,0:T(8,128)(2,1)S(1)} %get-tuple-element.181), channel_id=1, source_target_pairs={{0,24},{4,28},{8,16},{12,20},{16,8},{20,12},{24,0},{28,4},{1,25},{... | collective-permute-start | bytes 147464 | tf_op jit(solution)/shard_map/ppermute | solution.py:82
  161.6 17.3 %collective-permute-start.50 = (bf16[1,96,768]{2,1,0:T(8,128)(2,1)S(1)}, bf16[1,96,768]{2,1,0:T(8,128)(2,1)S(1)}, u32[]{:S(2)}, u32[]{:S(2)}) collective-permute-start(bf16[1,96,768]{2,1,0:T(8,128)(2,1)S(1)} %get-tuple-element.174.refs_0_), channel_id=1, source_target_pairs={{0,16},{4,20},{8,24},{12,28},{16,0},{20,4},{24,8},{28,12},{1,17},{... | collective-permute-start | bytes 442376 | tf_op jit(solution)/shard_map/ppermute | solution.py:82
  165.4 4.2 %collective-permute-start.46 = (f32[4,8,128]{2,1,0:T(8,128)S(1)}, f32[4,8,128]{2,1,0:T(8,128)S(1)}, u32[]{:S(2)}, u32[]{:S(2)}) collective-permute-start(f32[4,8,128]{2,1,0:T(8,128)S(1)} %get-tuple-element.183.refs_0_), channel_id=1, source_target_pairs={{0,4},{4,0},{8,12},{12,8},{16,20},{20,16},{24,28},{28,24},{1,5},{5... | collective-permute-start | bytes 49160 | tf_op jit(solution)/shard_map/ppermute | solution.py:82
  167.4 12.3 %collective-permute-start.52 = (bf16[1,96,768]{2,1,0:T(8,128)(2,1)S(1)}, bf16[1,96,768]{2,1,0:T(8,128)(2,1)S(1)}, u32[]{:S(2)}, u32[]{:S(2)}) collective-permute-start(bf16[1,96,768]{2,1,0:T(8,128)(2,1)S(1)} %second_last.1), channel_id=1, source_target_pairs={{0,16},{4,20},{8,24},{12,28},{16,0},{20,4},{24,8},{28,12},{1,17},{... | collective-permute-start | bytes 442376 | tf_op jit(solution)/shard_map/ppermute | solution.py:82
  169.7 5.8 %collective-permute-start.47 = (f32[2,8,128]{2,1,0:T(8,128)S(1)}, f32[2,8,128]{2,1,0:T(8,128)S(1)}, u32[]{:S(2)}, u32[]{:S(2)}) collective-permute-start(f32[2,8,128]{2,1,0:T(8,128)S(1)} %get-tuple-element.185), channel_id=1, source_target_pairs={{0,8},{4,12},{8,0},{12,4},{16,24},{20,28},{24,16},{28,20},{1,9},{5... | collective-permute-start | bytes 24584 | tf_op jit(solution)/shard_map/ppermute | solution.py:82
  171.6 5.8 %collective-permute-start.48 = (f32[2,8,128]{2,1,0:T(8,128)S(1)}, f32[2,8,128]{2,1,0:T(8,128)S(1)}, u32[]{:S(2)}, u32[]{:S(2)}) collective-permute-start(f32[2,8,128]{2,1,0:T(8,128)S(1)} %get-tuple-element.186), channel_id=1, source_target_pairs={{0,16},{4,20},{8,24},{12,28},{16,0},{20,4},{24,8},{28,12},{1,17},{... | collective-permute-start | bytes 24584 | tf_op jit(solution)/shard_map/ppermute | solution.py:82
  172.7 5.4 %collective-permute-start.49 = (f32[2,8,128]{2,1,0:T(8,128)S(1)}, f32[2,8,128]{2,1,0:T(8,128)S(1)}, u32[]{:S(2)}, u32[]{:S(2)}) collective-permute-start(f32[2,8,128]{2,1,0:T(8,128)S(1)} %get-tuple-element.187), channel_id=1, source_target_pairs={{0,24},{4,28},{8,16},{12,20},{16,8},{20,12},{24,0},{28,4},{1,25},{... | collective-permute-start | bytes 24584 | tf_op jit(solution)/shard_map/ppermute | solution.py:82
  (23 other events, 133.0 us)
